TPU v7x, 32 devices: a whole 2x2x4 slice. The times are simulated.
32 devices in a mesh: leaf: 4 (over z), clusters: 8 (over y, x, core).
Axes of the slice: x: 2, y: 2, z: 4, core: 2. Of those that a mesh axis runs over, the one named last changes fastest.
Arguments:
- samples: float32 [16384, 256], P(('clusters', 'leaf')), may hold values from -6 to 6
- probes: float32 [16384, 256], P(('clusters', 'leaf')), may hold values from -6 to 6
- near_blocks: float32 [16384, 2, 512], P(('clusters', 'leaf')), may hold values from -0.15625 to 0.15625
- couplings: float32 [8, 3, 2, 128, 128], P('clusters'), may hold values from -0.375 to 0.375
- node_slot: int32 [8, 3], P('clusters'), may hold values from 0 to 2, each once within a row
Outputs:
- leaf_bases: float32 [16384, 128], P(('clusters', 'leaf'))
- transfer_bases: float32 [32, 2, 256, 128], P(('clusters', 'leaf'))
- top_samples: float32 [8, 128, 256], P('clusters')
- top_probes: float32 [8, 128, 256], P('clusters')
Inputs may be any that keep to these rules, and one draw needn't show every extreme that they name: Every row of node_slot names each of 0 to 2 exactly once.
All inputs are finite; a program needn't handle non-finite values.
Results may differ from a plain program's by a relative error of at most 0.00016.
Values sent between devices are 32-bit elements; how exact they have to be, the bound alone decides.
No kernel may reach another device: no remote copies, remote signals or barrier semaphores. Data moves between devices by JAX's collectives and lax.ppermute only.
A program may use at most 64 MiB of HBM per device.

v0:
```python
import jax
import jax.numpy as jnp
from jax import lax
from jax.sharding import PartitionSpec as P

full_precision = lax.Precision.HIGHEST


def shifted(value, axis, by):
    peers = lax.axis_size(axis)
    return lax.ppermute(value, axis, [(i, (i + by) % peers) for i in range(peers)])


def shifted_2(value, axis, by):
    peers = lax.axis_size(axis)
    pairs = [(i, i + by) for i in range(peers) if 0 <= i + by < peers]
    return lax.ppermute(value, axis, pairs)


def from_partner(value, axis, stride):
    mask = 2**stride
    pairs = [(source, source ^ mask) for source in range(lax.axis_size(axis))]
    return lax.ppermute(value, axis, pairs)


def orthonormal(tall_block):
    gram_matrix = jnp.einsum("...rk,...rj->...kj", tall_block, tall_block, precision=full_precision)
    lower_factor = jnp.linalg.cholesky(gram_matrix)
    flipped = jax.scipy.linalg.solve_triangular(
        lower_factor, jnp.swapaxes(tall_block, -1, -2), lower=True
    )
    return jnp.swapaxes(flipped, -1, -2)


def project(node_basis, target):
    return jnp.einsum("...rk,...rs->...ks", node_basis, target, precision=full_precision)


def far_from_left(values, stride, subtree, member):
    if stride < subtree:
        inside = shifted(values, "leaf", stride)
        across = shifted_2(inside, "clusters", 1)
        return jnp.where(member < stride, across, inside)
    return shifted_2(values, "clusters", stride // subtree)


def far_from_right(values, stride, subtree, member):
    if stride < subtree:
        inside = shifted(values, "leaf", -stride)
        across = shifted_2(inside, "clusters", -1)
        return jnp.where(member >= subtree - stride, across, inside)
    return shifted_2(values, "clusters", -(stride // subtree))


def body(samples, probes, near_blocks, couplings, node_slot):
    columns = couplings.shape[-1]
    subtree = lax.axis_size("leaf")
    levels = subtree.bit_length() - 1
    member = lax.axis_index("leaf")
    diag_block = near_blocks[:, 0, :]
    upper_block = near_blocks[:, 1, :]
    handed = jnp.einsum("nm,ns->ms", upper_block, probes, precision=full_precision)
    lower_inner = shifted(handed, "leaf", 1)
    lower_outer = shifted_2(lower_inner, "clusters", 1)
    from_lower = jnp.where(member == 0, lower_outer, lower_inner)
    upper_inner = shifted(probes, "leaf", -1)
    upper_outer = shifted_2(upper_inner, "clusters", -1)
    from_upper = jnp.where(member == subtree - 1, upper_outer, upper_inner)
    diag_term = jnp.dot(
        diag_block, probes, precision=full_precision, preferred_element_type=jnp.float32
    )
    upper_term = jnp.dot(
        upper_block, from_upper, precision=full_precision, preferred_element_type=jnp.float32
    )
    far_samples = samples - diag_term - upper_term - from_lower
    leaf_basis = orthonormal(far_samples[:, :columns])
    sample_coef = project(leaf_basis, far_samples)
    probe_coef = project(leaf_basis, probes)
    slot_row = node_slot[0]
    coupling_table = couplings[0]
    ancestors = []
    for level_index in range(1, levels + 1):
        stride = 2**level_index
        from_left = far_from_left(probe_coef, stride, subtree, member)
        from_right = far_from_right(probe_coef, stride, subtree, member)
        parity = member >> level_index - 1 & 1
        main_far = jnp.where(parity == 0, from_left, from_right)
        other_far = jnp.where(parity == 0, from_right, from_left)
        node_index = subtree - (subtree >> level_index - 1) + (member >> level_index)
        slot_index = lax.dynamic_index_in_dim(slot_row, node_index, 0, keepdims=False)
        coupling_pair = lax.dynamic_index_in_dim(coupling_table, slot_index, 0, keepdims=False)
        coupling = lax.dynamic_index_in_dim(coupling_pair, parity, 0, keepdims=False)
        main_term = jnp.dot(
            coupling, main_far, precision=full_precision, preferred_element_type=jnp.float32
        )
        other_term = jnp.dot(
            coupling.T, other_far, precision=full_precision, preferred_element_type=jnp.float32
        )
        corrected = sample_coef - main_term - other_term
        sibling_samples, sibling_probes = from_partner(
            (corrected, probe_coef), "leaf", level_index - 1
        )
        lower_first = parity == 0
        stacked = jnp.where(
            lower_first,
            jnp.concatenate([corrected, sibling_samples], axis=0),
            jnp.concatenate([sibling_samples, corrected], axis=0),
        )
        stacked_probes = jnp.where(
            lower_first,
            jnp.concatenate([probe_coef, sibling_probes], axis=0),
            jnp.concatenate([sibling_probes, probe_coef], axis=0),
        )
        node_basis = orthonormal(stacked[:, :columns])
        ancestors.append(node_basis)
        sample_coef = project(node_basis, stacked)
        probe_coef = project(node_basis, stacked_probes)
    transfer_bases = jnp.stack(ancestors, axis=0)[None]
    return (leaf_basis, transfer_bases, sample_coef[None], probe_coef[None])


def solution(mesh):
    in_specs = (
        P(("clusters", "leaf"), None),
        P(("clusters", "leaf"), None),
        P(("clusters", "leaf"), None, None),
        P("clusters", None, None, None, None),
        P("clusters", None),
    )
    out_specs = (
        P(("clusters", "leaf"), None),
        P(("clusters", "leaf"), None, None, None),
        P("clusters", None, None),
        P("clusters", None, None),
    )
    return jax.shard_map(body, mesh=mesh, in_specs=in_specs, out_specs=out_specs, check_vma=False)
```

profile of v0, /device:TPU:4, one launch (start us, length us, event | category | flops | bytes accessed | tf_op | source)
XLA Modules:
  0.0 168.8 jit_solution(8206383594285124936)
XLA Ops:
  0.7 4.1 %fusion.71 = (f32[512,1,512]{2,1,0:T(1,128)S(1)}, f32[512,1,512]{2,1,0:T(1,128)S(1)}) fusion(f32[512,2,512]{2,1,0:T(2,128)} %param.10), kind=kLoop, calls=%fused_computation.99 | loop fusion | bytes 4194304 | tf_op jit(solution)/shard_map/slice | solution.py:61
  8.2 2.2 %collective-permute-start = (f32[512,256]{1,0:T(8,128)S(1)}, f32[512,256]{1,0:T(8,128)}, u32[]{:S(2)}, u32[]{:S(2)}) collective-permute-start(f32[512,256]{1,0:T(8,128)S(1)} %copy-done.1), channel_id=1, source_target_pairs={{0,24},{8,0},{16,8},{24,16},{1,25},{9,1},{17,9},{25,17},{2,26},{10... | collective-permute-start | bytes 1572872 | tf_op jit(solution)/shard_map/ppermute | solution.py:11
  10.5 12.9 %collective-permute-done.2 = f32[512,256]{1,0:T(8,128)} collective-permute-done((f32[512,256]{1,0:T(8,128)S(1)}, f32[512,256]{1,0:T(8,128)}, u32[]{:S(2)}, u32[]{:S(2)}) %collective-permute-start.2) | collective-permute-done | bytes 524320 | tf_op jit(solution)/shard_map/ppermute | solution.py:11
  23.4 1.9 %collective-permute-start.3 = (f32[512,256]{1,0:T(8,128)}, f32[512,256]{1,0:T(8,128)}, u32[]{:S(2)}, u32[]{:S(2)}) collective-permute-start(f32[512,256]{1,0:T(8,128)} %collective-permute-done.2), channel_id=1, source_target_pairs={{0,1},{1,2},{2,3},{3,4},{4,5},{5,6},{6,7},{8,9},{9,10},{10,11},{11... | collective-permute-start | bytes 1572872 | tf_op jit(solution)/shard_map/ppermute | solution.py:17
  25.3 7.6 %collective-permute-done = f32[512,256]{1,0:T(8,128)} collective-permute-done((f32[512,256]{1,0:T(8,128)S(1)}, f32[512,256]{1,0:T(8,128)}, u32[]{:S(2)}, u32[]{:S(2)}) %collective-permute-start) | collective-permute-done | bytes 524320 | tf_op jit(solution)/shard_map/ppermute | solution.py:11
  33.0 2.5 %collective-permute-start.1 = (f32[512,256]{1,0:T(8,128)}, f32[512,256]{1,0:T(8,128)}, u32[]{:S(2)}, u32[]{:S(2)}) collective-permute-start(f32[512,256]{1,0:T(8,128)} %collective-permute-done), channel_id=1, source_target_pairs={{1,0},{2,1},{3,2},{4,3},{5,4},{6,5},{7,6},{9,8},{10,9},{11,10},{12... | collective-permute-start | bytes 1572872 | tf_op jit(solution)/shard_map/ppermute | solution.py:17
  36.5 5.8 %collective-permute-done.1 = f32[512,256]{1,0:T(8,128)} collective-permute-done((f32[512,256]{1,0:T(8,128)}, f32[512,256]{1,0:T(8,128)}, u32[]{:S(2)}, u32[]{:S(2)}) %collective-permute-start.1) | collective-permute-done | bytes 524320 | tf_op jit(solution)/shard_map/ppermute | solution.py:17
  42.3 2.2 %fusion.1 = f32[512,256]{1,0:T(8,128)S(1)} fusion(f32[512,256]{1,0:T(8,128)S(1)} %convolution_subtract_fusion, f32[512,1,512]{2,1,0:T(1,128)S(1)} %get-tuple-element.14, f32[512,256]{1,0:T(8,128)} %collective-permute-done.3, f32[512,256]{1,0:T(8,128)} %collective-permute-done.2, f32[512,256]{1,0:T(8,128)} %collective-permute-done.1, ...), kind=kOutput, calls=%fused_computation.3 | convolution fusion | flops 805830656 | bytes 4194306 | tf_op jit(solution)/shard_map/dot_general | solution.py:72
  45.2 11.7 %cholesky.59 = f32[128,128]{1,0:T(8,128)S(1)} custom-call(f32[128,128]{1,0:T(8,128)S(1)} %fusion.56), custom_call_target="Cholesky" | custom-call | tf_op jit(solution)/shard_map/jit(cholesky)/cholesky | solution.py:28
  58.3 9.8 %custom-call.9 = f32[1,128,128]{1,2,0:T(8,128)S(1)} custom-call(f32[1,128,128]{2,1,0:T(8,128)S(1)} %fusion.44), custom_call_target="InvertDiagBlocksLowerTriangular" | custom-call | tf_op jit(solution)/shard_map/jit(_solve_triangular)/triangular_solve | solution.py:29
  68.9 7.5 %collective-permute-start.4 = (f32[128,256]{1,0:T(8,128)S(1)}, f32[128,256]{1,0:T(8,128)S(1)}, u32[]{:S(2)}, u32[]{:S(2)}) collective-permute-start(f32[128,256]{1,0:T(8,128)S(1)} %fusion.73), channel_id=1, source_target_pairs={{0,16},{8,24},{16,0},{24,8},{1,17},{9,25},{17,1},{25,9},{2,18},{10... | collective-permute-start | bytes 393224 | tf_op jit(solution)/shard_map/ppermute | solution.py:11
  78.9 3.1 %collective-permute-done.4 = f32[128,256]{1,0:T(8,128)S(1)} collective-permute-done((f32[128,256]{1,0:T(8,128)S(1)}, f32[128,256]{1,0:T(8,128)S(1)}, u32[]{:S(2)}, u32[]{:S(2)}) %collective-permute-start.4) | collective-permute-done | bytes 131104 | tf_op jit(solution)/shard_map/ppermute | solution.py:11
  82.1 1.9 %collective-permute-start.5 = (f32[128,256]{1,0:T(8,128)S(1)}, f32[128,256]{1,0:T(8,128)S(1)}, u32[]{:S(2)}, u32[]{:S(2)}) collective-permute-start(f32[128,256]{1,0:T(8,128)S(1)} %collective-permute-done.4), channel_id=1, source_target_pairs={{0,1},{1,2},{2,3},{3,4},{4,5},{5,6},{6,7},{8,9},{9,10},{10,11},{11... | collective-permute-start | bytes 393224 | tf_op jit(solution)/shard_map/ppermute | solution.py:17
  84.0 4.8 %collective-permute-start.6 = (f32[128,256]{1,0:T(8,128)S(1)}, f32[128,256]{1,0:T(8,128)S(1)}, u32[]{:S(2)}, u32[]{:S(2)}) collective-permute-start(f32[128,256]{1,0:T(8,128)S(1)} %collective-permute-done.4), channel_id=1, source_target_pairs={{1,0},{2,1},{3,2},{4,3},{5,4},{6,5},{7,6},{9,8},{10,9},{11,10},{12... | collective-permute-start | bytes 393224 | tf_op jit(solution)/shard_map/ppermute | solution.py:17
  93.7 3.1 %collective-permute-done.7 = f32[128,256]{1,0:T(8,128)S(1)} collective-permute-done((f32[128,256]{1,0:T(8,128)S(1)}, f32[128,256]{1,0:T(8,128)S(1)}, u32[]{:S(2)}, u32[]{:S(2)}) %collective-permute-start.7) | collective-permute-done | bytes 131104 | tf_op jit(solution)/shard_map/ppermute | solution.py:23
  97.4 11.7 %cholesky.70 = f32[128,128]{1,0:T(8,128)S(1)} custom-call(f32[128,128]{1,0:T(8,128)S(1)} %fusion.52), custom_call_target="Cholesky" | custom-call | tf_op jit(solution)/shard_map/jit(cholesky)/cholesky | solution.py:28
  110.4 9.8 %custom-call.11 = f32[1,128,128]{1,2,0:T(8,128)S(1)} custom-call(f32[1,128,128]{2,1,0:T(8,128)S(1)} %fusion.45), custom_call_target="InvertDiagBlocksLowerTriangular" | custom-call | tf_op jit(solution)/shard_map/jit(_solve_triangular)/triangular_solve | solution.py:29
  120.9 4.7 %collective-permute-start.10 = (f32[128,256]{1,0:T(8,128)S(1)}, f32[128,256]{1,0:T(8,128)S(1)}, u32[]{:S(2)}, u32[]{:S(2)}) collective-permute-start(f32[128,256]{1,0:T(8,128)S(1)} %fusion.5), channel_id=1, source_target_pairs={{1,0},{2,1},{3,2},{4,3},{5,4},{6,5},{7,6},{9,8},{10,9},{11,10},{12... | collective-permute-start | bytes 393224 | tf_op jit(solution)/shard_map/ppermute | solution.py:17
  125.6 2.2 %collective-permute-start.9 = (f32[128,256]{1,0:T(8,128)S(1)}, f32[128,256]{1,0:T(8,128)S(1)}, u32[]{:S(2)}, u32[]{:S(2)}) collective-permute-start(f32[128,256]{1,0:T(8,128)S(1)} %fusion.5), channel_id=1, source_target_pairs={{0,1},{1,2},{2,3},{3,4},{4,5},{5,6},{6,7},{8,9},{9,10},{10,11},{11... | collective-permute-start | bytes 393224 | tf_op jit(solution)/shard_map/ppermute | solution.py:17
  129.7 3.0 %collective-permute-done.9 = f32[128,256]{1,0:T(8,128)S(1)} collective-permute-done((f32[128,256]{1,0:T(8,128)S(1)}, f32[128,256]{1,0:T(8,128)S(1)}, u32[]{:S(2)}, u32[]{:S(2)}) %collective-permute-start.9) | collective-permute-done | bytes 131104 | tf_op jit(solution)/shard_map/ppermute | solution.py:17
  133.7 2.9 %collective-permute-start.11 = (f32[128,256]{1,0:T(8,128)S(1)}, f32[128,256]{1,0:T(8,128)S(1)}, u32[]{:S(2)}, u32[]{:S(2)}) collective-permute-start(f32[128,256]{1,0:T(8,128)S(1)} %fusion.2), channel_id=1, source_target_pairs={{0,16},{8,24},{16,0},{24,8},{1,17},{9,25},{17,1},{25,9},{2,18},{10... | collective-permute-start | bytes 393224 | tf_op jit(solution)/shard_map/ppermute | solution.py:23
  137.5 4.8 %collective-permute-done.11 = f32[128,256]{1,0:T(8,128)S(1)} collective-permute-done((f32[128,256]{1,0:T(8,128)S(1)}, f32[128,256]{1,0:T(8,128)S(1)}, u32[]{:S(2)}, u32[]{:S(2)}) %collective-permute-start.11) | collective-permute-done | bytes 131104 | tf_op jit(solution)/shard_map/ppermute | solution.py:23
  142.8 11.7 %cholesky.81 = f32[128,128]{1,0:T(8,128)S(1)} custom-call(f32[128,128]{1,0:T(8,128)S(1)} %fusion.48), custom_call_target="Cholesky" | custom-call | tf_op jit(solution)/shard_map/jit(cholesky)/cholesky | solution.py:28
  155.9 9.8 %custom-call.12 = f32[1,128,128]{1,2,0:T(8,128)S(1)} custom-call(f32[1,128,128]{2,1,0:T(8,128)S(1)} %fusion.46), custom_call_target="InvertDiagBlocksLowerTriangular" | custom-call | tf_op jit(solution)/shard_map/jit(_solve_triangular)/triangular_solve | solution.py:29
  (57 shorter events, 21.9 us)
Async XLA Ops:
  0.6 90.4 %copy-start = (f32[1,3,2,128,128]{4,3,2,1,0:T(8,128)S(1)}, f32[1,3,2,128,128]{4,3,2,1,0:T(8,128)}, u32[]{:S(2)}) copy-start(f32[1,3,2,128,128]{4,3,2,1,0:T(8,128)} %param.11) | copy-start | bytes 1179652
  0.6 4.1 %copy-start.1 = (f32[512,256]{1,0:T(8,128)S(1)}, f32[512,256]{1,0:T(8,128)}, u32[]{:S(2)}) copy-start(f32[512,256]{1,0:T(8,128)} %param.9) | copy-start | bytes 1572868
  4.8 30.7 %copy-start.2 = (f32[512,256]{1,0:T(8,128)S(1)}, f32[512,256]{1,0:T(8,128)}, u32[]{:S(2)}) copy-start(f32[512,256]{1,0:T(8,128)} %param.8) | copy-start | bytes 1572868
  6.6 16.8 %collective-permute-start.2 = (f32[512,256]{1,0:T(8,128)S(1)}, f32[512,256]{1,0:T(8,128)}, u32[]{:S(2)}, u32[]{:S(2)}) collective-permute-start(f32[512,256]{1,0:T(8,128)S(1)} %fusion.3), channel_id=1, source_target_pairs={{0,8},{8,16},{16,24},{24,0},{1,9},{9,17},{17,25},{25,1},{2,10},{10... | collective-permute-start | bytes 1572872 | tf_op jit(solution)/shard_map/ppermute | solution.py:11
  8.2 24.7 %collective-permute-start = (f32[512,256]{1,0:T(8,128)S(1)}, f32[512,256]{1,0:T(8,128)}, u32[]{:S(2)}, u32[]{:S(2)}) collective-permute-start(f32[512,256]{1,0:T(8,128)S(1)} %copy-done.1), channel_id=1, source_target_pairs={{0,24},{8,0},{16,8},{24,16},{1,25},{9,1},{17,9},{25,17},{2,26},{10... | collective-permute-start | bytes 1572872 | tf_op jit(solution)/shard_map/ppermute | solution.py:11
  23.4 13.1 %collective-permute-start.3 = (f32[512,256]{1,0:T(8,128)}, f32[512,256]{1,0:T(8,128)}, u32[]{:S(2)}, u32[]{:S(2)}) collective-permute-start(f32[512,256]{1,0:T(8,128)} %collective-permute-done.2), channel_id=1, source_target_pairs={{0,1},{1,2},{2,3},{3,4},{4,5},{5,6},{6,7},{8,9},{9,10},{10,11},{11... | collective-permute-start | bytes 1572872 | tf_op jit(solution)/shard_map/ppermute | solution.py:17
  33.0 9.3 %collective-permute-start.1 = (f32[512,256]{1,0:T(8,128)}, f32[512,256]{1,0:T(8,128)}, u32[]{:S(2)}, u32[]{:S(2)}) collective-permute-start(f32[512,256]{1,0:T(8,128)} %collective-permute-done), channel_id=1, source_target_pairs={{1,0},{2,1},{3,2},{4,3},{5,4},{6,5},{7,6},{9,8},{10,9},{11,10},{12... | collective-permute-start | bytes 1572872 | tf_op jit(solution)/shard_map/ppermute | solution.py:17
  44.5 31.9 %copy-start.3 = (s32[1,3]{1,0:T(1,128)S(1)}, s32[1,3]{1,0:T(1,128)}, u32[]{:S(2)}) copy-start(s32[1,3]{1,0:T(1,128)} %param.12) | copy-start | bytes 40
  68.9 13.1 %collective-permute-start.4 = (f32[128,256]{1,0:T(8,128)S(1)}, f32[128,256]{1,0:T(8,128)S(1)}, u32[]{:S(2)}, u32[]{:S(2)}) collective-permute-start(f32[128,256]{1,0:T(8,128)S(1)} %fusion.73), channel_id=1, source_target_pairs={{0,16},{8,24},{16,0},{24,8},{1,17},{9,25},{17,1},{25,9},{2,18},{10... | collective-permute-start | bytes 393224 | tf_op jit(solution)/shard_map/ppermute | solution.py:11
  82.1 7.2 %collective-permute-start.5 = (f32[128,256]{1,0:T(8,128)S(1)}, f32[128,256]{1,0:T(8,128)S(1)}, u32[]{:S(2)}, u32[]{:S(2)}) collective-permute-start(f32[128,256]{1,0:T(8,128)S(1)} %collective-permute-done.4), channel_id=1, source_target_pairs={{0,1},{1,2},{2,3},{3,4},{4,5},{5,6},{6,7},{8,9},{9,10},{10,11},{11... | collective-permute-start | bytes 393224 | tf_op jit(solution)/shard_map/ppermute | solution.py:17
  84.0 7.0 %collective-permute-start.6 = (f32[128,256]{1,0:T(8,128)S(1)}, f32[128,256]{1,0:T(8,128)S(1)}, u32[]{:S(2)}, u32[]{:S(2)}) collective-permute-start(f32[128,256]{1,0:T(8,128)S(1)} %collective-permute-done.4), channel_id=1, source_target_pairs={{1,0},{2,1},{3,2},{4,3},{5,4},{6,5},{7,6},{9,8},{10,9},{11,10},{12... | collective-permute-start | bytes 393224 | tf_op jit(solution)/shard_map/ppermute | solution.py:17
  91.6 5.2 %collective-permute-start.7 = (f32[128,256]{1,0:T(8,128)S(1)}, f32[128,256]{1,0:T(8,128)S(1)}, u32[]{:S(2)}, u32[]{:S(2)}) collective-permute-start(f32[128,256]{1,0:T(8,128)S(1)} %fusion.31), channel_id=1, source_target_pairs={{0,8},{8,0},{16,24},{24,16},{1,9},{9,1},{17,25},{25,17},{2,10},{10... | collective-permute-start | bytes 393224 | tf_op jit(solution)/shard_map/ppermute | solution.py:23
  92.8 27.8 %collective-permute-start.8 = (f32[128,256]{1,0:T(8,128)S(1)}, f32[128,256]{1,0:T(8,128)S(1)}, u32[]{:S(2)}, u32[]{:S(2)}) collective-permute-start(f32[128,256]{1,0:T(8,128)S(1)} %fusion.73), channel_id=1, source_target_pairs={{0,8},{8,0},{16,24},{24,16},{1,9},{9,1},{17,25},{25,17},{2,10},{10... | collective-permute-start | bytes 393224 | tf_op jit(solution)/shard_map/ppermute | solution.py:23
  120.9 8.9 %collective-permute-start.10 = (f32[128,256]{1,0:T(8,128)S(1)}, f32[128,256]{1,0:T(8,128)S(1)}, u32[]{:S(2)}, u32[]{:S(2)}) collective-permute-start(f32[128,256]{1,0:T(8,128)S(1)} %fusion.5), channel_id=1, source_target_pairs={{1,0},{2,1},{3,2},{4,3},{5,4},{6,5},{7,6},{9,8},{10,9},{11,10},{12... | collective-permute-start | bytes 393224 | tf_op jit(solution)/shard_map/ppermute | solution.py:17
  125.6 7.2 %collective-permute-start.9 = (f32[128,256]{1,0:T(8,128)S(1)}, f32[128,256]{1,0:T(8,128)S(1)}, u32[]{:S(2)}, u32[]{:S(2)}) collective-permute-start(f32[128,256]{1,0:T(8,128)S(1)} %fusion.5), channel_id=1, source_target_pairs={{0,1},{1,2},{2,3},{3,4},{4,5},{5,6},{6,7},{8,9},{9,10},{10,11},{11... | collective-permute-start | bytes 393224 | tf_op jit(solution)/shard_map/ppermute | solution.py:17
  133.7 8.7 %collective-permute-start.11 = (f32[128,256]{1,0:T(8,128)S(1)}, f32[128,256]{1,0:T(8,128)S(1)}, u32[]{:S(2)}, u32[]{:S(2)}) collective-permute-start(f32[128,256]{1,0:T(8,128)S(1)} %fusion.2), channel_id=1, source_target_pairs={{0,16},{8,24},{16,0},{24,8},{1,17},{9,25},{17,1},{25,9},{2,18},{10... | collective-permute-start | bytes 393224 | tf_op jit(solution)/shard_map/ppermute | solution.py:23
  137.4 30.4 %collective-permute-start.12 = (f32[128,256]{1,0:T(8,128)S(1)}, f32[128,256]{1,0:T(8,128)S(1)}, u32[]{:S(2)}, u32[]{:S(2)}) collective-permute-start(f32[128,256]{1,0:T(8,128)S(1)} %fusion.5), channel_id=1, source_target_pairs={{0,16},{8,24},{16,0},{24,8},{1,17},{9,25},{17,1},{25,9},{2,18},{10... | collective-permute-start | bytes 393224 | tf_op jit(solution)/shard_map/ppermute | solution.py:23
where the time goes:
time: 172 us; the launch traced here: 169 us
  other arithmetic  68.7 us (40%)
  waiting for transfers between devices  42.3 us (25%)
  starting transfers between devices  34.4 us (20%)
  matrix products  11.9 us (7%)
  local copies, waits for them, and re-layouts  6.65 us (4%)
  between operations  4.92 us (3%)
    another operation x9, other arithmetic, orthonormal(): lower_factor = jnp.linalg.cholesky(gram_matrix)  37.2 us
    another operation x6, other arithmetic, orthonormal(): jax.scipy.linalg.solve_triangular(lower_factor, jnp.swapaxes(tall_block,...  31.4 us
    ppermute x3, waiting for transfers between devices, shifted(): lax.ppermute(value, axis, [(i, (i + by) % peers) for i in range(peers)])  23.7 us
    ppermute x6, starting transfers between devices, shifted_2(): return lax.ppermute(value, axis, pairs)  18 us
    ppermute x3, starting transfers between devices, shifted(): lax.ppermute(value, axis, [(i, (i + by) % peers) for i in range(peers)])  11.3 us
    ppermute x6, waiting for transfers between devices, shifted_2(): return lax.ppermute(value, axis, pairs)  10.7 us
    ppermute x4, waiting for transfers between devices, from_partner(): return lax.ppermute(value, axis, pairs)  7.95 us
    ppermute x4, starting transfers between devices, from_partner(): return lax.ppermute(value, axis, pairs)  5.08 us
  transfers between devices with their start and end apart: 13, of which 9 were waited for; matrix products, arithmetic and copies ran while one was open for 31% of the time, Pallas kernels for 0%

commit v1 on v0

v1 whole, which is shorter than its diff:
```python
import functools

import jax
import jax.numpy as jnp
from jax import lax
from jax.experimental import pallas as pl
from jax.experimental.pallas import tpu as pltpu
from jax.sharding import PartitionSpec as P

HIGHEST = lax.Precision.HIGHEST
ROWS = 8
GROUP = 4
BOTH = ("leaf", "clusters")


def dot(a, b, ca=1, cb=0):
    return lax.dot_general(
        a, b, (((ca,), (cb,)), ((), ())), precision=HIGHEST, preferred_element_type=jnp.float32
    )


def across_lanes(tile, lane):
    return jnp.broadcast_to(tile[:, lane : lane + 1], tile.shape)


def across_rows(tile, row):
    return jnp.broadcast_to(tile[row : row + 1, :], tile.shape)


def inverse_factor(gram):
    size = gram.shape[0]
    blocks = size // ROWS
    sub = lax.broadcasted_iota(jnp.int32, (ROWS, size), 0)
    lane = lax.broadcasted_iota(jnp.int32, (ROWS, size), 1)
    left = [gram[ROWS * i : ROWS * (i + 1), :] for i in range(blocks)]
    right = [jnp.where(lane == sub + ROWS * i, 1.0, 0.0).astype(jnp.float32) for i in range(blocks)]
    scaled = [None] * blocks
    for first in range(0, blocks, GROUP):
        last = first + GROUP
        scales = []
        for k in range(first, last):
            cols = {
                i: [across_lanes(left[i], ROWS * k + c) for c in range(ROWS)] for i in range(k, last)
            }
            pivots = jnp.ones((ROWS, size), jnp.float32)
            for j in range(ROWS):
                pivot = across_rows(cols[k][j], j)
                inverse = 1.0 / pivot
                pivots = jnp.where(sub == j, pivot, pivots)
                left_row = across_rows(left[k], j)
                right_row = across_rows(right[k], j)
                col_row = [across_rows(cols[k][c], j) for c in range(j + 1, ROWS)]
                for i in range(k, last):
                    if i == k and j == ROWS - 1:
                        continue
                    col = cols[i][j]
                    if i == k:
                        col = jnp.where(sub > j, col, 0.0)
                    factor = col * inverse
                    for c in range(j + 1, ROWS):
                        cols[i][c] = cols[i][c] - factor * col_row[c - j - 1]
                    left[i] = left[i] - factor * left_row
                    right[i] = right[i] - factor * right_row
            scales.append(lax.rsqrt(pivots))
        for k in range(first, last):
            scaled[k] = right[k] * scales[k - first]
        if last < blocks:
            upper = jnp.concatenate([left[k] * scales[k - first] for k in range(first, last)], axis=0)
            lower = jnp.concatenate(scaled[first:last], axis=0)
            change = dot(upper, jnp.concatenate([upper, lower], axis=1), 0, 0)
            for i in range(last, blocks):
                piece = change[ROWS * i : ROWS * (i + 1), :]
                left[i] = left[i] - piece[:, :size]
                right[i] = right[i] - piece[:, size:]
    return jnp.concatenate(scaled, axis=0)


def near_half(view, which, rows):
    chunks = rows // 128
    return jnp.concatenate(
        [view[pl.ds(2 * c + which, rows, stride=2 * chunks), :] for c in range(chunks)], axis=1
    )


def handed_first_kernel(near, probes, out):
    upper = near_half(near, 1, probes.shape[0])
    out[...] = dot(probes[:, : out.shape[1]].T, upper).T


def near_kernel(near, probes, samples, rest, handed):
    rows = probes.shape[0]
    half = handed.shape[1]
    upper = near_half(near, 1, rows)
    handed[...] = dot(probes[:, half:].T, upper).T
    diag = near_half(near, 0, rows)
    rest[...] = samples[...] - dot(diag, probes[...])


def leaf_kernel(near, rest, following, handed, probes, far, inverse, probe_coef, basis, sample_coef):
    columns = far.shape[1]
    upper = near_half(near, 1, rest.shape[0])
    block = rest[:, :columns] - dot(upper, following[...]) - handed[...]
    far[...] = block
    gram = dot(block, block, 0, 0)
    cross = dot(block, probes[...], 0, 0)
    factor = inverse_factor(gram)
    inverse[...] = factor
    probe_coef[...] = dot(factor, cross)
    sample_coef[...] = dot(factor, gram)
    basis[...] = dot(block, factor, 1, 1)


def second_kernel(near, rest, following, handed, basis, sample_coef):
    columns = handed.shape[1]
    upper = near_half(near, 1, rest.shape[0])
    block = rest[:, columns:] - dot(upper, following[...]) - handed[...]
    sample_coef[...] = dot(basis[...], block, 0, 0)


def coupling_kernel(where, couplings, main, other, out):
    block = couplings[where[0], where[1]]
    out[...] = dot(block, main[...]) + dot(block, other[...], 0, 0)


def corrected_kernel(where, couplings, main, other, coef, out):
    block = couplings[where[0], where[1]]
    out[...] = coef[...] - dot(block, main[...]) - dot(block, other[...], 0, 0)


def node_kernel(where, own, sibling, own_probes, sibling_probes, basis, sample_coef, probe_coef):
    size = own.shape[0]
    mine = own[...]
    theirs = sibling[...]
    gram_all = dot(mine[:, :size], mine, 0, 0) + dot(theirs[:, :size], theirs, 0, 0)
    cross = dot(mine[:, :size], own_probes[...], 0, 0) + dot(
        theirs[:, :size], sibling_probes[...], 0, 0
    )
    factor = inverse_factor(gram_all[:, :size])
    sample_coef[...] = dot(factor, gram_all)
    probe_coef[...] = dot(factor, cross)
    at = pl.multiple_of(where[1] * size, size)
    basis[pl.ds(at, size), :] = dot(mine[:, :size], factor, 1, 1)
    at = pl.multiple_of((1 - where[1]) * size, size)
    basis[pl.ds(at, size), :] = dot(theirs[:, :size], factor, 1, 1)


VMEM = pl.BlockSpec(memory_space=pltpu.VMEM)
SMEM = pl.BlockSpec(memory_space=pltpu.SMEM)


def call(kernel, shapes, *operands, scalars=0, flops=0):
    outs = [jax.ShapeDtypeStruct(shape, jnp.float32) for shape in shapes]
    specs = [SMEM] * scalars + [VMEM] * (len(operands) - scalars)
    moved = 4 * (sum(o.size for o in operands) + sum(o.size for o in outs))
    return pl.pallas_call(
        kernel,
        out_shape=outs,
        in_specs=specs,
        out_specs=[VMEM] * len(outs),
        compiler_params=pltpu.CompilerParams(vmem_limit_bytes=32 * 2**20),
        cost_estimate=pl.CostEstimate(flops=flops, bytes_accessed=moved, transcendentals=0),
    )(*operands)


def permuted(value, target):
    trees, subtree = lax.axis_size("clusters"), lax.axis_size("leaf")
    pairs = []
    for member in range(subtree):
        for tree in range(trees):
            to_tree, to_member = target(tree, member)
            if 0 <= to_tree < trees:
                pairs.append((member * trees + tree, to_member * trees + to_tree))
    return lax.ppermute(value, BOTH, pairs)


def flat_shift(value, by):
    subtree = lax.axis_size("leaf")
    return permuted(value, lambda tree, member: divmod(tree * subtree + member + by, subtree))


def tree_shift(value, by):
    peers = lax.axis_size("clusters")
    pairs = [(i, i + by) for i in range(peers) if 0 <= i + by < peers]
    return lax.ppermute(value, "clusters", pairs)


def swapped(value, mask):
    pairs = [(i, i ^ mask) for i in range(lax.axis_size("leaf"))]
    return lax.ppermute(value, "leaf", pairs)


def outward(value, half):
    return permuted(value, lambda tree, member: (tree - 1 if member < half else tree + 1, member))


def body(samples, probes, near_blocks, couplings, node_slot):
    rows, width = probes.shape
    columns = couplings.shape[-1]
    subtree = lax.axis_size("leaf")
    levels = subtree.bit_length() - 1
    member = lax.axis_index("leaf")
    chunks = rows // 128
    near = near_blocks.reshape(rows, 2, chunks, 128).transpose(0, 2, 1, 3).reshape(-1, 128)
    table = couplings[0]

    following = flat_shift(probes[:, :columns], -1)
    (handed,) = call(handed_first_kernel, [(rows, columns)], near, probes, flops=2 * rows * rows * columns)
    handed = flat_shift(handed, 1)
    rest, handed_2 = call(
        near_kernel, [(rows, width), (rows, width - columns)], near, probes, samples,
        flops=12 * rows * rows * width,
    )
    following_2 = flat_shift(probes[:, columns:], -1)
    handed_2 = flat_shift(handed_2, 1)
    far, inverse, probe_coef, leaf_basis, sample_first = call(
        leaf_kernel,
        [(rows, columns), (columns, columns), (columns, width), (rows, columns), (columns, columns)],
        near, rest, following, handed, probes, flops=10 * rows * rows * width,
    )
    (sample_last,) = call(
        second_kernel, [(columns, width - columns)], near, rest, following_2, handed_2, leaf_basis,
        flops=4 * rows * rows * width,
    )
    sample_coef = jnp.concatenate([sample_first, sample_last], axis=1)

    def place(level, node):
        index = subtree - (subtree >> level - 1) + (node >> 1)
        slot = lax.dynamic_index_in_dim(node_slot[0], index, 0, keepdims=False)
        return jnp.stack([slot, node & 1]).astype(jnp.int32)

    shape = (columns, width)
    ancestors = []
    for level in range(1, levels + 1):
        copies = 2 ** (level - 1)
        node = member // copies
        count = subtree // copies
        own_place = place(level, node)
        if count == 4:
            away = outward(probe_coef, 2 * copies)
            outer = (node == 0) | (node == 3)
            main = jnp.where(outer, probe_coef, away)
            other = jnp.where(outer, away, probe_coef)
            (term,) = call(coupling_kernel, [shape], place(level, node ^ 2), table, main, other, scalars=1)
            sibling_coef, sibling_probes = swapped((sample_coef, probe_coef), copies)
            own = sample_coef - swapped(term, 2 * copies)
            sibling = sibling_coef - swapped(term, 3 * copies)
        else:
            if count == 2:
                from_left, from_right = tree_shift(probe_coef, 1), tree_shift(probe_coef, -1)
            else:
                from_left = flat_shift(probe_coef, 2 * copies)
                from_right = flat_shift(probe_coef, -2 * copies)
            even = node & 1 == 0
            main = jnp.where(even, from_left, from_right)
            other = jnp.where(even, from_right, from_left)
            (own,) = call(
                corrected_kernel, [shape], own_place, table, main, other, sample_coef, scalars=1
            )
            sibling, sibling_probes = swapped((own, probe_coef), copies)
        basis, sample_coef, probe_coef = call(
            node_kernel, [(2 * columns, columns), shape, shape],
            own_place, own, sibling, probe_coef, sibling_probes, scalars=1,
        )
        ancestors.append(basis)
    transfer_bases = jnp.stack(ancestors, axis=0)[None]
    return (leaf_basis, transfer_bases, sample_coef[None], probe_coef[None])


def solution(mesh):
    in_specs = (
        P(("clusters", "leaf"), None),
        P(("clusters", "leaf"), None),
        P(("clusters", "leaf"), None, None),
        P("clusters", None, None, None, None),
        P("clusters", None),
    )
    out_specs = (
        P(("clusters", "leaf"), None),
        P(("clusters", "leaf"), None, None, None),
        P("clusters", None, None),
        P("clusters", None, None),
    )
    return jax.shard_map(body, mesh=mesh, in_specs=in_specs, out_specs=out_specs, check_vma=False)
```

time: 172 us -> 102 us (0.59); the launches traced: 169 us -> 101 us
  other arithmetic: 68.7 us -> 3.04 us
  Pallas kernels: 0 us -> 27.4 us
  matrix products: 11.9 us -> 0 us
  starting transfers between devices: 34.4 us -> 24.8 us
  between operations: 4.92 us -> 0.85 us
  waiting for transfers between devices: 42.3 us -> 38.3 us
    another operation x15 -> x3, other arithmetic: 68.6 us -> 2.24 us  [place(): return jnp.stack([slot, node & 1]).astype(jnp.int32)]
    pallas_call x0 -> x8, Pallas kernels: none -> 27.4 us  [call(): pl.pallas_call(kernel, out_shape=outs, in_specs=specs, out_specs=[VMEM] *...]
    dot_general x16 -> x0, matrix products: 10.8 us -> none  [the longest x6 3.26 us: project(): jnp.einsum('...rk,...rs->...ks', node_basis, target, precision=full_preci...]
    ppermute x13, starting transfers between devices: 34.4 us -> 24.8 us  [the longest x5 15.7 us: permuted(): return lax.ppermute(value, BOTH, pairs)]
    ppermute x13, waiting for transfers between devices: 42.3 us -> 38.3 us  [the longest x6 17.7 us: swapped(): return lax.ppermute(value, 'leaf', pairs)]
    unnamed x10 -> x18, local copies, waits for them, and re-layouts: 1.7 us -> 4.23 us
    slice x1, local copies, waits for them, and re-layouts: 4.1 us -> 1.83 us  [body(): following_2 = flat_shift(probes[:, columns:], -1)]
  transfers between devices with their start and end apart: 13 -> 13, of which waited for: 9 -> 9; matrix products, arithmetic and copies ran while one was open for 31% -> 3% of each run, Pallas kernels for 0% -> 8%
where the time goes in v1:
time: 102 us; the launch traced here: 101 us
  waiting for transfers between devices  38.3 us (38%)
  Pallas kernels  27.4 us (27%)
  starting transfers between devices  24.8 us (24%)
  local copies, waits for them, and re-layouts  6.73 us (7%)
  other arithmetic  3.04 us (3%)
    pallas_call x8, Pallas kernels, call(): pl.pallas_call(kernel, out_shape=outs, in_specs=specs, out_specs=[VMEM] *...  27.4 us
    ppermute x6, waiting for transfers between devices, swapped(): return lax.ppermute(value, 'leaf', pairs)  17.7 us
    ppermute x5, waiting for transfers between devices, permuted(): return lax.ppermute(value, BOTH, pairs)  17.2 us
    ppermute x5, starting transfers between devices, permuted(): return lax.ppermute(value, BOTH, pairs)  15.7 us
    ppermute x6, starting transfers between devices, swapped(): return lax.ppermute(value, 'leaf', pairs)  4.84 us
    ppermute x2, starting transfers between devices, tree_shift(): return lax.ppermute(value, 'clusters', pairs)  4.33 us
    unnamed x18, local copies, waits for them, and re-layouts  4.23 us
    ppermute x2, waiting for transfers between devices, tree_shift(): return lax.ppermute(value, 'clusters', pairs)  3.42 us
  transfers between devices with their start and end apart: 13, of which 9 were waited for; matrix products, arithmetic and copies ran while one was open for 3% of the time, Pallas kernels for 8%

profile of v1, /device:TPU:4, one launch (start us, length us, event | category | flops | bytes accessed | tf_op | source)
XLA Modules:
  0.0 101.2 jit_solution(13569283923545538521)
XLA Ops:
  0.6 1.8 %fusion.1 = (f32[512,128]{1,0:T(8,128)}, f32[512,128]{1,0:T(8,128)S(1)}) fusion(f32[512,256]{1,0:T(8,128)} %probes.5), kind=kLoop, calls=%fused_computation.13 | loop fusion | bytes 1048576 | tf_op jit(solution)/shard_map/slice | solution.py:213
  2.5 5.8 %collective-permute-start = (f32[512,128]{1,0:T(8,128)S(1)}, f32[512,128]{1,0:T(8,128)S(1)}, u32[]{:S(2)}, u32[]{:S(2)}) collective-permute-start(f32[512,128]{1,0:T(8,128)S(1)} %get-tuple-element.27), channel_id=1, source_target_pairs={{1,24},{2,25},{3,26},{4,27},{5,28},{6,29},{7,30},{8,0},{9,1},{10,2... | collective-permute-start | bytes 786440 | tf_op jit(solution)/shard_map/ppermute | solution.py:173
  8.3 1.6 %copy-done = f32[512,2,512]{2,1,0:T(2,128)S(1)} copy-done((f32[512,2,512]{2,1,0:T(2,128)S(1)}, f32[512,2,512]{2,1,0:T(2,128)}, u32[]{:S(2)}) %copy-start) | copy-done | bytes 2097176
  11.8 1.9 %collective-permute-start.1 = (f32[512,128]{1,0:T(8,128)S(1)}, f32[512,128]{1,0:T(8,128)S(1)}, u32[]{:S(2)}, u32[]{:S(2)}) collective-permute-start(f32[512,128]{1,0:T(8,128)S(1)} %shard_map.85), channel_id=1, source_target_pairs={{0,8},{1,9},{2,10},{3,11},{4,12},{5,13},{6,14},{7,15},{8,16},{9,17... | collective-permute-start | bytes 786440 | tf_op jit(solution)/shard_map/ppermute | solution.py:173
  13.8 2.4 %shard_map.84 = (f32[512,256]{1,0:T(8,128)S(1)}, f32[512,128]{1,0:T(8,128)}) custom-call(f32[4096,128]{1,0:T(8,128)S(1)} %bitcast.19, f32[512,256]{1,0:T(8,128)S(1)} %copy-done.2, f32[512,256]{1,0:T(8,128)S(1)} %copy-done.4), custom_call_target="tpu_custom_call" | custom-call | flops 805306368 | bytes 3932160 | tf_op jit(solution)/shard_map/pallas_call | solution.py:155
  16.2 8.8 %collective-permute-done.1.handed = f32[512,128]{1,0:T(8,128)S(1)} collective-permute-done((f32[512,128]{1,0:T(8,128)S(1)}, f32[512,128]{1,0:T(8,128)S(1)}, u32[]{:S(2)}, u32[]{:S(2)}) %collective-permute-start.1) | collective-permute-done | bytes 262176 | tf_op jit(solution)/shard_map/ppermute | solution.py:173
  25.0 7.6 %shard_map.86 = (f32[512,128]{1,0:T(8,128)}, f32[128,128]{1,0:T(8,128)}, f32[128,256]{1,0:T(8,128)S(1)}, f32[512,128]{1,0:T(8,128)}, f32[128,128]{1,0:T(8,128)S(1)}) custom-call(f32[4096,128]{1,0:T(8,128)S(1)} %bitcast.20, f32[512,256]{1,0:T(8,128)S(1)} %get-tuple-element.15.rest, f32[512,128]{1,0:T(8,128)S(1)} %collective-permute-done.following, ...), custom_call_target="tpu_custom_call" | custom-call | flops 671088640 | bytes 4456448 | tf_op jit(solution)/shard_map/pallas_call | solution.py:155
  33.2 1.9 %collective-permute-start.4 = (f32[128,256]{1,0:T(8,128)S(1)}, f32[128,256]{1,0:T(8,128)S(1)}, u32[]{:S(2)}, u32[]{:S(2)}) collective-permute-start(f32[128,256]{1,0:T(8,128)S(1)} %get-tuple-element.19.own_probes), channel_id=1, source_target_pairs={{1,0},{2,1},{3,2},{4,3},{5,4},{6,5},{7,6},{9,8},{10,9},{11,10},{12... | collective-permute-start | bytes 393224 | tf_op jit(solution)/shard_map/ppermute | solution.py:173
  35.1 3.0 %collective-permute-start.2 = (f32[512,128]{1,0:T(8,128)}, f32[512,128]{1,0:T(8,128)S(1)}, u32[]{:S(2)}, u32[]{:S(2)}) collective-permute-start(f32[512,128]{1,0:T(8,128)} %get-tuple-element.26), channel_id=1, source_target_pairs={{1,24},{2,25},{3,26},{4,27},{5,28},{6,29},{7,30},{8,0},{9,1},{10,2... | collective-permute-start | bytes 786440 | tf_op jit(solution)/shard_map/ppermute | solution.py:173
  38.1 3.0 %collective-permute-start.3 = (f32[512,128]{1,0:T(8,128)}, f32[512,128]{1,0:T(8,128)}, u32[]{:S(2)}, u32[]{:S(2)}) collective-permute-start(f32[512,128]{1,0:T(8,128)} %get-tuple-element.18), channel_id=1, source_target_pairs={{0,8},{1,9},{2,10},{3,11},{4,12},{5,13},{6,14},{7,15},{8,16},{9,17... | collective-permute-start | bytes 786440 | tf_op jit(solution)/shard_map/ppermute | solution.py:173
  43.7 8.0 %collective-permute-done.2.following = f32[512,128]{1,0:T(8,128)S(1)} collective-permute-done((f32[512,128]{1,0:T(8,128)}, f32[512,128]{1,0:T(8,128)S(1)}, u32[]{:S(2)}, u32[]{:S(2)}) %collective-permute-start.2) | collective-permute-done | bytes 262176 | tf_op jit(solution)/shard_map/ppermute | solution.py:173
  53.0 2.6 %shard_map.87 = f32[128,128]{1,0:T(8,128)S(1)} custom-call(f32[4096,128]{1,0:T(8,128)S(1)} %bitcast.21, f32[512,256]{1,0:T(8,128)S(1)} %get-tuple-element.15.rest, f32[512,128]{1,0:T(8,128)S(1)} %collective-permute-done.2.following, f32[512,128]{1,0:T(8,128)} %collective-permute-done.3.handed, f32[512,128]{1,0:T(8,128)S(1)} %copy-done.5), custom_call_target="tpu_custom_call" | custom-call | flops 268435456 | bytes 3473408 | tf_op jit(solution)/shard_map/pallas_call | solution.py:155
  55.6 1.4 %collective-permute-start.7 = (f32[128,256]{1,0:T(8,128)S(1)}, f32[128,256]{1,0:T(8,128)S(1)}, u32[]{:S(2)}, u32[]{:S(2)}) collective-permute-start(f32[128,256]{1,0:T(8,128)S(1)} %shard_map.88), channel_id=1, source_target_pairs={{0,24},{8,16},{16,8},{24,0},{1,25},{9,17},{17,9},{25,1},{2,26},{10... | collective-permute-start | bytes 393224 | tf_op jit(solution)/shard_map/ppermute | solution.py:189
  57.0 1.5 %collective-permute-start.6 = (f32[128,256]{1,0:T(8,128)S(1)}, f32[128,256]{1,0:T(8,128)S(1)}, u32[]{:S(2)}, u32[]{:S(2)}) collective-permute-start(f32[128,256]{1,0:T(8,128)S(1)} %get-tuple-element.32), channel_id=1, source_target_pairs={{0,8},{8,0},{16,24},{24,16},{1,9},{9,1},{17,25},{25,17},{2,10},{10... | collective-permute-start | bytes 393224 | tf_op jit(solution)/shard_map/ppermute | solution.py:189
  59.9 4.0 %collective-permute-done.7 = f32[128,256]{1,0:T(8,128)S(1)} collective-permute-done((f32[128,256]{1,0:T(8,128)S(1)}, f32[128,256]{1,0:T(8,128)S(1)}, u32[]{:S(2)}, u32[]{:S(2)}) %collective-permute-start.7) | collective-permute-done | bytes 131104 | tf_op jit(solution)/shard_map/ppermute | solution.py:189
  63.9 1.4 %collective-permute-done.6 = f32[128,256]{1,0:T(8,128)S(1)} collective-permute-done((f32[128,256]{1,0:T(8,128)S(1)}, f32[128,256]{1,0:T(8,128)S(1)}, u32[]{:S(2)}, u32[]{:S(2)}) %collective-permute-start.6) | collective-permute-done | bytes 131104 | tf_op jit(solution)/shard_map/ppermute | solution.py:189
  65.3 2.6 %collective-permute-done.8.sibling_probes = f32[128,256]{1,0:T(8,128)S(1)} collective-permute-done((f32[128,256]{1,0:T(8,128)S(1)}, f32[128,256]{1,0:T(8,128)S(1)}, u32[]{:S(2)}, u32[]{:S(2)}) %collective-permute-start.8) | collective-permute-done | bytes 131104 | tf_op jit(solution)/shard_map/ppermute | solution.py:189
  67.9 5.8 %shard_map.89 = (f32[256,128]{1,0:T(8,128)S(1)}, f32[128,256]{1,0:T(8,128)S(1)}, f32[128,256]{1,0:T(8,128)S(1)}) custom-call(s32[2]{0:T(128)S(1)} %pad_add_fusion.where, f32[128,256]{1,0:T(8,128)S(1)} %get-tuple-element.33.own, f32[128,256]{1,0:T(8,128)S(1)} %sub.12.sibling, f32[128,256]{1,0:T(8,128)S(1)} %get-tuple-element.19.own_probes, ...), custom_call_target="tpu_custom_call" | custom-call | bytes 917512 | tf_op jit(solution)/shard_map/pallas_call | solution.py:155
  73.7 1.9 %collective-permute-start.10 = (f32[128,256]{1,0:T(8,128)S(1)}, f32[128,256]{1,0:T(8,128)S(1)}, u32[]{:S(2)}, u32[]{:S(2)}) collective-permute-start(f32[128,256]{1,0:T(8,128)S(1)} %get-tuple-element.21.own_probes), channel_id=1, source_target_pairs={{1,0},{2,1},{3,2},{4,3},{5,4},{6,5},{7,6},{9,8},{10,9},{11,10},{12... | collective-permute-start | bytes 393224 | tf_op jit(solution)/shard_map/ppermute | solution.py:184
  75.6 2.4 %collective-permute-start.9 = (f32[128,256]{1,0:T(8,128)S(1)}, f32[128,256]{1,0:T(8,128)S(1)}, u32[]{:S(2)}, u32[]{:S(2)}) collective-permute-start(f32[128,256]{1,0:T(8,128)S(1)} %get-tuple-element.21.own_probes), channel_id=1, source_target_pairs={{0,1},{1,2},{2,3},{3,4},{4,5},{5,6},{6,7},{8,9},{9,10},{10,11},{11... | collective-permute-start | bytes 393224 | tf_op jit(solution)/shard_map/ppermute | solution.py:184
  79.4 3.4 %collective-permute-done.9 = f32[128,256]{1,0:T(8,128)S(1)} collective-permute-done((f32[128,256]{1,0:T(8,128)S(1)}, f32[128,256]{1,0:T(8,128)S(1)}, u32[]{:S(2)}, u32[]{:S(2)}) %collective-permute-start.9) | collective-permute-done | bytes 131104 | tf_op jit(solution)/shard_map/ppermute | solution.py:184
  84.5 6.9 %collective-permute-done.12.sibling_probes = f32[128,256]{1,0:T(8,128)S(1)} collective-permute-done((f32[128,256]{1,0:T(8,128)S(1)}, f32[128,256]{1,0:T(8,128)S(1)}, u32[]{:S(2)}, u32[]{:S(2)}) %collective-permute-start.12) | collective-permute-done | bytes 131104 | tf_op jit(solution)/shard_map/ppermute | solution.py:189
  91.4 2.8 %collective-permute-done.11.sibling = f32[128,256]{1,0:T(8,128)S(1)} collective-permute-done((f32[128,256]{1,0:T(8,128)S(1)}, f32[128,256]{1,0:T(8,128)S(1)}, u32[]{:S(2)}, u32[]{:S(2)}) %collective-permute-start.11) | collective-permute-done | bytes 131104 | tf_op jit(solution)/shard_map/ppermute | solution.py:189
  94.2 6.2 %shard_map.91 = (f32[256,128]{1,0:T(8,128)S(1)}, f32[128,256]{1,0:T(8,128)}, f32[128,256]{1,0:T(8,128)}) custom-call(s32[2]{0:T(128)S(1)} %pad_add_fusion.2.where, f32[128,256]{1,0:T(8,128)S(1)} %shard_map.90.own, f32[128,256]{1,0:T(8,128)S(1)} %collective-permute-done.11.sibling, f32[128,256]{1,0:T(8,128)S(1)} %get-tuple-element.21.own_probes, ...), custom_call_target="tpu_custom_call" | custom-call | bytes 917512 | tf_op jit(solution)/shard_map/pallas_call | solution.py:155
  (38 shorter events, 11.6 us)
Async XLA Ops:
  0.6 13.1 %copy-start.4 = (f32[512,256]{1,0:T(8,128)S(1)}, f32[512,256]{1,0:T(8,128)}, u32[]{:S(2)}) copy-start(f32[512,256]{1,0:T(8,128)} %samples.1) | copy-start | bytes 1572868
  2.5 13.7 %collective-permute-start = (f32[512,128]{1,0:T(8,128)S(1)}, f32[512,128]{1,0:T(8,128)S(1)}, u32[]{:S(2)}, u32[]{:S(2)}) collective-permute-start(f32[512,128]{1,0:T(8,128)S(1)} %get-tuple-element.27), channel_id=1, source_target_pairs={{1,24},{2,25},{3,26},{4,27},{5,28},{6,29},{7,30},{8,0},{9,1},{10,2... | collective-permute-start | bytes 786440 | tf_op jit(solution)/shard_map/ppermute | solution.py:173
  8.3 1.6 %copy-start = (f32[512,2,512]{2,1,0:T(2,128)S(1)}, f32[512,2,512]{2,1,0:T(2,128)}, u32[]{:S(2)}) copy-start(f32[512,2,512]{2,1,0:T(2,128)} %param.7) | copy-start | bytes 6291460
  9.9 1.0 %copy-start.2 = (f32[512,256]{1,0:T(8,128)S(1)}, f32[512,256]{1,0:T(8,128)}, u32[]{:S(2)}) copy-start(f32[512,256]{1,0:T(8,128)} %probes.5) | copy-start | bytes 1572868
  11.8 13.2 %collective-permute-start.1 = (f32[512,128]{1,0:T(8,128)S(1)}, f32[512,128]{1,0:T(8,128)S(1)}, u32[]{:S(2)}, u32[]{:S(2)}) collective-permute-start(f32[512,128]{1,0:T(8,128)S(1)} %shard_map.85), channel_id=1, source_target_pairs={{0,8},{1,9},{2,10},{3,11},{4,12},{5,13},{6,14},{7,15},{8,16},{9,17... | collective-permute-start | bytes 786440 | tf_op jit(solution)/shard_map/ppermute | solution.py:173
  16.2 25.0 %copy-start.8 = (s32[1,3]{1,0:T(1,128)S(1)}, s32[1,3]{1,0:T(1,128)}, u32[]{:S(2)}) copy-start(s32[1,3]{1,0:T(1,128)} %param.9) | copy-start | bytes 40
  25.0 17.6 %copy-start.3 = (f32[1,3,2,128,128]{4,3,2,1,0:T(8,128)S(1)}, f32[1,3,2,128,128]{4,3,2,1,0:T(8,128)}, u32[]{:S(2)}) copy-start(f32[1,3,2,128,128]{4,3,2,1,0:T(8,128)} %param.8) | copy-start | bytes 1179652
  25.0 27.1 %copy-start.1 = (f32[512,2,512]{2,1,0:T(2,128)S(1)}, f32[512,2,512]{2,1,0:T(2,128)}, u32[]{:S(2)}) copy-start(f32[512,2,512]{2,1,0:T(2,128)} %param.7) | copy-start | bytes 6291460
  32.6 0.6 copy-start.6
  33.2 9.4 %collective-permute-start.4 = (f32[128,256]{1,0:T(8,128)S(1)}, f32[128,256]{1,0:T(8,128)S(1)}, u32[]{:S(2)}, u32[]{:S(2)}) collective-permute-start(f32[128,256]{1,0:T(8,128)S(1)} %get-tuple-element.19.own_probes), channel_id=1, source_target_pairs={{1,0},{2,1},{3,2},{4,3},{5,4},{6,5},{7,6},{9,8},{10,9},{11,10},{12... | collective-permute-start | bytes 393224 | tf_op jit(solution)/shard_map/ppermute | solution.py:173
  35.1 16.5 %collective-permute-start.2 = (f32[512,128]{1,0:T(8,128)}, f32[512,128]{1,0:T(8,128)S(1)}, u32[]{:S(2)}, u32[]{:S(2)}) collective-permute-start(f32[512,128]{1,0:T(8,128)} %get-tuple-element.26), channel_id=1, source_target_pairs={{1,24},{2,25},{3,26},{4,27},{5,28},{6,29},{7,30},{8,0},{9,1},{10,2... | collective-permute-start | bytes 786440 | tf_op jit(solution)/shard_map/ppermute | solution.py:173
  38.1 14.0 %collective-permute-start.3 = (f32[512,128]{1,0:T(8,128)}, f32[512,128]{1,0:T(8,128)}, u32[]{:S(2)}, u32[]{:S(2)}) collective-permute-start(f32[512,128]{1,0:T(8,128)} %get-tuple-element.18), channel_id=1, source_target_pairs={{0,8},{1,9},{2,10},{3,11},{4,12},{5,13},{6,14},{7,15},{8,16},{9,17... | collective-permute-start | bytes 786440 | tf_op jit(solution)/shard_map/ppermute | solution.py:173
  42.6 14.4 %copy-start.7 = (f32[128,128]{1,0:T(8,128)S(1)}, f32[128,128]{1,0:T(8,128)}, u32[]{:S(2)}) copy-start(f32[128,128]{1,0:T(8,128)} %copy-done.6) | copy-start | bytes 196612
  43.6 13.4 %collective-permute-start.5 = (f32[128,256]{1,0:T(8,128)S(1)}, f32[128,256]{1,0:T(8,128)S(1)}, u32[]{:S(2)}, u32[]{:S(2)}) collective-permute-start(f32[128,256]{1,0:T(8,128)S(1)} %shard_map.88), channel_id=1, source_target_pairs={{0,16},{8,24},{16,0},{24,8},{1,17},{9,25},{17,1},{25,9},{2,18},{10... | collective-permute-start | bytes 393224 | tf_op jit(solution)/shard_map/ppermute | solution.py:189
  52.1 1.0 copy-start.5
  55.6 8.3 %collective-permute-start.7 = (f32[128,256]{1,0:T(8,128)S(1)}, f32[128,256]{1,0:T(8,128)S(1)}, u32[]{:S(2)}, u32[]{:S(2)}) collective-permute-start(f32[128,256]{1,0:T(8,128)S(1)} %shard_map.88), channel_id=1, source_target_pairs={{0,24},{8,16},{16,8},{24,0},{1,25},{9,17},{17,9},{25,1},{2,26},{10... | collective-permute-start | bytes 393224 | tf_op jit(solution)/shard_map/ppermute | solution.py:189
  57.0 8.3 %collective-permute-start.6 = (f32[128,256]{1,0:T(8,128)S(1)}, f32[128,256]{1,0:T(8,128)S(1)}, u32[]{:S(2)}, u32[]{:S(2)}) collective-permute-start(f32[128,256]{1,0:T(8,128)S(1)} %get-tuple-element.32), channel_id=1, source_target_pairs={{0,8},{8,0},{16,24},{24,16},{1,9},{9,1},{17,25},{25,17},{2,10},{10... | collective-permute-start | bytes 393224 | tf_op jit(solution)/shard_map/ppermute | solution.py:189
  58.5 9.5 %collective-permute-start.8 = (f32[128,256]{1,0:T(8,128)S(1)}, f32[128,256]{1,0:T(8,128)S(1)}, u32[]{:S(2)}, u32[]{:S(2)}) collective-permute-start(f32[128,256]{1,0:T(8,128)S(1)} %get-tuple-element.19.own_probes), channel_id=1, source_target_pairs={{0,8},{8,0},{16,24},{24,16},{1,9},{9,1},{17,25},{25,17},{2,10},{10... | collective-permute-start | bytes 393224 | tf_op jit(solution)/shard_map/ppermute | solution.py:189
  73.7 5.7 %collective-permute-start.10 = (f32[128,256]{1,0:T(8,128)S(1)}, f32[128,256]{1,0:T(8,128)S(1)}, u32[]{:S(2)}, u32[]{:S(2)}) collective-permute-start(f32[128,256]{1,0:T(8,128)S(1)} %get-tuple-element.21.own_probes), channel_id=1, source_target_pairs={{1,0},{2,1},{3,2},{4,3},{5,4},{6,5},{7,6},{9,8},{10,9},{11,10},{12... | collective-permute-start | bytes 393224 | tf_op jit(solution)/shard_map/ppermute | solution.py:184
  75.6 7.2 %collective-permute-start.9 = (f32[128,256]{1,0:T(8,128)S(1)}, f32[128,256]{1,0:T(8,128)S(1)}, u32[]{:S(2)}, u32[]{:S(2)}) collective-permute-start(f32[128,256]{1,0:T(8,128)S(1)} %get-tuple-element.21.own_probes), channel_id=1, source_target_pairs={{0,1},{1,2},{2,3},{3,4},{4,5},{5,6},{6,7},{8,9},{9,10},{10,11},{11... | collective-permute-start | bytes 393224 | tf_op jit(solution)/shard_map/ppermute | solution.py:184
  78.8 12.6 %collective-permute-start.12 = (f32[128,256]{1,0:T(8,128)S(1)}, f32[128,256]{1,0:T(8,128)S(1)}, u32[]{:S(2)}, u32[]{:S(2)}) collective-permute-start(f32[128,256]{1,0:T(8,128)S(1)} %get-tuple-element.21.own_probes), channel_id=1, source_target_pairs={{0,16},{8,24},{16,0},{24,8},{1,17},{9,25},{17,1},{25,9},{2,18},{10... | collective-permute-start | bytes 393224 | tf_op jit(solution)/shard_map/ppermute | solution.py:189
  83.8 10.4 %collective-permute-start.11 = (f32[128,256]{1,0:T(8,128)S(1)}, f32[128,256]{1,0:T(8,128)S(1)}, u32[]{:S(2)}, u32[]{:S(2)}) collective-permute-start(f32[128,256]{1,0:T(8,128)S(1)} %shard_map.90.own), channel_id=1, source_target_pairs={{0,16},{8,24},{16,0},{24,8},{1,17},{9,25},{17,1},{25,9},{2,18},{10... | collective-permute-start | bytes 393224 | tf_op jit(solution)/shard_map/ppermute | solution.py:189

commit v2 on v1

--- a/solution.py
+++ b/solution.py
@@ -82,21 +82,20 @@
     )
 
 
-def handed_first_kernel(near, probes, out):
+def handed_kernel(near, probes, first, last, probes_last):
+    columns = first.shape[1]
     upper = near_half(near, 1, probes.shape[0])
-    out[...] = dot(probes[:, : out.shape[1]].T, upper).T
-
-
-def near_kernel(near, probes, samples, rest, handed):
-    rows = probes.shape[0]
-    half = handed.shape[1]
-    upper = near_half(near, 1, rows)
-    handed[...] = dot(probes[:, half:].T, upper).T
-    diag = near_half(near, 0, rows)
-    rest[...] = samples[...] - dot(diag, probes[...])
-
-
-def leaf_kernel(near, rest, following, handed, probes, far, inverse, probe_coef, basis, sample_coef):
+    handed = dot(probes[...].T, upper).T
+    first[...] = handed[:, :columns]
+    last[...] = handed[:, columns:]
+    probes_last[...] = probes[:, columns:]
+
+
+def rest_kernel(near, probes, samples, rest):
+    rest[...] = samples[...] - dot(near_half(near, 0, probes.shape[0]), probes[...])
+
+
+def leaf_kernel(near, rest, following, handed, probes, far, inverse, sample_coef, probe_coef):
     columns = far.shape[1]
     upper = near_half(near, 1, rest.shape[0])
     block = rest[:, :columns] - dot(upper, following[...]) - handed[...]
@@ -107,50 +106,94 @@
     inverse[...] = factor
     probe_coef[...] = dot(factor, cross)
     sample_coef[...] = dot(factor, gram)
-    basis[...] = dot(block, factor, 1, 1)
-
-
-def second_kernel(near, rest, following, handed, basis, sample_coef):
-    columns = handed.shape[1]
+
+
+def leaf_last_kernel(near, rest, following, handed, far, inverse, basis, sample_coef):
+    columns = far.shape[1]
     upper = near_half(near, 1, rest.shape[0])
+    basis[...] = dot(far[...], inverse[...], 1, 1)
     block = rest[:, columns:] - dot(upper, following[...]) - handed[...]
     sample_coef[...] = dot(basis[...], block, 0, 0)
 
 
-def coupling_kernel(where, couplings, main, other, out):
-    block = couplings[where[0], where[1]]
-    out[...] = dot(block, main[...]) + dot(block, other[...], 0, 0)
-
-
-def corrected_kernel(where, couplings, main, other, coef, out):
-    block = couplings[where[0], where[1]]
-    out[...] = coef[...] - dot(block, main[...]) - dot(block, other[...], 0, 0)
-
-
-def node_kernel(where, own, sibling, own_probes, sibling_probes, basis, sample_coef, probe_coef):
-    size = own.shape[0]
-    mine = own[...]
-    theirs = sibling[...]
-    gram_all = dot(mine[:, :size], mine, 0, 0) + dot(theirs[:, :size], theirs, 0, 0)
-    cross = dot(mine[:, :size], own_probes[...], 0, 0) + dot(
-        theirs[:, :size], sibling_probes[...], 0, 0
-    )
-    factor = inverse_factor(gram_all[:, :size])
-    sample_coef[...] = dot(factor, gram_all)
-    probe_coef[...] = dot(factor, cross)
-    at = pl.multiple_of(where[1] * size, size)
-    basis[pl.ds(at, size), :] = dot(mine[:, :size], factor, 1, 1)
-    at = pl.multiple_of((1 - where[1]) * size, size)
-    basis[pl.ds(at, size), :] = dot(theirs[:, :size], factor, 1, 1)
+def coupling_of(slots, couplings, level, node):
+    subtree = lax.axis_size("leaf")
+    index = subtree - (subtree >> level - 1) + (node >> 1)
+    return couplings[0, slots[0, index], node & 1]
+
+
+def member_node(level):
+    return lax.axis_index("leaf") >> level - 1
+
+
+def term_kernel(level, slots, couplings, mine, away, out):
+    node = member_node(level)
+    block = coupling_of(slots, couplings, level, node ^ 2)
+    outer = (node == 0) | (node == 3)
+    main = jnp.where(outer, mine[...], away[...])
+    other = jnp.where(outer, away[...], mine[...])
+    out[...] = dot(block, main) + dot(block, other, 0, 0)
+
+
+def corrected_kernel(level, slots, couplings, from_left, from_right, first, last, out_first, out_last):
+    columns = first.shape[1]
+    node = member_node(level)
+    block = coupling_of(slots, couplings, level, node)
+    even = node & 1 == 0
+    main = jnp.where(even, from_left[...], from_right[...])
+    other = jnp.where(even, from_right[...], from_left[...])
+    term = dot(block, main) + dot(block, other, 0, 0)
+    out_first[...] = first[...] - term[:, :columns]
+    out_last[...] = last[...] - term[:, columns:]
+
+
+def factor_kernel(level, mine, theirs, *refs):
+    earlier, (inverse, bases) = refs[:-2], refs[-2:]
+    for at, done in enumerate(earlier):
+        bases[0, at] = done[0, 0]
+    size = mine.shape[0]
+    gram = dot(mine[...], mine[...], 0, 0) + dot(theirs[...], theirs[...], 0, 0)
+    factor = inverse_factor(gram)
+    inverse[...] = factor
+    parity = member_node(level) & 1
+    at = pl.multiple_of(parity * size, size)
+    bases[0, len(earlier), pl.ds(at, size), :] = dot(mine[...], factor, 1, 1)
+    at = pl.multiple_of((1 - parity) * size, size)
+    bases[0, len(earlier), pl.ds(at, size), :] = dot(theirs[...], factor, 1, 1)
+
+
+def node_kernel(inverse, mine, mine_last, mine_probes, theirs, theirs_last, theirs_probes, first, last, probe_coef):
+    def both(own, sibling):
+        return dot(mine[...], own[...], 0, 0) + dot(theirs[...], sibling[...], 0, 0)
+
+    factor = inverse[...]
+    probe_coef[...] = dot(factor, both(mine_probes, theirs_probes))
+    first[...] = dot(factor, both(mine, theirs))
+    last[...] = dot(factor, both(mine_last, theirs_last))
+
+
+def top_kernel(inverse, mine, mine_last, mine_probes, theirs, theirs_last, theirs_probes, samples, probe_coef):
+    size = mine.shape[0]
+
+    def both(own, sibling):
+        return dot(mine[...], own[...], 0, 0) + dot(theirs[...], sibling[...], 0, 0)
+
+    factor = inverse[...]
+    probe_coef[0] = dot(factor, both(mine_probes, theirs_probes))
+    samples[0, :, :size] = dot(factor, both(mine, theirs))
+    samples[0, :, size:] = dot(factor, both(mine_last, theirs_last))
 
 
 VMEM = pl.BlockSpec(memory_space=pltpu.VMEM)
 SMEM = pl.BlockSpec(memory_space=pltpu.SMEM)
 
 
-def call(kernel, shapes, *operands, scalars=0, flops=0):
+def call(kernel, shapes, *operands, slots=None, flops=0):
     outs = [jax.ShapeDtypeStruct(shape, jnp.float32) for shape in shapes]
-    specs = [SMEM] * scalars + [VMEM] * (len(operands) - scalars)
+    specs = [VMEM] * len(operands)
+    if slots is not None:
+        operands = (slots,) + operands
+        specs = [SMEM] + specs
     moved = 4 * (sum(o.size for o in operands) + sum(o.size for o in outs))
     return pl.pallas_call(
         kernel,
@@ -198,72 +241,69 @@
     columns = couplings.shape[-1]
     subtree = lax.axis_size("leaf")
     levels = subtree.bit_length() - 1
-    member = lax.axis_index("leaf")
     chunks = rows // 128
     near = near_blocks.reshape(rows, 2, chunks, 128).transpose(0, 2, 1, 3).reshape(-1, 128)
-    table = couplings[0]
-
+    work = 12 * rows * rows * width
+
+    tall, tall_last = (rows, columns), (rows, width - columns)
     following = flat_shift(probes[:, :columns], -1)
-    (handed,) = call(handed_first_kernel, [(rows, columns)], near, probes, flops=2 * rows * rows * columns)
+    handed, handed_last, probes_last = call(
+        handed_kernel, [tall, tall_last, tall_last], near, probes, flops=work
+    )
     handed = flat_shift(handed, 1)
-    rest, handed_2 = call(
-        near_kernel, [(rows, width), (rows, width - columns)], near, probes, samples,
-        flops=12 * rows * rows * width,
-    )
-    following_2 = flat_shift(probes[:, columns:], -1)
-    handed_2 = flat_shift(handed_2, 1)
-    far, inverse, probe_coef, leaf_basis, sample_first = call(
-        leaf_kernel,
-        [(rows, columns), (columns, columns), (columns, width), (rows, columns), (columns, columns)],
-        near, rest, following, handed, probes, flops=10 * rows * rows * width,
-    )
-    (sample_last,) = call(
-        second_kernel, [(columns, width - columns)], near, rest, following_2, handed_2, leaf_basis,
-        flops=4 * rows * rows * width,
-    )
-    sample_coef = jnp.concatenate([sample_first, sample_last], axis=1)
-
-    def place(level, node):
-        index = subtree - (subtree >> level - 1) + (node >> 1)
-        slot = lax.dynamic_index_in_dim(node_slot[0], index, 0, keepdims=False)
-        return jnp.stack([slot, node & 1]).astype(jnp.int32)
-
-    shape = (columns, width)
+    handed_last = flat_shift(handed_last, 1)
+    following_last = flat_shift(probes_last, -1)
+    (rest,) = call(rest_kernel, [(rows, width)], near, probes, samples, flops=work)
+    square, square_last, shape = (columns, columns), (columns, width - columns), (columns, width)
+    far, inverse, first, probe_coef = call(
+        leaf_kernel, [tall, square, square, shape], near, rest, following, handed, probes, flops=work
+    )
+    leaf_basis, last = call(
+        leaf_last_kernel, [tall, square_last],
+        near, rest, following_last, handed_last, far, inverse, flops=work,
+    )
+
     ancestors = []
     for level in range(1, levels + 1):
         copies = 2 ** (level - 1)
-        node = member // copies
         count = subtree // copies
-        own_place = place(level, node)
         if count == 4:
             away = outward(probe_coef, 2 * copies)
-            outer = (node == 0) | (node == 3)
-            main = jnp.where(outer, probe_coef, away)
-            other = jnp.where(outer, away, probe_coef)
-            (term,) = call(coupling_kernel, [shape], place(level, node ^ 2), table, main, other, scalars=1)
-            sibling_coef, sibling_probes = swapped((sample_coef, probe_coef), copies)
-            own = sample_coef - swapped(term, 2 * copies)
-            sibling = sibling_coef - swapped(term, 3 * copies)
+            (term,) = call(
+                functools.partial(term_kernel, level), [shape], couplings, probe_coef, away,
+                slots=node_slot,
+            )
+            term = swapped(term, 2 * copies)
+            first = first - term[:, :columns]
+            last = last - term[:, columns:]
         else:
             if count == 2:
                 from_left, from_right = tree_shift(probe_coef, 1), tree_shift(probe_coef, -1)
             else:
                 from_left = flat_shift(probe_coef, 2 * copies)
                 from_right = flat_shift(probe_coef, -2 * copies)
-            even = node & 1 == 0
-            main = jnp.where(even, from_left, from_right)
-            other = jnp.where(even, from_right, from_left)
-            (own,) = call(
-                corrected_kernel, [shape], own_place, table, main, other, sample_coef, scalars=1
+            first, last = call(
+                functools.partial(corrected_kernel, level), [square, square_last],
+                couplings, from_left, from_right, first, last, slots=node_slot,
             )
-            sibling, sibling_probes = swapped((own, probe_coef), copies)
-        basis, sample_coef, probe_coef = call(
-            node_kernel, [(2 * columns, columns), shape, shape],
-            own_place, own, sibling, probe_coef, sibling_probes, scalars=1,
+        mine = (first, last, probe_coef)
+        theirs = tuple(swapped(value, copies) for value in mine)
+        final = level == levels
+        bases = (1, level if final else 1, 2 * columns, columns)
+        inverse, basis = call(
+            functools.partial(factor_kernel, level), [square, bases],
+            mine[0], theirs[0], *(ancestors if final else []), flops=work,
         )
         ancestors.append(basis)
-    transfer_bases = jnp.stack(ancestors, axis=0)[None]
-    return (leaf_basis, transfer_bases, sample_coef[None], probe_coef[None])
+        if final:
+            top_samples, top_probes = call(
+                top_kernel, [(1,) + shape, (1,) + shape], inverse, *mine, *theirs
+            )
+        else:
+            first, last, probe_coef = call(
+                node_kernel, [square, square_last, shape], inverse, *mine, *theirs
+            )
+    return (leaf_basis, ancestors[-1], top_samples, top_probes)
 
 
 def solution(mesh):

time: 102 us -> 85.1 us (0.83)
  waiting for transfers between devices: 38.3 us -> 22.1 us
  starting transfers between devices: 24.8 us -> 29.7 us
  local copies, waits for them, and re-layouts: 6.73 us -> 3.68 us
  other arithmetic: 3.04 us -> 0.02 us
    ppermute x5, waiting for transfers between devices: 17.2 us -> 4.13 us  [permuted(): return lax.ppermute(value, BOTH, pairs)]
    ppermute x6 -> x7, waiting for transfers between devices: 17.7 us -> 12.7 us  [swapped(): return lax.ppermute(value, 'leaf', pairs)]
    ppermute x5, starting transfers between devices: 15.7 us -> 19 us  [permuted(): return lax.ppermute(value, BOTH, pairs)]
    another operation x3 -> x0, other arithmetic: 2.24 us -> none  [place(): return jnp.stack([slot, node & 1]).astype(jnp.int32)]
    ppermute x2, waiting for transfers between devices: 3.42 us -> 5.26 us  [tree_shift(): return lax.ppermute(value, 'clusters', pairs)]
    unnamed x18 -> x12, local copies, waits for them, and re-layouts: 4.23 us -> 2.65 us
    ppermute x6 -> x7, starting transfers between devices: 4.84 us -> 6.2 us  [swapped(): return lax.ppermute(value, 'leaf', pairs)]
    pallas_call x8 -> x10, Pallas kernels: 27.4 us -> 27.6 us  [call(): pl.pallas_call(kernel, out_shape=outs, in_specs=specs, out_specs=[VMEM] *...]
  transfers between devices with their start and end apart: 13 -> 14, of which waited for: 9 -> 7; matrix products, arithmetic and copies ran while one was open for 3% -> 0% of each run, Pallas kernels for 8% -> 27%
where the time goes in v2:
time: 85.1 us; the launch traced here: 83.9 us
  starting transfers between devices  29.7 us (35%)
  Pallas kernels  27.6 us (32%)
  waiting for transfers between devices  22.1 us (26%)
  local copies, waits for them, and re-layouts  3.68 us (4%)
  between operations  0.86 us (1%)
    pallas_call x10, Pallas kernels, call(): pl.pallas_call(kernel, out_shape=outs, in_specs=specs, out_specs=[VMEM] *...  27.6 us
    ppermute x5, starting transfers between devices, permuted(): return lax.ppermute(value, BOTH, pairs)  19 us
    ppermute x7, waiting for transfers between devices, swapped(): return lax.ppermute(value, 'leaf', pairs)  12.7 us
    ppermute x7, starting transfers between devices, swapped(): return lax.ppermute(value, 'leaf', pairs)  6.2 us
    ppermute x2, waiting for transfers between devices, tree_shift(): return lax.ppermute(value, 'clusters', pairs)  5.26 us
    ppermute x2, starting transfers between devices, tree_shift(): return lax.ppermute(value, 'clusters', pairs)  4.49 us
    ppermute x5, waiting for transfers between devices, permuted(): return lax.ppermute(value, BOTH, pairs)  4.13 us
    unnamed x12, local copies, waits for them, and re-layouts  2.65 us
  transfers between devices with their start and end apart: 14, of which 7 were waited for; matrix products, arithmetic and copies ran while one was open for 0% of the time, Pallas kernels for 27%

profile of v2, /device:TPU:4, one launch (start us, length us, event | category | flops | bytes accessed | tf_op | source)
XLA Modules:
  0.0 83.9 jit_solution(4521325056731596544)
XLA Ops:
  1.7 5.8 %collective-permute-start.2 = (f32[512,128]{1,0:T(8,128)S(1)}, f32[512,128]{1,0:T(8,128)S(1)}, u32[]{:S(2)}, u32[]{:S(2)}) collective-permute-start(f32[512,128]{1,0:T(8,128)S(1)} %slice.9), channel_id=1, source_target_pairs={{1,24},{2,25},{3,26},{4,27},{5,28},{6,29},{7,30},{8,0},{9,1},{10,2... | collective-permute-start | bytes 786440 | tf_op jit(solution)/shard_map/ppermute | solution.py:216
  7.5 1.6 %copy-done = f32[512,2,512]{2,1,0:T(2,128)S(1)} copy-done((f32[512,2,512]{2,1,0:T(2,128)S(1)}, f32[512,2,512]{2,1,0:T(2,128)}, u32[]{:S(2)}) %copy-start) | copy-done | bytes 2097176
  10.1 1.3 %shard_map.85 = (f32[512,128]{1,0:T(8,128)S(1)}, f32[512,128]{1,0:T(8,128)S(1)}, f32[512,128]{1,0:T(8,128)S(1)}) custom-call(f32[4096,128]{1,0:T(8,128)S(1)} %bitcast.5, f32[512,256]{1,0:T(8,128)S(1)} %copy-done.2), custom_call_target="tpu_custom_call" | custom-call | flops 805306368 | bytes 3407872 | tf_op jit(solution)/shard_map/pallas_call | solution.py:198
  11.4 1.9 %collective-permute-start.3 = (f32[512,128]{1,0:T(8,128)S(1)}, f32[512,128]{1,0:T(8,128)S(1)}, u32[]{:S(2)}, u32[]{:S(2)}) collective-permute-start(f32[512,128]{1,0:T(8,128)S(1)} %get-tuple-element.26), channel_id=1, source_target_pairs={{0,8},{1,9},{2,10},{3,11},{4,12},{5,13},{6,14},{7,15},{8,16},{9,17... | collective-permute-start | bytes 786440 | tf_op jit(solution)/shard_map/ppermute | solution.py:216
  13.4 7.2 %collective-permute-start = (f32[512,128]{1,0:T(8,128)S(1)}, f32[512,128]{1,0:T(8,128)S(1)}, u32[]{:S(2)}, u32[]{:S(2)}) collective-permute-start(f32[512,128]{1,0:T(8,128)S(1)} %get-tuple-element.24), channel_id=1, source_target_pairs={{1,24},{2,25},{3,26},{4,27},{5,28},{6,29},{7,30},{8,0},{9,1},{10,2... | collective-permute-start | bytes 786440 | tf_op jit(solution)/shard_map/ppermute | solution.py:216
  20.6 1.9 %collective-permute-start.1 = (f32[512,128]{1,0:T(8,128)S(1)}, f32[512,128]{1,0:T(8,128)S(1)}, u32[]{:S(2)}, u32[]{:S(2)}) collective-permute-start(f32[512,128]{1,0:T(8,128)S(1)} %get-tuple-element.25), channel_id=1, source_target_pairs={{0,8},{1,9},{2,10},{3,11},{4,12},{5,13},{6,14},{7,15},{8,16},{9,17... | collective-permute-start | bytes 786440 | tf_op jit(solution)/shard_map/ppermute | solution.py:216
  22.5 1.2 %shard_map.84.rest = f32[512,256]{1,0:T(8,128)S(1)} custom-call(f32[4096,128]{1,0:T(8,128)S(1)} %bitcast.6, f32[512,256]{1,0:T(8,128)S(1)} %copy-done.2, f32[512,256]{1,0:T(8,128)S(1)} %copy-done.4), custom_call_target="tpu_custom_call" | custom-call | flops 805306368 | bytes 3670016 | tf_op jit(solution)/shard_map/pallas_call | solution.py:198
  23.7 1.8 %collective-permute-done.3.handed = f32[512,128]{1,0:T(8,128)S(1)} collective-permute-done((f32[512,128]{1,0:T(8,128)S(1)}, f32[512,128]{1,0:T(8,128)S(1)}, u32[]{:S(2)}, u32[]{:S(2)}) %collective-permute-start.3) | collective-permute-done | bytes 262176 | tf_op jit(solution)/shard_map/ppermute | solution.py:216
  25.6 6.8 %shard_map.86 = (f32[512,128]{1,0:T(8,128)S(1)}, f32[128,128]{1,0:T(8,128)S(1)}, f32[128,128]{1,0:T(8,128)S(1)}, f32[128,256]{1,0:T(8,128)S(1)}) custom-call(f32[4096,128]{1,0:T(8,128)S(1)} %bitcast.7, f32[512,256]{1,0:T(8,128)S(1)} %shard_map.84.rest, f32[512,128]{1,0:T(8,128)S(1)} %collective-permute-done.2.following, ...), custom_call_target="tpu_custom_call" | custom-call | flops 805306368 | bytes 4194304 | tf_op jit(solution)/shard_map/pallas_call | solution.py:198
  32.4 2.1 %collective-permute-start.4 = (f32[128,256]{1,0:T(8,128)S(1)}, f32[128,256]{1,0:T(8,128)S(1)}, u32[]{:S(2)}, u32[]{:S(2)}) collective-permute-start(f32[128,256]{1,0:T(8,128)S(1)} %get-tuple-element.31.mine.mine_probes), channel_id=1, source_target_pairs={{1,0},{2,1},{3,2},{4,3},{5,4},{6,5},{7,6},{9,8},{10,9},{11,10},{12... | collective-permute-start | bytes 393224 | tf_op jit(solution)/shard_map/ppermute | solution.py:216
  34.5 2.3 %collective-permute-done.4.away = f32[128,256]{1,0:T(8,128)S(1)} collective-permute-done((f32[128,256]{1,0:T(8,128)S(1)}, f32[128,256]{1,0:T(8,128)S(1)}, u32[]{:S(2)}, u32[]{:S(2)}) %collective-permute-start.4) | collective-permute-done | bytes 131104 | tf_op jit(solution)/shard_map/ppermute | solution.py:216
  37.9 2.1 %shard_map.87 = (f32[512,128]{1,0:T(8,128)}, f32[128,128]{1,0:T(8,128)S(1)}) custom-call(f32[4096,128]{1,0:T(8,128)S(1)} %bitcast.8, f32[512,256]{1,0:T(8,128)S(1)} %shard_map.84.rest, f32[512,128]{1,0:T(8,128)S(1)} %collective-permute-done.following, f32[512,128]{1,0:T(8,128)S(1)} %collective-permute-done.1.handed, f32[512,128]{1,0:T(8,128)S(1)} %get-tuple-element.27.far, ...), custom_call_target="tpu_custom_call" | custom-call | flops 805306368 | bytes 3801088 | tf_op jit(solution)/shard_map/pallas_call | solution.py:198
  40.0 5.7 %collective-permute-done.5 = f32[128,256]{1,0:T(8,128)S(1)} collective-permute-done((f32[128,256]{1,0:T(8,128)S(1)}, f32[128,256]{1,0:T(8,128)S(1)}, u32[]{:S(2)}, u32[]{:S(2)}) %collective-permute-start.5) | collective-permute-done | bytes 131104 | tf_op jit(solution)/shard_map/ppermute | solution.py:232
  45.8 2.0 %collective-permute-start.8 = (f32[128,256]{1,0:T(8,128)S(1)}, f32[128,256]{1,0:T(8,128)S(1)}, u32[]{:S(2)}, u32[]{:S(2)}) collective-permute-start(f32[128,256]{1,0:T(8,128)S(1)} %get-tuple-element.31.mine.mine_probes), channel_id=1, source_target_pairs={{0,8},{8,0},{16,24},{24,16},{1,9},{9,1},{17,25},{25,17},{2,10},{10... | collective-permute-start | bytes 393224 | tf_op jit(solution)/shard_map/ppermute | solution.py:232
  47.9 2.2 %collective-permute-done.6.theirs = f32[128,128]{1,0:T(8,128)S(1)} collective-permute-done((f32[128,128]{1,0:T(8,128)S(1)}, f32[128,128]{1,0:T(8,128)S(1)}, u32[]{:S(2)}, u32[]{:S(2)}) %collective-permute-start.6) | collective-permute-done | bytes 65568 | tf_op jit(solution)/shard_map/ppermute | solution.py:232
  50.0 4.9 %shard_map.89 = (f32[128,128]{1,0:T(8,128)S(1)}, f32[1,1,256,128]{3,2,1,0:T(8,128)S(1)}) custom-call(f32[128,128]{1,0:T(8,128)S(1)} %get-tuple-element.45.mine, f32[128,128]{1,0:T(8,128)S(1)} %collective-permute-done.6.theirs), custom_call_target="tpu_custom_call" | custom-call | flops 805306368 | bytes 327680 | tf_op jit(solution)/shard_map/pallas_call | solution.py:198
  55.0 1.5 %shard_map.90 = (f32[128,128]{1,0:T(8,128)S(1)}, f32[128,128]{1,0:T(8,128)S(1)}, f32[128,256]{1,0:T(8,128)S(1)}) custom-call(f32[128,128]{1,0:T(8,128)S(1)} %get-tuple-element.32.inverse, f32[128,128]{1,0:T(8,128)S(1)} %get-tuple-element.45.mine, f32[128,128]{1,0:T(8,128)S(1)} %get-tuple-element.44.mine_last, ...), custom_call_target="tpu_custom_call" | custom-call | bytes 851968 | tf_op jit(solution)/shard_map/pallas_call | solution.py:198
  56.5 2.6 %collective-permute-start.10 = (f32[128,256]{1,0:T(8,128)S(1)}, f32[128,256]{1,0:T(8,128)S(1)}, u32[]{:S(2)}, u32[]{:S(2)}) collective-permute-start(f32[128,256]{1,0:T(8,128)S(1)} %get-tuple-element.34.mine_probes), channel_id=1, source_target_pairs={{1,0},{2,1},{3,2},{4,3},{5,4},{6,5},{7,6},{9,8},{10,9},{11,10},{12... | collective-permute-start | bytes 393224 | tf_op jit(solution)/shard_map/ppermute | solution.py:227
  59.1 1.9 %collective-permute-start.9 = (f32[128,256]{1,0:T(8,128)S(1)}, f32[128,256]{1,0:T(8,128)S(1)}, u32[]{:S(2)}, u32[]{:S(2)}) collective-permute-start(f32[128,256]{1,0:T(8,128)S(1)} %get-tuple-element.34.mine_probes), channel_id=1, source_target_pairs={{0,1},{1,2},{2,3},{3,4},{4,5},{5,6},{6,7},{8,9},{9,10},{10,11},{11... | collective-permute-start | bytes 393224 | tf_op jit(solution)/shard_map/ppermute | solution.py:227
  61.9 4.4 %collective-permute-done.9.from_left = f32[128,256]{1,0:T(8,128)S(1)} collective-permute-done((f32[128,256]{1,0:T(8,128)S(1)}, f32[128,256]{1,0:T(8,128)S(1)}, u32[]{:S(2)}, u32[]{:S(2)}) %collective-permute-start.9) | collective-permute-done | bytes 131104 | tf_op jit(solution)/shard_map/ppermute | solution.py:227
  68.3 1.9 %collective-permute-start.13 = (f32[128,256]{1,0:T(8,128)S(1)}, f32[128,256]{1,0:T(8,128)S(1)}, u32[]{:S(2)}, u32[]{:S(2)}) collective-permute-start(f32[128,256]{1,0:T(8,128)S(1)} %get-tuple-element.34.mine_probes), channel_id=1, source_target_pairs={{0,16},{8,24},{16,0},{24,8},{1,17},{9,25},{17,1},{25,9},{2,18},{10... | collective-permute-start | bytes 393224 | tf_op jit(solution)/shard_map/ppermute | solution.py:232
  71.2 4.8 %collective-permute-done.11.theirs = f32[128,128]{1,0:T(8,128)S(1)} collective-permute-done((f32[128,128]{1,0:T(8,128)S(1)}, f32[128,128]{1,0:T(8,128)S(1)}, u32[]{:S(2)}, u32[]{:S(2)}) %collective-permute-start.11) | collective-permute-done | bytes 65568 | tf_op jit(solution)/shard_map/ppermute | solution.py:232
  76.1 5.6 %shard_map.92 = (f32[128,128]{1,0:T(8,128)S(1)}, f32[1,2,256,128]{3,2,1,0:T(8,128)}) custom-call(f32[128,128]{1,0:T(8,128)S(1)} %get-tuple-element.37.mine, f32[128,128]{1,0:T(8,128)S(1)} %collective-permute-done.11.theirs, f32[1,1,256,128]{3,2,1,0:T(8,128)S(1)} %get-tuple-element.38.refs_0_), custom_call_target="tpu_custom_call" | custom-call | flops 805306368 | bytes 589824 | tf_op jit(solution)/shard_map/pallas_call | solution.py:198
  81.7 2.2 %shard_map.93 = (f32[1,128,256]{2,1,0:T(8,128)}, f32[1,128,256]{2,1,0:T(8,128)}) custom-call(f32[128,128]{1,0:T(8,128)S(1)} %get-tuple-element.40.inverse, f32[128,128]{1,0:T(8,128)S(1)} %get-tuple-element.37.mine, f32[128,128]{1,0:T(8,128)S(1)} %get-tuple-element.41.mine_last, f32[128,256]{1,0:T(8,128)S(1)} %get-tuple-element.34.mine_probes, ...), custom_call_target="tpu_custom_call" | custom-call | bytes 851968 | tf_op jit(solution)/shard_map/pallas_call | solution.py:198
  (28 shorter events, 7.1 us)
Async XLA Ops:
  0.6 21.9 %copy-start.4 = (f32[512,256]{1,0:T(8,128)S(1)}, f32[512,256]{1,0:T(8,128)}, u32[]{:S(2)}) copy-start(f32[512,256]{1,0:T(8,128)} %samples.1) | copy-start | bytes 1572868
  1.7 22.1 %collective-permute-start.2 = (f32[512,128]{1,0:T(8,128)S(1)}, f32[512,128]{1,0:T(8,128)S(1)}, u32[]{:S(2)}, u32[]{:S(2)}) collective-permute-start(f32[512,128]{1,0:T(8,128)S(1)} %slice.9), channel_id=1, source_target_pairs={{1,24},{2,25},{3,26},{4,27},{5,28},{6,29},{7,30},{8,0},{9,1},{10,2... | collective-permute-start | bytes 786440 | tf_op jit(solution)/shard_map/ppermute | solution.py:216
  7.5 1.6 %copy-start = (f32[512,2,512]{2,1,0:T(2,128)S(1)}, f32[512,2,512]{2,1,0:T(2,128)}, u32[]{:S(2)}) copy-start(f32[512,2,512]{2,1,0:T(2,128)} %param.7) | copy-start | bytes 6291460
  9.1 1.0 %copy-start.2 = (f32[512,256]{1,0:T(8,128)S(1)}, f32[512,256]{1,0:T(8,128)}, u32[]{:S(2)}) copy-start(f32[512,256]{1,0:T(8,128)} %probes.5) | copy-start | bytes 1572868
  11.4 14.1 %collective-permute-start.3 = (f32[512,128]{1,0:T(8,128)S(1)}, f32[512,128]{1,0:T(8,128)S(1)}, u32[]{:S(2)}, u32[]{:S(2)}) collective-permute-start(f32[512,128]{1,0:T(8,128)S(1)} %get-tuple-element.26), channel_id=1, source_target_pairs={{0,8},{1,9},{2,10},{3,11},{4,12},{5,13},{6,14},{7,15},{8,16},{9,17... | collective-permute-start | bytes 786440 | tf_op jit(solution)/shard_map/ppermute | solution.py:216
  13.4 24.5 %collective-permute-start = (f32[512,128]{1,0:T(8,128)S(1)}, f32[512,128]{1,0:T(8,128)S(1)}, u32[]{:S(2)}, u32[]{:S(2)}) collective-permute-start(f32[512,128]{1,0:T(8,128)S(1)} %get-tuple-element.24), channel_id=1, source_target_pairs={{1,24},{2,25},{3,26},{4,27},{5,28},{6,29},{7,30},{8,0},{9,1},{10,2... | collective-permute-start | bytes 786440 | tf_op jit(solution)/shard_map/ppermute | solution.py:216
  20.6 17.3 %collective-permute-start.1 = (f32[512,128]{1,0:T(8,128)S(1)}, f32[512,128]{1,0:T(8,128)S(1)}, u32[]{:S(2)}, u32[]{:S(2)}) collective-permute-start(f32[512,128]{1,0:T(8,128)S(1)} %get-tuple-element.25), channel_id=1, source_target_pairs={{0,8},{1,9},{2,10},{3,11},{4,12},{5,13},{6,14},{7,15},{8,16},{9,17... | collective-permute-start | bytes 786440 | tf_op jit(solution)/shard_map/ppermute | solution.py:216
  23.7 13.1 %copy-start.3 = (f32[1,3,2,128,128]{4,3,2,1,0:T(8,128)S(1)}, f32[1,3,2,128,128]{4,3,2,1,0:T(8,128)}, u32[]{:S(2)}) copy-start(f32[1,3,2,128,128]{4,3,2,1,0:T(8,128)} %couplings.3) | copy-start | bytes 1179652
  23.7 13.1 %copy-start.5 = (s32[1,3]{1,0:T(1,128)S(1)}, s32[1,3]{1,0:T(1,128)}, u32[]{:S(2)}) copy-start(s32[1,3]{1,0:T(1,128)} %slots.3) | copy-start | bytes 40
  23.7 14.2 %copy-start.1 = (f32[512,2,512]{2,1,0:T(2,128)S(1)}, f32[512,2,512]{2,1,0:T(2,128)}, u32[]{:S(2)}) copy-start(f32[512,2,512]{2,1,0:T(2,128)} %param.7) | copy-start | bytes 6291460
  32.4 4.4 %collective-permute-start.4 = (f32[128,256]{1,0:T(8,128)S(1)}, f32[128,256]{1,0:T(8,128)S(1)}, u32[]{:S(2)}, u32[]{:S(2)}) collective-permute-start(f32[128,256]{1,0:T(8,128)S(1)} %get-tuple-element.31.mine.mine_probes), channel_id=1, source_target_pairs={{1,0},{2,1},{3,2},{4,3},{5,4},{6,5},{7,6},{9,8},{10,9},{11,10},{12... | collective-permute-start | bytes 393224 | tf_op jit(solution)/shard_map/ppermute | solution.py:216
  37.8 7.9 %collective-permute-start.5 = (f32[128,256]{1,0:T(8,128)S(1)}, f32[128,256]{1,0:T(8,128)S(1)}, u32[]{:S(2)}, u32[]{:S(2)}) collective-permute-start(f32[128,256]{1,0:T(8,128)S(1)} %shard_map.88), channel_id=1, source_target_pairs={{0,16},{8,24},{16,0},{24,8},{1,17},{9,25},{17,1},{25,9},{2,18},{10... | collective-permute-start | bytes 393224 | tf_op jit(solution)/shard_map/ppermute | solution.py:232
  45.7 4.3 %collective-permute-start.6 = (f32[128,128]{1,0:T(8,128)S(1)}, f32[128,128]{1,0:T(8,128)S(1)}, u32[]{:S(2)}, u32[]{:S(2)}) collective-permute-start(f32[128,128]{1,0:T(8,128)S(1)} %get-tuple-element.45.mine), channel_id=1, source_target_pairs={{0,8},{8,0},{16,24},{24,16},{1,9},{9,1},{17,25},{25,17},{2,10},{10... | collective-permute-start | bytes 196616 | tf_op jit(solution)/shard_map/ppermute | solution.py:232
  45.8 9.2 %collective-permute-start.8 = (f32[128,256]{1,0:T(8,128)S(1)}, f32[128,256]{1,0:T(8,128)S(1)}, u32[]{:S(2)}, u32[]{:S(2)}) collective-permute-start(f32[128,256]{1,0:T(8,128)S(1)} %get-tuple-element.31.mine.mine_probes), channel_id=1, source_target_pairs={{0,8},{8,0},{16,24},{24,16},{1,9},{9,1},{17,25},{25,17},{2,10},{10... | collective-permute-start | bytes 393224 | tf_op jit(solution)/shard_map/ppermute | solution.py:232
  47.8 7.2 %collective-permute-start.7 = (f32[128,128]{1,0:T(8,128)S(1)}, f32[128,128]{1,0:T(8,128)S(1)}, u32[]{:S(2)}, u32[]{:S(2)}) collective-permute-start(f32[128,128]{1,0:T(8,128)S(1)} %get-tuple-element.44.mine_last), channel_id=1, source_target_pairs={{0,8},{8,0},{16,24},{24,16},{1,9},{9,1},{17,25},{25,17},{2,10},{10... | collective-permute-start | bytes 196616 | tf_op jit(solution)/shard_map/ppermute | solution.py:232
  56.5 5.4 %collective-permute-start.10 = (f32[128,256]{1,0:T(8,128)S(1)}, f32[128,256]{1,0:T(8,128)S(1)}, u32[]{:S(2)}, u32[]{:S(2)}) collective-permute-start(f32[128,256]{1,0:T(8,128)S(1)} %get-tuple-element.34.mine_probes), channel_id=1, source_target_pairs={{1,0},{2,1},{3,2},{4,3},{5,4},{6,5},{7,6},{9,8},{10,9},{11,10},{12... | collective-permute-start | bytes 393224 | tf_op jit(solution)/shard_map/ppermute | solution.py:227
  59.1 7.2 %collective-permute-start.9 = (f32[128,256]{1,0:T(8,128)S(1)}, f32[128,256]{1,0:T(8,128)S(1)}, u32[]{:S(2)}, u32[]{:S(2)}) collective-permute-start(f32[128,256]{1,0:T(8,128)S(1)} %get-tuple-element.34.mine_probes), channel_id=1, source_target_pairs={{0,1},{1,2},{2,3},{3,4},{4,5},{5,6},{6,7},{8,9},{9,10},{10,11},{11... | collective-permute-start | bytes 393224 | tf_op jit(solution)/shard_map/ppermute | solution.py:227
  67.3 8.8 %collective-permute-start.11 = (f32[128,128]{1,0:T(8,128)S(1)}, f32[128,128]{1,0:T(8,128)S(1)}, u32[]{:S(2)}, u32[]{:S(2)}) collective-permute-start(f32[128,128]{1,0:T(8,128)S(1)} %get-tuple-element.37.mine), channel_id=1, source_target_pairs={{0,16},{8,24},{16,0},{24,8},{1,17},{9,25},{17,1},{25,9},{2,18},{10... | collective-permute-start | bytes 196616 | tf_op jit(solution)/shard_map/ppermute | solution.py:232
  68.3 13.4 %collective-permute-start.13 = (f32[128,256]{1,0:T(8,128)S(1)}, f32[128,256]{1,0:T(8,128)S(1)}, u32[]{:S(2)}, u32[]{:S(2)}) collective-permute-start(f32[128,256]{1,0:T(8,128)S(1)} %get-tuple-element.34.mine_probes), channel_id=1, source_target_pairs={{0,16},{8,24},{16,0},{24,8},{1,17},{9,25},{17,1},{25,9},{2,18},{10... | collective-permute-start | bytes 393224 | tf_op jit(solution)/shard_map/ppermute | solution.py:232
  70.3 11.5 %collective-permute-start.12 = (f32[128,128]{1,0:T(8,128)S(1)}, f32[128,128]{1,0:T(8,128)S(1)}, u32[]{:S(2)}, u32[]{:S(2)}) collective-permute-start(f32[128,128]{1,0:T(8,128)S(1)} %get-tuple-element.41.mine_last), channel_id=1, source_target_pairs={{0,16},{8,24},{16,0},{24,8},{1,17},{9,25},{17,1},{25,9},{2,18},{10... | collective-permute-start | bytes 196616 | tf_op jit(solution)/shard_map/ppermute | solution.py:232

commit v3 on v2

v3 whole, which is shorter than its diff:
```python
import functools

import jax
import jax.numpy as jnp
from jax import lax
from jax.experimental import pallas as pl
from jax.experimental.pallas import tpu as pltpu
from jax.sharding import PartitionSpec as P

HIGHEST = lax.Precision.HIGHEST
ROWS = 8
GROUP = 4
BOTH = ("leaf", "clusters")


def dot(a, b, ca=1, cb=0):
    return lax.dot_general(
        a, b, (((ca,), (cb,)), ((), ())), precision=HIGHEST, preferred_element_type=jnp.float32
    )


def across_lanes(tile, lane):
    return jnp.broadcast_to(tile[:, lane : lane + 1], tile.shape)


def across_rows(tile, row):
    return jnp.broadcast_to(tile[row : row + 1, :], tile.shape)


def inverse_factor(gram):
    size = gram.shape[0]
    blocks = size // ROWS
    sub = lax.broadcasted_iota(jnp.int32, (ROWS, size), 0)
    lane = lax.broadcasted_iota(jnp.int32, (ROWS, size), 1)
    left = [gram[ROWS * i : ROWS * (i + 1), :] for i in range(blocks)]
    right = [jnp.where(lane == sub + ROWS * i, 1.0, 0.0).astype(jnp.float32) for i in range(blocks)]
    scaled = [None] * blocks
    for first in range(0, blocks, GROUP):
        last = first + GROUP
        ahead = min(last + 1, blocks)
        scales = []
        for k in range(first, last):
            cols = {
                i: [across_lanes(left[i], ROWS * k + c) for c in range(ROWS)] for i in range(k, ahead)
            }
            pivots = jnp.ones((ROWS, size), jnp.float32)
            for j in range(0, ROWS, 2):
                a = across_rows(cols[k][j], j)
                b = across_rows(cols[k][j], j + 1)
                c = across_rows(cols[k][j + 1], j + 1)
                det = a * c - b * b
                inverse = 1.0 / det
                inverse_a = 1.0 / a
                ratio = b * inverse_a
                pivots = jnp.where(sub == j, a, jnp.where(sub == j + 1, det * inverse_a, pivots))
                left_rows = across_rows(left[k], j), across_rows(left[k], j + 1)
                right_rows = across_rows(right[k], j), across_rows(right[k], j + 1)
                col_rows = [
                    (across_rows(cols[k][n], j), across_rows(cols[k][n], j + 1))
                    for n in range(j + 2, ROWS)
                ]
                for i in range(k, ahead):
                    u, v = cols[i][j], cols[i][j + 1]
                    f = (u * c - v * b) * inverse
                    g = (v * a - u * b) * inverse
                    if i == k:
                        f = jnp.where(sub > j + 1, f, jnp.where(sub == j + 1, ratio, 0.0))
                        g = jnp.where(sub > j + 1, g, 0.0)
                    for n in range(j + 2, ROWS):
                        x, y = col_rows[n - j - 2]
                        cols[i][n] = cols[i][n] - (f * x + g * y)
                    left[i] = left[i] - (f * left_rows[0] + g * left_rows[1])
                    right[i] = right[i] - (f * right_rows[0] + g * right_rows[1])
            scales.append(lax.rsqrt(pivots))
        for k in range(first, last):
            scaled[k] = right[k] * scales[k - first]
        if ahead < blocks:
            upper = jnp.concatenate([left[k] * scales[k - first] for k in range(first, last)], axis=0)
            lower = jnp.concatenate(scaled[first:last], axis=0)
            change = dot(upper, jnp.concatenate([upper, lower], axis=1), 0, 0)
            for i in range(ahead, blocks):
                piece = change[ROWS * i : ROWS * (i + 1), :]
                left[i] = left[i] - piece[:, :size]
                right[i] = right[i] - piece[:, size:]
    return jnp.concatenate(scaled, axis=0)


def near_half(view, which, rows):
    chunks = rows // 128
    return jnp.concatenate(
        [view[pl.ds(2 * c + which, rows, stride=2 * chunks), :] for c in range(chunks)], axis=1
    )


def handed_kernel(near, probes, first):
    upper = near_half(near, 1, probes.shape[0])
    first[...] = dot(probes[:, : first.shape[1]].T, upper).T


def rest_kernel(near, probes, samples, rest, handed_last, probes_last):
    rows = probes.shape[0]
    columns = rest.shape[1] - probes_last.shape[1]
    probes_last[...] = probes[:, columns:]
    rest[...] = samples[...] - dot(near_half(near, 0, rows), probes[...])
    handed_last[...] = dot(probes[:, columns:].T, near_half(near, 1, rows)).T


def leaf_kernel(near, rest, following, handed, probes, far, inverse, sample_coef, probe_first, probe_last):
    columns = far.shape[1]
    upper = near_half(near, 1, rest.shape[0])
    block = rest[:, :columns] - dot(upper, following[...]) - handed[...]
    far[...] = block
    gram = dot(block, block, 0, 0)
    cross = dot(block, probes[...], 0, 0)
    factor = inverse_factor(gram)
    inverse[...] = factor
    coef = dot(factor, jnp.concatenate([cross, gram], axis=1))
    width = cross.shape[1]
    probe_first[...] = coef[:, :columns]
    probe_last[...] = coef[:, columns:width]
    sample_coef[...] = coef[:, width:]


def leaf_last_kernel(near, rest, following, handed, far, inverse, basis, sample_coef):
    columns = far.shape[1]
    upper = near_half(near, 1, rest.shape[0])
    basis[...] = dot(far[...], inverse[...], 1, 1)
    block = rest[:, columns:] - dot(upper, following[...]) - handed[...]
    sample_coef[...] = dot(basis[...], block, 0, 0)


def coupling_of(slots, couplings, level, node):
    subtree = lax.axis_size("leaf")
    index = subtree - (subtree >> level - 1) + (node >> 1)
    return couplings[0, slots[0, index], node & 1]


def member_node(level):
    return lax.axis_index("leaf") >> level - 1


def corrected_kernel(level, kind, slots, couplings, one, two, *refs):
    node = member_node(level)
    block = coupling_of(slots, couplings, level, node)
    if kind == "given":
        first_main = node >= 0
    elif kind == "quad":
        first_main = (node == 1) | (node == 2)
    else:
        first_main = (lax.axis_index("clusters") ^ node) & 1 == 1
    main = jnp.where(first_main, one[...], two[...])
    other = jnp.where(first_main, two[...], one[...])
    term = dot(block, main) + dot(block, other, 0, 0)
    half, at = len(refs) // 2, 0
    for coef, out in zip(refs[:half], refs[half:]):
        out[...] = coef[...] - term[:, at : at + out.shape[1]]
        at += out.shape[1]


def factor_kernel(level, mine, theirs, *refs):
    earlier, (inverse, bases) = refs[:-2], refs[-2:]
    for at, done in enumerate(earlier):
        bases[0, at] = done[0, 0]
    size = mine.shape[0]
    gram = dot(mine[...], mine[...], 0, 0) + dot(theirs[...], theirs[...], 0, 0)
    factor = inverse_factor(gram)
    inverse[...] = factor
    parity = member_node(level) & 1
    at = pl.multiple_of(parity * size, size)
    bases[0, len(earlier), pl.ds(at, size), :] = dot(mine[...], factor, 1, 1)
    at = pl.multiple_of((1 - parity) * size, size)
    bases[0, len(earlier), pl.ds(at, size), :] = dot(theirs[...], factor, 1, 1)


def level_coefs(refs):
    half = len(refs) // 2
    inverse = refs[0][...]
    mine, theirs = [ref[...] for ref in refs[1 : half + 1]], [ref[...] for ref in refs[half + 1 :]]
    own, sibling = jnp.concatenate(mine, axis=1), jnp.concatenate(theirs, axis=1)
    mine, theirs = mine[0], theirs[0]
    return dot(inverse, dot(mine, own, 0, 0) + dot(theirs, sibling, 0, 0))


def node_kernel(inputs, *refs):
    coef = level_coefs(refs[:inputs])
    at = 0
    for out in refs[inputs:]:
        out[...] = coef[:, at : at + out.shape[1]]
        at += out.shape[1]


def top_kernel(*refs):
    coef = level_coefs(refs[:-2])
    samples, probe_coef = refs[-2:]
    width = samples.shape[2]
    samples[0] = coef[:, :width]
    probe_coef[0] = coef[:, width:]


VMEM = pl.BlockSpec(memory_space=pltpu.VMEM)
SMEM = pl.BlockSpec(memory_space=pltpu.SMEM)


def call(kernel, shapes, *operands, slots=None, flops=0):
    outs = [jax.ShapeDtypeStruct(shape, jnp.float32) for shape in shapes]
    specs = [VMEM] * len(operands)
    if slots is not None:
        operands = (slots,) + operands
        specs = [SMEM] + specs
    moved = 4 * (sum(o.size for o in operands) + sum(o.size for o in outs))
    return pl.pallas_call(
        kernel,
        out_shape=outs,
        in_specs=specs,
        out_specs=[VMEM] * len(outs),
        compiler_params=pltpu.CompilerParams(vmem_limit_bytes=32 * 2**20),
        cost_estimate=pl.CostEstimate(flops=flops, bytes_accessed=moved, transcendentals=0),
    )(*operands)


def permuted(value, target):
    trees, subtree = lax.axis_size("clusters"), lax.axis_size("leaf")
    pairs = []
    for member in range(subtree):
        for tree in range(trees):
            to_tree, to_member = target(tree, member)
            if 0 <= to_tree < trees:
                pairs.append((member * trees + tree, to_member * trees + to_tree))
    return lax.ppermute(value, BOTH, pairs)


def flat_shift(value, by):
    subtree = lax.axis_size("leaf")
    return permuted(value, lambda tree, member: divmod(tree * subtree + member + by, subtree))


def swapped(value, mask):
    return permuted(value, lambda tree, member: (tree, member ^ mask))


def outer_swapped(value, half):
    return permuted(
        value, lambda tree, member: (tree - 1 if member < half else tree + 1, member ^ half)
    )


def tree_swapped(value, odd):
    return permuted(value, lambda tree, member: (tree + 1 if tree & 1 == odd else tree - 1, member))


def body(samples, probes, near_blocks, couplings, node_slot):
    rows, width = probes.shape
    columns = couplings.shape[-1]
    subtree = lax.axis_size("leaf")
    levels = subtree.bit_length() - 1
    chunks = rows // 128
    near = near_blocks.reshape(rows, 2, chunks, 128).transpose(0, 2, 1, 3).reshape(-1, 128)
    work = 12 * rows * rows * width

    tall, tall_last = (rows, columns), (rows, width - columns)
    following = flat_shift(probes[:, :columns], -1)
    (handed,) = call(handed_kernel, [tall], near, probes, flops=work)
    handed = flat_shift(handed, 1)
    rest, handed_last, probes_last = call(
        rest_kernel, [(rows, width), tall_last, tall_last], near, probes, samples, flops=work
    )
    handed_last = flat_shift(handed_last, 1)
    following_last = flat_shift(probes_last, -1)
    square, square_last = (columns, columns), (columns, width - columns)
    far, inverse, first, *probe_coefs = call(
        leaf_kernel, [tall, square, square, square, square_last],
        near, rest, following, handed, probes, flops=work,
    )
    leaf_basis, last = call(
        leaf_last_kernel, [tall, square_last],
        near, rest, following_last, handed_last, far, inverse, flops=work,
    )

    ancestors = []
    for level in range(1, levels + 1):
        copies = 2 ** (level - 1)
        count = subtree // copies
        if count == 2:
            meet = [functools.partial(tree_swapped, odd=odd) for odd in (0, 1)]
        elif count == 4:
            meet = [
                functools.partial(swapped, mask=2 * copies),
                functools.partial(outer_swapped, half=2 * copies),
            ]
        else:
            meet = [functools.partial(flat_shift, by=by) for by in (2 * copies, -2 * copies)]
        fields = [[go(coef) for go in meet] for coef in probe_coefs]
        if count > 4:
            even = (lax.axis_index("leaf") >> level - 1) & 1 == 0
            fields = [[jnp.where(even, *pair), jnp.where(even, *pair[::-1])] for pair in fields]
        kind = "given" if count > 4 else "quad" if count == 4 else "trees"
        correct = functools.partial(corrected_kernel, level, kind)
        if count == 2:
            first, last = call(
                correct, [square, square_last], couplings, *fields[0], first, last, slots=node_slot
            )
        else:
            (first,) = call(correct, [square], couplings, *fields[0], first, slots=node_slot)
            (last,) = call(correct, [square_last], couplings, *fields[1], last, slots=node_slot)
        mine = first, last, *probe_coefs
        theirs = [swapped(value, copies) for value in mine]
        final = level == levels
        bases = (1, level if final else 1, 2 * columns, columns)
        inverse, basis = call(
            functools.partial(factor_kernel, level), [square, bases],
            mine[0], theirs[0], *(ancestors if final else []), flops=work,
        )
        ancestors.append(basis)
        if final:
            top_samples, top_probes = call(
                top_kernel, [(1, columns, width), (1, columns, width)], inverse, *mine, *theirs
            )
        else:
            pieces = [(columns, width)] if count == 4 else [square, square_last]
            first, last, *probe_coefs = call(
                functools.partial(node_kernel, 1 + 2 * len(mine)),
                [square, square_last, *pieces], inverse, *mine, *theirs,
            )
    return (leaf_basis, ancestors[-1], top_samples, top_probes)


def solution(mesh):
    in_specs = (
        P(("clusters", "leaf"), None),
        P(("clusters", "leaf"), None),
        P(("clusters", "leaf"), None, None),
        P("clusters", None, None, None, None),
        P("clusters", None),
    )
    out_specs = (
        P(("clusters", "leaf"), None),
        P(("clusters", "leaf"), None, None, None),
        P("clusters", None, None),
        P("clusters", None, None),
    )
    return jax.shard_map(body, mesh=mesh, in_specs=in_specs, out_specs=out_specs, check_vma=False)
```

time: 85.1 us -> 84.5 us (level)
  starting transfers between devices: 29.7 us -> 36 us
  waiting for transfers between devices: 22.1 us -> 16.5 us
    ppermute x9 -> x0, waiting for transfers between devices: 17.9 us -> none  [the longest x7 12.7 us: swapped(): return lax.ppermute(value, 'leaf', pairs)]
    ppermute x5 -> x17, starting transfers between devices: 19 us -> 36 us  [permuted(): return lax.ppermute(value, BOTH, pairs)]
    ppermute x5 -> x17, waiting for transfers between devices: 4.13 us -> 16.5 us  [permuted(): return lax.ppermute(value, BOTH, pairs)]
    ppermute x9 -> x0, starting transfers between devices: 10.7 us -> none  [the longest x7 6.2 us: swapped(): return lax.ppermute(value, 'leaf', pairs)]
    pallas_call x10 -> x11, Pallas kernels: 27.6 us -> 27 us  [call(): pl.pallas_call(kernel, out_shape=outs, in_specs=specs, out_specs=[VMEM] *...]
  transfers between devices with their start and end apart: 14 -> 17, of which waited for: 7 -> 5; matrix products, arithmetic and copies ran while one was open for 0% -> 0% of each run, Pallas kernels for 27% -> 28%
where the time goes in v3:
time: 84.5 us; the launch traced here: 84.1 us
  starting transfers between devices  36 us (43%)
  Pallas kernels  27 us (32%)
  waiting for transfers between devices  16.5 us (20%)
  local copies, waits for them, and re-layouts  3.67 us (4%)
  between operations  0.86 us (1%)
    ppermute x17, starting transfers between devices, permuted(): return lax.ppermute(value, BOTH, pairs)  36 us
    pallas_call x11, Pallas kernels, call(): pl.pallas_call(kernel, out_shape=outs, in_specs=specs, out_specs=[VMEM] *...  27 us
    ppermute x17, waiting for transfers between devices, permuted(): return lax.ppermute(value, BOTH, pairs)  16.5 us
    unnamed x12, local copies, waits for them, and re-layouts  2.65 us
  transfers between devices with their start and end apart: 17, of which 5 were waited for; matrix products, arithmetic and copies ran while one was open for 0% of the time, Pallas kernels for 28%

profile of v3, /device:TPU:4, one launch (start us, length us, event | category | flops | bytes accessed | tf_op | source)
XLA Modules:
  0.0 84.1 jit_solution(15722243024633201471)
XLA Ops:
  0.6 1.0 %slice.3 = f32[512,128]{1,0:T(8,128)S(1)} slice(f32[512,256]{1,0:T(8,128)} %probes.5), slice={[0:512], [0:128]} | slice | bytes 524288 | tf_op jit(solution)/shard_map/slice | solution.py:261
  1.7 5.8 %collective-permute-start.2 = (f32[512,128]{1,0:T(8,128)S(1)}, f32[512,128]{1,0:T(8,128)S(1)}, u32[]{:S(2)}, u32[]{:S(2)}) collective-permute-start(f32[512,128]{1,0:T(8,128)S(1)} %slice.3), channel_id=1, source_target_pairs={{1,24},{2,25},{3,26},{4,27},{5,28},{6,29},{7,30},{8,0},{9,1},{10,2... | collective-permute-start | bytes 786440 | tf_op jit(solution)/shard_map/ppermute | solution.py:229
  7.5 1.6 %copy-done = f32[512,2,512]{2,1,0:T(2,128)S(1)} copy-done((f32[512,2,512]{2,1,0:T(2,128)S(1)}, f32[512,2,512]{2,1,0:T(2,128)}, u32[]{:S(2)}) %copy-start) | copy-done | bytes 2097176
  9.1 1.0 %copy-done.3 = f32[512,256]{1,0:T(8,128)S(1)} copy-done((f32[512,256]{1,0:T(8,128)S(1)}, f32[512,256]{1,0:T(8,128)}, u32[]{:S(2)}) %copy-start.3) | copy-done | bytes 524312
  11.0 1.9 %collective-permute-start.3 = (f32[512,128]{1,0:T(8,128)S(1)}, f32[512,128]{1,0:T(8,128)S(1)}, u32[]{:S(2)}, u32[]{:S(2)}) collective-permute-start(f32[512,128]{1,0:T(8,128)S(1)} %shard_map.85), channel_id=1, source_target_pairs={{0,8},{1,9},{2,10},{3,11},{4,12},{5,13},{6,14},{7,15},{8,16},{9,17... | collective-permute-start | bytes 786440 | tf_op jit(solution)/shard_map/ppermute | solution.py:229
  13.0 1.6 %shard_map.84 = (f32[512,256]{1,0:T(8,128)S(1)}, f32[512,128]{1,0:T(8,128)S(1)}, f32[512,128]{1,0:T(8,128)S(1)}) custom-call(f32[4096,128]{1,0:T(8,128)S(1)} %bitcast.6, f32[512,256]{1,0:T(8,128)S(1)} %copy-done.3, f32[512,256]{1,0:T(8,128)S(1)} %copy-done.4), custom_call_target="tpu_custom_call" | custom-call | flops 805306368 | bytes 4194304 | tf_op jit(solution)/shard_map/pallas_call | solution.py:211
  14.6 7.4 %collective-permute-start = (f32[512,128]{1,0:T(8,128)S(1)}, f32[512,128]{1,0:T(8,128)S(1)}, u32[]{:S(2)}, u32[]{:S(2)}) collective-permute-start(f32[512,128]{1,0:T(8,128)S(1)} %get-tuple-element.26), channel_id=1, source_target_pairs={{1,24},{2,25},{3,26},{4,27},{5,28},{6,29},{7,30},{8,0},{9,1},{10,2... | collective-permute-start | bytes 786440 | tf_op jit(solution)/shard_map/ppermute | solution.py:229
  22.0 1.9 %collective-permute-start.1 = (f32[512,128]{1,0:T(8,128)S(1)}, f32[512,128]{1,0:T(8,128)S(1)}, u32[]{:S(2)}, u32[]{:S(2)}) collective-permute-start(f32[512,128]{1,0:T(8,128)S(1)} %get-tuple-element.27), channel_id=1, source_target_pairs={{0,8},{1,9},{2,10},{3,11},{4,12},{5,13},{6,14},{7,15},{8,16},{9,17... | collective-permute-start | bytes 786440 | tf_op jit(solution)/shard_map/ppermute | solution.py:229
  23.9 1.2 %collective-permute-done.3.handed = f32[512,128]{1,0:T(8,128)S(1)} collective-permute-done((f32[512,128]{1,0:T(8,128)S(1)}, f32[512,128]{1,0:T(8,128)S(1)}, u32[]{:S(2)}, u32[]{:S(2)}) %collective-permute-start.3) | collective-permute-done | bytes 262176 | tf_op jit(solution)/shard_map/ppermute | solution.py:229
  25.2 6.7 %shard_map.86 = (f32[512,128]{1,0:T(8,128)S(1)}, f32[128,128]{1,0:T(8,128)S(1)}, f32[128,128]{1,0:T(8,128)S(1)}, f32[128,128]{1,0:T(8,128)S(1)}, f32[128,128]{1,0:T(8,128)S(1)}) custom-call(f32[4096,128]{1,0:T(8,128)S(1)} %bitcast.7, f32[512,256]{1,0:T(8,128)S(1)} %get-tuple-element.25.rest, f32[512,128]{1,0:T(8,128)S(1)} %collective-permute-done.2.following, ...), custom_call_target="tpu_custom_call" | custom-call | flops 805306368 | bytes 4194304 | tf_op jit(solution)/shard_map/pallas_call | solution.py:211
  32.0 2.4 %collective-permute-start.5 = (f32[128,128]{1,0:T(8,128)S(1)}, f32[128,128]{1,0:T(8,128)S(1)}, u32[]{:S(2)}, u32[]{:S(2)}) collective-permute-start(f32[128,128]{1,0:T(8,128)S(1)} %get-tuple-element.31.refs_3_), channel_id=1, source_target_pairs={{1,16},{2,17},{3,18},{4,19},{5,20},{6,21},{7,22},{9,24},{10,25},{1... | collective-permute-start | bytes 196616 | tf_op jit(solution)/shard_map/ppermute | solution.py:229
  34.4 2.5 %collective-permute-start.7 = (f32[128,128]{1,0:T(8,128)S(1)}, f32[128,128]{1,0:T(8,128)S(1)}, u32[]{:S(2)}, u32[]{:S(2)}) collective-permute-start(f32[128,128]{1,0:T(8,128)S(1)} %get-tuple-element.34.refs_4_), channel_id=1, source_target_pairs={{0,16},{1,17},{2,18},{3,19},{4,20},{5,21},{6,22},{7,23},{8,24},{9,... | collective-permute-start | bytes 196616 | tf_op jit(solution)/shard_map/ppermute | solution.py:229
  37.9 2.7 %collective-permute-start.8 = (f32[128,128]{1,0:T(8,128)S(1)}, f32[128,128]{1,0:T(8,128)S(1)}, u32[]{:S(2)}, u32[]{:S(2)}) collective-permute-start(f32[128,128]{1,0:T(8,128)S(1)} %get-tuple-element.34.refs_4_), channel_id=1, source_target_pairs={{1,16},{2,17},{3,18},{4,19},{5,20},{6,21},{7,22},{9,24},{10,25},{1... | collective-permute-start | bytes 196616 | tf_op jit(solution)/shard_map/ppermute | solution.py:229
  40.6 1.1 %collective-permute-done.5.two = f32[128,128]{1,0:T(8,128)S(1)} collective-permute-done((f32[128,128]{1,0:T(8,128)S(1)}, f32[128,128]{1,0:T(8,128)S(1)}, u32[]{:S(2)}, u32[]{:S(2)}) %collective-permute-start.5) | collective-permute-done | bytes 65568 | tf_op jit(solution)/shard_map/ppermute | solution.py:229
  41.7 3.5 %collective-permute-start.10 = (f32[128,128]{1,0:T(8,128)S(1)}, f32[128,128]{1,0:T(8,128)S(1)}, u32[]{:S(2)}, u32[]{:S(2)}) collective-permute-start(f32[128,128]{1,0:T(8,128)S(1)} %get-tuple-element.31.refs_3_), channel_id=1, source_target_pairs={{0,8},{1,9},{2,10},{3,11},{4,12},{5,13},{6,14},{7,15},{8,0},{9,1},... | collective-permute-start | bytes 196616 | tf_op jit(solution)/shard_map/ppermute | solution.py:229
  46.1 2.0 %collective-permute-start.6 = (f32[128,128]{1,0:T(8,128)S(1)}, f32[128,128]{1,0:T(8,128)S(1)}, u32[]{:S(2)}, u32[]{:S(2)}) collective-permute-start(f32[128,128]{1,0:T(8,128)S(1)} %shard_map.88.mine.refs_1_), channel_id=1, source_target_pairs={{0,8},{1,9},{2,10},{3,11},{4,12},{5,13},{6,14},{7,15},{8,0},{9,1},... | collective-permute-start | bytes 196616 | tf_op jit(solution)/shard_map/ppermute | solution.py:229
  48.1 2.1 %shard_map.87 = (f32[512,128]{1,0:T(8,128)}, f32[128,128]{1,0:T(8,128)S(1)}) custom-call(f32[4096,128]{1,0:T(8,128)S(1)} %bitcast.8, f32[512,256]{1,0:T(8,128)S(1)} %get-tuple-element.25.rest, f32[512,128]{1,0:T(8,128)S(1)} %collective-permute-done.following, f32[512,128]{1,0:T(8,128)S(1)} %collective-permute-done.1.handed, ...), custom_call_target="tpu_custom_call" | custom-call | flops 805306368 | bytes 3801088 | tf_op jit(solution)/shard_map/pallas_call | solution.py:211
  51.3 4.8 %shard_map.89 = (f32[128,128]{1,0:T(8,128)S(1)}, f32[1,1,256,128]{3,2,1,0:T(8,128)S(1)}) custom-call(f32[128,128]{1,0:T(8,128)S(1)} %shard_map.88.mine.refs_1_, f32[128,128]{1,0:T(8,128)S(1)} %collective-permute-done.6.theirs.refs_5_), custom_call_target="tpu_custom_call" | custom-call | flops 805306368 | bytes 327680 | tf_op jit(solution)/shard_map/pallas_call | solution.py:211
  57.2 1.9 %collective-permute-start.13 = (f32[128,256]{1,0:T(8,128)S(1)}, f32[128,256]{1,0:T(8,128)S(1)}, u32[]{:S(2)}, u32[]{:S(2)}) collective-permute-start(f32[128,256]{1,0:T(8,128)S(1)} %get-tuple-element.36.refs_3_), channel_id=1, source_target_pairs={{1,2},{2,1},{3,4},{4,3},{5,6},{6,5},{9,10},{10,9},{11,12},{12,11},... | collective-permute-start | bytes 393224 | tf_op jit(solution)/shard_map/ppermute | solution.py:229
  59.2 5.2 %collective-permute-done.13.two = f32[128,256]{1,0:T(8,128)S(1)} collective-permute-done((f32[128,256]{1,0:T(8,128)S(1)}, f32[128,256]{1,0:T(8,128)S(1)}, u32[]{:S(2)}, u32[]{:S(2)}) %collective-permute-start.13) | collective-permute-done | bytes 131104 | tf_op jit(solution)/shard_map/ppermute | solution.py:229
  66.1 2.3 %collective-permute-start.16 = (f32[128,256]{1,0:T(8,128)S(1)}, f32[128,256]{1,0:T(8,128)S(1)}, u32[]{:S(2)}, u32[]{:S(2)}) collective-permute-start(f32[128,256]{1,0:T(8,128)S(1)} %get-tuple-element.36.refs_3_), channel_id=1, source_target_pairs={{0,16},{1,17},{2,18},{3,19},{4,20},{5,21},{6,22},{7,23},{8,24},{9,... | collective-permute-start | bytes 393224 | tf_op jit(solution)/shard_map/ppermute | solution.py:229
  69.0 7.9 %collective-permute-done.14.theirs.refs_4_ = f32[128,128]{1,0:T(8,128)S(1)} collective-permute-done((f32[128,128]{1,0:T(8,128)S(1)}, f32[128,128]{1,0:T(8,128)S(1)}, u32[]{:S(2)}, u32[]{:S(2)}) %collective-permute-start.14) | collective-permute-done | bytes 65568 | tf_op jit(solution)/shard_map/ppermute | solution.py:229
  76.9 5.5 %shard_map.93 = (f32[128,128]{1,0:T(8,128)S(1)}, f32[1,2,256,128]{3,2,1,0:T(8,128)}) custom-call(f32[128,128]{1,0:T(8,128)S(1)} %get-tuple-element.39.mine.refs_1_, f32[128,128]{1,0:T(8,128)S(1)} %collective-permute-done.14.theirs.refs_4_, f32[1,1,256,128]{3,2,1,0:T(8,128)S(1)} %get-tuple-element.40.refs_0_), custom_call_target="tpu_custom_call" | custom-call | flops 805306368 | bytes 589824 | tf_op jit(solution)/shard_map/pallas_call | solution.py:211
  82.5 1.7 %shard_map.94 = (f32[1,128,256]{2,1,0:T(8,128)}, f32[1,128,256]{2,1,0:T(8,128)}) custom-call(f32[128,128]{1,0:T(8,128)S(1)} %get-tuple-element.42.refs_0_, f32[128,128]{1,0:T(8,128)S(1)} %get-tuple-element.39.mine.refs_1_, f32[128,128]{1,0:T(8,128)S(1)} %get-tuple-element.43.refs_2_, f32[128,256]{1,0:T(8,128)S(1)} %get-tuple-element.36.refs_3_, ...), custom_call_target="tpu_custom_call" | custom-call | bytes 851968 | tf_op jit(solution)/shard_map/pallas_call | solution.py:211
  (34 shorter events, 7.3 us)
Async XLA Ops:
  0.6 12.3 %copy-start.4 = (f32[512,256]{1,0:T(8,128)S(1)}, f32[512,256]{1,0:T(8,128)}, u32[]{:S(2)}) copy-start(f32[512,256]{1,0:T(8,128)} %samples.1) | copy-start | bytes 1572868
  1.7 22.3 %collective-permute-start.2 = (f32[512,128]{1,0:T(8,128)S(1)}, f32[512,128]{1,0:T(8,128)S(1)}, u32[]{:S(2)}, u32[]{:S(2)}) collective-permute-start(f32[512,128]{1,0:T(8,128)S(1)} %slice.3), channel_id=1, source_target_pairs={{1,24},{2,25},{3,26},{4,27},{5,28},{6,29},{7,30},{8,0},{9,1},{10,2... | collective-permute-start | bytes 786440 | tf_op jit(solution)/shard_map/ppermute | solution.py:229
  7.5 1.6 %copy-start = (f32[512,2,512]{2,1,0:T(2,128)S(1)}, f32[512,2,512]{2,1,0:T(2,128)}, u32[]{:S(2)}) copy-start(f32[512,2,512]{2,1,0:T(2,128)} %param.7) | copy-start | bytes 6291460
  9.1 1.0 %copy-start.3 = (f32[512,256]{1,0:T(8,128)S(1)}, f32[512,256]{1,0:T(8,128)}, u32[]{:S(2)}) copy-start(f32[512,256]{1,0:T(8,128)} %probes.5) | copy-start | bytes 1572868
  11.0 14.2 %collective-permute-start.3 = (f32[512,128]{1,0:T(8,128)S(1)}, f32[512,128]{1,0:T(8,128)S(1)}, u32[]{:S(2)}, u32[]{:S(2)}) collective-permute-start(f32[512,128]{1,0:T(8,128)S(1)} %shard_map.85), channel_id=1, source_target_pairs={{0,8},{1,9},{2,10},{3,11},{4,12},{5,13},{6,14},{7,15},{8,16},{9,17... | collective-permute-start | bytes 786440 | tf_op jit(solution)/shard_map/ppermute | solution.py:229
  14.6 30.6 %copy-start.2 = (f32[1,3,2,128,128]{4,3,2,1,0:T(8,128)S(1)}, f32[1,3,2,128,128]{4,3,2,1,0:T(8,128)}, u32[]{:S(2)}) copy-start(f32[1,3,2,128,128]{4,3,2,1,0:T(8,128)} %couplings.5) | copy-start | bytes 1179652
  14.6 30.6 %copy-start.5 = (s32[1,3]{1,0:T(1,128)S(1)}, s32[1,3]{1,0:T(1,128)}, u32[]{:S(2)}) copy-start(s32[1,3]{1,0:T(1,128)} %slots.5) | copy-start | bytes 40
  14.6 31.4 %collective-permute-start = (f32[512,128]{1,0:T(8,128)S(1)}, f32[512,128]{1,0:T(8,128)S(1)}, u32[]{:S(2)}, u32[]{:S(2)}) collective-permute-start(f32[512,128]{1,0:T(8,128)S(1)} %get-tuple-element.26), channel_id=1, source_target_pairs={{1,24},{2,25},{3,26},{4,27},{5,28},{6,29},{7,30},{8,0},{9,1},{10,2... | collective-permute-start | bytes 786440 | tf_op jit(solution)/shard_map/ppermute | solution.py:229
  22.0 24.1 %collective-permute-start.1 = (f32[512,128]{1,0:T(8,128)S(1)}, f32[512,128]{1,0:T(8,128)S(1)}, u32[]{:S(2)}, u32[]{:S(2)}) collective-permute-start(f32[512,128]{1,0:T(8,128)S(1)} %get-tuple-element.27), channel_id=1, source_target_pairs={{0,8},{1,9},{2,10},{3,11},{4,12},{5,13},{6,14},{7,15},{8,16},{9,17... | collective-permute-start | bytes 786440 | tf_op jit(solution)/shard_map/ppermute | solution.py:229
  25.2 23.0 %copy-start.1 = (f32[512,2,512]{2,1,0:T(2,128)S(1)}, f32[512,2,512]{2,1,0:T(2,128)}, u32[]{:S(2)}) copy-start(f32[512,2,512]{2,1,0:T(2,128)} %param.7) | copy-start | bytes 6291460
  31.9 5.9 %collective-permute-start.4 = (f32[128,128]{1,0:T(8,128)S(1)}, f32[128,128]{1,0:T(8,128)S(1)}, u32[]{:S(2)}, u32[]{:S(2)}) collective-permute-start(f32[128,128]{1,0:T(8,128)S(1)} %get-tuple-element.31.refs_3_), channel_id=1, source_target_pairs={{0,16},{1,17},{2,18},{3,19},{4,20},{5,21},{6,22},{7,23},{8,24},{9,... | collective-permute-start | bytes 196616 | tf_op jit(solution)/shard_map/ppermute | solution.py:229
  32.0 9.7 %collective-permute-start.5 = (f32[128,128]{1,0:T(8,128)S(1)}, f32[128,128]{1,0:T(8,128)S(1)}, u32[]{:S(2)}, u32[]{:S(2)}) collective-permute-start(f32[128,128]{1,0:T(8,128)S(1)} %get-tuple-element.31.refs_3_), channel_id=1, source_target_pairs={{1,16},{2,17},{3,18},{4,19},{5,20},{6,21},{7,22},{9,24},{10,25},{1... | collective-permute-start | bytes 196616 | tf_op jit(solution)/shard_map/ppermute | solution.py:229
  34.4 15.9 %collective-permute-start.7 = (f32[128,128]{1,0:T(8,128)S(1)}, f32[128,128]{1,0:T(8,128)S(1)}, u32[]{:S(2)}, u32[]{:S(2)}) collective-permute-start(f32[128,128]{1,0:T(8,128)S(1)} %get-tuple-element.34.refs_4_), channel_id=1, source_target_pairs={{0,16},{1,17},{2,18},{3,19},{4,20},{5,21},{6,22},{7,23},{8,24},{9,... | collective-permute-start | bytes 196616 | tf_op jit(solution)/shard_map/ppermute | solution.py:229
  37.9 12.4 %collective-permute-start.8 = (f32[128,128]{1,0:T(8,128)S(1)}, f32[128,128]{1,0:T(8,128)S(1)}, u32[]{:S(2)}, u32[]{:S(2)}) collective-permute-start(f32[128,128]{1,0:T(8,128)S(1)} %get-tuple-element.34.refs_4_), channel_id=1, source_target_pairs={{1,16},{2,17},{3,18},{4,19},{5,20},{6,21},{7,22},{9,24},{10,25},{1... | collective-permute-start | bytes 196616 | tf_op jit(solution)/shard_map/ppermute | solution.py:229
  41.7 14.5 %collective-permute-start.10 = (f32[128,128]{1,0:T(8,128)S(1)}, f32[128,128]{1,0:T(8,128)S(1)}, u32[]{:S(2)}, u32[]{:S(2)}) collective-permute-start(f32[128,128]{1,0:T(8,128)S(1)} %get-tuple-element.31.refs_3_), channel_id=1, source_target_pairs={{0,8},{1,9},{2,10},{3,11},{4,12},{5,13},{6,14},{7,15},{8,0},{9,1},... | collective-permute-start | bytes 196616 | tf_op jit(solution)/shard_map/ppermute | solution.py:229
  46.1 10.1 %collective-permute-start.11 = (f32[128,128]{1,0:T(8,128)S(1)}, f32[128,128]{1,0:T(8,128)S(1)}, u32[]{:S(2)}, u32[]{:S(2)}) collective-permute-start(f32[128,128]{1,0:T(8,128)S(1)} %get-tuple-element.34.refs_4_), channel_id=1, source_target_pairs={{0,8},{1,9},{2,10},{3,11},{4,12},{5,13},{6,14},{7,15},{8,0},{9,1},... | collective-permute-start | bytes 196616 | tf_op jit(solution)/shard_map/ppermute | solution.py:229
  46.1 5.2 %collective-permute-start.6 = (f32[128,128]{1,0:T(8,128)S(1)}, f32[128,128]{1,0:T(8,128)S(1)}, u32[]{:S(2)}, u32[]{:S(2)}) collective-permute-start(f32[128,128]{1,0:T(8,128)S(1)} %shard_map.88.mine.refs_1_), channel_id=1, source_target_pairs={{0,8},{1,9},{2,10},{3,11},{4,12},{5,13},{6,14},{7,15},{8,0},{9,1},... | collective-permute-start | bytes 196616 | tf_op jit(solution)/shard_map/ppermute | solution.py:229
  51.1 5.0 %collective-permute-start.9 = (f32[128,128]{1,0:T(8,128)S(1)}, f32[128,128]{1,0:T(8,128)S(1)}, u32[]{:S(2)}, u32[]{:S(2)}) collective-permute-start(f32[128,128]{1,0:T(8,128)S(1)} %shard_map.90.refs_2_), channel_id=1, source_target_pairs={{0,8},{1,9},{2,10},{3,11},{4,12},{5,13},{6,14},{7,15},{8,0},{9,1},... | collective-permute-start | bytes 196616 | tf_op jit(solution)/shard_map/ppermute | solution.py:229
  57.1 2.0 %collective-permute-start.12 = (f32[128,256]{1,0:T(8,128)S(1)}, f32[128,256]{1,0:T(8,128)S(1)}, u32[]{:S(2)}, u32[]{:S(2)}) collective-permute-start(f32[128,256]{1,0:T(8,128)S(1)} %get-tuple-element.36.refs_3_), channel_id=1, source_target_pairs={{0,1},{1,0},{2,3},{3,2},{4,5},{5,4},{6,7},{7,6},{8,9},{9,8},{10,11... | collective-permute-start | bytes 393224 | tf_op jit(solution)/shard_map/ppermute | solution.py:229
  57.2 7.2 %collective-permute-start.13 = (f32[128,256]{1,0:T(8,128)S(1)}, f32[128,256]{1,0:T(8,128)S(1)}, u32[]{:S(2)}, u32[]{:S(2)}) collective-permute-start(f32[128,256]{1,0:T(8,128)S(1)} %get-tuple-element.36.refs_3_), channel_id=1, source_target_pairs={{1,2},{2,1},{3,4},{4,3},{5,6},{6,5},{9,10},{10,9},{11,12},{12,11},... | collective-permute-start | bytes 393224 | tf_op jit(solution)/shard_map/ppermute | solution.py:229
  65.4 11.6 %collective-permute-start.14 = (f32[128,128]{1,0:T(8,128)S(1)}, f32[128,128]{1,0:T(8,128)S(1)}, u32[]{:S(2)}, u32[]{:S(2)}) collective-permute-start(f32[128,128]{1,0:T(8,128)S(1)} %get-tuple-element.39.mine.refs_1_), channel_id=1, source_target_pairs={{0,16},{1,17},{2,18},{3,19},{4,20},{5,21},{6,22},{7,23},{8,24},{9,... | collective-permute-start | bytes 196616 | tf_op jit(solution)/shard_map/ppermute | solution.py:229
  66.1 16.4 %collective-permute-start.16 = (f32[128,256]{1,0:T(8,128)S(1)}, f32[128,256]{1,0:T(8,128)S(1)}, u32[]{:S(2)}, u32[]{:S(2)}) collective-permute-start(f32[128,256]{1,0:T(8,128)S(1)} %get-tuple-element.36.refs_3_), channel_id=1, source_target_pairs={{0,16},{1,17},{2,18},{3,19},{4,20},{5,21},{6,22},{7,23},{8,24},{9,... | collective-permute-start | bytes 393224 | tf_op jit(solution)/shard_map/ppermute | solution.py:229
  68.4 14.1 %collective-permute-start.15 = (f32[128,128]{1,0:T(8,128)S(1)}, f32[128,128]{1,0:T(8,128)S(1)}, u32[]{:S(2)}, u32[]{:S(2)}) collective-permute-start(f32[128,128]{1,0:T(8,128)S(1)} %get-tuple-element.43.refs_2_), channel_id=1, source_target_pairs={{0,16},{1,17},{2,18},{3,19},{4,20},{5,21},{6,22},{7,23},{8,24},{9,... | collective-permute-start | bytes 196616 | tf_op jit(solution)/shard_map/ppermute | solution.py:229

commit v4 on v3

--- a/solution.py
+++ b/solution.py
@@ -85,16 +85,30 @@
     return jnp.concatenate(scaled, axis=0)
 
 
-def near_half(view, which, rows):
-    chunks = rows // 128
+def near_half(view, which, rows, chunks=None):
+    chunks = rows // 128 if chunks is None else chunks
     return jnp.concatenate(
         [view[pl.ds(2 * c + which, rows, stride=2 * chunks), :] for c in range(chunks)], axis=1
     )
 
 
-def handed_kernel(near, probes, first):
-    upper = near_half(near, 1, probes.shape[0])
-    first[...] = dot(probes[:, : first.shape[1]].T, upper).T
+def handed_kernel(near, probes, handed, probes_first, near_copy, arrived):
+    rows, columns = handed.shape
+    chunks = rows // 128
+    part = near.shape[0] // chunks
+    coming = [pltpu.make_async_copy(probes.at[:, pl.ds(0, columns)], probes_first, arrived.at[chunks])]
+    for c in range(chunks):
+        at = pl.ds(c * part, part)
+        coming.append(pltpu.make_async_copy(near.at[at, :], near_copy.at[at, :], arrived.at[c]))
+    for copy in coming:
+        copy.start()
+    coming[0].wait()
+    total = jnp.zeros((columns, rows), jnp.float32)
+    for c in range(chunks):
+        coming[c + 1].wait()
+        upper = near_half(near_copy.at[pl.ds(c * part, part), :], 1, 128, chunks)
+        total += dot(probes_first[128 * c : 128 * (c + 1), :].T, upper)
+    handed[...] = total.T
 
 
 def rest_kernel(near, probes, samples, rest, handed_last, probes_last):
@@ -105,20 +119,22 @@
     handed_last[...] = dot(probes[:, columns:].T, near_half(near, 1, rows)).T
 
 
-def leaf_kernel(near, rest, following, handed, probes, far, inverse, sample_coef, probe_first, probe_last):
+def following_kernel(near, rest, following, handed_last, probes_last, out, *passed):
+    columns = out.shape[1]
+    out[...] = rest[:, :columns] - dot(near_half(near, 1, rest.shape[0]), following[...])
+
+
+def leaf_kernel(rest, handed, probes, far, inverse, sample_coef, probe_coef):
     columns = far.shape[1]
-    upper = near_half(near, 1, rest.shape[0])
-    block = rest[:, :columns] - dot(upper, following[...]) - handed[...]
+    block = rest[...] - handed[...]
     far[...] = block
     gram = dot(block, block, 0, 0)
     cross = dot(block, probes[...], 0, 0)
     factor = inverse_factor(gram)
     inverse[...] = factor
-    coef = dot(factor, jnp.concatenate([cross, gram], axis=1))
-    width = cross.shape[1]
-    probe_first[...] = coef[:, :columns]
-    probe_last[...] = coef[:, columns:width]
-    sample_coef[...] = coef[:, width:]
+    coef = dot(factor, jnp.concatenate([gram, cross], axis=1))
+    sample_coef[...] = coef[:, :columns]
+    probe_coef[...] = coef[:, columns:]
 
 
 def leaf_last_kernel(near, rest, following, handed, far, inverse, basis, sample_coef):
@@ -139,71 +155,83 @@
     return lax.axis_index("leaf") >> level - 1
 
 
-def corrected_kernel(level, kind, slots, couplings, one, two, *refs):
+def term_kernel(level, slots, couplings, mine, away, first, last):
+    node = member_node(level)
+    block = coupling_of(slots, couplings, level, node ^ 2)
+    outer = (node == 0) | (node == 3)
+    main = jnp.where(outer, mine[...], away[...])
+    other = jnp.where(outer, away[...], mine[...])
+    term = dot(block, main) + dot(block, other, 0, 0)
+    first[...] = term[:, : first.shape[1]]
+    last[...] = term[:, first.shape[1] :]
+
+
+def corrected_kernel(level, trees, slots, couplings, one, two, first, last, out_first, out_last):
+    columns = first.shape[1]
     node = member_node(level)
     block = coupling_of(slots, couplings, level, node)
-    if kind == "given":
-        first_main = node >= 0
-    elif kind == "quad":
-        first_main = (node == 1) | (node == 2)
-    else:
-        first_main = (lax.axis_index("clusters") ^ node) & 1 == 1
-    main = jnp.where(first_main, one[...], two[...])
-    other = jnp.where(first_main, two[...], one[...])
+    main, other = one[...], two[...]
+    if trees:
+        straight = (lax.axis_index("clusters") ^ node) & 1 == 1
+        main, other = jnp.where(straight, main, other), jnp.where(straight, other, main)
     term = dot(block, main) + dot(block, other, 0, 0)
-    half, at = len(refs) // 2, 0
-    for coef, out in zip(refs[:half], refs[half:]):
-        out[...] = coef[...] - term[:, at : at + out.shape[1]]
-        at += out.shape[1]
-
-
-def factor_kernel(level, mine, theirs, *refs):
-    earlier, (inverse, bases) = refs[:-2], refs[-2:]
-    for at, done in enumerate(earlier):
-        bases[0, at] = done[0, 0]
+    out_first[...] = first[...] - term[:, :columns]
+    out_last[...] = last[...] - term[:, columns:]
+
+
+def factor_kernel(mine, theirs, inverse):
+    gram = dot(mine[...], mine[...], 0, 0) + dot(theirs[...], theirs[...], 0, 0)
+    inverse[...] = inverse_factor(gram)
+
+
+def write_basis(level, at, mine, theirs, inverse, bases):
     size = mine.shape[0]
-    gram = dot(mine[...], mine[...], 0, 0) + dot(theirs[...], theirs[...], 0, 0)
-    factor = inverse_factor(gram)
-    inverse[...] = factor
-    parity = member_node(level) & 1
-    at = pl.multiple_of(parity * size, size)
-    bases[0, len(earlier), pl.ds(at, size), :] = dot(mine[...], factor, 1, 1)
-    at = pl.multiple_of((1 - parity) * size, size)
-    bases[0, len(earlier), pl.ds(at, size), :] = dot(theirs[...], factor, 1, 1)
-
-
-def level_coefs(refs):
-    half = len(refs) // 2
-    inverse = refs[0][...]
-    mine, theirs = [ref[...] for ref in refs[1 : half + 1]], [ref[...] for ref in refs[half + 1 :]]
-    own, sibling = jnp.concatenate(mine, axis=1), jnp.concatenate(theirs, axis=1)
-    mine, theirs = mine[0], theirs[0]
-    return dot(inverse, dot(mine, own, 0, 0) + dot(theirs, sibling, 0, 0))
-
-
-def node_kernel(inputs, *refs):
-    coef = level_coefs(refs[:inputs])
+    own = (lax.axis_index("leaf") >> level - 1) & 1
+    for block, half in ((mine, own), (theirs, 1 - own)):
+        rows = pl.ds(pl.multiple_of(half * size, size), size)
+        bases[0, at, rows, :] = dot(block, inverse, 1, 1)
+
+
+def basis_kernel(level, inverse, mine, theirs, basis):
+    write_basis(level, 0, mine[...], theirs[...], inverse[...], basis)
+
+
+def level_coefs(inverse, mine, theirs):
+    own = jnp.concatenate([ref[...] for ref in mine], axis=1)
+    sibling = jnp.concatenate([ref[...] for ref in theirs], axis=1)
+    return dot(inverse, dot(mine[0][...], own, 0, 0) + dot(theirs[0][...], sibling, 0, 0))
+
+
+def node_kernel(inverse, *refs):
+    coef = level_coefs(inverse[...], refs[:3], refs[3:6])
     at = 0
-    for out in refs[inputs:]:
+    for out in refs[6:]:
         out[...] = coef[:, at : at + out.shape[1]]
         at += out.shape[1]
 
 
-def top_kernel(*refs):
-    coef = level_coefs(refs[:-2])
-    samples, probe_coef = refs[-2:]
+def top_kernel(level, inverse, *refs):
+    factor = inverse[...]
+    earlier, (bases, samples, probe_coef) = refs[6:-3], refs[-3:]
+    coef = level_coefs(factor, refs[:3], refs[3:6])
     width = samples.shape[2]
     samples[0] = coef[:, :width]
     probe_coef[0] = coef[:, width:]
+    for at, done in enumerate(earlier):
+        bases[0, at] = done[0, 0]
+    write_basis(level, len(earlier), refs[0][...], refs[3][...], factor, bases)
 
 
 VMEM = pl.BlockSpec(memory_space=pltpu.VMEM)
 SMEM = pl.BlockSpec(memory_space=pltpu.SMEM)
-
-
-def call(kernel, shapes, *operands, slots=None, flops=0):
+HBM = pl.BlockSpec(memory_space=pltpu.HBM)
+ANY = pl.BlockSpec(memory_space=pl.ANY)
+
+
+def call(kernel, shapes, *operands, slots=None, flops=0, specs=None, out_specs=None, **options):
     outs = [jax.ShapeDtypeStruct(shape, jnp.float32) for shape in shapes]
-    specs = [VMEM] * len(operands)
+    specs = [VMEM] * len(operands) if specs is None else specs
+    out_specs = [VMEM] * len(outs) if out_specs is None else out_specs
     if slots is not None:
         operands = (slots,) + operands
         specs = [SMEM] + specs
@@ -212,9 +240,10 @@
         kernel,
         out_shape=outs,
         in_specs=specs,
-        out_specs=[VMEM] * len(outs),
+        out_specs=out_specs,
         compiler_params=pltpu.CompilerParams(vmem_limit_bytes=32 * 2**20),
         cost_estimate=pl.CostEstimate(flops=flops, bytes_accessed=moved, transcendentals=0),
+        **options,
     )(*operands)
 
 
@@ -238,10 +267,8 @@
     return permuted(value, lambda tree, member: (tree, member ^ mask))
 
 
-def outer_swapped(value, half):
-    return permuted(
-        value, lambda tree, member: (tree - 1 if member < half else tree + 1, member ^ half)
-    )
+def outward(value, half):
+    return permuted(value, lambda tree, member: (tree - 1 if member < half else tree + 1, member))
 
 
 def tree_swapped(value, odd):
@@ -256,20 +283,28 @@
     chunks = rows // 128
     near = near_blocks.reshape(rows, 2, chunks, 128).transpose(0, 2, 1, 3).reshape(-1, 128)
     work = 12 * rows * rows * width
-
     tall, tall_last = (rows, columns), (rows, width - columns)
-    following = flat_shift(probes[:, :columns], -1)
-    (handed,) = call(handed_kernel, [tall], near, probes, flops=work)
+    square, square_last = (columns, columns), (columns, width - columns)
+
+    handed, probes_first = call(
+        handed_kernel, [tall, tall], near, probes, flops=work, specs=[HBM, HBM],
+        scratch_shapes=[pltpu.VMEM(near.shape, jnp.float32), pltpu.SemaphoreType.DMA((chunks + 1,))],
+    )
+    following = flat_shift(probes_first, -1)
     handed = flat_shift(handed, 1)
     rest, handed_last, probes_last = call(
         rest_kernel, [(rows, width), tall_last, tall_last], near, probes, samples, flops=work
     )
+    rest_first, handed_last, probes_last = call(
+        following_kernel, [tall, tall_last, tall_last],
+        near, rest, following, handed_last, probes_last, flops=work,
+        specs=[VMEM, VMEM, VMEM, ANY, ANY], out_specs=[VMEM, ANY, ANY],
+        input_output_aliases={3: 1, 4: 2},
+    )
+    following_last = flat_shift(probes_last, -1)
     handed_last = flat_shift(handed_last, 1)
-    following_last = flat_shift(probes_last, -1)
-    square, square_last = (columns, columns), (columns, width - columns)
-    far, inverse, first, *probe_coefs = call(
-        leaf_kernel, [tall, square, square, square, square_last],
-        near, rest, following, handed, probes, flops=work,
+    far, inverse, first, probe_coef = call(
+        leaf_kernel, [tall, square, square, (columns, width)], rest_first, handed, probes, flops=work
     )
     leaf_basis, last = call(
         leaf_last_kernel, [tall, square_last],
@@ -280,48 +315,43 @@
     for level in range(1, levels + 1):
         copies = 2 ** (level - 1)
         count = subtree // copies
-        if count == 2:
-            meet = [functools.partial(tree_swapped, odd=odd) for odd in (0, 1)]
-        elif count == 4:
-            meet = [
-                functools.partial(swapped, mask=2 * copies),
-                functools.partial(outer_swapped, half=2 * copies),
-            ]
+        theirs_probe = swapped(probe_coef, copies)
+        if count == 4:
+            away = outward(probe_coef, 2 * copies)
+            terms = call(
+                functools.partial(term_kernel, level), [square, square_last],
+                couplings, probe_coef, away, slots=node_slot,
+            )
+            first = first - swapped(terms[0], 2 * copies)
+            last = last - swapped(terms[1], 2 * copies)
         else:
-            meet = [functools.partial(flat_shift, by=by) for by in (2 * copies, -2 * copies)]
-        fields = [[go(coef) for go in meet] for coef in probe_coefs]
-        if count > 4:
-            even = (lax.axis_index("leaf") >> level - 1) & 1 == 0
-            fields = [[jnp.where(even, *pair), jnp.where(even, *pair[::-1])] for pair in fields]
-        kind = "given" if count > 4 else "quad" if count == 4 else "trees"
-        correct = functools.partial(corrected_kernel, level, kind)
-        if count == 2:
+            if count == 2:
+                fields = [tree_swapped(probe_coef, odd) for odd in (0, 1)]
+            else:
+                even = (lax.axis_index("leaf") >> level - 1) & 1 == 0
+                fields = [flat_shift(probe_coef, by) for by in (2 * copies, -2 * copies)]
+                fields = [jnp.where(even, *fields), jnp.where(even, *fields[::-1])]
             first, last = call(
-                correct, [square, square_last], couplings, *fields[0], first, last, slots=node_slot
+                functools.partial(corrected_kernel, level, count == 2), [square, square_last],
+                couplings, *fields, first, last, slots=node_slot,
             )
-        else:
-            (first,) = call(correct, [square], couplings, *fields[0], first, slots=node_slot)
-            (last,) = call(correct, [square_last], couplings, *fields[1], last, slots=node_slot)
-        mine = first, last, *probe_coefs
-        theirs = [swapped(value, copies) for value in mine]
-        final = level == levels
-        bases = (1, level if final else 1, 2 * columns, columns)
-        inverse, basis = call(
-            functools.partial(factor_kernel, level), [square, bases],
-            mine[0], theirs[0], *(ancestors if final else []), flops=work,
-        )
-        ancestors.append(basis)
-        if final:
-            top_samples, top_probes = call(
-                top_kernel, [(1, columns, width), (1, columns, width)], inverse, *mine, *theirs
+        mine = first, last, probe_coef
+        theirs = swapped(first, copies), swapped(last, copies), theirs_probe
+        (inverse,) = call(factor_kernel, [square], mine[0], theirs[0])
+        if level < levels:
+            ancestors += call(
+                functools.partial(basis_kernel, level), [(1, 1, 2 * columns, columns)],
+                inverse, mine[0], theirs[0],
             )
-        else:
-            pieces = [(columns, width)] if count == 4 else [square, square_last]
-            first, last, *probe_coefs = call(
-                functools.partial(node_kernel, 1 + 2 * len(mine)),
-                [square, square_last, *pieces], inverse, *mine, *theirs,
+            first, last, probe_coef = call(
+                node_kernel, [square, square_last, (columns, width)], inverse, *mine, *theirs
             )
-    return (leaf_basis, ancestors[-1], top_samples, top_probes)
+    transfer_bases, top_samples, top_probes = call(
+        functools.partial(top_kernel, levels),
+        [(1, levels, 2 * columns, columns), (1, columns, width), (1, columns, width)],
+        inverse, *mine, *theirs, *ancestors,
+    )
+    return (leaf_basis, transfer_bases, top_samples, top_probes)
 
 
 def solution(mesh):

time: 84.5 us -> 81.5 us (0.964)
  the two profiles are of different devices: /device:TPU:4 before, /device:TPU:0 now
where the time goes in v4:
time: 81.5 us; the launch traced here: 81.1 us
  starting transfers between devices  33.4 us (41%)
  Pallas kernels  25.6 us (31%)
  waiting for transfers between devices  18.6 us (23%)
  local copies, waits for them, and re-layouts  2.65 us (3%)
  between operations  0.86 us (1%)
    ppermute x15, starting transfers between devices, permuted(): return lax.ppermute(value, BOTH, pairs)  33.4 us
    pallas_call x12, Pallas kernels, call(): pl.pallas_call(kernel, out_shape=outs, in_specs=specs, out_specs=out_spec...  25.6 us
    ppermute x15, waiting for transfers between devices, permuted(): return lax.ppermute(value, BOTH, pairs)  18.6 us
    unnamed x12, local copies, waits for them, and re-layouts  2.65 us
  transfers between devices with their start and end apart: 15, of which 5 were waited for; matrix products, arithmetic and copies ran while one was open for 0% of the time, Pallas kernels for 26%

profile of v4, /device:TPU:0, one launch (start us, length us, event | category | flops | bytes accessed | tf_op | source)
XLA Modules:
  0.0 81.1 jit_solution(2208701313904245700)
XLA Ops:
  0.6 1.6 %copy-done = f32[512,2,512]{2,1,0:T(2,128)S(1)} copy-done((f32[512,2,512]{2,1,0:T(2,128)S(1)}, f32[512,2,512]{2,1,0:T(2,128)}, u32[]{:S(2)}) %copy-start) | copy-done | bytes 2097176
  2.2 1.0 %copy-done.4 = f32[512,256]{1,0:T(8,128)S(1)} copy-done((f32[512,256]{1,0:T(8,128)S(1)}, f32[512,256]{1,0:T(8,128)}, u32[]{:S(2)}) %copy-start.4) | copy-done | bytes 524312
  3.3 1.7 %shard_map.85 = (f32[512,128]{1,0:T(8,128)S(1)}, f32[512,128]{1,0:T(8,128)S(1)}) custom-call(f32[4096,128]{1,0:T(8,128)S(1)} %bitcast.5, f32[512,256]{1,0:T(8,128)S(1)} %copy-done.4), custom_call_target="tpu_custom_call" | custom-call | flops 805306368 | bytes 3145728 | tf_op jit(solution)/shard_map/pallas_call | solution.py:239
  5.0 1.3 %collective-permute-start = (f32[512,128]{1,0:T(8,128)S(1)}, f32[512,128]{1,0:T(8,128)S(1)}, u32[]{:S(2)}, u32[]{:S(2)}) collective-permute-start(f32[512,128]{1,0:T(8,128)S(1)} %get-tuple-element.29), channel_id=1, source_target_pairs={{1,24},{2,25},{3,26},{4,27},{5,28},{6,29},{7,30},{8,0},{9,1},{10,2... | collective-permute-start | bytes 786440 | tf_op jit(solution)/shard_map/ppermute | solution.py:258
  6.3 5.6 %collective-permute-start.3 = (f32[512,128]{1,0:T(8,128)S(1)}, f32[512,128]{1,0:T(8,128)S(1)}, u32[]{:S(2)}, u32[]{:S(2)}) collective-permute-start(f32[512,128]{1,0:T(8,128)S(1)} %get-tuple-element.35), channel_id=1, source_target_pairs={{0,8},{1,9},{2,10},{3,11},{4,12},{5,13},{6,14},{7,15},{8,16},{9,17... | collective-permute-start | bytes 786440 | tf_op jit(solution)/shard_map/ppermute | solution.py:258
  11.9 1.6 %shard_map.84 = (f32[512,256]{1,0:T(8,128)S(1)}, f32[512,128]{1,0:T(8,128)S(1)}, f32[512,128]{1,0:T(8,128)S(1)}) custom-call(f32[4096,128]{1,0:T(8,128)S(1)} %bitcast.6, f32[512,256]{1,0:T(8,128)S(1)} %copy-done.4, f32[512,256]{1,0:T(8,128)S(1)} %copy-done.3), custom_call_target="tpu_custom_call" | custom-call | flops 805306368 | bytes 4194304 | tf_op jit(solution)/shard_map/pallas_call | solution.py:239
  13.5 2.7 %collective-permute-done.following = f32[512,128]{1,0:T(8,128)S(1)} collective-permute-done((f32[512,128]{1,0:T(8,128)S(1)}, f32[512,128]{1,0:T(8,128)S(1)}, u32[]{:S(2)}, u32[]{:S(2)}) %collective-permute-start) | collective-permute-done | bytes 262176 | tf_op jit(solution)/shard_map/ppermute | solution.py:258
  16.2 1.1 %shard_map.86 = (f32[512,128]{1,0:T(8,128)S(1)}, f32[512,128]{1,0:T(8,128)S(1)}, f32[512,128]{1,0:T(8,128)S(1)}) custom-call(f32[4096,128]{1,0:T(8,128)S(1)} %bitcast.7, f32[512,256]{1,0:T(8,128)S(1)} %get-tuple-element.28.rest, f32[512,128]{1,0:T(8,128)S(1)} %collective-permute-done.following, ...), custom_call_target="tpu_custom_call", output_to_operand_aliasing={{1}: (3, {}), {2}: (4, {})} | custom-call | flops 805306368 | bytes 4194304 | tf_op jit(solution)/shard_map/pallas_call | solution.py:239
  17.4 1.4 %collective-permute-start.1 = (f32[512,128]{1,0:T(8,128)S(1)}, f32[512,128]{1,0:T(8,128)S(1)}, u32[]{:S(2)}, u32[]{:S(2)}) collective-permute-start(f32[512,128]{1,0:T(8,128)S(1)} %get-tuple-element.32), channel_id=1, source_target_pairs={{1,24},{2,25},{3,26},{4,27},{5,28},{6,29},{7,30},{8,0},{9,1},{10,2... | collective-permute-start | bytes 786440 | tf_op jit(solution)/shard_map/ppermute | solution.py:258
  18.8 4.6 %collective-permute-start.2 = (f32[512,128]{1,0:T(8,128)S(1)}, f32[512,128]{1,0:T(8,128)S(1)}, u32[]{:S(2)}, u32[]{:S(2)}) collective-permute-start(f32[512,128]{1,0:T(8,128)S(1)} %get-tuple-element.33), channel_id=1, source_target_pairs={{0,8},{1,9},{2,10},{3,11},{4,12},{5,13},{6,14},{7,15},{8,16},{9,17... | collective-permute-start | bytes 786440 | tf_op jit(solution)/shard_map/ppermute | solution.py:258
  23.4 4.9 %shard_map.87 = (f32[512,128]{1,0:T(8,128)S(1)}, f32[128,128]{1,0:T(8,128)S(1)}, f32[128,128]{1,0:T(8,128)S(1)}, f32[128,256]{1,0:T(8,128)S(1)}) custom-call(f32[512,128]{1,0:T(8,128)S(1)} %get-tuple-element.34.rest, f32[512,128]{1,0:T(8,128)S(1)} %collective-permute-done.3.handed, f32[512,256]{1,0:T(8,128)S(1)} %copy-done.4), custom_call_target="tpu_custom_call" | custom-call | flops 805306368 | bytes 1572864 | tf_op jit(solution)/shard_map/pallas_call | solution.py:239
  28.3 1.5 %collective-permute-start.4 = (f32[128,256]{1,0:T(8,128)S(1)}, f32[128,256]{1,0:T(8,128)S(1)}, u32[]{:S(2)}, u32[]{:S(2)}) collective-permute-start(f32[128,256]{1,0:T(8,128)S(1)} %get-tuple-element.40.mine.refs_2_), channel_id=1, source_target_pairs={{1,0},{2,1},{3,2},{4,3},{5,4},{6,5},{7,6},{9,8},{10,9},{11,10},{12... | collective-permute-start | bytes 393224 | tf_op jit(solution)/shard_map/ppermute | solution.py:258
  29.7 5.1 %collective-permute-done.4.away = f32[128,256]{1,0:T(8,128)S(1)} collective-permute-done((f32[128,256]{1,0:T(8,128)S(1)}, f32[128,256]{1,0:T(8,128)S(1)}, u32[]{:S(2)}, u32[]{:S(2)}) %collective-permute-start.4) | collective-permute-done | bytes 131104 | tf_op jit(solution)/shard_map/ppermute | solution.py:258
  35.8 1.6 %collective-permute-start.5 = (f32[128,128]{1,0:T(8,128)S(1)}, f32[128,128]{1,0:T(8,128)S(1)}, u32[]{:S(2)}, u32[]{:S(2)}) collective-permute-start(f32[128,128]{1,0:T(8,128)S(1)} %get-tuple-element.41), channel_id=1, source_target_pairs={{0,16},{1,17},{2,18},{3,19},{4,20},{5,21},{6,22},{7,23},{8,24},{9,... | collective-permute-start | bytes 196616 | tf_op jit(solution)/shard_map/ppermute | solution.py:258
  37.4 4.7 %collective-permute-start.9 = (f32[128,256]{1,0:T(8,128)S(1)}, f32[128,256]{1,0:T(8,128)S(1)}, u32[]{:S(2)}, u32[]{:S(2)}) collective-permute-start(f32[128,256]{1,0:T(8,128)S(1)} %get-tuple-element.40.mine.refs_2_), channel_id=1, source_target_pairs={{0,8},{1,9},{2,10},{3,11},{4,12},{5,13},{6,14},{7,15},{8,0},{9,1},... | collective-permute-start | bytes 393224 | tf_op jit(solution)/shard_map/ppermute | solution.py:258
  42.2 3.0 %collective-permute-start.6 = (f32[128,128]{1,0:T(8,128)S(1)}, f32[128,128]{1,0:T(8,128)S(1)}, u32[]{:S(2)}, u32[]{:S(2)}) collective-permute-start(f32[128,128]{1,0:T(8,128)S(1)} %sub.6.mine.refs_0_), channel_id=1, source_target_pairs={{0,8},{1,9},{2,10},{3,11},{4,12},{5,13},{6,14},{7,15},{8,0},{9,1},... | collective-permute-start | bytes 196616 | tf_op jit(solution)/shard_map/ppermute | solution.py:258
  45.3 2.1 %shard_map.88 = (f32[512,128]{1,0:T(8,128)}, f32[128,128]{1,0:T(8,128)S(1)}) custom-call(f32[4096,128]{1,0:T(8,128)S(1)} %bitcast.8, f32[512,256]{1,0:T(8,128)S(1)} %get-tuple-element.28.rest, f32[512,128]{1,0:T(8,128)S(1)} %collective-permute-done.1.following, f32[512,128]{1,0:T(8,128)S(1)} %collective-permute-done.2.handed, ...), custom_call_target="tpu_custom_call" | custom-call | flops 805306368 | bytes 3801088 | tf_op jit(solution)/shard_map/pallas_call | solution.py:239
  47.4 1.7 %collective-permute-done.7 = f32[128,128]{1,0:T(8,128)S(1)} collective-permute-done((f32[128,128]{1,0:T(8,128)S(1)}, f32[128,128]{1,0:T(8,128)S(1)}, u32[]{:S(2)}, u32[]{:S(2)}) %collective-permute-start.7) | collective-permute-done | bytes 65568 | tf_op jit(solution)/shard_map/ppermute | solution.py:258
  49.6 4.5 %shard_map.90.inverse = f32[128,128]{1,0:T(8,128)S(1)} custom-call(f32[128,128]{1,0:T(8,128)S(1)} %sub.6.mine.refs_0_, f32[128,128]{1,0:T(8,128)S(1)} %collective-permute-done.6.theirs.refs_3_), custom_call_target="tpu_custom_call" | custom-call | bytes 196608 | tf_op jit(solution)/shard_map/pallas_call | solution.py:239
  55.8 5.0 %collective-permute-start.10 = (f32[128,256]{1,0:T(8,128)S(1)}, f32[128,256]{1,0:T(8,128)S(1)}, u32[]{:S(2)}, u32[]{:S(2)}) collective-permute-start(f32[128,256]{1,0:T(8,128)S(1)} %get-tuple-element.44.refs_2_), channel_id=1, source_target_pairs={{0,1},{1,0},{2,3},{3,2},{4,5},{5,4},{6,7},{7,6},{8,9},{9,8},{10,11... | collective-permute-start | bytes 393224 | tf_op jit(solution)/shard_map/ppermute | solution.py:258
  62.7 2.0 %collective-permute-start.12 = (f32[128,128]{1,0:T(8,128)S(1)}, f32[128,128]{1,0:T(8,128)S(1)}, u32[]{:S(2)}, u32[]{:S(2)}) collective-permute-start(f32[128,128]{1,0:T(8,128)S(1)} %get-tuple-element.47.mine.refs_0_), channel_id=1, source_target_pairs={{0,16},{1,17},{2,18},{3,19},{4,20},{5,21},{6,22},{7,23},{8,24},{9,... | collective-permute-start | bytes 196616 | tf_op jit(solution)/shard_map/ppermute | solution.py:258
  66.1 8.6 %collective-permute-done.12.theirs.refs_3_ = f32[128,128]{1,0:T(8,128)S(1)} collective-permute-done((f32[128,128]{1,0:T(8,128)S(1)}, f32[128,128]{1,0:T(8,128)S(1)}, u32[]{:S(2)}, u32[]{:S(2)}) %collective-permute-start.12) | collective-permute-done | bytes 65568 | tf_op jit(solution)/shard_map/ppermute | solution.py:258
  74.7 4.5 %shard_map.93.inverse = f32[128,128]{1,0:T(8,128)S(1)} custom-call(f32[128,128]{1,0:T(8,128)S(1)} %get-tuple-element.47.mine.refs_0_, f32[128,128]{1,0:T(8,128)S(1)} %collective-permute-done.12.theirs.refs_3_), custom_call_target="tpu_custom_call" | custom-call | bytes 196608 | tf_op jit(solution)/shard_map/pallas_call | solution.py:239
  79.2 1.9 %shard_map.95 = (f32[1,2,256,128]{3,2,1,0:T(8,128)}, f32[1,128,256]{2,1,0:T(8,128)}, f32[1,128,256]{2,1,0:T(8,128)}) custom-call(f32[128,128]{1,0:T(8,128)S(1)} %shard_map.93.inverse, f32[128,128]{1,0:T(8,128)S(1)} %get-tuple-element.47.mine.refs_0_, f32[128,128]{1,0:T(8,128)S(1)} %get-tuple-element.48.refs_1_, f32[128,256]{1,0:T(8,128)S(1)} %get-tuple-element.44.refs_2_, ...), custom_call_target="tpu_custom_call" | custom-call | bytes 1245184 | tf_op jit(solution)/shard_map/pallas_call | solution.py:239
  (32 shorter events, 6.6 us)
Async XLA Ops:
  0.6 1.6 %copy-start = (f32[512,2,512]{2,1,0:T(2,128)S(1)}, f32[512,2,512]{2,1,0:T(2,128)}, u32[]{:S(2)}) copy-start(f32[512,2,512]{2,1,0:T(2,128)} %param.7) | copy-start | bytes 6291460
  2.2 1.0 %copy-start.4 = (f32[512,256]{1,0:T(8,128)S(1)}, f32[512,256]{1,0:T(8,128)}, u32[]{:S(2)}) copy-start(f32[512,256]{1,0:T(8,128)} %probes.5) | copy-start | bytes 1572868
  3.3 8.6 %copy-start.3 = (f32[512,256]{1,0:T(8,128)S(1)}, f32[512,256]{1,0:T(8,128)}, u32[]{:S(2)}) copy-start(f32[512,256]{1,0:T(8,128)} %samples.1) | copy-start | bytes 1572868
  5.0 11.2 %collective-permute-start = (f32[512,128]{1,0:T(8,128)S(1)}, f32[512,128]{1,0:T(8,128)S(1)}, u32[]{:S(2)}, u32[]{:S(2)}) collective-permute-start(f32[512,128]{1,0:T(8,128)S(1)} %get-tuple-element.29), channel_id=1, source_target_pairs={{1,24},{2,25},{3,26},{4,27},{5,28},{6,29},{7,30},{8,0},{9,1},{10,2... | collective-permute-start | bytes 786440 | tf_op jit(solution)/shard_map/ppermute | solution.py:258
  6.3 17.1 %collective-permute-start.3 = (f32[512,128]{1,0:T(8,128)S(1)}, f32[512,128]{1,0:T(8,128)S(1)}, u32[]{:S(2)}, u32[]{:S(2)}) collective-permute-start(f32[512,128]{1,0:T(8,128)S(1)} %get-tuple-element.35), channel_id=1, source_target_pairs={{0,8},{1,9},{2,10},{3,11},{4,12},{5,13},{6,14},{7,15},{8,16},{9,17... | collective-permute-start | bytes 786440 | tf_op jit(solution)/shard_map/ppermute | solution.py:258
  17.3 17.5 %copy-start.2 = (f32[1,3,2,128,128]{4,3,2,1,0:T(8,128)S(1)}, f32[1,3,2,128,128]{4,3,2,1,0:T(8,128)}, u32[]{:S(2)}) copy-start(f32[1,3,2,128,128]{4,3,2,1,0:T(8,128)} %couplings.3) | copy-start | bytes 1179652
  17.3 17.5 %copy-start.5 = (s32[1,3]{1,0:T(1,128)S(1)}, s32[1,3]{1,0:T(1,128)}, u32[]{:S(2)}) copy-start(s32[1,3]{1,0:T(1,128)} %slots.3) | copy-start | bytes 40
  17.4 27.9 %copy-start.1 = (f32[512,2,512]{2,1,0:T(2,128)S(1)}, f32[512,2,512]{2,1,0:T(2,128)}, u32[]{:S(2)}) copy-start(f32[512,2,512]{2,1,0:T(2,128)} %param.7) | copy-start | bytes 6291460
  17.4 27.9 %collective-permute-start.1 = (f32[512,128]{1,0:T(8,128)S(1)}, f32[512,128]{1,0:T(8,128)S(1)}, u32[]{:S(2)}, u32[]{:S(2)}) collective-permute-start(f32[512,128]{1,0:T(8,128)S(1)} %get-tuple-element.32), channel_id=1, source_target_pairs={{1,24},{2,25},{3,26},{4,27},{5,28},{6,29},{7,30},{8,0},{9,1},{10,2... | collective-permute-start | bytes 786440 | tf_op jit(solution)/shard_map/ppermute | solution.py:258
  18.8 26.5 %collective-permute-start.2 = (f32[512,128]{1,0:T(8,128)S(1)}, f32[512,128]{1,0:T(8,128)S(1)}, u32[]{:S(2)}, u32[]{:S(2)}) collective-permute-start(f32[512,128]{1,0:T(8,128)S(1)} %get-tuple-element.33), channel_id=1, source_target_pairs={{0,8},{1,9},{2,10},{3,11},{4,12},{5,13},{6,14},{7,15},{8,16},{9,17... | collective-permute-start | bytes 786440 | tf_op jit(solution)/shard_map/ppermute | solution.py:258
  28.3 6.6 %collective-permute-start.4 = (f32[128,256]{1,0:T(8,128)S(1)}, f32[128,256]{1,0:T(8,128)S(1)}, u32[]{:S(2)}, u32[]{:S(2)}) collective-permute-start(f32[128,256]{1,0:T(8,128)S(1)} %get-tuple-element.40.mine.refs_2_), channel_id=1, source_target_pairs={{1,0},{2,1},{3,2},{4,3},{5,4},{6,5},{7,6},{9,8},{10,9},{11,10},{12... | collective-permute-start | bytes 393224 | tf_op jit(solution)/shard_map/ppermute | solution.py:258
  35.8 6.4 %collective-permute-start.5 = (f32[128,128]{1,0:T(8,128)S(1)}, f32[128,128]{1,0:T(8,128)S(1)}, u32[]{:S(2)}, u32[]{:S(2)}) collective-permute-start(f32[128,128]{1,0:T(8,128)S(1)} %get-tuple-element.41), channel_id=1, source_target_pairs={{0,16},{1,17},{2,18},{3,19},{4,20},{5,21},{6,22},{7,23},{8,24},{9,... | collective-permute-start | bytes 196616 | tf_op jit(solution)/shard_map/ppermute | solution.py:258
  37.4 16.7 %collective-permute-start.9 = (f32[128,256]{1,0:T(8,128)S(1)}, f32[128,256]{1,0:T(8,128)S(1)}, u32[]{:S(2)}, u32[]{:S(2)}) collective-permute-start(f32[128,256]{1,0:T(8,128)S(1)} %get-tuple-element.40.mine.refs_2_), channel_id=1, source_target_pairs={{0,8},{1,9},{2,10},{3,11},{4,12},{5,13},{6,14},{7,15},{8,0},{9,1},... | collective-permute-start | bytes 393224 | tf_op jit(solution)/shard_map/ppermute | solution.py:258
  42.1 6.9 %collective-permute-start.7 = (f32[128,128]{1,0:T(8,128)S(1)}, f32[128,128]{1,0:T(8,128)S(1)}, u32[]{:S(2)}, u32[]{:S(2)}) collective-permute-start(f32[128,128]{1,0:T(8,128)S(1)} %get-tuple-element.43), channel_id=1, source_target_pairs={{0,16},{1,17},{2,18},{3,19},{4,20},{5,21},{6,22},{7,23},{8,24},{9,... | collective-permute-start | bytes 196616 | tf_op jit(solution)/shard_map/ppermute | solution.py:258
  42.2 7.4 %collective-permute-start.6 = (f32[128,128]{1,0:T(8,128)S(1)}, f32[128,128]{1,0:T(8,128)S(1)}, u32[]{:S(2)}, u32[]{:S(2)}) collective-permute-start(f32[128,128]{1,0:T(8,128)S(1)} %sub.6.mine.refs_0_), channel_id=1, source_target_pairs={{0,8},{1,9},{2,10},{3,11},{4,12},{5,13},{6,14},{7,15},{8,0},{9,1},... | collective-permute-start | bytes 196616 | tf_op jit(solution)/shard_map/ppermute | solution.py:258
  49.1 5.0 %collective-permute-start.8 = (f32[128,128]{1,0:T(8,128)S(1)}, f32[128,128]{1,0:T(8,128)S(1)}, u32[]{:S(2)}, u32[]{:S(2)}) collective-permute-start(f32[128,128]{1,0:T(8,128)S(1)} %sub.7.refs_1_), channel_id=1, source_target_pairs={{0,8},{1,9},{2,10},{3,11},{4,12},{5,13},{6,14},{7,15},{8,0},{9,1},... | collective-permute-start | bytes 196616 | tf_op jit(solution)/shard_map/ppermute | solution.py:258
  55.1 6.6 %collective-permute-start.11 = (f32[128,256]{1,0:T(8,128)S(1)}, f32[128,256]{1,0:T(8,128)S(1)}, u32[]{:S(2)}, u32[]{:S(2)}) collective-permute-start(f32[128,256]{1,0:T(8,128)S(1)} %get-tuple-element.44.refs_2_), channel_id=1, source_target_pairs={{1,2},{2,1},{3,4},{4,3},{5,6},{6,5},{9,10},{10,9},{11,12},{12,11},... | collective-permute-start | bytes 393224 | tf_op jit(solution)/shard_map/ppermute | solution.py:258
  55.8 6.0 %collective-permute-start.10 = (f32[128,256]{1,0:T(8,128)S(1)}, f32[128,256]{1,0:T(8,128)S(1)}, u32[]{:S(2)}, u32[]{:S(2)}) collective-permute-start(f32[128,256]{1,0:T(8,128)S(1)} %get-tuple-element.44.refs_2_), channel_id=1, source_target_pairs={{0,1},{1,0},{2,3},{3,2},{4,5},{5,4},{6,7},{7,6},{8,9},{9,8},{10,11... | collective-permute-start | bytes 393224 | tf_op jit(solution)/shard_map/ppermute | solution.py:258
  60.8 18.4 %collective-permute-start.14 = (f32[128,256]{1,0:T(8,128)S(1)}, f32[128,256]{1,0:T(8,128)S(1)}, u32[]{:S(2)}, u32[]{:S(2)}) collective-permute-start(f32[128,256]{1,0:T(8,128)S(1)} %get-tuple-element.44.refs_2_), channel_id=1, source_target_pairs={{0,16},{1,17},{2,18},{3,19},{4,20},{5,21},{6,22},{7,23},{8,24},{9,... | collective-permute-start | bytes 393224 | tf_op jit(solution)/shard_map/ppermute | solution.py:258
  62.7 12.0 %collective-permute-start.12 = (f32[128,128]{1,0:T(8,128)S(1)}, f32[128,128]{1,0:T(8,128)S(1)}, u32[]{:S(2)}, u32[]{:S(2)}) collective-permute-start(f32[128,128]{1,0:T(8,128)S(1)} %get-tuple-element.47.mine.refs_0_), channel_id=1, source_target_pairs={{0,16},{1,17},{2,18},{3,19},{4,20},{5,21},{6,22},{7,23},{8,24},{9,... | collective-permute-start | bytes 196616 | tf_op jit(solution)/shard_map/ppermute | solution.py:258
  64.7 14.5 %collective-permute-start.13 = (f32[128,128]{1,0:T(8,128)S(1)}, f32[128,128]{1,0:T(8,128)S(1)}, u32[]{:S(2)}, u32[]{:S(2)}) collective-permute-start(f32[128,128]{1,0:T(8,128)S(1)} %get-tuple-element.48.refs_1_), channel_id=1, source_target_pairs={{0,16},{1,17},{2,18},{3,19},{4,20},{5,21},{6,22},{7,23},{8,24},{9,... | collective-permute-start | bytes 196616 | tf_op jit(solution)/shard_map/ppermute | solution.py:258

commit v5 on v4

--- a/solution.py
+++ b/solution.py
@@ -23,40 +23,47 @@
     return jnp.broadcast_to(tile[:, lane : lane + 1], tile.shape)
 
 
-def across_rows(tile, row):
-    return jnp.broadcast_to(tile[row : row + 1, :], tile.shape)
-
-
-def inverse_factor(gram):
+def row_of(ref, row):
+    return jnp.broadcast_to(ref[pl.ds(row, 1), :], (ROWS, ref.shape[1]))
+
+
+def inverse_factor(gram, scratch):
     size = gram.shape[0]
     blocks = size // ROWS
     sub = lax.broadcasted_iota(jnp.int32, (ROWS, size), 0)
     lane = lax.broadcasted_iota(jnp.int32, (ROWS, size), 1)
-    left = [gram[ROWS * i : ROWS * (i + 1), :] for i in range(blocks)]
-    right = [jnp.where(lane == sub + ROWS * i, 1.0, 0.0).astype(jnp.float32) for i in range(blocks)]
+    rows = [gram[ROWS * i : ROWS * (i + 1), :] for i in range(blocks)]
     scaled = [None] * blocks
+    used = 0
     for first in range(0, blocks, GROUP):
         last = first + GROUP
         ahead = min(last + 1, blocks)
-        scales = []
         for k in range(first, last):
             cols = {
-                i: [across_lanes(left[i], ROWS * k + c) for c in range(ROWS)] for i in range(k, ahead)
+                i: [across_lanes(rows[i], ROWS * k + c) for c in range(ROWS)] for i in range(k, ahead)
             }
             pivots = jnp.ones((ROWS, size), jnp.float32)
             for j in range(0, ROWS, 2):
-                a = across_rows(cols[k][j], j)
-                b = across_rows(cols[k][j], j + 1)
-                c = across_rows(cols[k][j + 1], j + 1)
+                pair = (lane == ROWS * k + j) | (lane == ROWS * k + j + 1)
+                for i in range(k, ahead):
+                    rows[i] = jnp.where(pair, 0.0, rows[i])
+                rows[k] = jnp.where(pair & (lane == sub + ROWS * k), 1.0, rows[k])
+                held = scratch.at[pl.ds(used, ROWS * (ROWS - j + 1)), :]
+                used += ROWS * (ROWS - j + 1)
+                held[pl.ds(0, ROWS), :] = rows[k]
+                for n in range(j, ROWS):
+                    held[pl.ds(ROWS * (n - j + 1), ROWS), :] = cols[k][n]
+                a = row_of(held, ROWS + j)
+                b = row_of(held, ROWS + j + 1)
+                c = row_of(held, 2 * ROWS + j + 1)
                 det = a * c - b * b
                 inverse = 1.0 / det
                 inverse_a = 1.0 / a
                 ratio = b * inverse_a
                 pivots = jnp.where(sub == j, a, jnp.where(sub == j + 1, det * inverse_a, pivots))
-                left_rows = across_rows(left[k], j), across_rows(left[k], j + 1)
-                right_rows = across_rows(right[k], j), across_rows(right[k], j + 1)
+                row, next_row = row_of(held, j), row_of(held, j + 1)
                 col_rows = [
-                    (across_rows(cols[k][n], j), across_rows(cols[k][n], j + 1))
+                    (row_of(held, ROWS * (n - j + 1) + j), row_of(held, ROWS * (n - j + 1) + j + 1))
                     for n in range(j + 2, ROWS)
                 ]
                 for i in range(k, ahead):
@@ -69,20 +76,23 @@
                     for n in range(j + 2, ROWS):
                         x, y = col_rows[n - j - 2]
                         cols[i][n] = cols[i][n] - (f * x + g * y)
-                    left[i] = left[i] - (f * left_rows[0] + g * left_rows[1])
-                    right[i] = right[i] - (f * right_rows[0] + g * right_rows[1])
-            scales.append(lax.rsqrt(pivots))
-        for k in range(first, last):
-            scaled[k] = right[k] * scales[k - first]
+                    rows[i] = rows[i] - (f * row + g * next_row)
+            kept = (lane <= sub + ROWS * k) | (lane >= ROWS * last)
+            scaled[k] = jnp.where(kept, rows[k] * lax.rsqrt(pivots), 0.0)
         if ahead < blocks:
-            upper = jnp.concatenate([left[k] * scales[k - first] for k in range(first, last)], axis=0)
-            lower = jnp.concatenate(scaled[first:last], axis=0)
-            change = dot(upper, jnp.concatenate([upper, lower], axis=1), 0, 0)
+            done = jnp.concatenate(scaled[first:last], axis=0)
+            change = dot(done.T[ROWS * ahead :, :], done)
+            old = (lane >= ROWS * first) & (lane < ROWS * last)
             for i in range(ahead, blocks):
-                piece = change[ROWS * i : ROWS * (i + 1), :]
-                left[i] = left[i] - piece[:, :size]
-                right[i] = right[i] - piece[:, size:]
-    return jnp.concatenate(scaled, axis=0)
+                piece = change[ROWS * (i - ahead) : ROWS * (i - ahead + 1), :]
+                rows[i] = jnp.where(old, 0.0, rows[i]) - piece
+    return jnp.concatenate(
+        [jnp.where(lane <= sub + ROWS * k, scaled[k], 0.0) for k in range(blocks)], axis=0
+    )
+
+
+def scratch_rows(size):
+    return size // ROWS * sum(ROWS * (ROWS - j + 1) for j in range(0, ROWS, 2))
 
 
 def near_half(view, which, rows, chunks=None):
@@ -92,45 +102,50 @@
     )
 
 
-def handed_kernel(near, probes, handed, probes_first, near_copy, arrived):
-    rows, columns = handed.shape
+def handed_kernel(near, probes, first, last, probes_first, probes_last, near_copy, arrived):
+    rows, columns = first.shape
     chunks = rows // 128
     part = near.shape[0] // chunks
-    coming = [pltpu.make_async_copy(probes.at[:, pl.ds(0, columns)], probes_first, arrived.at[chunks])]
+    coming = [
+        pltpu.make_async_copy(probes.at[:, pl.ds(0, columns)], probes_first, arrived.at[chunks]),
+        pltpu.make_async_copy(
+            probes.at[:, pl.ds(columns, probes_last.shape[1])], probes_last, arrived.at[chunks + 1]
+        ),
+    ]
     for c in range(chunks):
         at = pl.ds(c * part, part)
         coming.append(pltpu.make_async_copy(near.at[at, :], near_copy.at[at, :], arrived.at[c]))
     for copy in coming:
         copy.start()
     coming[0].wait()
-    total = jnp.zeros((columns, rows), jnp.float32)
+    coming[1].wait()
+    total = jnp.zeros((columns + probes_last.shape[1], rows), jnp.float32)
     for c in range(chunks):
-        coming[c + 1].wait()
+        coming[c + 2].wait()
         upper = near_half(near_copy.at[pl.ds(c * part, part), :], 1, 128, chunks)
-        total += dot(probes_first[128 * c : 128 * (c + 1), :].T, upper)
-    handed[...] = total.T
-
-
-def rest_kernel(near, probes, samples, rest, handed_last, probes_last):
-    rows = probes.shape[0]
-    columns = rest.shape[1] - probes_last.shape[1]
-    probes_last[...] = probes[:, columns:]
-    rest[...] = samples[...] - dot(near_half(near, 0, rows), probes[...])
-    handed_last[...] = dot(probes[:, columns:].T, near_half(near, 1, rows)).T
-
-
-def following_kernel(near, rest, following, handed_last, probes_last, out, *passed):
+        at = pl.ds(128 * c, 128)
+        piece = jnp.concatenate([probes_first[at, :], probes_last[at, :]], axis=1)
+        total += dot(piece.T, upper)
+    first[...] = total[:columns].T
+    last[...] = total[columns:].T
+
+
+def rest_kernel(near, probes, samples, rest):
+    rest[...] = samples[...] - dot(near_half(near, 0, probes.shape[0]), probes[...])
+
+
+def following_kernel(near, rest, following, out):
     columns = out.shape[1]
     out[...] = rest[:, :columns] - dot(near_half(near, 1, rest.shape[0]), following[...])
 
 
-def leaf_kernel(rest, handed, probes, far, inverse, sample_coef, probe_coef):
+def leaf_kernel(rest, handed, probes, far, inverse, sample_coef, probe_coef, scratch):
     columns = far.shape[1]
     block = rest[...] - handed[...]
     far[...] = block
     gram = dot(block, block, 0, 0)
     cross = dot(block, probes[...], 0, 0)
-    factor = inverse_factor(gram)
+    factor = inverse_factor(gram, scratch)
     inverse[...] = factor
     coef = dot(factor, jnp.concatenate([gram, cross], axis=1))
     sample_coef[...] = coef[:, :columns]
@@ -155,7 +170,7 @@
     return lax.axis_index("leaf") >> level - 1
 
 
-def term_kernel(level, slots, couplings, mine, away, first, last):
+def term_kernel(level, slots, couplings, mine, away, unused, first, last):
     node = member_node(level)
     block = coupling_of(slots, couplings, level, node ^ 2)
     outer = (node == 0) | (node == 3)
@@ -179,9 +194,9 @@
     out_last[...] = last[...] - term[:, columns:]
 
 
-def factor_kernel(mine, theirs, inverse):
+def factor_kernel(mine, theirs, inverse, scratch):
     gram = dot(mine[...], mine[...], 0, 0) + dot(theirs[...], theirs[...], 0, 0)
-    inverse[...] = inverse_factor(gram)
+    inverse[...] = inverse_factor(gram, scratch)
 
 
 def write_basis(level, at, mine, theirs, inverse, bases):
@@ -224,11 +239,10 @@
 
 VMEM = pl.BlockSpec(memory_space=pltpu.VMEM)
 SMEM = pl.BlockSpec(memory_space=pltpu.SMEM)
-HBM = pl.BlockSpec(memory_space=pltpu.HBM)
 ANY = pl.BlockSpec(memory_space=pl.ANY)
 
 
-def call(kernel, shapes, *operands, slots=None, flops=0, specs=None, out_specs=None, **options):
+def call(kernel, shapes, *operands, slots=None, flops=0, specs=None, out_specs=None, vmem=32, **options):
     outs = [jax.ShapeDtypeStruct(shape, jnp.float32) for shape in shapes]
     specs = [VMEM] * len(operands) if specs is None else specs
     out_specs = [VMEM] * len(outs) if out_specs is None else out_specs
@@ -241,7 +255,7 @@
         out_shape=outs,
         in_specs=specs,
         out_specs=out_specs,
-        compiler_params=pltpu.CompilerParams(vmem_limit_bytes=32 * 2**20),
+        compiler_params=pltpu.CompilerParams(vmem_limit_bytes=vmem * 2**20),
         cost_estimate=pl.CostEstimate(flops=flops, bytes_accessed=moved, transcendentals=0),
         **options,
     )(*operands)
@@ -286,25 +300,21 @@
     tall, tall_last = (rows, columns), (rows, width - columns)
     square, square_last = (columns, columns), (columns, width - columns)
 
-    handed, probes_first = call(
-        handed_kernel, [tall, tall], near, probes, flops=work, specs=[HBM, HBM],
-        scratch_shapes=[pltpu.VMEM(near.shape, jnp.float32), pltpu.SemaphoreType.DMA((chunks + 1,))],
+    handed, handed_last, probes_first, probes_last = call(
+        handed_kernel, [tall, tall_last, tall, tall_last], near, probes, flops=work,
+        specs=[ANY, ANY], vmem=62,
+        scratch_shapes=[pltpu.VMEM(near.shape, jnp.float32), pltpu.SemaphoreType.DMA((chunks + 2,))],
     )
     following = flat_shift(probes_first, -1)
     handed = flat_shift(handed, 1)
-    rest, handed_last, probes_last = call(
-        rest_kernel, [(rows, width), tall_last, tall_last], near, probes, samples, flops=work
-    )
-    rest_first, handed_last, probes_last = call(
-        following_kernel, [tall, tall_last, tall_last],
-        near, rest, following, handed_last, probes_last, flops=work,
-        specs=[VMEM, VMEM, VMEM, ANY, ANY], out_specs=[VMEM, ANY, ANY],
-        input_output_aliases={3: 1, 4: 2},
-    )
     following_last = flat_shift(probes_last, -1)
     handed_last = flat_shift(handed_last, 1)
+    (rest,) = call(rest_kernel, [(rows, width)], near, probes, samples, flops=work)
+    (rest_first,) = call(following_kernel, [tall], near, rest, following, flops=work)
+    scratch = dict(scratch_shapes=[pltpu.VMEM((scratch_rows(columns), columns), jnp.float32)])
     far, inverse, first, probe_coef = call(
-        leaf_kernel, [tall, square, square, (columns, width)], rest_first, handed, probes, flops=work
+        leaf_kernel, [tall, square, square, (columns, width)], rest_first, handed, probes,
+        flops=work, **scratch,
     )
     leaf_basis, last = call(
         leaf_last_kernel, [tall, square_last],
@@ -320,7 +330,7 @@
             away = outward(probe_coef, 2 * copies)
             terms = call(
                 functools.partial(term_kernel, level), [square, square_last],
-                couplings, probe_coef, away, slots=node_slot,
+                couplings, probe_coef, away, last, specs=[VMEM, VMEM, VMEM, ANY], slots=node_slot,
             )
             first = first - swapped(terms[0], 2 * copies)
             last = last - swapped(terms[1], 2 * copies)
@@ -337,7 +347,7 @@
             )
         mine = first, last, probe_coef
         theirs = swapped(first, copies), swapped(last, copies), theirs_probe
-        (inverse,) = call(factor_kernel, [square], mine[0], theirs[0])
+        (inverse,) = call(factor_kernel, [square], mine[0], theirs[0], **scratch)
         if level < levels:
             ancestors += call(
                 functools.partial(basis_kernel, level), [(1, 1, 2 * columns, columns)],

time: 81.5 us -> 82.1 us (level)
  starting transfers between devices: 33.4 us -> 43.2 us
  waiting for transfers between devices: 18.6 us -> 10 us
  local copies, waits for them, and re-layouts: 2.65 us -> 1.61 us
    ppermute x15, starting transfers between devices: 33.4 us -> 43.2 us  [permuted(): return lax.ppermute(value, BOTH, pairs)]
    ppermute x15, waiting for transfers between devices: 18.6 us -> 10 us  [permuted(): return lax.ppermute(value, BOTH, pairs)]
    unnamed x12, local copies, waits for them, and re-layouts: 2.65 us -> 1.61 us
  transfers between devices with their start and end apart: 15 -> 15, of which waited for: 5 -> 2; matrix products, arithmetic and copies ran while one was open for 0% -> 0% of each run, Pallas kernels for 26% -> 22%
where the time goes in v5:
time: 82.1 us; the launch traced here: 81.9 us
  starting transfers between devices  43.2 us (53%)
  Pallas kernels  26.2 us (32%)
  waiting for transfers between devices  10 us (12%)
  local copies, waits for them, and re-layouts  1.61 us (2%)
  between operations  0.9 us (1%)
    ppermute x15, starting transfers between devices, permuted(): return lax.ppermute(value, BOTH, pairs)  43.2 us
    pallas_call x12, Pallas kernels, call(): pl.pallas_call(kernel, out_shape=outs, in_specs=specs, out_specs=out_spec...  26.2 us
    ppermute x15, waiting for transfers between devices, permuted(): return lax.ppermute(value, BOTH, pairs)  10 us
  transfers between devices with their start and end apart: 15, of which 2 were waited for; matrix products, arithmetic and copies ran while one was open for 0% of the time, Pallas kernels for 22%

profile of v5, /device:TPU:0, one launch (start us, length us, event | category | flops | bytes accessed | tf_op | source)
XLA Modules:
  0.0 81.9 jit_solution(14287809408632087746)
XLA Ops:
  0.7 4.5 %shard_map.85 = (f32[512,128]{1,0:T(8,128)}, f32[512,128]{1,0:T(8,128)}, f32[512,128]{1,0:T(8,128)}, f32[512,128]{1,0:T(8,128)}) custom-call(f32[4096,128]{1,0:T(8,128)} %bitcast.5, f32[512,256]{1,0:T(8,128)} %probes.5), custom_call_target="tpu_custom_call" | custom-call | flops 805306368 | bytes 3670016 | tf_op jit(solution)/shard_map/pallas_call | solution.py:253
  5.1 1.3 %collective-permute-start.2 = (f32[512,128]{1,0:T(8,128)}, f32[512,128]{1,0:T(8,128)S(1)}, u32[]{:S(2)}, u32[]{:S(2)}) collective-permute-start(f32[512,128]{1,0:T(8,128)} %get-tuple-element.26), channel_id=1, source_target_pairs={{1,24},{2,25},{3,26},{4,27},{5,28},{6,29},{7,30},{8,0},{9,1},{10,2... | collective-permute-start | bytes 786440 | tf_op jit(solution)/shard_map/ppermute | solution.py:272
  6.4 5.6 %collective-permute-start.3 = (f32[512,128]{1,0:T(8,128)}, f32[512,128]{1,0:T(8,128)S(1)}, u32[]{:S(2)}, u32[]{:S(2)}) collective-permute-start(f32[512,128]{1,0:T(8,128)} %get-tuple-element.27), channel_id=1, source_target_pairs={{0,8},{1,9},{2,10},{3,11},{4,12},{5,13},{6,14},{7,15},{8,16},{9,17... | collective-permute-start | bytes 786440 | tf_op jit(solution)/shard_map/ppermute | solution.py:272
  12.0 1.3 %collective-permute-start = (f32[512,128]{1,0:T(8,128)}, f32[512,128]{1,0:T(8,128)S(1)}, u32[]{:S(2)}, u32[]{:S(2)}) collective-permute-start(f32[512,128]{1,0:T(8,128)} %get-tuple-element.24), channel_id=1, source_target_pairs={{1,24},{2,25},{3,26},{4,27},{5,28},{6,29},{7,30},{8,0},{9,1},{10,2... | collective-permute-start | bytes 786440 | tf_op jit(solution)/shard_map/ppermute | solution.py:272
  13.3 4.6 %collective-permute-start.1 = (f32[512,128]{1,0:T(8,128)}, f32[512,128]{1,0:T(8,128)S(1)}, u32[]{:S(2)}, u32[]{:S(2)}) collective-permute-start(f32[512,128]{1,0:T(8,128)} %get-tuple-element.25), channel_id=1, source_target_pairs={{0,8},{1,9},{2,10},{3,11},{4,12},{5,13},{6,14},{7,15},{8,16},{9,17... | collective-permute-start | bytes 786440 | tf_op jit(solution)/shard_map/ppermute | solution.py:272
  17.9 1.6 %copy-done = f32[512,2,512]{2,1,0:T(2,128)S(1)} copy-done((f32[512,2,512]{2,1,0:T(2,128)S(1)}, f32[512,2,512]{2,1,0:T(2,128)}, u32[]{:S(2)}) %copy-start) | copy-done | bytes 2097176
  19.5 1.2 %shard_map.84.rest = f32[512,256]{1,0:T(8,128)S(1)} custom-call(f32[4096,128]{1,0:T(8,128)S(1)} %bitcast.6, f32[512,256]{1,0:T(8,128)S(1)} %copy-done.4, f32[512,256]{1,0:T(8,128)S(1)} %copy-done.3), custom_call_target="tpu_custom_call" | custom-call | flops 805306368 | bytes 3670016 | tf_op jit(solution)/shard_map/pallas_call | solution.py:253
  20.7 1.1 %shard_map.86.rest = f32[512,128]{1,0:T(8,128)S(1)} custom-call(f32[4096,128]{1,0:T(8,128)S(1)} %bitcast.7, f32[512,256]{1,0:T(8,128)S(1)} %shard_map.84.rest, f32[512,128]{1,0:T(8,128)S(1)} %collective-permute-done.2.following), custom_call_target="tpu_custom_call" | custom-call | flops 805306368 | bytes 3145728 | tf_op jit(solution)/shard_map/pallas_call | solution.py:253
  21.8 4.3 %shard_map.87 = (f32[512,128]{1,0:T(8,128)S(1)}, f32[128,128]{1,0:T(8,128)S(1)}, f32[128,128]{1,0:T(8,128)S(1)}, f32[128,256]{1,0:T(8,128)S(1)}) custom-call(f32[512,128]{1,0:T(8,128)S(1)} %shard_map.86.rest, f32[512,128]{1,0:T(8,128)S(1)} %collective-permute-done.3.handed, f32[512,256]{1,0:T(8,128)S(1)} %copy-done.4), custom_call_target="tpu_custom_call" | custom-call | flops 805306368 | bytes 1572864 | tf_op jit(solution)/shard_map/pallas_call | solution.py:253
  26.1 1.6 %collective-permute-start.4 = (f32[128,256]{1,0:T(8,128)S(1)}, f32[128,256]{1,0:T(8,128)S(1)}, u32[]{:S(2)}, u32[]{:S(2)}) collective-permute-start(f32[128,256]{1,0:T(8,128)S(1)} %get-tuple-element.32.mine.refs_2_), channel_id=1, source_target_pairs={{1,0},{2,1},{3,2},{4,3},{5,4},{6,5},{7,6},{9,8},{10,9},{11,10},{12... | collective-permute-start | bytes 393224 | tf_op jit(solution)/shard_map/ppermute | solution.py:272
  27.8 2.1 %shard_map.88 = (f32[512,128]{1,0:T(8,128)}, f32[128,128]{1,0:T(8,128)S(1)}) custom-call(f32[4096,128]{1,0:T(8,128)S(1)} %bitcast.8, f32[512,256]{1,0:T(8,128)S(1)} %shard_map.84.rest, f32[512,128]{1,0:T(8,128)S(1)} %collective-permute-done.following, f32[512,128]{1,0:T(8,128)S(1)} %collective-permute-done.1.handed, f32[512,128]{1,0:T(8,128)S(1)} %get-tuple-element.28.far, ...), custom_call_target="tpu_custom_call" | custom-call | flops 805306368 | bytes 3801088 | tf_op jit(solution)/shard_map/pallas_call | solution.py:253
  29.9 2.8 %collective-permute-done.4.away = f32[128,256]{1,0:T(8,128)S(1)} collective-permute-done((f32[128,256]{1,0:T(8,128)S(1)}, f32[128,256]{1,0:T(8,128)S(1)}, u32[]{:S(2)}, u32[]{:S(2)}) %collective-permute-start.4) | collective-permute-done | bytes 131104 | tf_op jit(solution)/shard_map/ppermute | solution.py:272
  33.6 2.5 %collective-permute-start.5 = (f32[128,128]{1,0:T(8,128)S(1)}, f32[128,128]{1,0:T(8,128)S(1)}, u32[]{:S(2)}, u32[]{:S(2)}) collective-permute-start(f32[128,128]{1,0:T(8,128)S(1)} %get-tuple-element.34), channel_id=1, source_target_pairs={{0,16},{1,17},{2,18},{3,19},{4,20},{5,21},{6,22},{7,23},{8,24},{9,... | collective-permute-start | bytes 196616 | tf_op jit(solution)/shard_map/ppermute | solution.py:272
  36.6 4.3 %collective-permute-start.9 = (f32[128,256]{1,0:T(8,128)S(1)}, f32[128,256]{1,0:T(8,128)S(1)}, u32[]{:S(2)}, u32[]{:S(2)}) collective-permute-start(f32[128,256]{1,0:T(8,128)S(1)} %get-tuple-element.32.mine.refs_2_), channel_id=1, source_target_pairs={{0,8},{1,9},{2,10},{3,11},{4,12},{5,13},{6,14},{7,15},{8,0},{9,1},... | collective-permute-start | bytes 393224 | tf_op jit(solution)/shard_map/ppermute | solution.py:272
  40.9 2.2 %collective-permute-start.6 = (f32[128,128]{1,0:T(8,128)S(1)}, f32[128,128]{1,0:T(8,128)S(1)}, u32[]{:S(2)}, u32[]{:S(2)}) collective-permute-start(f32[128,128]{1,0:T(8,128)S(1)} %sub.6.mine.refs_0_), channel_id=1, source_target_pairs={{0,8},{1,9},{2,10},{3,11},{4,12},{5,13},{6,14},{7,15},{8,0},{9,1},... | collective-permute-start | bytes 196616 | tf_op jit(solution)/shard_map/ppermute | solution.py:272
  43.1 2.9 %collective-permute-start.8 = (f32[128,128]{1,0:T(8,128)S(1)}, f32[128,128]{1,0:T(8,128)S(1)}, u32[]{:S(2)}, u32[]{:S(2)}) collective-permute-start(f32[128,128]{1,0:T(8,128)S(1)} %sub.7.refs_1_), channel_id=1, source_target_pairs={{0,8},{1,9},{2,10},{3,11},{4,12},{5,13},{6,14},{7,15},{8,0},{9,1},... | collective-permute-start | bytes 196616 | tf_op jit(solution)/shard_map/ppermute | solution.py:272
  46.0 3.9 %shard_map.90.inverse = f32[128,128]{1,0:T(8,128)S(1)} custom-call(f32[128,128]{1,0:T(8,128)S(1)} %sub.6.mine.refs_0_, f32[128,128]{1,0:T(8,128)S(1)} %collective-permute-done.6.theirs.refs_3_), custom_call_target="tpu_custom_call" | custom-call | bytes 196608 | tf_op jit(solution)/shard_map/pallas_call | solution.py:253
  51.6 10.3 %collective-permute-start.10 = (f32[128,256]{1,0:T(8,128)S(1)}, f32[128,256]{1,0:T(8,128)S(1)}, u32[]{:S(2)}, u32[]{:S(2)}) collective-permute-start(f32[128,256]{1,0:T(8,128)S(1)} %get-tuple-element.36.refs_2_), channel_id=1, source_target_pairs={{0,1},{1,0},{2,3},{3,2},{4,5},{5,4},{6,7},{7,6},{8,9},{9,8},{10,11... | collective-permute-start | bytes 393224 | tf_op jit(solution)/shard_map/ppermute | solution.py:272
  61.9 2.5 %collective-permute-start.14 = (f32[128,256]{1,0:T(8,128)S(1)}, f32[128,256]{1,0:T(8,128)S(1)}, u32[]{:S(2)}, u32[]{:S(2)}) collective-permute-start(f32[128,256]{1,0:T(8,128)S(1)} %get-tuple-element.36.refs_2_), channel_id=1, source_target_pairs={{0,16},{1,17},{2,18},{3,19},{4,20},{5,21},{6,22},{7,23},{8,24},{9,... | collective-permute-start | bytes 393224 | tf_op jit(solution)/shard_map/ppermute | solution.py:272
  65.4 1.0 %collective-permute-start.12 = (f32[128,128]{1,0:T(8,128)S(1)}, f32[128,128]{1,0:T(8,128)S(1)}, u32[]{:S(2)}, u32[]{:S(2)}) collective-permute-start(f32[128,128]{1,0:T(8,128)S(1)} %get-tuple-element.39.mine.refs_0_), channel_id=1, source_target_pairs={{0,16},{1,17},{2,18},{3,19},{4,20},{5,21},{6,22},{7,23},{8,24},{9,... | collective-permute-start | bytes 196616 | tf_op jit(solution)/shard_map/ppermute | solution.py:272
  66.5 1.9 %collective-permute-start.13 = (f32[128,128]{1,0:T(8,128)S(1)}, f32[128,128]{1,0:T(8,128)S(1)}, u32[]{:S(2)}, u32[]{:S(2)}) collective-permute-start(f32[128,128]{1,0:T(8,128)S(1)} %get-tuple-element.40.refs_1_), channel_id=1, source_target_pairs={{0,16},{1,17},{2,18},{3,19},{4,20},{5,21},{6,22},{7,23},{8,24},{9,... | collective-permute-start | bytes 196616 | tf_op jit(solution)/shard_map/ppermute | solution.py:272
  68.8 7.2 %collective-permute-done.12.theirs.refs_3_ = f32[128,128]{1,0:T(8,128)S(1)} collective-permute-done((f32[128,128]{1,0:T(8,128)S(1)}, f32[128,128]{1,0:T(8,128)S(1)}, u32[]{:S(2)}, u32[]{:S(2)}) %collective-permute-start.12) | collective-permute-done | bytes 65568 | tf_op jit(solution)/shard_map/ppermute | solution.py:272
  76.0 3.9 %shard_map.93.inverse = f32[128,128]{1,0:T(8,128)S(1)} custom-call(f32[128,128]{1,0:T(8,128)S(1)} %get-tuple-element.39.mine.refs_0_, f32[128,128]{1,0:T(8,128)S(1)} %collective-permute-done.12.theirs.refs_3_), custom_call_target="tpu_custom_call" | custom-call | bytes 196608 | tf_op jit(solution)/shard_map/pallas_call | solution.py:253
  79.9 1.9 %shard_map.95 = (f32[1,2,256,128]{3,2,1,0:T(8,128)}, f32[1,128,256]{2,1,0:T(8,128)}, f32[1,128,256]{2,1,0:T(8,128)}) custom-call(f32[128,128]{1,0:T(8,128)S(1)} %shard_map.93.inverse, f32[128,128]{1,0:T(8,128)S(1)} %get-tuple-element.39.mine.refs_0_, f32[128,128]{1,0:T(8,128)S(1)} %get-tuple-element.40.refs_1_, f32[128,256]{1,0:T(8,128)S(1)} %get-tuple-element.36.refs_2_, ...), custom_call_target="tpu_custom_call" | custom-call | bytes 1245184 | tf_op jit(solution)/shard_map/pallas_call | solution.py:253
  (32 shorter events, 4.5 us)
Async XLA Ops:
  0.6 17.3 %copy-start.4 = (f32[512,256]{1,0:T(8,128)S(1)}, f32[512,256]{1,0:T(8,128)}, u32[]{:S(2)}) copy-start(f32[512,256]{1,0:T(8,128)} %probes.5) | copy-start | bytes 1572868
  0.6 17.3 %copy-start.3 = (f32[512,256]{1,0:T(8,128)S(1)}, f32[512,256]{1,0:T(8,128)}, u32[]{:S(2)}) copy-start(f32[512,256]{1,0:T(8,128)} %samples.1) | copy-start | bytes 1572868
  5.1 15.5 %collective-permute-start.2 = (f32[512,128]{1,0:T(8,128)}, f32[512,128]{1,0:T(8,128)S(1)}, u32[]{:S(2)}, u32[]{:S(2)}) collective-permute-start(f32[512,128]{1,0:T(8,128)} %get-tuple-element.26), channel_id=1, source_target_pairs={{1,24},{2,25},{3,26},{4,27},{5,28},{6,29},{7,30},{8,0},{9,1},{10,2... | collective-permute-start | bytes 786440 | tf_op jit(solution)/shard_map/ppermute | solution.py:272
  6.4 15.4 %collective-permute-start.3 = (f32[512,128]{1,0:T(8,128)}, f32[512,128]{1,0:T(8,128)S(1)}, u32[]{:S(2)}, u32[]{:S(2)}) collective-permute-start(f32[512,128]{1,0:T(8,128)} %get-tuple-element.27), channel_id=1, source_target_pairs={{0,8},{1,9},{2,10},{3,11},{4,12},{5,13},{6,14},{7,15},{8,16},{9,17... | collective-permute-start | bytes 786440 | tf_op jit(solution)/shard_map/ppermute | solution.py:272
  12.0 15.7 %collective-permute-start = (f32[512,128]{1,0:T(8,128)}, f32[512,128]{1,0:T(8,128)S(1)}, u32[]{:S(2)}, u32[]{:S(2)}) collective-permute-start(f32[512,128]{1,0:T(8,128)} %get-tuple-element.24), channel_id=1, source_target_pairs={{1,24},{2,25},{3,26},{4,27},{5,28},{6,29},{7,30},{8,0},{9,1},{10,2... | collective-permute-start | bytes 786440 | tf_op jit(solution)/shard_map/ppermute | solution.py:272
  13.3 14.4 %collective-permute-start.1 = (f32[512,128]{1,0:T(8,128)}, f32[512,128]{1,0:T(8,128)S(1)}, u32[]{:S(2)}, u32[]{:S(2)}) collective-permute-start(f32[512,128]{1,0:T(8,128)} %get-tuple-element.25), channel_id=1, source_target_pairs={{0,8},{1,9},{2,10},{3,11},{4,12},{5,13},{6,14},{7,15},{8,16},{9,17... | collective-permute-start | bytes 786440 | tf_op jit(solution)/shard_map/ppermute | solution.py:272
  17.9 1.6 %copy-start = (f32[512,2,512]{2,1,0:T(2,128)S(1)}, f32[512,2,512]{2,1,0:T(2,128)}, u32[]{:S(2)}) copy-start(f32[512,2,512]{2,1,0:T(2,128)} %param.7) | copy-start | bytes 6291460
  21.8 6.0 %copy-start.1 = (f32[512,2,512]{2,1,0:T(2,128)S(1)}, f32[512,2,512]{2,1,0:T(2,128)}, u32[]{:S(2)}) copy-start(f32[512,2,512]{2,1,0:T(2,128)} %param.7) | copy-start | bytes 6291460
  26.1 6.5 %copy-start.2 = (f32[1,3,2,128,128]{4,3,2,1,0:T(8,128)S(1)}, f32[1,3,2,128,128]{4,3,2,1,0:T(8,128)}, u32[]{:S(2)}) copy-start(f32[1,3,2,128,128]{4,3,2,1,0:T(8,128)} %couplings.3) | copy-start | bytes 1179652
  26.1 6.5 %copy-start.5 = (s32[1,3]{1,0:T(1,128)S(1)}, s32[1,3]{1,0:T(1,128)}, u32[]{:S(2)}) copy-start(s32[1,3]{1,0:T(1,128)} %slots.3) | copy-start | bytes 40
  26.1 6.5 %collective-permute-start.4 = (f32[128,256]{1,0:T(8,128)S(1)}, f32[128,256]{1,0:T(8,128)S(1)}, u32[]{:S(2)}, u32[]{:S(2)}) collective-permute-start(f32[128,256]{1,0:T(8,128)S(1)} %get-tuple-element.32.mine.refs_2_), channel_id=1, source_target_pairs={{1,0},{2,1},{3,2},{4,3},{5,4},{6,5},{7,6},{9,8},{10,9},{11,10},{12... | collective-permute-start | bytes 393224 | tf_op jit(solution)/shard_map/ppermute | solution.py:272
  33.6 7.3 %collective-permute-start.5 = (f32[128,128]{1,0:T(8,128)S(1)}, f32[128,128]{1,0:T(8,128)S(1)}, u32[]{:S(2)}, u32[]{:S(2)}) collective-permute-start(f32[128,128]{1,0:T(8,128)S(1)} %get-tuple-element.34), channel_id=1, source_target_pairs={{0,16},{1,17},{2,18},{3,19},{4,20},{5,21},{6,22},{7,23},{8,24},{9,... | collective-permute-start | bytes 196616 | tf_op jit(solution)/shard_map/ppermute | solution.py:272
  36.1 7.0 %collective-permute-start.7 = (f32[128,128]{1,0:T(8,128)S(1)}, f32[128,128]{1,0:T(8,128)S(1)}, u32[]{:S(2)}, u32[]{:S(2)}) collective-permute-start(f32[128,128]{1,0:T(8,128)S(1)} %get-tuple-element.35), channel_id=1, source_target_pairs={{0,16},{1,17},{2,18},{3,19},{4,20},{5,21},{6,22},{7,23},{8,24},{9,... | collective-permute-start | bytes 196616 | tf_op jit(solution)/shard_map/ppermute | solution.py:272
  36.6 13.4 %collective-permute-start.9 = (f32[128,256]{1,0:T(8,128)S(1)}, f32[128,256]{1,0:T(8,128)S(1)}, u32[]{:S(2)}, u32[]{:S(2)}) collective-permute-start(f32[128,256]{1,0:T(8,128)S(1)} %get-tuple-element.32.mine.refs_2_), channel_id=1, source_target_pairs={{0,8},{1,9},{2,10},{3,11},{4,12},{5,13},{6,14},{7,15},{8,0},{9,1},... | collective-permute-start | bytes 393224 | tf_op jit(solution)/shard_map/ppermute | solution.py:272
  40.9 5.2 %collective-permute-start.6 = (f32[128,128]{1,0:T(8,128)S(1)}, f32[128,128]{1,0:T(8,128)S(1)}, u32[]{:S(2)}, u32[]{:S(2)}) collective-permute-start(f32[128,128]{1,0:T(8,128)S(1)} %sub.6.mine.refs_0_), channel_id=1, source_target_pairs={{0,8},{1,9},{2,10},{3,11},{4,12},{5,13},{6,14},{7,15},{8,0},{9,1},... | collective-permute-start | bytes 196616 | tf_op jit(solution)/shard_map/ppermute | solution.py:272
  43.1 6.8 %collective-permute-start.8 = (f32[128,128]{1,0:T(8,128)S(1)}, f32[128,128]{1,0:T(8,128)S(1)}, u32[]{:S(2)}, u32[]{:S(2)}) collective-permute-start(f32[128,128]{1,0:T(8,128)S(1)} %sub.7.refs_1_), channel_id=1, source_target_pairs={{0,8},{1,9},{2,10},{3,11},{4,12},{5,13},{6,14},{7,15},{8,0},{9,1},... | collective-permute-start | bytes 196616 | tf_op jit(solution)/shard_map/ppermute | solution.py:272
  51.0 13.5 %collective-permute-start.11 = (f32[128,256]{1,0:T(8,128)S(1)}, f32[128,256]{1,0:T(8,128)S(1)}, u32[]{:S(2)}, u32[]{:S(2)}) collective-permute-start(f32[128,256]{1,0:T(8,128)S(1)} %get-tuple-element.36.refs_2_), channel_id=1, source_target_pairs={{1,2},{2,1},{3,4},{4,3},{5,6},{6,5},{9,10},{10,9},{11,12},{12,11},... | collective-permute-start | bytes 393224 | tf_op jit(solution)/shard_map/ppermute | solution.py:272
  51.6 12.8 %collective-permute-start.10 = (f32[128,256]{1,0:T(8,128)S(1)}, f32[128,256]{1,0:T(8,128)S(1)}, u32[]{:S(2)}, u32[]{:S(2)}) collective-permute-start(f32[128,256]{1,0:T(8,128)S(1)} %get-tuple-element.36.refs_2_), channel_id=1, source_target_pairs={{0,1},{1,0},{2,3},{3,2},{4,5},{5,4},{6,7},{7,6},{8,9},{9,8},{10,11... | collective-permute-start | bytes 393224 | tf_op jit(solution)/shard_map/ppermute | solution.py:272
  61.9 18.0 %collective-permute-start.14 = (f32[128,256]{1,0:T(8,128)S(1)}, f32[128,256]{1,0:T(8,128)S(1)}, u32[]{:S(2)}, u32[]{:S(2)}) collective-permute-start(f32[128,256]{1,0:T(8,128)S(1)} %get-tuple-element.36.refs_2_), channel_id=1, source_target_pairs={{0,16},{1,17},{2,18},{3,19},{4,20},{5,21},{6,22},{7,23},{8,24},{9,... | collective-permute-start | bytes 393224 | tf_op jit(solution)/shard_map/ppermute | solution.py:272
  65.4 10.6 %collective-permute-start.12 = (f32[128,128]{1,0:T(8,128)S(1)}, f32[128,128]{1,0:T(8,128)S(1)}, u32[]{:S(2)}, u32[]{:S(2)}) collective-permute-start(f32[128,128]{1,0:T(8,128)S(1)} %get-tuple-element.39.mine.refs_0_), channel_id=1, source_target_pairs={{0,16},{1,17},{2,18},{3,19},{4,20},{5,21},{6,22},{7,23},{8,24},{9,... | collective-permute-start | bytes 196616 | tf_op jit(solution)/shard_map/ppermute | solution.py:272
  66.5 13.5 %collective-permute-start.13 = (f32[128,128]{1,0:T(8,128)S(1)}, f32[128,128]{1,0:T(8,128)S(1)}, u32[]{:S(2)}, u32[]{:S(2)}) collective-permute-start(f32[128,128]{1,0:T(8,128)S(1)} %get-tuple-element.40.refs_1_), channel_id=1, source_target_pairs={{0,16},{1,17},{2,18},{3,19},{4,20},{5,21},{6,22},{7,23},{8,24},{9,... | collective-permute-start | bytes 196616 | tf_op jit(solution)/shard_map/ppermute | solution.py:272

commit v6 on v5

--- a/solution.py
+++ b/solution.py
@@ -102,36 +102,33 @@
     )
 
 
-def handed_kernel(near, probes, first, last, probes_first, probes_last, near_copy, arrived):
-    rows, columns = first.shape
+def handed_kernel(near, probes, handed, probes_first, near_copy, arrived):
+    rows, columns = handed.shape
     chunks = rows // 128
-    part = near.shape[0] // chunks
-    coming = [
-        pltpu.make_async_copy(probes.at[:, pl.ds(0, columns)], probes_first, arrived.at[chunks]),
-        pltpu.make_async_copy(
-            probes.at[:, pl.ds(columns, probes_last.shape[1])], probes_last, arrived.at[chunks + 1]
-        ),
-    ]
-    for c in range(chunks):
+    pieces = chunks // 2
+    part = near.shape[0] // pieces
+    coming = [pltpu.make_async_copy(probes.at[:, pl.ds(0, columns)], probes_first, arrived.at[pieces])]
+    for c in range(pieces):
         at = pl.ds(c * part, part)
         coming.append(pltpu.make_async_copy(near.at[at, :], near_copy.at[at, :], arrived.at[c]))
     for copy in coming:
         copy.start()
     coming[0].wait()
-    coming[1].wait()
-    total = jnp.zeros((columns + probes_last.shape[1], rows), jnp.float32)
-    for c in range(chunks):
-        coming[c + 2].wait()
-        upper = near_half(near_copy.at[pl.ds(c * part, part), :], 1, 128, chunks)
-        at = pl.ds(128 * c, 128)
-        piece = jnp.concatenate([probes_first[at, :], probes_last[at, :]], axis=1)
-        total += dot(piece.T, upper)
-    first[...] = total[:columns].T
-    last[...] = total[columns:].T
-
-
-def rest_kernel(near, probes, samples, rest):
-    rest[...] = samples[...] - dot(near_half(near, 0, probes.shape[0]), probes[...])
+    total = None
+    for c in range(pieces):
+        coming[c + 1].wait()
+        upper = near_half(near_copy.at[pl.ds(c * part, part), :], 1, 256, chunks)
+        piece = dot(probes_first[pl.ds(256 * c, 256), :].T, upper)
+        total = piece if total is None else total + piece
+    handed[...] = total.T
+
+
+def rest_kernel(near, probes, samples, rest, handed_last, probes_last):
+    rows = probes.shape[0]
+    columns = rest.shape[1] - probes_last.shape[1]
+    probes_last[...] = probes[:, columns:]
+    rest[...] = samples[...] - dot(near_half(near, 0, rows), probes[...])
+    handed_last[...] = dot(probes[:, columns:].T, near_half(near, 1, rows)).T
 
 
 def following_kernel(near, rest, following, out):
@@ -139,7 +136,7 @@
     out[...] = rest[:, :columns] - dot(near_half(near, 1, rest.shape[0]), following[...])
 
 
-def leaf_kernel(rest, handed, probes, far, inverse, sample_coef, probe_coef, scratch):
+def leaf_kernel(rest, handed, probes, _h, _p, far, inverse, sample_coef, probe_coef, _hout, _pout, scratch):
     columns = far.shape[1]
     block = rest[...] - handed[...]
     far[...] = block
@@ -170,7 +167,7 @@
     return lax.axis_index("leaf") >> level - 1
 
 
-def term_kernel(level, slots, couplings, mine, away, unused, first, last):
+def term_kernel(level, slots, couplings, mine, away, _h, first, last, _hout):
     node = member_node(level)
     block = coupling_of(slots, couplings, level, node ^ 2)
     outer = (node == 0) | (node == 3)
@@ -181,7 +178,7 @@
     last[...] = term[:, first.shape[1] :]
 
 
-def corrected_kernel(level, trees, slots, couplings, one, two, first, last, out_first, out_last):
+def corrected_kernel(level, trees, slots, couplings, one, two, first, out_first, out_last):
     columns = first.shape[1]
     node = member_node(level)
     block = coupling_of(slots, couplings, level, node)
@@ -191,7 +188,7 @@
         main, other = jnp.where(straight, main, other), jnp.where(straight, other, main)
     term = dot(block, main) + dot(block, other, 0, 0)
     out_first[...] = first[...] - term[:, :columns]
-    out_last[...] = last[...] - term[:, columns:]
+    out_last[...] = term[:, columns:]
 
 
 def factor_kernel(mine, theirs, inverse, scratch):
@@ -217,12 +214,16 @@
     return dot(inverse, dot(mine[0][...], own, 0, 0) + dot(theirs[0][...], sibling, 0, 0))
 
 
-def node_kernel(inverse, *refs):
-    coef = level_coefs(inverse[...], refs[:3], refs[3:6])
-    at = 0
-    for out in refs[6:]:
-        out[...] = coef[:, at : at + out.shape[1]]
-        at += out.shape[1]
+def node_kernel(inverse, mine, mine_probes, theirs, theirs_probes, first, probe_coef):
+    columns = first.shape[1]
+    coef = level_coefs(inverse[...], (mine, mine_probes), (theirs, theirs_probes))
+    first[...] = coef[:, :columns]
+    probe_coef[...] = coef[:, columns:]
+
+
+def node_last_kernel(inverse, mine, mine_last, theirs, theirs_last, last):
+    both = dot(mine[...], mine_last[...], 0, 0) + dot(theirs[...], theirs_last[...], 0, 0)
+    last[...] = dot(inverse[...], both)
 
 
 def top_kernel(level, inverse, *refs):
@@ -300,40 +301,43 @@
     tall, tall_last = (rows, columns), (rows, width - columns)
     square, square_last = (columns, columns), (columns, width - columns)
 
-    handed, handed_last, probes_first, probes_last = call(
-        handed_kernel, [tall, tall_last, tall, tall_last], near, probes, flops=work,
-        specs=[ANY, ANY], vmem=62,
-        scratch_shapes=[pltpu.VMEM(near.shape, jnp.float32), pltpu.SemaphoreType.DMA((chunks + 2,))],
+    handed, probes_first = call(
+        handed_kernel, [tall, tall], near, probes, flops=work, specs=[ANY, ANY], vmem=62,
+        scratch_shapes=[
+            pltpu.VMEM(near.shape, jnp.float32), pltpu.SemaphoreType.DMA((chunks // 2 + 1,))
+        ],
     )
     following = flat_shift(probes_first, -1)
     handed = flat_shift(handed, 1)
-    following_last = flat_shift(probes_last, -1)
-    handed_last = flat_shift(handed_last, 1)
-    (rest,) = call(rest_kernel, [(rows, width)], near, probes, samples, flops=work)
+    rest, handed_last, probes_last = call(
+        rest_kernel, [(rows, width), tall_last, tall_last], near, probes, samples, flops=work
+    )
     (rest_first,) = call(following_kernel, [tall], near, rest, following, flops=work)
     scratch = dict(scratch_shapes=[pltpu.VMEM((scratch_rows(columns), columns), jnp.float32)])
-    far, inverse, first, probe_coef = call(
-        leaf_kernel, [tall, square, square, (columns, width)], rest_first, handed, probes,
-        flops=work, **scratch,
-    )
-    leaf_basis, last = call(
-        leaf_last_kernel, [tall, square_last],
-        near, rest, following_last, handed_last, far, inverse, flops=work,
-    )
+    far, inverse, first, probe_coef, handed_last, probes_last = call(
+        leaf_kernel, [tall, square, square, (columns, width), tall_last, tall_last],
+        rest_first, handed, probes, handed_last, probes_last, flops=work,
+        specs=[VMEM, VMEM, VMEM, ANY, ANY], out_specs=[VMEM, VMEM, VMEM, VMEM, ANY, ANY],
+        input_output_aliases={3: 4, 4: 5}, **scratch,
+    )
+    following_last = flat_shift(probes_last, -1)
 
     ancestors = []
+    last = None
     for level in range(1, levels + 1):
         copies = 2 ** (level - 1)
         count = subtree // copies
         theirs_probe = swapped(probe_coef, copies)
         if count == 4:
             away = outward(probe_coef, 2 * copies)
-            terms = call(
-                functools.partial(term_kernel, level), [square, square_last],
-                couplings, probe_coef, away, last, specs=[VMEM, VMEM, VMEM, ANY], slots=node_slot,
-            )
-            first = first - swapped(terms[0], 2 * copies)
-            last = last - swapped(terms[1], 2 * copies)
+            term_first, term_last, handed_last = call(
+                functools.partial(term_kernel, level), [square, square_last, tall_last],
+                couplings, probe_coef, away, handed_last, slots=node_slot,
+                specs=[VMEM, VMEM, VMEM, ANY], out_specs=[VMEM, VMEM, ANY],
+                input_output_aliases={4: 2},
+            )
+            first = first - swapped(term_first, 2 * copies)
+            term_last = swapped(term_last, 2 * copies)
         else:
             if count == 2:
                 fields = [tree_swapped(probe_coef, odd) for odd in (0, 1)]
@@ -341,10 +345,16 @@
                 even = (lax.axis_index("leaf") >> level - 1) & 1 == 0
                 fields = [flat_shift(probe_coef, by) for by in (2 * copies, -2 * copies)]
                 fields = [jnp.where(even, *fields), jnp.where(even, *fields[::-1])]
-            first, last = call(
+            first, term_last = call(
                 functools.partial(corrected_kernel, level, count == 2), [square, square_last],
-                couplings, *fields, first, last, slots=node_slot,
-            )
+                couplings, *fields, first, slots=node_slot,
+            )
+        if last is None:
+            leaf_basis, last = call(
+                leaf_last_kernel, [tall, square_last],
+                near, rest, following_last, flat_shift(handed_last, 1), far, inverse, flops=work,
+            )
+        last = last - term_last
         mine = first, last, probe_coef
         theirs = swapped(first, copies), swapped(last, copies), theirs_probe
         (inverse,) = call(factor_kernel, [square], mine[0], theirs[0], **scratch)
@@ -353,8 +363,12 @@
                 functools.partial(basis_kernel, level), [(1, 1, 2 * columns, columns)],
                 inverse, mine[0], theirs[0],
             )
-            first, last, probe_coef = call(
-                node_kernel, [square, square_last, (columns, width)], inverse, *mine, *theirs
+            first, probe_coef = call(
+                node_kernel, [square, (columns, width)],
+                inverse, mine[0], mine[2], theirs[0], theirs[2],
+            )
+            (last,) = call(
+                node_last_kernel, [square_last], inverse, mine[0], mine[1], theirs[0], theirs[1]
             )
     transfer_bases, top_samples, top_probes = call(
         functools.partial(top_kernel, levels),

time: 82.1 us -> 87.5 us (1.066)
  waiting for transfers between devices: 10 us -> 19 us
  starting transfers between devices: 43.2 us -> 39.8 us
    ppermute x15, waiting for transfers between devices: 10 us -> 19 us  [permuted(): return lax.ppermute(value, BOTH, pairs)]
    ppermute x15, starting transfers between devices: 43.2 us -> 39.8 us  [permuted(): return lax.ppermute(value, BOTH, pairs)]
    pallas_call x12 -> x13, Pallas kernels: 26.2 us -> 25.9 us  [call(): pl.pallas_call(kernel, out_shape=outs, in_specs=specs, out_specs=out_spec...]
  transfers between devices with their start and end apart: 15 -> 15, of which waited for: 2 -> 5; matrix products, arithmetic and copies ran while one was open for 0% -> 0% of each run, Pallas kernels for 22% -> 19%
where the time goes in v6:
time: 87.5 us; the launch traced here: 87.2 us
  starting transfers between devices  39.8 us (45%)
  Pallas kernels  25.9 us (30%)
  waiting for transfers between devices  19 us (22%)
  local copies, waits for them, and re-layouts  1.61 us (2%)
  between operations  0.88 us (1%)
    ppermute x15, starting transfers between devices, permuted(): return lax.ppermute(value, BOTH, pairs)  39.8 us
    pallas_call x13, Pallas kernels, call(): pl.pallas_call(kernel, out_shape=outs, in_specs=specs, out_specs=out_spec...  25.9 us
    ppermute x15, waiting for transfers between devices, permuted(): return lax.ppermute(value, BOTH, pairs)  19 us
  transfers between devices with their start and end apart: 15, of which 5 were waited for; matrix products, arithmetic and copies ran while one was open for 0% of the time, Pallas kernels for 19%

profile of v6, /device:TPU:0, one launch (start us, length us, event | category | flops | bytes accessed | tf_op | source)
XLA Modules:
  0.0 87.2 jit_solution(2437594250007283201)
XLA Ops:
  0.7 3.3 %shard_map.85 = (f32[512,128]{1,0:T(8,128)}, f32[512,128]{1,0:T(8,128)}) custom-call(f32[4096,128]{1,0:T(8,128)} %bitcast.5, f32[512,256]{1,0:T(8,128)} %probes.5), custom_call_target="tpu_custom_call" | custom-call | flops 805306368 | bytes 3145728 | tf_op jit(solution)/shard_map/pallas_call | solution.py:254
  3.9 1.3 %collective-permute-start = (f32[512,128]{1,0:T(8,128)}, f32[512,128]{1,0:T(8,128)S(1)}, u32[]{:S(2)}, u32[]{:S(2)}) collective-permute-start(f32[512,128]{1,0:T(8,128)} %get-tuple-element.28), channel_id=1, source_target_pairs={{1,24},{2,25},{3,26},{4,27},{5,28},{6,29},{7,30},{8,0},{9,1},{10,2... | collective-permute-start | bytes 786440 | tf_op jit(solution)/shard_map/ppermute | solution.py:273
  5.2 5.6 %collective-permute-start.1 = (f32[512,128]{1,0:T(8,128)}, f32[512,128]{1,0:T(8,128)S(1)}, u32[]{:S(2)}, u32[]{:S(2)}) collective-permute-start(f32[512,128]{1,0:T(8,128)} %get-tuple-element.29), channel_id=1, source_target_pairs={{0,8},{1,9},{2,10},{3,11},{4,12},{5,13},{6,14},{7,15},{8,16},{9,17... | collective-permute-start | bytes 786440 | tf_op jit(solution)/shard_map/ppermute | solution.py:273
  10.8 1.6 %copy-done = f32[512,2,512]{2,1,0:T(2,128)S(1)} copy-done((f32[512,2,512]{2,1,0:T(2,128)S(1)}, f32[512,2,512]{2,1,0:T(2,128)}, u32[]{:S(2)}) %copy-start) | copy-done | bytes 2097176
  12.4 1.6 %shard_map.84 = (f32[512,256]{1,0:T(8,128)S(1)}, f32[512,128]{1,0:T(8,128)S(1)}, f32[512,128]{1,0:T(8,128)S(1)}) custom-call(f32[4096,128]{1,0:T(8,128)S(1)} %bitcast.6, f32[512,256]{1,0:T(8,128)S(1)} %copy-done.4, f32[512,256]{1,0:T(8,128)S(1)} %copy-done.3), custom_call_target="tpu_custom_call" | custom-call | flops 805306368 | bytes 4194304 | tf_op jit(solution)/shard_map/pallas_call | solution.py:254
  14.0 1.3 %collective-permute-done.following = f32[512,128]{1,0:T(8,128)S(1)} collective-permute-done((f32[512,128]{1,0:T(8,128)}, f32[512,128]{1,0:T(8,128)S(1)}, u32[]{:S(2)}, u32[]{:S(2)}) %collective-permute-start) | collective-permute-done | bytes 262176 | tf_op jit(solution)/shard_map/ppermute | solution.py:273
  17.7 4.3 %shard_map.87 = (f32[512,128]{1,0:T(8,128)S(1)}, f32[128,128]{1,0:T(8,128)S(1)}, f32[128,128]{1,0:T(8,128)S(1)}, f32[128,256]{1,0:T(8,128)S(1)}, f32[512,128]{1,0:T(8,128)S(1)}, /*index=5*/f32[512,128]{1,0:T(8,128)S(1)}) custom-call(f32[512,128]{1,0:T(8,128)S(1)} %shard_map.86.rest, ...), custom_call_target="tpu_custom_call", output_to_operand_aliasing={{4}: (3, {}), {5}: (4, {})} | custom-call | flops 805306368 | bytes 2621440 | tf_op jit(solution)/shard_map/pallas_call | solution.py:254
  22.0 1.3 %collective-permute-start.3 = (f32[128,256]{1,0:T(8,128)S(1)}, f32[128,256]{1,0:T(8,128)S(1)}, u32[]{:S(2)}, u32[]{:S(2)}) collective-permute-start(f32[128,256]{1,0:T(8,128)S(1)} %get-tuple-element.33.mine.mine_probes), channel_id=1, source_target_pairs={{1,0},{2,1},{3,2},{4,3},{5,4},{6,5},{7,6},{9,8},{10,9},{11,10},{12... | collective-permute-start | bytes 393224 | tf_op jit(solution)/shard_map/ppermute | solution.py:273
  23.3 1.3 %collective-permute-start.2 = (f32[512,128]{1,0:T(8,128)S(1)}, f32[512,128]{1,0:T(8,128)S(1)}, u32[]{:S(2)}, u32[]{:S(2)}) collective-permute-start(f32[512,128]{1,0:T(8,128)S(1)} %get-tuple-element.32), channel_id=1, source_target_pairs={{1,24},{2,25},{3,26},{4,27},{5,28},{6,29},{7,30},{8,0},{9,1},{10,2... | collective-permute-start | bytes 786440 | tf_op jit(solution)/shard_map/ppermute | solution.py:273
  24.6 5.9 %collective-permute-done.3.away = f32[128,256]{1,0:T(8,128)S(1)} collective-permute-done((f32[128,256]{1,0:T(8,128)S(1)}, f32[128,256]{1,0:T(8,128)S(1)}, u32[]{:S(2)}, u32[]{:S(2)}) %collective-permute-start.3) | collective-permute-done | bytes 131104 | tf_op jit(solution)/shard_map/ppermute | solution.py:273
  31.4 1.3 %collective-permute-start.4 = (f32[512,128]{1,0:T(8,128)S(1)}, f32[512,128]{1,0:T(8,128)S(1)}, u32[]{:S(2)}, u32[]{:S(2)}) collective-permute-start(f32[512,128]{1,0:T(8,128)S(1)} %get-tuple-element.35), channel_id=1, source_target_pairs={{0,8},{1,9},{2,10},{3,11},{4,12},{5,13},{6,14},{7,15},{8,16},{9,17... | collective-permute-start | bytes 786440 | tf_op jit(solution)/shard_map/ppermute | solution.py:273
  32.8 2.7 %collective-permute-start.5 = (f32[128,128]{1,0:T(8,128)S(1)}, f32[128,128]{1,0:T(8,128)S(1)}, u32[]{:S(2)}, u32[]{:S(2)}) collective-permute-start(f32[128,128]{1,0:T(8,128)S(1)} %get-tuple-element.40), channel_id=1, source_target_pairs={{0,16},{1,17},{2,18},{3,19},{4,20},{5,21},{6,22},{7,23},{8,24},{9,... | collective-permute-start | bytes 196616 | tf_op jit(solution)/shard_map/ppermute | solution.py:273
  35.5 5.5 %collective-permute-start.7 = (f32[128,256]{1,0:T(8,128)S(1)}, f32[128,256]{1,0:T(8,128)S(1)}, u32[]{:S(2)}, u32[]{:S(2)}) collective-permute-start(f32[128,256]{1,0:T(8,128)S(1)} %get-tuple-element.33.mine.mine_probes), channel_id=1, source_target_pairs={{0,8},{1,9},{2,10},{3,11},{4,12},{5,13},{6,14},{7,15},{8,0},{9,1},... | collective-permute-start | bytes 393224 | tf_op jit(solution)/shard_map/ppermute | solution.py:273
  41.0 5.9 %collective-permute-start.6 = (f32[128,128]{1,0:T(8,128)S(1)}, f32[128,128]{1,0:T(8,128)S(1)}, u32[]{:S(2)}, u32[]{:S(2)}) collective-permute-start(f32[128,128]{1,0:T(8,128)S(1)} %sub.9.mine), channel_id=1, source_target_pairs={{0,8},{1,9},{2,10},{3,11},{4,12},{5,13},{6,14},{7,15},{8,0},{9,1},... | collective-permute-start | bytes 196616 | tf_op jit(solution)/shard_map/ppermute | solution.py:273
  47.7 4.4 %collective-permute-done.6.theirs = f32[128,128]{1,0:T(8,128)S(1)} collective-permute-done((f32[128,128]{1,0:T(8,128)S(1)}, f32[128,128]{1,0:T(8,128)S(1)}, u32[]{:S(2)}, u32[]{:S(2)}) %collective-permute-start.6) | collective-permute-done | bytes 65568 | tf_op jit(solution)/shard_map/ppermute | solution.py:273
  52.1 3.9 %shard_map.90.inverse = f32[128,128]{1,0:T(8,128)S(1)} custom-call(f32[128,128]{1,0:T(8,128)S(1)} %sub.9.mine, f32[128,128]{1,0:T(8,128)S(1)} %collective-permute-done.6.theirs), custom_call_target="tpu_custom_call" | custom-call | bytes 196608 | tf_op jit(solution)/shard_map/pallas_call | solution.py:254
  57.8 5.2 %collective-permute-start.8 = (f32[128,256]{1,0:T(8,128)S(1)}, f32[128,256]{1,0:T(8,128)S(1)}, u32[]{:S(2)}, u32[]{:S(2)}) collective-permute-start(f32[128,256]{1,0:T(8,128)S(1)} %get-tuple-element.41.refs_2_), channel_id=1, source_target_pairs={{0,1},{1,0},{2,3},{3,2},{4,5},{5,4},{6,7},{7,6},{8,9},{9,8},{10,11... | collective-permute-start | bytes 393224 | tf_op jit(solution)/shard_map/ppermute | solution.py:273
  63.0 2.1 %shard_map.89 = (f32[512,128]{1,0:T(8,128)}, f32[128,128]{1,0:T(8,128)S(1)}) custom-call(f32[4096,128]{1,0:T(8,128)S(1)} %bitcast.8, f32[512,256]{1,0:T(8,128)S(1)} %get-tuple-element.27.rest, f32[512,128]{1,0:T(8,128)S(1)} %collective-permute-done.2.following, f32[512,128]{1,0:T(8,128)S(1)} %collective-permute-done.4.handed, ...), custom_call_target="tpu_custom_call" | custom-call | flops 805306368 | bytes 3801088 | tf_op jit(solution)/shard_map/pallas_call | solution.py:254
  65.2 1.5 %collective-permute-start.12 = (f32[128,128]{1,0:T(8,128)S(1)}, f32[128,128]{1,0:T(8,128)S(1)}, u32[]{:S(2)}, u32[]{:S(2)}) collective-permute-start(f32[128,128]{1,0:T(8,128)S(1)} %sub.10.mine_last), channel_id=1, source_target_pairs={{0,8},{1,9},{2,10},{3,11},{4,12},{5,13},{6,14},{7,15},{8,0},{9,1},... | collective-permute-start | bytes 196616 | tf_op jit(solution)/shard_map/ppermute | solution.py:273
  66.6 3.6 %collective-permute-start.14 = (f32[128,256]{1,0:T(8,128)S(1)}, f32[128,256]{1,0:T(8,128)S(1)}, u32[]{:S(2)}, u32[]{:S(2)}) collective-permute-start(f32[128,256]{1,0:T(8,128)S(1)} %get-tuple-element.41.refs_2_), channel_id=1, source_target_pairs={{0,16},{1,17},{2,18},{3,19},{4,20},{5,21},{6,22},{7,23},{8,24},{9,... | collective-permute-start | bytes 393224 | tf_op jit(solution)/shard_map/ppermute | solution.py:273
  71.9 3.0 %collective-permute-start.13 = (f32[128,128]{1,0:T(8,128)S(1)}, f32[128,128]{1,0:T(8,128)S(1)}, u32[]{:S(2)}, u32[]{:S(2)}) collective-permute-start(f32[128,128]{1,0:T(8,128)S(1)} %sub.11.refs_1_), channel_id=1, source_target_pairs={{0,16},{1,17},{2,18},{3,19},{4,20},{5,21},{6,22},{7,23},{8,24},{9,... | collective-permute-start | bytes 196616 | tf_op jit(solution)/shard_map/ppermute | solution.py:273
  75.2 6.1 %collective-permute-done.10.theirs.refs_3_ = f32[128,128]{1,0:T(8,128)S(1)} collective-permute-done((f32[128,128]{1,0:T(8,128)S(1)}, f32[128,128]{1,0:T(8,128)S(1)}, u32[]{:S(2)}, u32[]{:S(2)}) %collective-permute-start.10) | collective-permute-done | bytes 65568 | tf_op jit(solution)/shard_map/ppermute | solution.py:273
  81.3 3.9 %shard_map.93.inverse = f32[128,128]{1,0:T(8,128)S(1)} custom-call(f32[128,128]{1,0:T(8,128)S(1)} %get-tuple-element.43.mine.refs_0_, f32[128,128]{1,0:T(8,128)S(1)} %collective-permute-done.10.theirs.refs_3_), custom_call_target="tpu_custom_call" | custom-call | bytes 196608 | tf_op jit(solution)/shard_map/pallas_call | solution.py:254
  85.3 1.9 %shard_map.96 = (f32[1,2,256,128]{3,2,1,0:T(8,128)}, f32[1,128,256]{2,1,0:T(8,128)}, f32[1,128,256]{2,1,0:T(8,128)}) custom-call(f32[128,128]{1,0:T(8,128)S(1)} %shard_map.93.inverse, f32[128,128]{1,0:T(8,128)S(1)} %get-tuple-element.43.mine.refs_0_, f32[128,128]{1,0:T(8,128)S(1)} %sub.11.refs_1_, f32[128,256]{1,0:T(8,128)S(1)} %get-tuple-element.41.refs_2_, ...), custom_call_target="tpu_custom_call" | custom-call | bytes 1245184 | tf_op jit(solution)/shard_map/pallas_call | solution.py:254
  (34 shorter events, 7.9 us)
Async XLA Ops:
  0.6 10.2 %copy-start.4 = (f32[512,256]{1,0:T(8,128)S(1)}, f32[512,256]{1,0:T(8,128)}, u32[]{:S(2)}) copy-start(f32[512,256]{1,0:T(8,128)} %probes.5) | copy-start | bytes 1572868
  0.6 10.2 %copy-start.3 = (f32[512,256]{1,0:T(8,128)S(1)}, f32[512,256]{1,0:T(8,128)}, u32[]{:S(2)}) copy-start(f32[512,256]{1,0:T(8,128)} %samples.1) | copy-start | bytes 1572868
  3.9 11.4 %collective-permute-start = (f32[512,128]{1,0:T(8,128)}, f32[512,128]{1,0:T(8,128)S(1)}, u32[]{:S(2)}, u32[]{:S(2)}) collective-permute-start(f32[512,128]{1,0:T(8,128)} %get-tuple-element.28), channel_id=1, source_target_pairs={{1,24},{2,25},{3,26},{4,27},{5,28},{6,29},{7,30},{8,0},{9,1},{10,2... | collective-permute-start | bytes 786440 | tf_op jit(solution)/shard_map/ppermute | solution.py:273
  5.2 12.5 %collective-permute-start.1 = (f32[512,128]{1,0:T(8,128)}, f32[512,128]{1,0:T(8,128)S(1)}, u32[]{:S(2)}, u32[]{:S(2)}) collective-permute-start(f32[512,128]{1,0:T(8,128)} %get-tuple-element.29), channel_id=1, source_target_pairs={{0,8},{1,9},{2,10},{3,11},{4,12},{5,13},{6,14},{7,15},{8,16},{9,17... | collective-permute-start | bytes 786440 | tf_op jit(solution)/shard_map/ppermute | solution.py:273
  10.8 1.6 %copy-start = (f32[512,2,512]{2,1,0:T(2,128)S(1)}, f32[512,2,512]{2,1,0:T(2,128)}, u32[]{:S(2)}) copy-start(f32[512,2,512]{2,1,0:T(2,128)} %param.7) | copy-start | bytes 6291460
  16.5 14.0 %copy-start.2 = (f32[1,3,2,128,128]{4,3,2,1,0:T(8,128)S(1)}, f32[1,3,2,128,128]{4,3,2,1,0:T(8,128)}, u32[]{:S(2)}) copy-start(f32[1,3,2,128,128]{4,3,2,1,0:T(8,128)} %couplings.3) | copy-start | bytes 1179652
  16.5 14.0 %copy-start.5 = (s32[1,3]{1,0:T(1,128)S(1)}, s32[1,3]{1,0:T(1,128)}, u32[]{:S(2)}) copy-start(s32[1,3]{1,0:T(1,128)} %slots.3) | copy-start | bytes 40
  17.7 45.3 %copy-start.1 = (f32[512,2,512]{2,1,0:T(2,128)S(1)}, f32[512,2,512]{2,1,0:T(2,128)}, u32[]{:S(2)}) copy-start(f32[512,2,512]{2,1,0:T(2,128)} %param.7) | copy-start | bytes 6291460
  22.0 8.5 %collective-permute-start.3 = (f32[128,256]{1,0:T(8,128)S(1)}, f32[128,256]{1,0:T(8,128)S(1)}, u32[]{:S(2)}, u32[]{:S(2)}) collective-permute-start(f32[128,256]{1,0:T(8,128)S(1)} %get-tuple-element.33.mine.mine_probes), channel_id=1, source_target_pairs={{1,0},{2,1},{3,2},{4,3},{5,4},{6,5},{7,6},{9,8},{10,9},{11,10},{12... | collective-permute-start | bytes 393224 | tf_op jit(solution)/shard_map/ppermute | solution.py:273
  23.3 39.7 %collective-permute-start.2 = (f32[512,128]{1,0:T(8,128)S(1)}, f32[512,128]{1,0:T(8,128)S(1)}, u32[]{:S(2)}, u32[]{:S(2)}) collective-permute-start(f32[512,128]{1,0:T(8,128)S(1)} %get-tuple-element.32), channel_id=1, source_target_pairs={{1,24},{2,25},{3,26},{4,27},{5,28},{6,29},{7,30},{8,0},{9,1},{10,2... | collective-permute-start | bytes 786440 | tf_op jit(solution)/shard_map/ppermute | solution.py:273
  31.4 31.6 %collective-permute-start.4 = (f32[512,128]{1,0:T(8,128)S(1)}, f32[512,128]{1,0:T(8,128)S(1)}, u32[]{:S(2)}, u32[]{:S(2)}) collective-permute-start(f32[512,128]{1,0:T(8,128)S(1)} %get-tuple-element.35), channel_id=1, source_target_pairs={{0,8},{1,9},{2,10},{3,11},{4,12},{5,13},{6,14},{7,15},{8,16},{9,17... | collective-permute-start | bytes 786440 | tf_op jit(solution)/shard_map/ppermute | solution.py:273
  32.8 8.3 %collective-permute-start.5 = (f32[128,128]{1,0:T(8,128)S(1)}, f32[128,128]{1,0:T(8,128)S(1)}, u32[]{:S(2)}, u32[]{:S(2)}) collective-permute-start(f32[128,128]{1,0:T(8,128)S(1)} %get-tuple-element.40), channel_id=1, source_target_pairs={{0,16},{1,17},{2,18},{3,19},{4,20},{5,21},{6,22},{7,23},{8,24},{9,... | collective-permute-start | bytes 196616 | tf_op jit(solution)/shard_map/ppermute | solution.py:273
  35.5 20.5 %collective-permute-start.7 = (f32[128,256]{1,0:T(8,128)S(1)}, f32[128,256]{1,0:T(8,128)S(1)}, u32[]{:S(2)}, u32[]{:S(2)}) collective-permute-start(f32[128,256]{1,0:T(8,128)S(1)} %get-tuple-element.33.mine.mine_probes), channel_id=1, source_target_pairs={{0,8},{1,9},{2,10},{3,11},{4,12},{5,13},{6,14},{7,15},{8,0},{9,1},... | collective-permute-start | bytes 393224 | tf_op jit(solution)/shard_map/ppermute | solution.py:273
  41.0 11.1 %collective-permute-start.6 = (f32[128,128]{1,0:T(8,128)S(1)}, f32[128,128]{1,0:T(8,128)S(1)}, u32[]{:S(2)}, u32[]{:S(2)}) collective-permute-start(f32[128,128]{1,0:T(8,128)S(1)} %sub.9.mine), channel_id=1, source_target_pairs={{0,8},{1,9},{2,10},{3,11},{4,12},{5,13},{6,14},{7,15},{8,0},{9,1},... | collective-permute-start | bytes 196616 | tf_op jit(solution)/shard_map/ppermute | solution.py:273
  46.9 18.2 %collective-permute-start.11 = (f32[128,128]{1,0:T(8,128)S(1)}, f32[128,128]{1,0:T(8,128)S(1)}, u32[]{:S(2)}, u32[]{:S(2)}) collective-permute-start(f32[128,128]{1,0:T(8,128)S(1)} %get-tuple-element.45), channel_id=1, source_target_pairs={{0,16},{1,17},{2,18},{3,19},{4,20},{5,21},{6,22},{7,23},{8,24},{9,... | collective-permute-start | bytes 196616 | tf_op jit(solution)/shard_map/ppermute | solution.py:273
  56.9 13.3 %collective-permute-start.9 = (f32[128,256]{1,0:T(8,128)S(1)}, f32[128,256]{1,0:T(8,128)S(1)}, u32[]{:S(2)}, u32[]{:S(2)}) collective-permute-start(f32[128,256]{1,0:T(8,128)S(1)} %get-tuple-element.41.refs_2_), channel_id=1, source_target_pairs={{1,2},{2,1},{3,4},{4,3},{5,6},{6,5},{9,10},{10,9},{11,12},{12,11},... | collective-permute-start | bytes 393224 | tf_op jit(solution)/shard_map/ppermute | solution.py:273
  57.8 12.4 %collective-permute-start.8 = (f32[128,256]{1,0:T(8,128)S(1)}, f32[128,256]{1,0:T(8,128)S(1)}, u32[]{:S(2)}, u32[]{:S(2)}) collective-permute-start(f32[128,256]{1,0:T(8,128)S(1)} %get-tuple-element.41.refs_2_), channel_id=1, source_target_pairs={{0,1},{1,0},{2,3},{3,2},{4,5},{5,4},{6,7},{7,6},{8,9},{9,8},{10,11... | collective-permute-start | bytes 393224 | tf_op jit(solution)/shard_map/ppermute | solution.py:273
  65.2 6.1 %collective-permute-start.12 = (f32[128,128]{1,0:T(8,128)S(1)}, f32[128,128]{1,0:T(8,128)S(1)}, u32[]{:S(2)}, u32[]{:S(2)}) collective-permute-start(f32[128,128]{1,0:T(8,128)S(1)} %sub.10.mine_last), channel_id=1, source_target_pairs={{0,8},{1,9},{2,10},{3,11},{4,12},{5,13},{6,14},{7,15},{8,0},{9,1},... | collective-permute-start | bytes 196616 | tf_op jit(solution)/shard_map/ppermute | solution.py:273
  66.6 18.6 %collective-permute-start.14 = (f32[128,256]{1,0:T(8,128)S(1)}, f32[128,256]{1,0:T(8,128)S(1)}, u32[]{:S(2)}, u32[]{:S(2)}) collective-permute-start(f32[128,256]{1,0:T(8,128)S(1)} %get-tuple-element.41.refs_2_), channel_id=1, source_target_pairs={{0,16},{1,17},{2,18},{3,19},{4,20},{5,21},{6,22},{7,23},{8,24},{9,... | collective-permute-start | bytes 393224 | tf_op jit(solution)/shard_map/ppermute | solution.py:273
  71.2 10.2 %collective-permute-start.10 = (f32[128,128]{1,0:T(8,128)S(1)}, f32[128,128]{1,0:T(8,128)S(1)}, u32[]{:S(2)}, u32[]{:S(2)}) collective-permute-start(f32[128,128]{1,0:T(8,128)S(1)} %get-tuple-element.43.mine.refs_0_), channel_id=1, source_target_pairs={{0,16},{1,17},{2,18},{3,19},{4,20},{5,21},{6,22},{7,23},{8,24},{9,... | collective-permute-start | bytes 196616 | tf_op jit(solution)/shard_map/ppermute | solution.py:273
  71.9 13.4 %collective-permute-start.13 = (f32[128,128]{1,0:T(8,128)S(1)}, f32[128,128]{1,0:T(8,128)S(1)}, u32[]{:S(2)}, u32[]{:S(2)}) collective-permute-start(f32[128,128]{1,0:T(8,128)S(1)} %sub.11.refs_1_), channel_id=1, source_target_pairs={{0,16},{1,17},{2,18},{3,19},{4,20},{5,21},{6,22},{7,23},{8,24},{9,... | collective-permute-start | bytes 196616 | tf_op jit(solution)/shard_map/ppermute | solution.py:273

commit v7 on v5

--- a/solution.py
+++ b/solution.py
@@ -102,41 +102,21 @@
     )
 
 
-def handed_kernel(near, probes, first, last, probes_first, probes_last, near_copy, arrived):
-    rows, columns = first.shape
-    chunks = rows // 128
-    part = near.shape[0] // chunks
-    coming = [
-        pltpu.make_async_copy(probes.at[:, pl.ds(0, columns)], probes_first, arrived.at[chunks]),
-        pltpu.make_async_copy(
-            probes.at[:, pl.ds(columns, probes_last.shape[1])], probes_last, arrived.at[chunks + 1]
-        ),
-    ]
-    for c in range(chunks):
-        at = pl.ds(c * part, part)
-        coming.append(pltpu.make_async_copy(near.at[at, :], near_copy.at[at, :], arrived.at[c]))
-    for copy in coming:
-        copy.start()
-    coming[0].wait()
-    coming[1].wait()
-    total = jnp.zeros((columns + probes_last.shape[1], rows), jnp.float32)
-    for c in range(chunks):
-        coming[c + 2].wait()
-        upper = near_half(near_copy.at[pl.ds(c * part, part), :], 1, 128, chunks)
-        at = pl.ds(128 * c, 128)
-        piece = jnp.concatenate([probes_first[at, :], probes_last[at, :]], axis=1)
-        total += dot(piece.T, upper)
-    first[...] = total[:columns].T
-    last[...] = total[columns:].T
-
-
-def rest_kernel(near, probes, samples, rest):
-    rest[...] = samples[...] - dot(near_half(near, 0, probes.shape[0]), probes[...])
-
-
-def following_kernel(near, rest, following, out):
-    columns = out.shape[1]
-    out[...] = rest[:, :columns] - dot(near_half(near, 1, rest.shape[0]), following[...])
+def handed_kernel(near, probes, handed):
+    handed[...] = dot(probes[:, : handed.shape[1]].T, near_half(near, 1, probes.shape[0])).T
+
+
+def rest_kernel(near, probes, samples, rest, handed_last):
+    rows, columns = handed_last.shape
+    rest[...] = samples[...] - dot(near_half(near, 0, rows), probes[...])
+    handed_last[...] = dot(probes[:, probes.shape[1] - columns :].T, near_half(near, 1, rows)).T
+
+
+def following_kernel(near, rest, following, _h, first, last, _hout):
+    columns = first.shape[1]
+    block = rest[...] - dot(near_half(near, 1, rest.shape[0]), following[...])
+    first[...] = block[:, :columns]
+    last[...] = block[:, columns:]
 
 
 def leaf_kernel(rest, handed, probes, far, inverse, sample_coef, probe_coef, scratch):
@@ -152,12 +132,9 @@
     probe_coef[...] = coef[:, columns:]
 
 
-def leaf_last_kernel(near, rest, following, handed, far, inverse, basis, sample_coef):
-    columns = far.shape[1]
-    upper = near_half(near, 1, rest.shape[0])
+def leaf_last_kernel(rest, handed, far, inverse, basis, sample_coef):
     basis[...] = dot(far[...], inverse[...], 1, 1)
-    block = rest[:, columns:] - dot(upper, following[...]) - handed[...]
-    sample_coef[...] = dot(basis[...], block, 0, 0)
+    sample_coef[...] = dot(basis[...], rest[...] - handed[...], 0, 0)
 
 
 def coupling_of(slots, couplings, level, node):
@@ -170,7 +147,7 @@
     return lax.axis_index("leaf") >> level - 1
 
 
-def term_kernel(level, slots, couplings, mine, away, unused, first, last):
+def term_kernel(level, slots, couplings, mine, away, _last, first, last):
     node = member_node(level)
     block = coupling_of(slots, couplings, level, node ^ 2)
     outer = (node == 0) | (node == 3)
@@ -181,7 +158,7 @@
     last[...] = term[:, first.shape[1] :]
 
 
-def corrected_kernel(level, trees, slots, couplings, one, two, first, last, out_first, out_last):
+def corrected_kernel(level, trees, slots, couplings, one, two, first, out_first, out_last):
     columns = first.shape[1]
     node = member_node(level)
     block = coupling_of(slots, couplings, level, node)
@@ -191,7 +168,7 @@
         main, other = jnp.where(straight, main, other), jnp.where(straight, other, main)
     term = dot(block, main) + dot(block, other, 0, 0)
     out_first[...] = first[...] - term[:, :columns]
-    out_last[...] = last[...] - term[:, columns:]
+    out_last[...] = term[:, columns:]
 
 
 def factor_kernel(mine, theirs, inverse, scratch):
@@ -300,25 +277,24 @@
     tall, tall_last = (rows, columns), (rows, width - columns)
     square, square_last = (columns, columns), (columns, width - columns)
 
-    handed, handed_last, probes_first, probes_last = call(
-        handed_kernel, [tall, tall_last, tall, tall_last], near, probes, flops=work,
-        specs=[ANY, ANY], vmem=62,
-        scratch_shapes=[pltpu.VMEM(near.shape, jnp.float32), pltpu.SemaphoreType.DMA((chunks + 2,))],
-    )
-    following = flat_shift(probes_first, -1)
+    following = flat_shift(probes, -1)
+    (handed,) = call(handed_kernel, [tall], near, probes, flops=work)
     handed = flat_shift(handed, 1)
-    following_last = flat_shift(probes_last, -1)
+    rest, handed_last = call(
+        rest_kernel, [(rows, width), tall_last], near, probes, samples, flops=work
+    )
+    rest_first, rest_last, handed_last = call(
+        following_kernel, [tall, tall_last, tall_last], near, rest, following, handed_last, flops=work,
+        specs=[VMEM, VMEM, VMEM, ANY], out_specs=[VMEM, VMEM, ANY], input_output_aliases={3: 2},
+    )
     handed_last = flat_shift(handed_last, 1)
-    (rest,) = call(rest_kernel, [(rows, width)], near, probes, samples, flops=work)
-    (rest_first,) = call(following_kernel, [tall], near, rest, following, flops=work)
     scratch = dict(scratch_shapes=[pltpu.VMEM((scratch_rows(columns), columns), jnp.float32)])
     far, inverse, first, probe_coef = call(
         leaf_kernel, [tall, square, square, (columns, width)], rest_first, handed, probes,
         flops=work, **scratch,
     )
     leaf_basis, last = call(
-        leaf_last_kernel, [tall, square_last],
-        near, rest, following_last, handed_last, far, inverse, flops=work,
+        leaf_last_kernel, [tall, square_last], rest_last, handed_last, far, inverse, flops=work
     )
 
     ancestors = []
@@ -328,12 +304,12 @@
         theirs_probe = swapped(probe_coef, copies)
         if count == 4:
             away = outward(probe_coef, 2 * copies)
-            terms = call(
+            term_first, term_last = call(
                 functools.partial(term_kernel, level), [square, square_last],
-                couplings, probe_coef, away, last, specs=[VMEM, VMEM, VMEM, ANY], slots=node_slot,
+                couplings, probe_coef, away, last, slots=node_slot, specs=[VMEM, VMEM, VMEM, ANY],
             )
-            first = first - swapped(terms[0], 2 * copies)
-            last = last - swapped(terms[1], 2 * copies)
+            first = first - swapped(term_first, 2 * copies)
+            term_last = swapped(term_last, 2 * copies)
         else:
             if count == 2:
                 fields = [tree_swapped(probe_coef, odd) for odd in (0, 1)]
@@ -341,10 +317,11 @@
                 even = (lax.axis_index("leaf") >> level - 1) & 1 == 0
                 fields = [flat_shift(probe_coef, by) for by in (2 * copies, -2 * copies)]
                 fields = [jnp.where(even, *fields), jnp.where(even, *fields[::-1])]
-            first, last = call(
+            first, term_last = call(
                 functools.partial(corrected_kernel, level, count == 2), [square, square_last],
-                couplings, *fields, first, last, slots=node_slot,
+                couplings, *fields, first, slots=node_slot,
             )
+        last = last - term_last
         mine = first, last, probe_coef
         theirs = swapped(first, copies), swapped(last, copies), theirs_probe
         (inverse,) = call(factor_kernel, [square], mine[0], theirs[0], **scratch)

time: 82.1 us -> 78.6 us (0.957)
  starting transfers between devices: 43.2 us -> 29.2 us
  waiting for transfers between devices: 10 us -> 23.2 us
  Pallas kernels: 26.2 us -> 22.4 us
  local copies, waits for them, and re-layouts: 1.61 us -> 2.65 us
    ppermute x15 -> x14, starting transfers between devices: 43.2 us -> 29.2 us  [permuted(): return lax.ppermute(value, BOTH, pairs)]
    ppermute x15 -> x14, waiting for transfers between devices: 10 us -> 23.2 us  [permuted(): return lax.ppermute(value, BOTH, pairs)]
    pallas_call x12, Pallas kernels: 26.2 us -> 22.4 us  [call(): pl.pallas_call(kernel, out_shape=outs, in_specs=specs, out_specs=out_spec...]
    unnamed x12, local copies, waits for them, and re-layouts: 1.61 us -> 2.65 us
  transfers between devices with their start and end apart: 15 -> 14, of which waited for: 2 -> 6; matrix products, arithmetic and copies ran while one was open for 0% -> 0% of each run, Pallas kernels for 22% -> 24%
where the time goes in v7:
time: 78.6 us; the launch traced here: 78.3 us
  starting transfers between devices  29.2 us (37%)
  waiting for transfers between devices  23.2 us (30%)
  Pallas kernels  22.4 us (28%)
  local copies, waits for them, and re-layouts  2.65 us (3%)
  between operations  0.88 us (1%)
    ppermute x14, starting transfers between devices, permuted(): return lax.ppermute(value, BOTH, pairs)  29.2 us
    ppermute x14, waiting for transfers between devices, permuted(): return lax.ppermute(value, BOTH, pairs)  23.2 us
    pallas_call x12, Pallas kernels, call(): pl.pallas_call(kernel, out_shape=outs, in_specs=specs, out_specs=out_spec...  22.4 us
    unnamed x12, local copies, waits for them, and re-layouts  2.65 us
  transfers between devices with their start and end apart: 14, of which 6 were waited for; matrix products, arithmetic and copies ran while one was open for 0% of the time, Pallas kernels for 24%

profile of v7, /device:TPU:0, one launch (start us, length us, event | category | flops | bytes accessed | tf_op | source)
XLA Modules:
  0.0 78.3 jit_solution(9871244846373879655)
XLA Ops:
  0.6 1.3 %collective-permute-start = (f32[512,256]{1,0:T(8,128)}, f32[512,256]{1,0:T(8,128)S(1)}, u32[]{:S(2)}, u32[]{:S(2)}) collective-permute-start(f32[512,256]{1,0:T(8,128)} %probes.5), channel_id=1, source_target_pairs={{1,24},{2,25},{3,26},{4,27},{5,28},{6,29},{7,30},{8,0},{9,1},{10,2... | collective-permute-start | bytes 1572872 | tf_op jit(solution)/shard_map/ppermute | solution.py:249
  1.9 1.6 %copy-done = f32[512,2,512]{2,1,0:T(2,128)S(1)} copy-done((f32[512,2,512]{2,1,0:T(2,128)S(1)}, f32[512,2,512]{2,1,0:T(2,128)}, u32[]{:S(2)}) %copy-start) | copy-done | bytes 2097176
  3.5 1.0 %copy-done.3 = f32[512,256]{1,0:T(8,128)S(1)} copy-done((f32[512,256]{1,0:T(8,128)S(1)}, f32[512,256]{1,0:T(8,128)}, u32[]{:S(2)}) %copy-start.3) | copy-done | bytes 524312
  5.5 5.6 %collective-permute-start.2 = (f32[512,128]{1,0:T(8,128)S(1)}, f32[512,128]{1,0:T(8,128)S(1)}, u32[]{:S(2)}, u32[]{:S(2)}) collective-permute-start(f32[512,128]{1,0:T(8,128)S(1)} %shard_map.86), channel_id=1, source_target_pairs={{0,8},{1,9},{2,10},{3,11},{4,12},{5,13},{6,14},{7,15},{8,16},{9,17... | collective-permute-start | bytes 786440 | tf_op jit(solution)/shard_map/ppermute | solution.py:249
  11.1 1.6 %shard_map.84 = (f32[512,256]{1,0:T(8,128)S(1)}, f32[512,128]{1,0:T(8,128)S(1)}) custom-call(f32[4096,128]{1,0:T(8,128)S(1)} %bitcast.6, f32[512,256]{1,0:T(8,128)S(1)} %copy-done.3, f32[512,256]{1,0:T(8,128)S(1)} %copy-done.2), custom_call_target="tpu_custom_call" | custom-call | flops 805306368 | bytes 3932160 | tf_op jit(solution)/shard_map/pallas_call | solution.py:230
  12.7 5.0 %collective-permute-done.following = f32[512,256]{1,0:T(8,128)S(1)} collective-permute-done((f32[512,256]{1,0:T(8,128)}, f32[512,256]{1,0:T(8,128)S(1)}, u32[]{:S(2)}, u32[]{:S(2)}) %collective-permute-start) | collective-permute-done | bytes 524320 | tf_op jit(solution)/shard_map/ppermute | solution.py:249
  17.7 1.2 %shard_map.85 = (f32[512,128]{1,0:T(8,128)S(1)}, f32[512,128]{1,0:T(8,128)S(1)}, f32[512,128]{1,0:T(8,128)S(1)}) custom-call(f32[4096,128]{1,0:T(8,128)S(1)} %bitcast.7, f32[512,256]{1,0:T(8,128)S(1)} %get-tuple-element.25.rest, f32[512,256]{1,0:T(8,128)S(1)} %collective-permute-done.following, ...), custom_call_target="tpu_custom_call", output_to_operand_aliasing={{2}: (3, {})} | custom-call | flops 805306368 | bytes 4194304 | tf_op jit(solution)/shard_map/pallas_call | solution.py:230
  18.9 3.8 %collective-permute-start.1 = (f32[512,128]{1,0:T(8,128)S(1)}, f32[512,128]{1,0:T(8,128)S(1)}, u32[]{:S(2)}, u32[]{:S(2)}) collective-permute-start(f32[512,128]{1,0:T(8,128)S(1)} %get-tuple-element.28), channel_id=1, source_target_pairs={{0,8},{1,9},{2,10},{3,11},{4,12},{5,13},{6,14},{7,15},{8,16},{9,17... | collective-permute-start | bytes 786440 | tf_op jit(solution)/shard_map/ppermute | solution.py:249
  22.7 4.3 %shard_map.87 = (f32[512,128]{1,0:T(8,128)S(1)}, f32[128,128]{1,0:T(8,128)S(1)}, f32[128,128]{1,0:T(8,128)S(1)}, f32[128,256]{1,0:T(8,128)S(1)}) custom-call(f32[512,128]{1,0:T(8,128)S(1)} %get-tuple-element.29.rest, f32[512,128]{1,0:T(8,128)S(1)} %collective-permute-done.2.handed, f32[512,256]{1,0:T(8,128)S(1)} %copy-done.4), custom_call_target="tpu_custom_call" | custom-call | flops 805306368 | bytes 1572864 | tf_op jit(solution)/shard_map/pallas_call | solution.py:230
  27.0 1.4 %collective-permute-start.3 = (f32[128,256]{1,0:T(8,128)S(1)}, f32[128,256]{1,0:T(8,128)S(1)}, u32[]{:S(2)}, u32[]{:S(2)}) collective-permute-start(f32[128,256]{1,0:T(8,128)S(1)} %get-tuple-element.34.mine.refs_2_), channel_id=1, source_target_pairs={{1,0},{2,1},{3,2},{4,3},{5,4},{6,5},{7,6},{9,8},{10,9},{11,10},{12... | collective-permute-start | bytes 393224 | tf_op jit(solution)/shard_map/ppermute | solution.py:249
  28.4 1.5 %shard_map.88 = (f32[512,128]{1,0:T(8,128)}, f32[128,128]{1,0:T(8,128)S(1)}) custom-call(f32[512,128]{1,0:T(8,128)S(1)} %get-tuple-element.27.rest, f32[512,128]{1,0:T(8,128)S(1)} %collective-permute-done.1.handed, f32[512,128]{1,0:T(8,128)S(1)} %get-tuple-element.30.far, f32[128,128]{1,0:T(8,128)S(1)} %get-tuple-element.31.inverse), custom_call_target="tpu_custom_call" | custom-call | flops 805306368 | bytes 1179648 | tf_op jit(solution)/shard_map/pallas_call | solution.py:230
  29.9 2.6 %collective-permute-done.3.away = f32[128,256]{1,0:T(8,128)S(1)} collective-permute-done((f32[128,256]{1,0:T(8,128)S(1)}, f32[128,256]{1,0:T(8,128)S(1)}, u32[]{:S(2)}, u32[]{:S(2)}) %collective-permute-start.3) | collective-permute-done | bytes 131104 | tf_op jit(solution)/shard_map/ppermute | solution.py:249
  33.5 3.5 %collective-permute-start.4 = (f32[128,128]{1,0:T(8,128)S(1)}, f32[128,128]{1,0:T(8,128)S(1)}, u32[]{:S(2)}, u32[]{:S(2)}) collective-permute-start(f32[128,128]{1,0:T(8,128)S(1)} %get-tuple-element.36), channel_id=1, source_target_pairs={{0,16},{1,17},{2,18},{3,19},{4,20},{5,21},{6,22},{7,23},{8,24},{9,... | collective-permute-start | bytes 196616 | tf_op jit(solution)/shard_map/ppermute | solution.py:249
  37.3 2.3 %collective-permute-done.4 = f32[128,128]{1,0:T(8,128)S(1)} collective-permute-done((f32[128,128]{1,0:T(8,128)S(1)}, f32[128,128]{1,0:T(8,128)S(1)}, u32[]{:S(2)}, u32[]{:S(2)}) %collective-permute-start.4) | collective-permute-done | bytes 65568 | tf_op jit(solution)/shard_map/ppermute | solution.py:249
  39.7 4.7 %collective-permute-done.6 = f32[128,128]{1,0:T(8,128)S(1)} collective-permute-done((f32[128,128]{1,0:T(8,128)S(1)}, f32[128,128]{1,0:T(8,128)S(1)}, u32[]{:S(2)}, u32[]{:S(2)}) %collective-permute-start.6) | collective-permute-done | bytes 65568 | tf_op jit(solution)/shard_map/ppermute | solution.py:249
  44.5 1.3 %collective-permute-done.5.theirs.refs_3_ = f32[128,128]{1,0:T(8,128)S(1)} collective-permute-done((f32[128,128]{1,0:T(8,128)S(1)}, f32[128,128]{1,0:T(8,128)S(1)}, u32[]{:S(2)}, u32[]{:S(2)}) %collective-permute-start.5) | collective-permute-done | bytes 65568 | tf_op jit(solution)/shard_map/ppermute | solution.py:249
  45.8 3.9 %shard_map.90.inverse = f32[128,128]{1,0:T(8,128)S(1)} custom-call(f32[128,128]{1,0:T(8,128)S(1)} %sub.9.mine.refs_0_, f32[128,128]{1,0:T(8,128)S(1)} %collective-permute-done.5.theirs.refs_3_), custom_call_target="tpu_custom_call" | custom-call | bytes 196608 | tf_op jit(solution)/shard_map/pallas_call | solution.py:230
  51.6 6.8 %collective-permute-start.9 = (f32[128,256]{1,0:T(8,128)S(1)}, f32[128,256]{1,0:T(8,128)S(1)}, u32[]{:S(2)}, u32[]{:S(2)}) collective-permute-start(f32[128,256]{1,0:T(8,128)S(1)} %get-tuple-element.38.refs_2_), channel_id=1, source_target_pairs={{0,1},{1,0},{2,3},{3,2},{4,5},{5,4},{6,7},{7,6},{8,9},{9,8},{10,11... | collective-permute-start | bytes 393224 | tf_op jit(solution)/shard_map/ppermute | solution.py:249
  58.3 2.4 %collective-permute-start.13 = (f32[128,256]{1,0:T(8,128)S(1)}, f32[128,256]{1,0:T(8,128)S(1)}, u32[]{:S(2)}, u32[]{:S(2)}) collective-permute-start(f32[128,256]{1,0:T(8,128)S(1)} %get-tuple-element.38.refs_2_), channel_id=1, source_target_pairs={{0,16},{1,17},{2,18},{3,19},{4,20},{5,21},{6,22},{7,23},{8,24},{9,... | collective-permute-start | bytes 393224 | tf_op jit(solution)/shard_map/ppermute | solution.py:249
  61.7 1.0 %collective-permute-start.11 = (f32[128,128]{1,0:T(8,128)S(1)}, f32[128,128]{1,0:T(8,128)S(1)}, u32[]{:S(2)}, u32[]{:S(2)}) collective-permute-start(f32[128,128]{1,0:T(8,128)S(1)} %get-tuple-element.40.mine.refs_0_), channel_id=1, source_target_pairs={{0,16},{1,17},{2,18},{3,19},{4,20},{5,21},{6,22},{7,23},{8,24},{9,... | collective-permute-start | bytes 196616 | tf_op jit(solution)/shard_map/ppermute | solution.py:249
  62.8 2.0 %collective-permute-start.12 = (f32[128,128]{1,0:T(8,128)S(1)}, f32[128,128]{1,0:T(8,128)S(1)}, u32[]{:S(2)}, u32[]{:S(2)}) collective-permute-start(f32[128,128]{1,0:T(8,128)S(1)} %sub.11.refs_1_), channel_id=1, source_target_pairs={{0,16},{1,17},{2,18},{3,19},{4,20},{5,21},{6,22},{7,23},{8,24},{9,... | collective-permute-start | bytes 196616 | tf_op jit(solution)/shard_map/ppermute | solution.py:249
  65.2 7.2 %collective-permute-done.11.theirs.refs_3_ = f32[128,128]{1,0:T(8,128)S(1)} collective-permute-done((f32[128,128]{1,0:T(8,128)S(1)}, f32[128,128]{1,0:T(8,128)S(1)}, u32[]{:S(2)}, u32[]{:S(2)}) %collective-permute-start.11) | collective-permute-done | bytes 65568 | tf_op jit(solution)/shard_map/ppermute | solution.py:249
  72.4 3.9 %shard_map.93.inverse = f32[128,128]{1,0:T(8,128)S(1)} custom-call(f32[128,128]{1,0:T(8,128)S(1)} %get-tuple-element.40.mine.refs_0_, f32[128,128]{1,0:T(8,128)S(1)} %collective-permute-done.11.theirs.refs_3_), custom_call_target="tpu_custom_call" | custom-call | bytes 196608 | tf_op jit(solution)/shard_map/pallas_call | solution.py:230
  76.4 1.9 %shard_map.95 = (f32[1,2,256,128]{3,2,1,0:T(8,128)}, f32[1,128,256]{2,1,0:T(8,128)}, f32[1,128,256]{2,1,0:T(8,128)}) custom-call(f32[128,128]{1,0:T(8,128)S(1)} %shard_map.93.inverse, f32[128,128]{1,0:T(8,128)S(1)} %get-tuple-element.40.mine.refs_0_, f32[128,128]{1,0:T(8,128)S(1)} %sub.11.refs_1_, f32[128,256]{1,0:T(8,128)S(1)} %get-tuple-element.38.refs_2_, ...), custom_call_target="tpu_custom_call" | custom-call | bytes 1245184 | tf_op jit(solution)/shard_map/pallas_call | solution.py:230
  (31 shorter events, 5.6 us)
Async XLA Ops:
  0.6 17.1 %collective-permute-start = (f32[512,256]{1,0:T(8,128)}, f32[512,256]{1,0:T(8,128)S(1)}, u32[]{:S(2)}, u32[]{:S(2)}) collective-permute-start(f32[512,256]{1,0:T(8,128)} %probes.5), channel_id=1, source_target_pairs={{1,24},{2,25},{3,26},{4,27},{5,28},{6,29},{7,30},{8,0},{9,1},{10,2... | collective-permute-start | bytes 1572872 | tf_op jit(solution)/shard_map/ppermute | solution.py:249
  1.9 1.6 %copy-start = (f32[512,2,512]{2,1,0:T(2,128)S(1)}, f32[512,2,512]{2,1,0:T(2,128)}, u32[]{:S(2)}) copy-start(f32[512,2,512]{2,1,0:T(2,128)} %param.7) | copy-start | bytes 6291460
  3.5 1.0 %copy-start.3 = (f32[512,256]{1,0:T(8,128)S(1)}, f32[512,256]{1,0:T(8,128)}, u32[]{:S(2)}) copy-start(f32[512,256]{1,0:T(8,128)} %probes.5) | copy-start | bytes 1572868
  4.6 6.5 %copy-start.2 = (f32[512,256]{1,0:T(8,128)S(1)}, f32[512,256]{1,0:T(8,128)}, u32[]{:S(2)}) copy-start(f32[512,256]{1,0:T(8,128)} %samples.1) | copy-start | bytes 1572868
  5.5 17.2 %collective-permute-start.2 = (f32[512,128]{1,0:T(8,128)S(1)}, f32[512,128]{1,0:T(8,128)S(1)}, u32[]{:S(2)}, u32[]{:S(2)}) collective-permute-start(f32[512,128]{1,0:T(8,128)S(1)} %shard_map.86), channel_id=1, source_target_pairs={{0,8},{1,9},{2,10},{3,11},{4,12},{5,13},{6,14},{7,15},{8,16},{9,17... | collective-permute-start | bytes 786440 | tf_op jit(solution)/shard_map/ppermute | solution.py:249
  12.7 10.0 %copy-start.4 = (f32[512,256]{1,0:T(8,128)S(1)}, f32[512,256]{1,0:T(8,128)}, u32[]{:S(2)}) copy-start(f32[512,256]{1,0:T(8,128)} %probes.5) | copy-start | bytes 1572868
  18.9 9.6 %collective-permute-start.1 = (f32[512,128]{1,0:T(8,128)S(1)}, f32[512,128]{1,0:T(8,128)S(1)}, u32[]{:S(2)}, u32[]{:S(2)}) collective-permute-start(f32[512,128]{1,0:T(8,128)S(1)} %get-tuple-element.28), channel_id=1, source_target_pairs={{0,8},{1,9},{2,10},{3,11},{4,12},{5,13},{6,14},{7,15},{8,16},{9,17... | collective-permute-start | bytes 786440 | tf_op jit(solution)/shard_map/ppermute | solution.py:249
  26.9 5.5 %copy-start.1 = (f32[1,3,2,128,128]{4,3,2,1,0:T(8,128)S(1)}, f32[1,3,2,128,128]{4,3,2,1,0:T(8,128)}, u32[]{:S(2)}) copy-start(f32[1,3,2,128,128]{4,3,2,1,0:T(8,128)} %couplings.3) | copy-start | bytes 1179652
  27.0 5.5 %copy-start.5 = (s32[1,3]{1,0:T(1,128)S(1)}, s32[1,3]{1,0:T(1,128)}, u32[]{:S(2)}) copy-start(s32[1,3]{1,0:T(1,128)} %slots.3) | copy-start | bytes 40
  27.0 5.5 %collective-permute-start.3 = (f32[128,256]{1,0:T(8,128)S(1)}, f32[128,256]{1,0:T(8,128)S(1)}, u32[]{:S(2)}, u32[]{:S(2)}) collective-permute-start(f32[128,256]{1,0:T(8,128)S(1)} %get-tuple-element.34.mine.refs_2_), channel_id=1, source_target_pairs={{1,0},{2,1},{3,2},{4,3},{5,4},{6,5},{7,6},{9,8},{10,9},{11,10},{12... | collective-permute-start | bytes 393224 | tf_op jit(solution)/shard_map/ppermute | solution.py:249
  33.5 6.1 %collective-permute-start.4 = (f32[128,128]{1,0:T(8,128)S(1)}, f32[128,128]{1,0:T(8,128)S(1)}, u32[]{:S(2)}, u32[]{:S(2)}) collective-permute-start(f32[128,128]{1,0:T(8,128)S(1)} %get-tuple-element.36), channel_id=1, source_target_pairs={{0,16},{1,17},{2,18},{3,19},{4,20},{5,21},{6,22},{7,23},{8,24},{9,... | collective-permute-start | bytes 196616 | tf_op jit(solution)/shard_map/ppermute | solution.py:249
  36.9 7.5 %collective-permute-start.6 = (f32[128,128]{1,0:T(8,128)S(1)}, f32[128,128]{1,0:T(8,128)S(1)}, u32[]{:S(2)}, u32[]{:S(2)}) collective-permute-start(f32[128,128]{1,0:T(8,128)S(1)} %get-tuple-element.37), channel_id=1, source_target_pairs={{0,16},{1,17},{2,18},{3,19},{4,20},{5,21},{6,22},{7,23},{8,24},{9,... | collective-permute-start | bytes 196616 | tf_op jit(solution)/shard_map/ppermute | solution.py:249
  37.0 12.7 %collective-permute-start.8 = (f32[128,256]{1,0:T(8,128)S(1)}, f32[128,256]{1,0:T(8,128)S(1)}, u32[]{:S(2)}, u32[]{:S(2)}) collective-permute-start(f32[128,256]{1,0:T(8,128)S(1)} %get-tuple-element.34.mine.refs_2_), channel_id=1, source_target_pairs={{0,8},{1,9},{2,10},{3,11},{4,12},{5,13},{6,14},{7,15},{8,0},{9,1},... | collective-permute-start | bytes 393224 | tf_op jit(solution)/shard_map/ppermute | solution.py:249
  39.6 6.2 %collective-permute-start.5 = (f32[128,128]{1,0:T(8,128)S(1)}, f32[128,128]{1,0:T(8,128)S(1)}, u32[]{:S(2)}, u32[]{:S(2)}) collective-permute-start(f32[128,128]{1,0:T(8,128)S(1)} %sub.9.mine.refs_0_), channel_id=1, source_target_pairs={{0,8},{1,9},{2,10},{3,11},{4,12},{5,13},{6,14},{7,15},{8,0},{9,1},... | collective-permute-start | bytes 196616 | tf_op jit(solution)/shard_map/ppermute | solution.py:249
  44.4 5.3 %collective-permute-start.7 = (f32[128,128]{1,0:T(8,128)S(1)}, f32[128,128]{1,0:T(8,128)S(1)}, u32[]{:S(2)}, u32[]{:S(2)}) collective-permute-start(f32[128,128]{1,0:T(8,128)S(1)} %sub.10.refs_1_), channel_id=1, source_target_pairs={{0,8},{1,9},{2,10},{3,11},{4,12},{5,13},{6,14},{7,15},{8,0},{9,1},... | collective-permute-start | bytes 196616 | tf_op jit(solution)/shard_map/ppermute | solution.py:249
  50.7 10.1 %collective-permute-start.10 = (f32[128,256]{1,0:T(8,128)S(1)}, f32[128,256]{1,0:T(8,128)S(1)}, u32[]{:S(2)}, u32[]{:S(2)}) collective-permute-start(f32[128,256]{1,0:T(8,128)S(1)} %get-tuple-element.38.refs_2_), channel_id=1, source_target_pairs={{1,2},{2,1},{3,4},{4,3},{5,6},{6,5},{9,10},{10,9},{11,12},{12,11},... | collective-permute-start | bytes 393224 | tf_op jit(solution)/shard_map/ppermute | solution.py:249
  51.6 9.2 %collective-permute-start.9 = (f32[128,256]{1,0:T(8,128)S(1)}, f32[128,256]{1,0:T(8,128)S(1)}, u32[]{:S(2)}, u32[]{:S(2)}) collective-permute-start(f32[128,256]{1,0:T(8,128)S(1)} %get-tuple-element.38.refs_2_), channel_id=1, source_target_pairs={{0,1},{1,0},{2,3},{3,2},{4,5},{5,4},{6,7},{7,6},{8,9},{9,8},{10,11... | collective-permute-start | bytes 393224 | tf_op jit(solution)/shard_map/ppermute | solution.py:249
  58.3 18.0 %collective-permute-start.13 = (f32[128,256]{1,0:T(8,128)S(1)}, f32[128,256]{1,0:T(8,128)S(1)}, u32[]{:S(2)}, u32[]{:S(2)}) collective-permute-start(f32[128,256]{1,0:T(8,128)S(1)} %get-tuple-element.38.refs_2_), channel_id=1, source_target_pairs={{0,16},{1,17},{2,18},{3,19},{4,20},{5,21},{6,22},{7,23},{8,24},{9,... | collective-permute-start | bytes 393224 | tf_op jit(solution)/shard_map/ppermute | solution.py:249
  61.7 10.7 %collective-permute-start.11 = (f32[128,128]{1,0:T(8,128)S(1)}, f32[128,128]{1,0:T(8,128)S(1)}, u32[]{:S(2)}, u32[]{:S(2)}) collective-permute-start(f32[128,128]{1,0:T(8,128)S(1)} %get-tuple-element.40.mine.refs_0_), channel_id=1, source_target_pairs={{0,16},{1,17},{2,18},{3,19},{4,20},{5,21},{6,22},{7,23},{8,24},{9,... | collective-permute-start | bytes 196616 | tf_op jit(solution)/shard_map/ppermute | solution.py:249
  62.8 13.6 %collective-permute-start.12 = (f32[128,128]{1,0:T(8,128)S(1)}, f32[128,128]{1,0:T(8,128)S(1)}, u32[]{:S(2)}, u32[]{:S(2)}) collective-permute-start(f32[128,128]{1,0:T(8,128)S(1)} %sub.11.refs_1_), channel_id=1, source_target_pairs={{0,16},{1,17},{2,18},{3,19},{4,20},{5,21},{6,22},{7,23},{8,24},{9,... | collective-permute-start | bytes 196616 | tf_op jit(solution)/shard_map/ppermute | solution.py:249

commit v8 on v7

--- a/solution.py
+++ b/solution.py
@@ -35,13 +35,18 @@
     rows = [gram[ROWS * i : ROWS * (i + 1), :] for i in range(blocks)]
     scaled = [None] * blocks
     used = 0
+    coming = None
+
+    def spread(tile, panel):
+        return [across_lanes(tile, ROWS * panel + n) for n in range(ROWS)]
+
     for first in range(0, blocks, GROUP):
         last = first + GROUP
         ahead = min(last + 1, blocks)
         for k in range(first, last):
-            cols = {
-                i: [across_lanes(rows[i], ROWS * k + c) for c in range(ROWS)] for i in range(k, ahead)
-            }
+            cols = {i: spread(rows[i], k) for i in range(k, ahead) if i > k or coming is None}
+            if coming is not None:
+                cols[k], coming = coming, None
             pivots = jnp.ones((ROWS, size), jnp.float32)
             for j in range(0, ROWS, 2):
                 pair = (lane == ROWS * k + j) | (lane == ROWS * k + j + 1)
@@ -57,8 +62,8 @@
                 b = row_of(held, ROWS + j + 1)
                 c = row_of(held, 2 * ROWS + j + 1)
                 det = a * c - b * b
-                inverse = 1.0 / det
-                inverse_a = 1.0 / a
+                inverse = pltpu.reciprocal(det, approx=True)
+                inverse_a = pltpu.reciprocal(a, approx=True)
                 ratio = b * inverse_a
                 pivots = jnp.where(sub == j, a, jnp.where(sub == j + 1, det * inverse_a, pivots))
                 row, next_row = row_of(held, j), row_of(held, j + 1)
@@ -76,6 +81,9 @@
                     for n in range(j + 2, ROWS):
                         x, y = col_rows[n - j - 2]
                         cols[i][n] = cols[i][n] - (f * x + g * y)
+                    if i == k + 1 and j == ROWS - 2:
+                        now, one, two = spread(rows[i], i), spread(row, i), spread(next_row, i)
+                        coming = [now[n] - (f * one[n] + g * two[n]) for n in range(ROWS)]
                     rows[i] = rows[i] - (f * row + g * next_row)
             kept = (lane <= sub + ROWS * k) | (lane >= ROWS * last)
             scaled[k] = jnp.where(kept, rows[k] * lax.rsqrt(pivots), 0.0)
@@ -147,7 +155,7 @@
     return lax.axis_index("leaf") >> level - 1
 
 
-def term_kernel(level, slots, couplings, mine, away, _last, first, last):
+def term_kernel(level, slots, couplings, mine, away, _theirs, _last, first, last):
     node = member_node(level)
     block = coupling_of(slots, couplings, level, node ^ 2)
     outer = (node == 0) | (node == 3)
@@ -194,12 +202,16 @@
     return dot(inverse, dot(mine[0][...], own, 0, 0) + dot(theirs[0][...], sibling, 0, 0))
 
 
-def node_kernel(inverse, *refs):
-    coef = level_coefs(inverse[...], refs[:3], refs[3:6])
-    at = 0
-    for out in refs[6:]:
-        out[...] = coef[:, at : at + out.shape[1]]
-        at += out.shape[1]
+def node_kernel(inverse, mine, mine_probes, theirs, theirs_probes, first, probe_coef):
+    columns = first.shape[1]
+    coef = level_coefs(inverse[...], (mine, mine_probes), (theirs, theirs_probes))
+    first[...] = coef[:, :columns]
+    probe_coef[...] = coef[:, columns:]
+
+
+def node_last_kernel(inverse, mine, mine_last, theirs, theirs_last, last):
+    both = dot(mine[...], mine_last[...], 0, 0) + dot(theirs[...], theirs_last[...], 0, 0)
+    last[...] = dot(inverse[...], both)
 
 
 def top_kernel(level, inverse, *refs):
@@ -306,7 +318,8 @@
             away = outward(probe_coef, 2 * copies)
             term_first, term_last = call(
                 functools.partial(term_kernel, level), [square, square_last],
-                couplings, probe_coef, away, last, slots=node_slot, specs=[VMEM, VMEM, VMEM, ANY],
+                couplings, probe_coef, away, theirs_probe, last, slots=node_slot,
+                specs=[VMEM, VMEM, VMEM, ANY, ANY],
             )
             first = first - swapped(term_first, 2 * copies)
             term_last = swapped(term_last, 2 * copies)
@@ -330,8 +343,12 @@
                 functools.partial(basis_kernel, level), [(1, 1, 2 * columns, columns)],
                 inverse, mine[0], theirs[0],
             )
-            first, last, probe_coef = call(
-                node_kernel, [square, square_last, (columns, width)], inverse, *mine, *theirs
+            first, probe_coef = call(
+                node_kernel, [square, (columns, width)],
+                inverse, mine[0], mine[2], theirs[0], theirs[2],
+            )
+            (last,) = call(
+                node_last_kernel, [square_last], inverse, mine[0], mine[1], theirs[0], theirs[1]
             )
     transfer_bases, top_samples, top_probes = call(
         functools.partial(top_kernel, levels),

time: 78.6 us -> 78.3 us (level)
  the two profiles are of different devices: /device:TPU:0 before, /device:TPU:4 now
where the time goes in v8:
time: 78.3 us; the launch traced here: 77.8 us
  starting transfers between devices  30.8 us (39%)
  Pallas kernels  23.7 us (30%)
  waiting for transfers between devices  19.7 us (25%)
  local copies, waits for them, and re-layouts  2.65 us (3%)
  between operations  0.87 us (1%)
    ppermute x14, starting transfers between devices, permuted(): return lax.ppermute(value, BOTH, pairs)  30.8 us
    pallas_call x13, Pallas kernels, call(): pl.pallas_call(kernel, out_shape=outs, in_specs=specs, out_specs=out_spec...  23.7 us
    ppermute x14, waiting for transfers between devices, permuted(): return lax.ppermute(value, BOTH, pairs)  19.7 us
    unnamed x12, local copies, waits for them, and re-layouts  2.65 us
  transfers between devices with their start and end apart: 14, of which 7 were waited for; matrix products, arithmetic and copies ran while one was open for 0% of the time, Pallas kernels for 27%

profile of v8, /device:TPU:4, one launch (start us, length us, event | category | flops | bytes accessed | tf_op | source)
XLA Modules:
  0.0 77.8 jit_solution(15419589366234885980)
XLA Ops:
  0.6 5.8 %collective-permute-start = (f32[512,256]{1,0:T(8,128)}, f32[512,256]{1,0:T(8,128)S(1)}, u32[]{:S(2)}, u32[]{:S(2)}) collective-permute-start(f32[512,256]{1,0:T(8,128)} %probes.5), channel_id=1, source_target_pairs={{1,24},{2,25},{3,26},{4,27},{5,28},{6,29},{7,30},{8,0},{9,1},{10,2... | collective-permute-start | bytes 1572872 | tf_op jit(solution)/shard_map/ppermute | solution.py:261
  6.5 1.6 %copy-done = f32[512,2,512]{2,1,0:T(2,128)S(1)} copy-done((f32[512,2,512]{2,1,0:T(2,128)S(1)}, f32[512,2,512]{2,1,0:T(2,128)}, u32[]{:S(2)}) %copy-start) | copy-done | bytes 2097176
  10.0 1.9 %collective-permute-start.2 = (f32[512,128]{1,0:T(8,128)S(1)}, f32[512,128]{1,0:T(8,128)S(1)}, u32[]{:S(2)}, u32[]{:S(2)}) collective-permute-start(f32[512,128]{1,0:T(8,128)S(1)} %shard_map.86), channel_id=1, source_target_pairs={{0,8},{1,9},{2,10},{3,11},{4,12},{5,13},{6,14},{7,15},{8,16},{9,17... | collective-permute-start | bytes 786440 | tf_op jit(solution)/shard_map/ppermute | solution.py:261
  11.9 1.6 %shard_map.84 = (f32[512,256]{1,0:T(8,128)S(1)}, f32[512,128]{1,0:T(8,128)S(1)}) custom-call(f32[4096,128]{1,0:T(8,128)S(1)} %bitcast.6, f32[512,256]{1,0:T(8,128)S(1)} %copy-done.3, f32[512,256]{1,0:T(8,128)S(1)} %copy-done.2), custom_call_target="tpu_custom_call" | custom-call | flops 805306368 | bytes 3932160 | tf_op jit(solution)/shard_map/pallas_call | solution.py:242
  13.6 5.5 %collective-permute-done.following = f32[512,256]{1,0:T(8,128)S(1)} collective-permute-done((f32[512,256]{1,0:T(8,128)}, f32[512,256]{1,0:T(8,128)S(1)}, u32[]{:S(2)}, u32[]{:S(2)}) %collective-permute-start) | collective-permute-done | bytes 524320 | tf_op jit(solution)/shard_map/ppermute | solution.py:261
  19.1 1.2 %shard_map.85 = (f32[512,128]{1,0:T(8,128)S(1)}, f32[512,128]{1,0:T(8,128)S(1)}, f32[512,128]{1,0:T(8,128)S(1)}) custom-call(f32[4096,128]{1,0:T(8,128)S(1)} %bitcast.7, f32[512,256]{1,0:T(8,128)S(1)} %get-tuple-element.24.rest, f32[512,256]{1,0:T(8,128)S(1)} %collective-permute-done.following, ...), custom_call_target="tpu_custom_call", output_to_operand_aliasing={{2}: (3, {})} | custom-call | flops 805306368 | bytes 4194304 | tf_op jit(solution)/shard_map/pallas_call | solution.py:242
  20.3 1.9 %collective-permute-start.1 = (f32[512,128]{1,0:T(8,128)S(1)}, f32[512,128]{1,0:T(8,128)S(1)}, u32[]{:S(2)}, u32[]{:S(2)}) collective-permute-start(f32[512,128]{1,0:T(8,128)S(1)} %get-tuple-element.27), channel_id=1, source_target_pairs={{0,8},{1,9},{2,10},{3,11},{4,12},{5,13},{6,14},{7,15},{8,16},{9,17... | collective-permute-start | bytes 786440 | tf_op jit(solution)/shard_map/ppermute | solution.py:261
  22.2 2.4 %collective-permute-done.2.handed = f32[512,128]{1,0:T(8,128)S(1)} collective-permute-done((f32[512,128]{1,0:T(8,128)S(1)}, f32[512,128]{1,0:T(8,128)S(1)}, u32[]{:S(2)}, u32[]{:S(2)}) %collective-permute-start.2) | collective-permute-done | bytes 262176 | tf_op jit(solution)/shard_map/ppermute | solution.py:261
  24.6 4.6 %shard_map.87 = (f32[512,128]{1,0:T(8,128)S(1)}, f32[128,128]{1,0:T(8,128)S(1)}, f32[128,128]{1,0:T(8,128)S(1)}, f32[128,256]{1,0:T(8,128)S(1)}) custom-call(f32[512,128]{1,0:T(8,128)S(1)} %get-tuple-element.28.rest, f32[512,128]{1,0:T(8,128)S(1)} %collective-permute-done.2.handed, f32[512,256]{1,0:T(8,128)S(1)} %copy-done.4), custom_call_target="tpu_custom_call" | custom-call | flops 805306368 | bytes 1572864 | tf_op jit(solution)/shard_map/pallas_call | solution.py:242
  29.2 2.5 %collective-permute-start.4 = (f32[128,256]{1,0:T(8,128)S(1)}, f32[128,256]{1,0:T(8,128)S(1)}, u32[]{:S(2)}, u32[]{:S(2)}) collective-permute-start(f32[128,256]{1,0:T(8,128)S(1)} %get-tuple-element.33.mine.mine_probes), channel_id=1, source_target_pairs={{0,8},{1,9},{2,10},{3,11},{4,12},{5,13},{6,14},{7,15},{8,0},{9,1},... | collective-permute-start | bytes 393224 | tf_op jit(solution)/shard_map/ppermute | solution.py:261
  31.7 2.1 %collective-permute-start.3 = (f32[128,256]{1,0:T(8,128)S(1)}, f32[128,256]{1,0:T(8,128)S(1)}, u32[]{:S(2)}, u32[]{:S(2)}) collective-permute-start(f32[128,256]{1,0:T(8,128)S(1)} %get-tuple-element.33.mine.mine_probes), channel_id=1, source_target_pairs={{1,0},{2,1},{3,2},{4,3},{5,4},{6,5},{7,6},{9,8},{10,9},{11,10},{12... | collective-permute-start | bytes 393224 | tf_op jit(solution)/shard_map/ppermute | solution.py:261
  33.9 1.5 %shard_map.88 = (f32[512,128]{1,0:T(8,128)}, f32[128,128]{1,0:T(8,128)S(1)}) custom-call(f32[512,128]{1,0:T(8,128)S(1)} %get-tuple-element.26.rest, f32[512,128]{1,0:T(8,128)S(1)} %collective-permute-done.1.handed, f32[512,128]{1,0:T(8,128)S(1)} %get-tuple-element.29.far, f32[128,128]{1,0:T(8,128)S(1)} %get-tuple-element.30.inverse), custom_call_target="tpu_custom_call" | custom-call | flops 805306368 | bytes 1179648 | tf_op jit(solution)/shard_map/pallas_call | solution.py:242
  37.1 4.3 %collective-permute-start.5 = (f32[128,128]{1,0:T(8,128)S(1)}, f32[128,128]{1,0:T(8,128)S(1)}, u32[]{:S(2)}, u32[]{:S(2)}) collective-permute-start(f32[128,128]{1,0:T(8,128)S(1)} %get-tuple-element.35), channel_id=1, source_target_pairs={{0,16},{1,17},{2,18},{3,19},{4,20},{5,21},{6,22},{7,23},{8,24},{9,... | collective-permute-start | bytes 196616 | tf_op jit(solution)/shard_map/ppermute | solution.py:261
  41.4 2.9 %collective-permute-done.5 = f32[128,128]{1,0:T(8,128)S(1)} collective-permute-done((f32[128,128]{1,0:T(8,128)S(1)}, f32[128,128]{1,0:T(8,128)S(1)}, u32[]{:S(2)}, u32[]{:S(2)}) %collective-permute-start.5) | collective-permute-done | bytes 65568 | tf_op jit(solution)/shard_map/ppermute | solution.py:261
  44.5 2.8 %collective-permute-start.10 = (f32[128,128]{1,0:T(8,128)S(1)}, f32[128,128]{1,0:T(8,128)S(1)}, u32[]{:S(2)}, u32[]{:S(2)}) collective-permute-start(f32[128,128]{1,0:T(8,128)S(1)} %get-tuple-element.39), channel_id=1, source_target_pairs={{0,16},{1,17},{2,18},{3,19},{4,20},{5,21},{6,22},{7,23},{8,24},{9,... | collective-permute-start | bytes 196616 | tf_op jit(solution)/shard_map/ppermute | solution.py:261
  47.3 1.4 %collective-permute-done.6.theirs = f32[128,128]{1,0:T(8,128)S(1)} collective-permute-done((f32[128,128]{1,0:T(8,128)S(1)}, f32[128,128]{1,0:T(8,128)S(1)}, u32[]{:S(2)}, u32[]{:S(2)}) %collective-permute-start.6) | collective-permute-done | bytes 65568 | tf_op jit(solution)/shard_map/ppermute | solution.py:261
  48.7 4.2 %shard_map.90.inverse = f32[128,128]{1,0:T(8,128)S(1)} custom-call(f32[128,128]{1,0:T(8,128)S(1)} %sub.9.mine, f32[128,128]{1,0:T(8,128)S(1)} %collective-permute-done.6.theirs), custom_call_target="tpu_custom_call" | custom-call | bytes 196608 | tf_op jit(solution)/shard_map/pallas_call | solution.py:242
  53.9 4.8 %collective-permute-start.8 = (f32[128,256]{1,0:T(8,128)S(1)}, f32[128,256]{1,0:T(8,128)S(1)}, u32[]{:S(2)}, u32[]{:S(2)}) collective-permute-start(f32[128,256]{1,0:T(8,128)S(1)} %get-tuple-element.36.refs_2_), channel_id=1, source_target_pairs={{1,2},{2,1},{3,4},{4,3},{5,6},{6,5},{9,10},{10,9},{11,12},{12,11},... | collective-permute-start | bytes 393224 | tf_op jit(solution)/shard_map/ppermute | solution.py:261
  58.8 1.3 %collective-permute-start.13 = (f32[128,256]{1,0:T(8,128)S(1)}, f32[128,256]{1,0:T(8,128)S(1)}, u32[]{:S(2)}, u32[]{:S(2)}) collective-permute-start(f32[128,256]{1,0:T(8,128)S(1)} %get-tuple-element.36.refs_2_), channel_id=1, source_target_pairs={{0,16},{1,17},{2,18},{3,19},{4,20},{5,21},{6,22},{7,23},{8,24},{9,... | collective-permute-start | bytes 393224 | tf_op jit(solution)/shard_map/ppermute | solution.py:261
  60.1 3.0 %collective-permute-done.11.theirs_last = f32[128,128]{1,0:T(8,128)S(1)} collective-permute-done((f32[128,128]{1,0:T(8,128)S(1)}, f32[128,128]{1,0:T(8,128)S(1)}, u32[]{:S(2)}, u32[]{:S(2)}) %collective-permute-start.11) | collective-permute-done | bytes 65568 | tf_op jit(solution)/shard_map/ppermute | solution.py:261
  65.2 2.4 %collective-permute-start.12 = (f32[128,128]{1,0:T(8,128)S(1)}, f32[128,128]{1,0:T(8,128)S(1)}, u32[]{:S(2)}, u32[]{:S(2)}) collective-permute-start(f32[128,128]{1,0:T(8,128)S(1)} %sub.11.refs_1_), channel_id=1, source_target_pairs={{0,16},{1,17},{2,18},{3,19},{4,20},{5,21},{6,22},{7,23},{8,24},{9,... | collective-permute-start | bytes 196616 | tf_op jit(solution)/shard_map/ppermute | solution.py:261
  68.0 3.6 %collective-permute-done.9.theirs.refs_3_ = f32[128,128]{1,0:T(8,128)S(1)} collective-permute-done((f32[128,128]{1,0:T(8,128)S(1)}, f32[128,128]{1,0:T(8,128)S(1)}, u32[]{:S(2)}, u32[]{:S(2)}) %collective-permute-start.9) | collective-permute-done | bytes 65568 | tf_op jit(solution)/shard_map/ppermute | solution.py:261
  71.7 4.2 %shard_map.93.inverse = f32[128,128]{1,0:T(8,128)S(1)} custom-call(f32[128,128]{1,0:T(8,128)S(1)} %get-tuple-element.38.mine.refs_0_, f32[128,128]{1,0:T(8,128)S(1)} %collective-permute-done.9.theirs.refs_3_), custom_call_target="tpu_custom_call" | custom-call | bytes 196608 | tf_op jit(solution)/shard_map/pallas_call | solution.py:242
  75.9 1.9 %shard_map.96 = (f32[1,2,256,128]{3,2,1,0:T(8,128)}, f32[1,128,256]{2,1,0:T(8,128)}, f32[1,128,256]{2,1,0:T(8,128)}) custom-call(f32[128,128]{1,0:T(8,128)S(1)} %shard_map.93.inverse, f32[128,128]{1,0:T(8,128)S(1)} %get-tuple-element.38.mine.refs_0_, f32[128,128]{1,0:T(8,128)S(1)} %sub.11.refs_1_, f32[128,256]{1,0:T(8,128)S(1)} %get-tuple-element.36.refs_2_, ...), custom_call_target="tpu_custom_call" | custom-call | bytes 1245184 | tf_op jit(solution)/shard_map/pallas_call | solution.py:242
  (32 shorter events, 7.5 us)
Async XLA Ops:
  0.6 18.5 %collective-permute-start = (f32[512,256]{1,0:T(8,128)}, f32[512,256]{1,0:T(8,128)S(1)}, u32[]{:S(2)}, u32[]{:S(2)}) collective-permute-start(f32[512,256]{1,0:T(8,128)} %probes.5), channel_id=1, source_target_pairs={{1,24},{2,25},{3,26},{4,27},{5,28},{6,29},{7,30},{8,0},{9,1},{10,2... | collective-permute-start | bytes 1572872 | tf_op jit(solution)/shard_map/ppermute | solution.py:261
  6.5 1.6 %copy-start = (f32[512,2,512]{2,1,0:T(2,128)S(1)}, f32[512,2,512]{2,1,0:T(2,128)}, u32[]{:S(2)}) copy-start(f32[512,2,512]{2,1,0:T(2,128)} %param.7) | copy-start | bytes 6291460
  8.1 1.0 %copy-start.3 = (f32[512,256]{1,0:T(8,128)S(1)}, f32[512,256]{1,0:T(8,128)}, u32[]{:S(2)}) copy-start(f32[512,256]{1,0:T(8,128)} %probes.5) | copy-start | bytes 1572868
  9.1 2.8 %copy-start.2 = (f32[512,256]{1,0:T(8,128)S(1)}, f32[512,256]{1,0:T(8,128)}, u32[]{:S(2)}) copy-start(f32[512,256]{1,0:T(8,128)} %samples.1) | copy-start | bytes 1572868
  10.0 14.6 %collective-permute-start.2 = (f32[512,128]{1,0:T(8,128)S(1)}, f32[512,128]{1,0:T(8,128)S(1)}, u32[]{:S(2)}, u32[]{:S(2)}) collective-permute-start(f32[512,128]{1,0:T(8,128)S(1)} %shard_map.86), channel_id=1, source_target_pairs={{0,8},{1,9},{2,10},{3,11},{4,12},{5,13},{6,14},{7,15},{8,16},{9,17... | collective-permute-start | bytes 786440 | tf_op jit(solution)/shard_map/ppermute | solution.py:261
  13.6 11.1 %copy-start.4 = (f32[512,256]{1,0:T(8,128)S(1)}, f32[512,256]{1,0:T(8,128)}, u32[]{:S(2)}) copy-start(f32[512,256]{1,0:T(8,128)} %probes.5) | copy-start | bytes 1572868
  20.3 13.6 %collective-permute-start.1 = (f32[512,128]{1,0:T(8,128)S(1)}, f32[512,128]{1,0:T(8,128)S(1)}, u32[]{:S(2)}, u32[]{:S(2)}) collective-permute-start(f32[512,128]{1,0:T(8,128)S(1)} %get-tuple-element.27), channel_id=1, source_target_pairs={{0,8},{1,9},{2,10},{3,11},{4,12},{5,13},{6,14},{7,15},{8,16},{9,17... | collective-permute-start | bytes 786440 | tf_op jit(solution)/shard_map/ppermute | solution.py:261
  29.2 7.0 %copy-start.1 = (f32[1,3,2,128,128]{4,3,2,1,0:T(8,128)S(1)}, f32[1,3,2,128,128]{4,3,2,1,0:T(8,128)}, u32[]{:S(2)}) copy-start(f32[1,3,2,128,128]{4,3,2,1,0:T(8,128)} %couplings.3) | copy-start | bytes 1179652
  29.2 7.0 %copy-start.5 = (s32[1,3]{1,0:T(1,128)S(1)}, s32[1,3]{1,0:T(1,128)}, u32[]{:S(2)}) copy-start(s32[1,3]{1,0:T(1,128)} %slots.3) | copy-start | bytes 40
  29.2 6.1 %collective-permute-start.4 = (f32[128,256]{1,0:T(8,128)S(1)}, f32[128,256]{1,0:T(8,128)S(1)}, u32[]{:S(2)}, u32[]{:S(2)}) collective-permute-start(f32[128,256]{1,0:T(8,128)S(1)} %get-tuple-element.33.mine.mine_probes), channel_id=1, source_target_pairs={{0,8},{1,9},{2,10},{3,11},{4,12},{5,13},{6,14},{7,15},{8,0},{9,1},... | collective-permute-start | bytes 393224 | tf_op jit(solution)/shard_map/ppermute | solution.py:261
  31.7 4.4 %collective-permute-start.3 = (f32[128,256]{1,0:T(8,128)S(1)}, f32[128,256]{1,0:T(8,128)S(1)}, u32[]{:S(2)}, u32[]{:S(2)}) collective-permute-start(f32[128,256]{1,0:T(8,128)S(1)} %get-tuple-element.33.mine.mine_probes), channel_id=1, source_target_pairs={{1,0},{2,1},{3,2},{4,3},{5,4},{6,5},{7,6},{9,8},{10,9},{11,10},{12... | collective-permute-start | bytes 393224 | tf_op jit(solution)/shard_map/ppermute | solution.py:261
  37.1 7.2 %collective-permute-start.5 = (f32[128,128]{1,0:T(8,128)S(1)}, f32[128,128]{1,0:T(8,128)S(1)}, u32[]{:S(2)}, u32[]{:S(2)}) collective-permute-start(f32[128,128]{1,0:T(8,128)S(1)} %get-tuple-element.35), channel_id=1, source_target_pairs={{0,16},{1,17},{2,18},{3,19},{4,20},{5,21},{6,22},{7,23},{8,24},{9,... | collective-permute-start | bytes 196616 | tf_op jit(solution)/shard_map/ppermute | solution.py:261
  44.4 4.3 %collective-permute-start.6 = (f32[128,128]{1,0:T(8,128)S(1)}, f32[128,128]{1,0:T(8,128)S(1)}, u32[]{:S(2)}, u32[]{:S(2)}) collective-permute-start(f32[128,128]{1,0:T(8,128)S(1)} %sub.9.mine), channel_id=1, source_target_pairs={{0,8},{1,9},{2,10},{3,11},{4,12},{5,13},{6,14},{7,15},{8,0},{9,1},... | collective-permute-start | bytes 196616 | tf_op jit(solution)/shard_map/ppermute | solution.py:261
  44.5 14.2 %collective-permute-start.10 = (f32[128,128]{1,0:T(8,128)S(1)}, f32[128,128]{1,0:T(8,128)S(1)}, u32[]{:S(2)}, u32[]{:S(2)}) collective-permute-start(f32[128,128]{1,0:T(8,128)S(1)} %get-tuple-element.39), channel_id=1, source_target_pairs={{0,16},{1,17},{2,18},{3,19},{4,20},{5,21},{6,22},{7,23},{8,24},{9,... | collective-permute-start | bytes 196616 | tf_op jit(solution)/shard_map/ppermute | solution.py:261
  53.8 9.8 %collective-permute-start.7 = (f32[128,256]{1,0:T(8,128)S(1)}, f32[128,256]{1,0:T(8,128)S(1)}, u32[]{:S(2)}, u32[]{:S(2)}) collective-permute-start(f32[128,256]{1,0:T(8,128)S(1)} %get-tuple-element.36.refs_2_), channel_id=1, source_target_pairs={{0,1},{1,0},{2,3},{3,2},{4,5},{5,4},{6,7},{7,6},{8,9},{9,8},{10,11... | collective-permute-start | bytes 393224 | tf_op jit(solution)/shard_map/ppermute | solution.py:261
  53.9 9.7 %collective-permute-start.8 = (f32[128,256]{1,0:T(8,128)S(1)}, f32[128,256]{1,0:T(8,128)S(1)}, u32[]{:S(2)}, u32[]{:S(2)}) collective-permute-start(f32[128,256]{1,0:T(8,128)S(1)} %get-tuple-element.36.refs_2_), channel_id=1, source_target_pairs={{1,2},{2,1},{3,4},{4,3},{5,6},{6,5},{9,10},{10,9},{11,12},{12,11},... | collective-permute-start | bytes 393224 | tf_op jit(solution)/shard_map/ppermute | solution.py:261
  58.7 4.3 %collective-permute-start.11 = (f32[128,128]{1,0:T(8,128)S(1)}, f32[128,128]{1,0:T(8,128)S(1)}, u32[]{:S(2)}, u32[]{:S(2)}) collective-permute-start(f32[128,128]{1,0:T(8,128)S(1)} %sub.10.mine_last), channel_id=1, source_target_pairs={{0,8},{1,9},{2,10},{3,11},{4,12},{5,13},{6,14},{7,15},{8,0},{9,1},... | collective-permute-start | bytes 196616 | tf_op jit(solution)/shard_map/ppermute | solution.py:261
  58.8 17.1 %collective-permute-start.13 = (f32[128,256]{1,0:T(8,128)S(1)}, f32[128,256]{1,0:T(8,128)S(1)}, u32[]{:S(2)}, u32[]{:S(2)}) collective-permute-start(f32[128,256]{1,0:T(8,128)S(1)} %get-tuple-element.36.refs_2_), channel_id=1, source_target_pairs={{0,16},{1,17},{2,18},{3,19},{4,20},{5,21},{6,22},{7,23},{8,24},{9,... | collective-permute-start | bytes 393224 | tf_op jit(solution)/shard_map/ppermute | solution.py:261
  64.6 7.1 %collective-permute-start.9 = (f32[128,128]{1,0:T(8,128)S(1)}, f32[128,128]{1,0:T(8,128)S(1)}, u32[]{:S(2)}, u32[]{:S(2)}) collective-permute-start(f32[128,128]{1,0:T(8,128)S(1)} %get-tuple-element.38.mine.refs_0_), channel_id=1, source_target_pairs={{0,16},{1,17},{2,18},{3,19},{4,20},{5,21},{6,22},{7,23},{8,24},{9,... | collective-permute-start | bytes 196616 | tf_op jit(solution)/shard_map/ppermute | solution.py:261
  65.2 10.6 %collective-permute-start.12 = (f32[128,128]{1,0:T(8,128)S(1)}, f32[128,128]{1,0:T(8,128)S(1)}, u32[]{:S(2)}, u32[]{:S(2)}) collective-permute-start(f32[128,128]{1,0:T(8,128)S(1)} %sub.11.refs_1_), channel_id=1, source_target_pairs={{0,16},{1,17},{2,18},{3,19},{4,20},{5,21},{6,22},{7,23},{8,24},{9,... | collective-permute-start | bytes 196616 | tf_op jit(solution)/shard_map/ppermute | solution.py:261

commit v9 on v7

--- a/solution.py
+++ b/solution.py
@@ -9,7 +9,7 @@
 
 HIGHEST = lax.Precision.HIGHEST
 ROWS = 8
-GROUP = 4
+GROUP = 2
 BOTH = ("leaf", "clusters")
 
 
@@ -57,8 +57,8 @@
                 b = row_of(held, ROWS + j + 1)
                 c = row_of(held, 2 * ROWS + j + 1)
                 det = a * c - b * b
-                inverse = 1.0 / det
-                inverse_a = 1.0 / a
+                inverse = pltpu.reciprocal(det, approx=True)
+                inverse_a = pltpu.reciprocal(a, approx=True)
                 ratio = b * inverse_a
                 pivots = jnp.where(sub == j, a, jnp.where(sub == j + 1, det * inverse_a, pivots))
                 row, next_row = row_of(held, j), row_of(held, j + 1)
@@ -119,7 +119,7 @@
     last[...] = block[:, columns:]
 
 
-def leaf_kernel(rest, handed, probes, far, inverse, sample_coef, probe_coef, scratch):
+def leaf_kernel(rest, handed, probes, far, inverse, coefs, sample_coef, probe_coef, scratch):
     columns = far.shape[1]
     block = rest[...] - handed[...]
     far[...] = block
@@ -128,6 +128,7 @@
     factor = inverse_factor(gram, scratch)
     inverse[...] = factor
     coef = dot(factor, jnp.concatenate([gram, cross], axis=1))
+    coefs[...] = coef
     sample_coef[...] = coef[:, :columns]
     probe_coef[...] = coef[:, columns:]
 
@@ -147,7 +148,7 @@
     return lax.axis_index("leaf") >> level - 1
 
 
-def term_kernel(level, slots, couplings, mine, away, _last, first, last):
+def term_kernel(level, slots, couplings, mine, away, _theirs, _last, first, last):
     node = member_node(level)
     block = coupling_of(slots, couplings, level, node ^ 2)
     outer = (node == 0) | (node == 3)
@@ -194,12 +195,17 @@
     return dot(inverse, dot(mine[0][...], own, 0, 0) + dot(theirs[0][...], sibling, 0, 0))
 
 
-def node_kernel(inverse, *refs):
-    coef = level_coefs(inverse[...], refs[:3], refs[3:6])
-    at = 0
-    for out in refs[6:]:
-        out[...] = coef[:, at : at + out.shape[1]]
-        at += out.shape[1]
+def node_kernel(inverse, mine, mine_probes, theirs, theirs_probes, _last, coefs, first, probe_coef):
+    columns = first.shape[1]
+    coef = level_coefs(inverse[...], (mine, mine_probes), (theirs, theirs_probes))
+    coefs[...] = coef
+    first[...] = coef[:, :columns]
+    probe_coef[...] = coef[:, columns:]
+
+
+def node_last_kernel(inverse, mine, mine_last, theirs, theirs_last, term, last):
+    both = dot(mine[...], mine_last[...], 0, 0) + dot(theirs[...], theirs_last[...], 0, 0)
+    last[...] = dot(inverse[...], both) - term[...]
 
 
 def top_kernel(level, inverse, *refs):
@@ -289,8 +295,9 @@
     )
     handed_last = flat_shift(handed_last, 1)
     scratch = dict(scratch_shapes=[pltpu.VMEM((scratch_rows(columns), columns), jnp.float32)])
-    far, inverse, first, probe_coef = call(
-        leaf_kernel, [tall, square, square, (columns, width)], rest_first, handed, probes,
+    both = (columns, columns + width)
+    far, inverse, coefs, first, probe_coef = call(
+        leaf_kernel, [tall, square, both, square, (columns, width)], rest_first, handed, probes,
         flops=work, **scratch,
     )
     leaf_basis, last = call(
@@ -298,19 +305,24 @@
     )
 
     ancestors = []
+    below = None
     for level in range(1, levels + 1):
         copies = 2 ** (level - 1)
         count = subtree // copies
-        theirs_probe = swapped(probe_coef, copies)
         if count == 4:
+            theirs_coefs = swapped(coefs, copies)
             away = outward(probe_coef, 2 * copies)
             term_first, term_last = call(
                 functools.partial(term_kernel, level), [square, square_last],
-                couplings, probe_coef, away, last, slots=node_slot, specs=[VMEM, VMEM, VMEM, ANY],
+                couplings, probe_coef, away, theirs_coefs, last, slots=node_slot,
+                specs=[VMEM, VMEM, VMEM, ANY, ANY],
             )
             first = first - swapped(term_first, 2 * copies)
+            theirs_first = theirs_coefs[:, :columns] - swapped(term_first, 3 * copies)
+            theirs_probe = theirs_coefs[:, columns:]
             term_last = swapped(term_last, 2 * copies)
         else:
+            theirs_probe = swapped(probe_coef, copies)
             if count == 2:
                 fields = [tree_swapped(probe_coef, odd) for odd in (0, 1)]
             else:
@@ -321,17 +333,26 @@
                 functools.partial(corrected_kernel, level, count == 2), [square, square_last],
                 couplings, *fields, first, slots=node_slot,
             )
-        last = last - term_last
-        mine = first, last, probe_coef
-        theirs = swapped(first, copies), swapped(last, copies), theirs_probe
-        (inverse,) = call(factor_kernel, [square], mine[0], theirs[0], **scratch)
+            theirs_first = swapped(first, copies)
+        if below is None:
+            last = last - term_last
+        else:
+            (last,) = call(node_last_kernel, [square_last], *below, term_last)
+        theirs_last = swapped(last, copies)
+        mine, theirs = (first, last, probe_coef), (theirs_first, theirs_last, theirs_probe)
+        (inverse,) = call(
+            factor_kernel, [square], first, theirs_first, flops=8 * work if count == 4 else 0, **scratch
+        )
         if level < levels:
             ancestors += call(
                 functools.partial(basis_kernel, level), [(1, 1, 2 * columns, columns)],
-                inverse, mine[0], theirs[0],
+                inverse, first, theirs_first,
             )
-            first, last, probe_coef = call(
-                node_kernel, [square, square_last, (columns, width)], inverse, *mine, *theirs
+            below = inverse, first, last, theirs_first, theirs_last
+            coefs, first, probe_coef = call(
+                node_kernel, [both, square, (columns, width)],
+                inverse, first, probe_coef, theirs_first, theirs_probe, last,
+                specs=[VMEM] * 5 + [ANY],
             )
     transfer_bases, top_samples, top_probes = call(
         functools.partial(top_kernel, levels),

time: 78.6 us -> 79.3 us (level)
  the two profiles are of different devices: /device:TPU:0 before, /device:TPU:4 now
where the time goes in v9:
time: 79.3 us; the launch traced here: 79 us
  starting transfers between devices  30.3 us (38%)
  Pallas kernels  25.2 us (32%)
  waiting for transfers between devices  19.9 us (25%)
  local copies, waits for them, and re-layouts  2.66 us (3%)
  between operations  0.87 us (1%)
    ppermute x14, starting transfers between devices, permuted(): return lax.ppermute(value, BOTH, pairs)  30.3 us
    pallas_call x13, Pallas kernels, call(): pl.pallas_call(kernel, out_shape=outs, in_specs=specs, out_specs=out_spec...  25.2 us
    ppermute x14, waiting for transfers between devices, permuted(): return lax.ppermute(value, BOTH, pairs)  19.9 us
    unnamed x12, local copies, waits for them, and re-layouts  2.65 us
  transfers between devices with their start and end apart: 14, of which 6 were waited for; matrix products, arithmetic and copies ran while one was open for 0% of the time, Pallas kernels for 26%

profile of v9, /device:TPU:4, one launch (start us, length us, event | category | flops | bytes accessed | tf_op | source)
XLA Modules:
  0.0 79.0 jit_solution(13687263758464710149)
XLA Ops:
  0.6 5.8 %collective-permute-start = (f32[512,256]{1,0:T(8,128)}, f32[512,256]{1,0:T(8,128)S(1)}, u32[]{:S(2)}, u32[]{:S(2)}) collective-permute-start(f32[512,256]{1,0:T(8,128)} %probes.5), channel_id=1, source_target_pairs={{1,24},{2,25},{3,26},{4,27},{5,28},{6,29},{7,30},{8,0},{9,1},{10,2... | collective-permute-start | bytes 1572872 | tf_op jit(solution)/shard_map/ppermute | solution.py:255
  6.5 1.6 %copy-done = f32[512,2,512]{2,1,0:T(2,128)S(1)} copy-done((f32[512,2,512]{2,1,0:T(2,128)S(1)}, f32[512,2,512]{2,1,0:T(2,128)}, u32[]{:S(2)}) %copy-start) | copy-done | bytes 2097176
  10.0 1.9 %collective-permute-start.2 = (f32[512,128]{1,0:T(8,128)S(1)}, f32[512,128]{1,0:T(8,128)S(1)}, u32[]{:S(2)}, u32[]{:S(2)}) collective-permute-start(f32[512,128]{1,0:T(8,128)S(1)} %shard_map.86), channel_id=1, source_target_pairs={{0,8},{1,9},{2,10},{3,11},{4,12},{5,13},{6,14},{7,15},{8,16},{9,17... | collective-permute-start | bytes 786440 | tf_op jit(solution)/shard_map/ppermute | solution.py:255
  11.9 1.6 %shard_map.84 = (f32[512,256]{1,0:T(8,128)S(1)}, f32[512,128]{1,0:T(8,128)S(1)}) custom-call(f32[4096,128]{1,0:T(8,128)S(1)} %bitcast.6, f32[512,256]{1,0:T(8,128)S(1)} %copy-done.3, f32[512,256]{1,0:T(8,128)S(1)} %copy-done.2), custom_call_target="tpu_custom_call" | custom-call | flops 805306368 | bytes 3932160 | tf_op jit(solution)/shard_map/pallas_call | solution.py:236
  13.6 5.5 %collective-permute-done.following = f32[512,256]{1,0:T(8,128)S(1)} collective-permute-done((f32[512,256]{1,0:T(8,128)}, f32[512,256]{1,0:T(8,128)S(1)}, u32[]{:S(2)}, u32[]{:S(2)}) %collective-permute-start) | collective-permute-done | bytes 524320 | tf_op jit(solution)/shard_map/ppermute | solution.py:255
  19.1 1.2 %shard_map.85 = (f32[512,128]{1,0:T(8,128)S(1)}, f32[512,128]{1,0:T(8,128)S(1)}, f32[512,128]{1,0:T(8,128)S(1)}) custom-call(f32[4096,128]{1,0:T(8,128)S(1)} %bitcast.7, f32[512,256]{1,0:T(8,128)S(1)} %get-tuple-element.25.rest, f32[512,256]{1,0:T(8,128)S(1)} %collective-permute-done.following, ...), custom_call_target="tpu_custom_call", output_to_operand_aliasing={{2}: (3, {})} | custom-call | flops 805306368 | bytes 4194304 | tf_op jit(solution)/shard_map/pallas_call | solution.py:236
  20.3 1.9 %collective-permute-start.1 = (f32[512,128]{1,0:T(8,128)S(1)}, f32[512,128]{1,0:T(8,128)S(1)}, u32[]{:S(2)}, u32[]{:S(2)}) collective-permute-start(f32[512,128]{1,0:T(8,128)S(1)} %get-tuple-element.28), channel_id=1, source_target_pairs={{0,8},{1,9},{2,10},{3,11},{4,12},{5,13},{6,14},{7,15},{8,16},{9,17... | collective-permute-start | bytes 786440 | tf_op jit(solution)/shard_map/ppermute | solution.py:255
  22.2 2.4 %collective-permute-done.2.handed = f32[512,128]{1,0:T(8,128)S(1)} collective-permute-done((f32[512,128]{1,0:T(8,128)S(1)}, f32[512,128]{1,0:T(8,128)S(1)}, u32[]{:S(2)}, u32[]{:S(2)}) %collective-permute-start.2) | collective-permute-done | bytes 262176 | tf_op jit(solution)/shard_map/ppermute | solution.py:255
  24.6 4.8 %shard_map.87 = (f32[512,128]{1,0:T(8,128)S(1)}, f32[128,128]{1,0:T(8,128)S(1)}, f32[128,384]{1,0:T(8,128)S(1)}, f32[128,128]{1,0:T(8,128)S(1)}, f32[128,256]{1,0:T(8,128)S(1)}) custom-call(f32[512,128]{1,0:T(8,128)S(1)} %get-tuple-element.29.rest, f32[512,128]{1,0:T(8,128)S(1)} %collective-permute-done.2.handed, f32[512,256]{1,0:T(8,128)S(1)} %copy-done.4), custom_call_target="tpu_custom_call" | custom-call | flops 805306368 | bytes 1769472 | tf_op jit(solution)/shard_map/pallas_call | solution.py:236
  29.5 2.6 %collective-permute-start.4 = (f32[128,384]{1,0:T(8,128)S(1)}, f32[128,384]{1,0:T(8,128)S(1)}, u32[]{:S(2)}, u32[]{:S(2)}) collective-permute-start(f32[128,384]{1,0:T(8,128)S(1)} %get-tuple-element.35), channel_id=1, source_target_pairs={{0,8},{1,9},{2,10},{3,11},{4,12},{5,13},{6,14},{7,15},{8,0},{9,1},... | collective-permute-start | bytes 589832 | tf_op jit(solution)/shard_map/ppermute | solution.py:255
  32.0 1.9 %collective-permute-start.3 = (f32[128,256]{1,0:T(8,128)S(1)}, f32[128,256]{1,0:T(8,128)S(1)}, u32[]{:S(2)}, u32[]{:S(2)}) collective-permute-start(f32[128,256]{1,0:T(8,128)S(1)} %get-tuple-element.34.mine.mine_probes), channel_id=1, source_target_pairs={{1,0},{2,1},{3,2},{4,3},{5,4},{6,5},{7,6},{9,8},{10,9},{11,10},{12... | collective-permute-start | bytes 393224 | tf_op jit(solution)/shard_map/ppermute | solution.py:255
  33.9 1.5 %shard_map.88 = (f32[512,128]{1,0:T(8,128)}, f32[128,128]{1,0:T(8,128)S(1)}) custom-call(f32[512,128]{1,0:T(8,128)S(1)} %get-tuple-element.27.rest, f32[512,128]{1,0:T(8,128)S(1)} %collective-permute-done.1.handed, f32[512,128]{1,0:T(8,128)S(1)} %get-tuple-element.30.far, f32[128,128]{1,0:T(8,128)S(1)} %get-tuple-element.31.inverse), custom_call_target="tpu_custom_call" | custom-call | flops 805306368 | bytes 1179648 | tf_op jit(solution)/shard_map/pallas_call | solution.py:236
  37.4 4.4 %collective-permute-start.6 = (f32[128,128]{1,0:T(8,128)S(1)}, f32[128,128]{1,0:T(8,128)S(1)}, u32[]{:S(2)}, u32[]{:S(2)}) collective-permute-start(f32[128,128]{1,0:T(8,128)S(1)} %get-tuple-element.37), channel_id=1, source_target_pairs={{0,24},{1,25},{2,26},{3,27},{4,28},{5,29},{6,30},{7,31},{8,16},{9,... | collective-permute-start | bytes 196616 | tf_op jit(solution)/shard_map/ppermute | solution.py:255
  41.9 2.9 %collective-permute-start.7 = (f32[128,128]{1,0:T(8,128)S(1)}, f32[128,128]{1,0:T(8,128)S(1)}, u32[]{:S(2)}, u32[]{:S(2)}) collective-permute-start(f32[128,128]{1,0:T(8,128)S(1)} %get-tuple-element.38), channel_id=1, source_target_pairs={{0,16},{1,17},{2,18},{3,19},{4,20},{5,21},{6,22},{7,23},{8,24},{9,... | collective-permute-start | bytes 196616 | tf_op jit(solution)/shard_map/ppermute | solution.py:255
  44.8 4.9 %collective-permute-done.5 = f32[128,128]{1,0:T(8,128)S(1)} collective-permute-done((f32[128,128]{1,0:T(8,128)S(1)}, f32[128,128]{1,0:T(8,128)S(1)}, u32[]{:S(2)}, u32[]{:S(2)}) %collective-permute-start.5) | collective-permute-done | bytes 65568 | tf_op jit(solution)/shard_map/ppermute | solution.py:255
  49.7 4.4 %shard_map.90.inverse = f32[128,128]{1,0:T(8,128)S(1)} custom-call(f32[128,128]{1,0:T(8,128)S(1)} %sub.9.mine, f32[128,128]{1,0:T(8,128)S(1)} %slice_subtract_fusion.theirs), custom_call_target="tpu_custom_call" | custom-call | flops 6442450944 | bytes 196608 | tf_op jit(solution)/shard_map/pallas_call | solution.py:236
  54.2 1.6 %shard_map.91 = (f32[128,384]{1,0:T(8,128)}, f32[128,128]{1,0:T(8,128)S(1)}, f32[128,256]{1,0:T(8,128)S(1)}) custom-call(f32[128,128]{1,0:T(8,128)S(1)} %shard_map.90.inverse, f32[128,128]{1,0:T(8,128)S(1)} %sub.9.mine, f32[128,256]{1,0:T(8,128)S(1)} %get-tuple-element.34.mine.mine_probes, f32[128,128]{1,0:T(8,128)S(1)} %slice_subtract_fusion.theirs, ...), custom_call_target="tpu_custom_call" | custom-call | bytes 917504 | tf_op jit(solution)/shard_map/pallas_call | solution.py:236
  55.8 3.0 %collective-permute-start.9 = (f32[128,256]{1,0:T(8,128)S(1)}, f32[128,256]{1,0:T(8,128)S(1)}, u32[]{:S(2)}, u32[]{:S(2)}) collective-permute-start(f32[128,256]{1,0:T(8,128)S(1)} %get-tuple-element.39.refs_2_), channel_id=1, source_target_pairs={{1,2},{2,1},{3,4},{4,3},{5,6},{6,5},{9,10},{10,9},{11,12},{12,11},... | collective-permute-start | bytes 393224 | tf_op jit(solution)/shard_map/ppermute | solution.py:255
  58.8 2.8 %collective-permute-start.13 = (f32[128,256]{1,0:T(8,128)S(1)}, f32[128,256]{1,0:T(8,128)S(1)}, u32[]{:S(2)}, u32[]{:S(2)}) collective-permute-start(f32[128,256]{1,0:T(8,128)S(1)} %get-tuple-element.39.refs_2_), channel_id=1, source_target_pairs={{0,16},{1,17},{2,18},{3,19},{4,20},{5,21},{6,22},{7,23},{8,24},{9,... | collective-permute-start | bytes 393224 | tf_op jit(solution)/shard_map/ppermute | solution.py:255
  61.6 1.4 %collective-permute-done.9.two = f32[128,256]{1,0:T(8,128)S(1)} collective-permute-done((f32[128,256]{1,0:T(8,128)S(1)}, f32[128,256]{1,0:T(8,128)S(1)}, u32[]{:S(2)}, u32[]{:S(2)}) %collective-permute-start.9) | collective-permute-done | bytes 131104 | tf_op jit(solution)/shard_map/ppermute | solution.py:255
  64.6 3.0 %collective-permute-start.12 = (f32[128,128]{1,0:T(8,128)S(1)}, f32[128,128]{1,0:T(8,128)S(1)}, u32[]{:S(2)}, u32[]{:S(2)}) collective-permute-start(f32[128,128]{1,0:T(8,128)S(1)} %shard_map.94.refs_1_), channel_id=1, source_target_pairs={{0,16},{1,17},{2,18},{3,19},{4,20},{5,21},{6,22},{7,23},{8,24},{9,... | collective-permute-start | bytes 196616 | tf_op jit(solution)/shard_map/ppermute | solution.py:255
  68.0 4.6 %collective-permute-done.10.theirs.refs_3_ = f32[128,128]{1,0:T(8,128)S(1)} collective-permute-done((f32[128,128]{1,0:T(8,128)S(1)}, f32[128,128]{1,0:T(8,128)S(1)}, u32[]{:S(2)}, u32[]{:S(2)}) %collective-permute-start.10) | collective-permute-done | bytes 65568 | tf_op jit(solution)/shard_map/ppermute | solution.py:255
  72.6 4.4 %shard_map.93.inverse = f32[128,128]{1,0:T(8,128)S(1)} custom-call(f32[128,128]{1,0:T(8,128)S(1)} %get-tuple-element.41.mine.refs_0_, f32[128,128]{1,0:T(8,128)S(1)} %collective-permute-done.10.theirs.refs_3_), custom_call_target="tpu_custom_call" | custom-call | bytes 196608 | tf_op jit(solution)/shard_map/pallas_call | solution.py:236
  77.1 1.9 %shard_map.96 = (f32[1,2,256,128]{3,2,1,0:T(8,128)}, f32[1,128,256]{2,1,0:T(8,128)}, f32[1,128,256]{2,1,0:T(8,128)}) custom-call(f32[128,128]{1,0:T(8,128)S(1)} %shard_map.93.inverse, f32[128,128]{1,0:T(8,128)S(1)} %get-tuple-element.41.mine.refs_0_, f32[128,128]{1,0:T(8,128)S(1)} %shard_map.94.refs_1_, f32[128,256]{1,0:T(8,128)S(1)} %get-tuple-element.39.refs_2_, ...), custom_call_target="tpu_custom_call" | custom-call | bytes 1245184 | tf_op jit(solution)/shard_map/pallas_call | solution.py:236
  (33 shorter events, 6.1 us)
Async XLA Ops:
  0.6 18.5 %collective-permute-start = (f32[512,256]{1,0:T(8,128)}, f32[512,256]{1,0:T(8,128)S(1)}, u32[]{:S(2)}, u32[]{:S(2)}) collective-permute-start(f32[512,256]{1,0:T(8,128)} %probes.5), channel_id=1, source_target_pairs={{1,24},{2,25},{3,26},{4,27},{5,28},{6,29},{7,30},{8,0},{9,1},{10,2... | collective-permute-start | bytes 1572872 | tf_op jit(solution)/shard_map/ppermute | solution.py:255
  6.5 1.6 %copy-start = (f32[512,2,512]{2,1,0:T(2,128)S(1)}, f32[512,2,512]{2,1,0:T(2,128)}, u32[]{:S(2)}) copy-start(f32[512,2,512]{2,1,0:T(2,128)} %param.7) | copy-start | bytes 6291460
  8.1 1.0 %copy-start.3 = (f32[512,256]{1,0:T(8,128)S(1)}, f32[512,256]{1,0:T(8,128)}, u32[]{:S(2)}) copy-start(f32[512,256]{1,0:T(8,128)} %probes.5) | copy-start | bytes 1572868
  9.1 2.8 %copy-start.2 = (f32[512,256]{1,0:T(8,128)S(1)}, f32[512,256]{1,0:T(8,128)}, u32[]{:S(2)}) copy-start(f32[512,256]{1,0:T(8,128)} %samples.1) | copy-start | bytes 1572868
  10.0 14.6 %collective-permute-start.2 = (f32[512,128]{1,0:T(8,128)S(1)}, f32[512,128]{1,0:T(8,128)S(1)}, u32[]{:S(2)}, u32[]{:S(2)}) collective-permute-start(f32[512,128]{1,0:T(8,128)S(1)} %shard_map.86), channel_id=1, source_target_pairs={{0,8},{1,9},{2,10},{3,11},{4,12},{5,13},{6,14},{7,15},{8,16},{9,17... | collective-permute-start | bytes 786440 | tf_op jit(solution)/shard_map/ppermute | solution.py:255
  13.6 11.1 %copy-start.4 = (f32[512,256]{1,0:T(8,128)S(1)}, f32[512,256]{1,0:T(8,128)}, u32[]{:S(2)}) copy-start(f32[512,256]{1,0:T(8,128)} %probes.5) | copy-start | bytes 1572868
  20.3 13.7 %collective-permute-start.1 = (f32[512,128]{1,0:T(8,128)S(1)}, f32[512,128]{1,0:T(8,128)S(1)}, u32[]{:S(2)}, u32[]{:S(2)}) collective-permute-start(f32[512,128]{1,0:T(8,128)S(1)} %get-tuple-element.28), channel_id=1, source_target_pairs={{0,8},{1,9},{2,10},{3,11},{4,12},{5,13},{6,14},{7,15},{8,16},{9,17... | collective-permute-start | bytes 786440 | tf_op jit(solution)/shard_map/ppermute | solution.py:255
  29.4 7.0 %copy-start.1 = (f32[1,3,2,128,128]{4,3,2,1,0:T(8,128)S(1)}, f32[1,3,2,128,128]{4,3,2,1,0:T(8,128)}, u32[]{:S(2)}) copy-start(f32[1,3,2,128,128]{4,3,2,1,0:T(8,128)} %couplings.3) | copy-start | bytes 1179652
  29.5 7.0 %copy-start.5 = (s32[1,3]{1,0:T(1,128)S(1)}, s32[1,3]{1,0:T(1,128)}, u32[]{:S(2)}) copy-start(s32[1,3]{1,0:T(1,128)} %slots.3) | copy-start | bytes 40
  29.5 7.0 %collective-permute-start.4 = (f32[128,384]{1,0:T(8,128)S(1)}, f32[128,384]{1,0:T(8,128)S(1)}, u32[]{:S(2)}, u32[]{:S(2)}) collective-permute-start(f32[128,384]{1,0:T(8,128)S(1)} %get-tuple-element.35), channel_id=1, source_target_pairs={{0,8},{1,9},{2,10},{3,11},{4,12},{5,13},{6,14},{7,15},{8,0},{9,1},... | collective-permute-start | bytes 589832 | tf_op jit(solution)/shard_map/ppermute | solution.py:255
  32.0 4.4 %collective-permute-start.3 = (f32[128,256]{1,0:T(8,128)S(1)}, f32[128,256]{1,0:T(8,128)S(1)}, u32[]{:S(2)}, u32[]{:S(2)}) collective-permute-start(f32[128,256]{1,0:T(8,128)S(1)} %get-tuple-element.34.mine.mine_probes), channel_id=1, source_target_pairs={{1,0},{2,1},{3,2},{4,3},{5,4},{6,5},{7,6},{9,8},{10,9},{11,10},{12... | collective-permute-start | bytes 393224 | tf_op jit(solution)/shard_map/ppermute | solution.py:255
  37.4 7.4 %collective-permute-start.6 = (f32[128,128]{1,0:T(8,128)S(1)}, f32[128,128]{1,0:T(8,128)S(1)}, u32[]{:S(2)}, u32[]{:S(2)}) collective-permute-start(f32[128,128]{1,0:T(8,128)S(1)} %get-tuple-element.37), channel_id=1, source_target_pairs={{0,24},{1,25},{2,26},{3,27},{4,28},{5,29},{6,30},{7,31},{8,16},{9,... | collective-permute-start | bytes 196616 | tf_op jit(solution)/shard_map/ppermute | solution.py:255
  41.8 7.9 %collective-permute-start.5 = (f32[128,128]{1,0:T(8,128)S(1)}, f32[128,128]{1,0:T(8,128)S(1)}, u32[]{:S(2)}, u32[]{:S(2)}) collective-permute-start(f32[128,128]{1,0:T(8,128)S(1)} %get-tuple-element.37), channel_id=1, source_target_pairs={{0,16},{1,17},{2,18},{3,19},{4,20},{5,21},{6,22},{7,23},{8,24},{9,... | collective-permute-start | bytes 196616 | tf_op jit(solution)/shard_map/ppermute | solution.py:255
  41.9 12.3 %collective-permute-start.7 = (f32[128,128]{1,0:T(8,128)S(1)}, f32[128,128]{1,0:T(8,128)S(1)}, u32[]{:S(2)}, u32[]{:S(2)}) collective-permute-start(f32[128,128]{1,0:T(8,128)S(1)} %get-tuple-element.38), channel_id=1, source_target_pairs={{0,16},{1,17},{2,18},{3,19},{4,20},{5,21},{6,22},{7,23},{8,24},{9,... | collective-permute-start | bytes 196616 | tf_op jit(solution)/shard_map/ppermute | solution.py:255
  55.8 5.8 %collective-permute-start.8 = (f32[128,256]{1,0:T(8,128)S(1)}, f32[128,256]{1,0:T(8,128)S(1)}, u32[]{:S(2)}, u32[]{:S(2)}) collective-permute-start(f32[128,256]{1,0:T(8,128)S(1)} %get-tuple-element.39.refs_2_), channel_id=1, source_target_pairs={{0,1},{1,0},{2,3},{3,2},{4,5},{5,4},{6,7},{7,6},{8,9},{9,8},{10,11... | collective-permute-start | bytes 393224 | tf_op jit(solution)/shard_map/ppermute | solution.py:255
  55.8 7.2 %collective-permute-start.9 = (f32[128,256]{1,0:T(8,128)S(1)}, f32[128,256]{1,0:T(8,128)S(1)}, u32[]{:S(2)}, u32[]{:S(2)}) collective-permute-start(f32[128,256]{1,0:T(8,128)S(1)} %get-tuple-element.39.refs_2_), channel_id=1, source_target_pairs={{1,2},{2,1},{3,4},{4,3},{5,6},{6,5},{9,10},{10,9},{11,12},{12,11},... | collective-permute-start | bytes 393224 | tf_op jit(solution)/shard_map/ppermute | solution.py:255
  58.8 5.2 %collective-permute-start.11 = (f32[128,128]{1,0:T(8,128)S(1)}, f32[128,128]{1,0:T(8,128)S(1)}, u32[]{:S(2)}, u32[]{:S(2)}) collective-permute-start(f32[128,128]{1,0:T(8,128)S(1)} %sub.11._last.mine_last), channel_id=1, source_target_pairs={{0,8},{1,9},{2,10},{3,11},{4,12},{5,13},{6,14},{7,15},{8,0},{9,1},... | collective-permute-start | bytes 196616 | tf_op jit(solution)/shard_map/ppermute | solution.py:255
  58.8 18.2 %collective-permute-start.13 = (f32[128,256]{1,0:T(8,128)S(1)}, f32[128,256]{1,0:T(8,128)S(1)}, u32[]{:S(2)}, u32[]{:S(2)}) collective-permute-start(f32[128,256]{1,0:T(8,128)S(1)} %get-tuple-element.39.refs_2_), channel_id=1, source_target_pairs={{0,16},{1,17},{2,18},{3,19},{4,20},{5,21},{6,22},{7,23},{8,24},{9,... | collective-permute-start | bytes 393224 | tf_op jit(solution)/shard_map/ppermute | solution.py:255
  63.9 8.7 %collective-permute-start.10 = (f32[128,128]{1,0:T(8,128)S(1)}, f32[128,128]{1,0:T(8,128)S(1)}, u32[]{:S(2)}, u32[]{:S(2)}) collective-permute-start(f32[128,128]{1,0:T(8,128)S(1)} %get-tuple-element.41.mine.refs_0_), channel_id=1, source_target_pairs={{0,16},{1,17},{2,18},{3,19},{4,20},{5,21},{6,22},{7,23},{8,24},{9,... | collective-permute-start | bytes 196616 | tf_op jit(solution)/shard_map/ppermute | solution.py:255
  64.6 12.5 %collective-permute-start.12 = (f32[128,128]{1,0:T(8,128)S(1)}, f32[128,128]{1,0:T(8,128)S(1)}, u32[]{:S(2)}, u32[]{:S(2)}) collective-permute-start(f32[128,128]{1,0:T(8,128)S(1)} %shard_map.94.refs_1_), channel_id=1, source_target_pairs={{0,16},{1,17},{2,18},{3,19},{4,20},{5,21},{6,22},{7,23},{8,24},{9,... | collective-permute-start | bytes 196616 | tf_op jit(solution)/shard_map/ppermute | solution.py:255

commit v10 on v9

--- a/solution.py
+++ b/solution.py
@@ -9,7 +9,7 @@
 
 HIGHEST = lax.Precision.HIGHEST
 ROWS = 8
-GROUP = 2
+GROUP = 4
 BOTH = ("leaf", "clusters")
 
 
@@ -35,57 +35,82 @@
     rows = [gram[ROWS * i : ROWS * (i + 1), :] for i in range(blocks)]
     scaled = [None] * blocks
     used = 0
+
+    def pair_of(k, j):
+        return (lane == ROWS * k + j) | (lane == ROWS * k + j + 1)
+
+    def columns_of(tile, k):
+        return [across_lanes(tile, ROWS * k + n) for n in range(ROWS)]
+
+    def factors(cols, j, step):
+        a, b, c, inverse = step[:4]
+        u, v = cols[j], cols[j + 1]
+        return (u * c - v * b) * inverse, (v * a - u * b) * inverse
+
+    def eliminated(tile, cols, j, f, g, step):
+        row, next_row, col_rows = step[4:]
+        for n, (x, y) in enumerate(col_rows, j + 2):
+            cols[n] = cols[n] - (f * x + g * y)
+        return tile - (f * row + g * next_row)
+
+    def diagonal(k):
+        nonlocal used
+        tile, cols, steps = rows[k], columns_of(rows[k], k), []
+        pivots = jnp.ones((ROWS, size), jnp.float32)
+        for j in range(0, ROWS, 2):
+            tile = jnp.where(pair_of(k, j), jnp.where(lane == sub + ROWS * k, 1.0, 0.0), tile)
+            held = scratch.at[pl.ds(used, ROWS * (ROWS - j + 1)), :]
+            used += ROWS * (ROWS - j + 1)
+            for n in range(j, ROWS):
+                held[pl.ds(ROWS * (n - j + 1), ROWS), :] = cols[n]
+            held[pl.ds(0, ROWS), :] = tile
+            a = row_of(held, ROWS + j)
+            b = row_of(held, ROWS + j + 1)
+            c = row_of(held, 2 * ROWS + j + 1)
+            det = a * c - b * b
+            inverse = pltpu.reciprocal(det, approx=True)
+            inverse_a = pltpu.reciprocal(a, approx=True)
+            pivots = jnp.where(sub == j, a, jnp.where(sub == j + 1, det * inverse_a, pivots))
+            col_rows = [
+                (row_of(held, ROWS * (n - j + 1) + j), row_of(held, ROWS * (n - j + 1) + j + 1))
+                for n in range(j + 2, ROWS)
+            ]
+            step = a, b, c, inverse, row_of(held, j), row_of(held, j + 1), col_rows
+            steps.append(step)
+            f, g = factors(cols, j, step)
+            f = jnp.where(sub > j + 1, f, jnp.where(sub == j + 1, b * inverse_a, 0.0))
+            g = jnp.where(sub > j + 1, g, 0.0)
+            tile = eliminated(tile, cols, j, f, g, step)
+        rows[k] = tile
+        return steps, pivots
+
+    def below(i, k, steps):
+        tile, cols = rows[i], columns_of(rows[i], k)
+        for j, step in zip(range(0, ROWS, 2), steps):
+            f, g = factors(cols, j, step)
+            tile = eliminated(jnp.where(pair_of(k, j), 0.0, tile), cols, j, f, g, step)
+        rows[i] = tile
+
+    waiting = None
     for first in range(0, blocks, GROUP):
         last = first + GROUP
         ahead = min(last + 1, blocks)
         for k in range(first, last):
-            cols = {
-                i: [across_lanes(rows[i], ROWS * k + c) for c in range(ROWS)] for i in range(k, ahead)
-            }
-            pivots = jnp.ones((ROWS, size), jnp.float32)
-            for j in range(0, ROWS, 2):
-                pair = (lane == ROWS * k + j) | (lane == ROWS * k + j + 1)
-                for i in range(k, ahead):
-                    rows[i] = jnp.where(pair, 0.0, rows[i])
-                rows[k] = jnp.where(pair & (lane == sub + ROWS * k), 1.0, rows[k])
-                held = scratch.at[pl.ds(used, ROWS * (ROWS - j + 1)), :]
-                used += ROWS * (ROWS - j + 1)
-                held[pl.ds(0, ROWS), :] = rows[k]
-                for n in range(j, ROWS):
-                    held[pl.ds(ROWS * (n - j + 1), ROWS), :] = cols[k][n]
-                a = row_of(held, ROWS + j)
-                b = row_of(held, ROWS + j + 1)
-                c = row_of(held, 2 * ROWS + j + 1)
-                det = a * c - b * b
-                inverse = pltpu.reciprocal(det, approx=True)
-                inverse_a = pltpu.reciprocal(a, approx=True)
-                ratio = b * inverse_a
-                pivots = jnp.where(sub == j, a, jnp.where(sub == j + 1, det * inverse_a, pivots))
-                row, next_row = row_of(held, j), row_of(held, j + 1)
-                col_rows = [
-                    (row_of(held, ROWS * (n - j + 1) + j), row_of(held, ROWS * (n - j + 1) + j + 1))
-                    for n in range(j + 2, ROWS)
-                ]
-                for i in range(k, ahead):
-                    u, v = cols[i][j], cols[i][j + 1]
-                    f = (u * c - v * b) * inverse
-                    g = (v * a - u * b) * inverse
-                    if i == k:
-                        f = jnp.where(sub > j + 1, f, jnp.where(sub == j + 1, ratio, 0.0))
-                        g = jnp.where(sub > j + 1, g, 0.0)
-                    for n in range(j + 2, ROWS):
-                        x, y = col_rows[n - j - 2]
-                        cols[i][n] = cols[i][n] - (f * x + g * y)
-                    rows[i] = rows[i] - (f * row + g * next_row)
+            steps, pivots = diagonal(k)
+            if waiting is not None:
+                done, start, stop = waiting
+                change = dot(done.T[ROWS * (stop + 1) :, :], done)
+                old = (lane >= ROWS * start) & (lane < ROWS * stop)
+                for i in range(stop + 1, blocks):
+                    piece = change[ROWS * (i - stop - 1) : ROWS * (i - stop), :]
+                    rows[i] = jnp.where(old, 0.0, rows[i]) - piece
+                waiting = None
+            for i in range(k + 1, ahead):
+                below(i, k, steps)
             kept = (lane <= sub + ROWS * k) | (lane >= ROWS * last)
             scaled[k] = jnp.where(kept, rows[k] * lax.rsqrt(pivots), 0.0)
         if ahead < blocks:
-            done = jnp.concatenate(scaled[first:last], axis=0)
-            change = dot(done.T[ROWS * ahead :, :], done)
-            old = (lane >= ROWS * first) & (lane < ROWS * last)
-            for i in range(ahead, blocks):
-                piece = change[ROWS * (i - ahead) : ROWS * (i - ahead + 1), :]
-                rows[i] = jnp.where(old, 0.0, rows[i]) - piece
+            waiting = jnp.concatenate(scaled[first:last], axis=0), first, last
     return jnp.concatenate(
         [jnp.where(lane <= sub + ROWS * k, scaled[k], 0.0) for k in range(blocks)], axis=0
     )
@@ -119,7 +144,7 @@
     last[...] = block[:, columns:]
 
 
-def leaf_kernel(rest, handed, probes, far, inverse, coefs, sample_coef, probe_coef, scratch):
+def leaf_kernel(rest, handed, probes, far, inverse, sample_coef, probe_coef, scratch):
     columns = far.shape[1]
     block = rest[...] - handed[...]
     far[...] = block
@@ -128,7 +153,6 @@
     factor = inverse_factor(gram, scratch)
     inverse[...] = factor
     coef = dot(factor, jnp.concatenate([gram, cross], axis=1))
-    coefs[...] = coef
     sample_coef[...] = coef[:, :columns]
     probe_coef[...] = coef[:, columns:]
 
@@ -148,18 +172,19 @@
     return lax.axis_index("leaf") >> level - 1
 
 
-def term_kernel(level, slots, couplings, mine, away, _theirs, _last, first, last):
+def term_kernel(level, slots, couplings, mine, away, _last, first, last):
     node = member_node(level)
     block = coupling_of(slots, couplings, level, node ^ 2)
     outer = (node == 0) | (node == 3)
     main = jnp.where(outer, mine[...], away[...])
     other = jnp.where(outer, away[...], mine[...])
-    term = dot(block, main) + dot(block, other, 0, 0)
+    term = dot(jnp.concatenate([block, block.T], axis=1), jnp.concatenate([main, other], axis=0))
     first[...] = term[:, : first.shape[1]]
     last[...] = term[:, first.shape[1] :]
 
 
-def corrected_kernel(level, trees, slots, couplings, one, two, first, out_first, out_last):
+def corrected_kernel(level, trees, slots, couplings, one, two, first, *outs):
+    out_first, out_last = outs[-3:-1] if trees else outs
     columns = first.shape[1]
     node = member_node(level)
     block = coupling_of(slots, couplings, level, node)
@@ -167,13 +192,14 @@
     if trees:
         straight = (lax.axis_index("clusters") ^ node) & 1 == 1
         main, other = jnp.where(straight, main, other), jnp.where(straight, other, main)
-    term = dot(block, main) + dot(block, other, 0, 0)
+    term = dot(jnp.concatenate([block, block.T], axis=1), jnp.concatenate([main, other], axis=0))
     out_first[...] = first[...] - term[:, :columns]
     out_last[...] = term[:, columns:]
 
 
 def factor_kernel(mine, theirs, inverse, scratch):
-    gram = dot(mine[...], mine[...], 0, 0) + dot(theirs[...], theirs[...], 0, 0)
+    both = jnp.concatenate([mine[...], theirs[...]], axis=0)
+    gram = dot(both, both, 0, 0)
     inverse[...] = inverse_factor(gram, scratch)
 
 
@@ -190,34 +216,43 @@
 
 
 def level_coefs(inverse, mine, theirs):
-    own = jnp.concatenate([ref[...] for ref in mine], axis=1)
-    sibling = jnp.concatenate([ref[...] for ref in theirs], axis=1)
-    return dot(inverse, dot(mine[0][...], own, 0, 0) + dot(theirs[0][...], sibling, 0, 0))
-
-
-def node_kernel(inverse, mine, mine_probes, theirs, theirs_probes, _last, coefs, first, probe_coef):
+    own = jnp.concatenate(mine, axis=1)
+    sibling = jnp.concatenate(theirs, axis=1)
+    size = inverse.shape[0]
+    both = jnp.concatenate([own, sibling], axis=0)
+    return dot(inverse, dot(both[:, :size], both, 0, 0))
+
+
+def node_kernel(inverse, mine, mine_probes, theirs, theirs_probes, _last, first, probe_coef, half):
     columns = first.shape[1]
-    coef = level_coefs(inverse[...], (mine, mine_probes), (theirs, theirs_probes))
-    coefs[...] = coef
+    coef = level_coefs(inverse[...], (mine[...], mine_probes[...]), (theirs[...], theirs_probes[...]))
     first[...] = coef[:, :columns]
     probe_coef[...] = coef[:, columns:]
+    width = half.shape[1]
+    upper = lax.axis_index("leaf") & 1 == 1
+    half[...] = jnp.where(upper, coef[:, columns + width :], coef[:, columns : columns + width])
 
 
 def node_last_kernel(inverse, mine, mine_last, theirs, theirs_last, term, last):
-    both = dot(mine[...], mine_last[...], 0, 0) + dot(theirs[...], theirs_last[...], 0, 0)
+    mine, theirs = mine[...], theirs[...]
+    both = dot(mine, mine_last[...], 0, 0) + dot(theirs, theirs_last[...], 0, 0)
     last[...] = dot(inverse[...], both) - term[...]
 
 
 def top_kernel(level, inverse, *refs):
     factor = inverse[...]
-    earlier, (bases, samples, probe_coef) = refs[6:-3], refs[-3:]
-    coef = level_coefs(factor, refs[:3], refs[3:6])
+    earlier, (bases, samples, probe_coef) = refs[7:-3], refs[-3:]
+    mine, theirs, (half, passed) = [r[...] for r in refs[:3]], [r[...] for r in refs[3:5]], refs[5:7]
+    upper = lax.axis_index("leaf") & 1 == 1
+    theirs.append(jnp.where(upper, passed[...], half[...]))
+    theirs.append(jnp.where(upper, half[...], passed[...]))
+    coef = level_coefs(factor, mine, theirs)
     width = samples.shape[2]
     samples[0] = coef[:, :width]
     probe_coef[0] = coef[:, width:]
     for at, done in enumerate(earlier):
         bases[0, at] = done[0, 0]
-    write_basis(level, len(earlier), refs[0][...], refs[3][...], factor, bases)
+    write_basis(level, len(earlier), mine[0], theirs[0], factor, bases)
 
 
 VMEM = pl.BlockSpec(memory_space=pltpu.VMEM)
@@ -295,9 +330,8 @@
     )
     handed_last = flat_shift(handed_last, 1)
     scratch = dict(scratch_shapes=[pltpu.VMEM((scratch_rows(columns), columns), jnp.float32)])
-    both = (columns, columns + width)
-    far, inverse, coefs, first, probe_coef = call(
-        leaf_kernel, [tall, square, both, square, (columns, width)], rest_first, handed, probes,
+    far, inverse, first, probe_coef = call(
+        leaf_kernel, [tall, square, square, (columns, width)], rest_first, handed, probes,
         flops=work, **scratch,
     )
     leaf_basis, last = call(
@@ -310,36 +344,42 @@
         copies = 2 ** (level - 1)
         count = subtree // copies
         if count == 4:
-            theirs_coefs = swapped(coefs, copies)
+            theirs_coefs = swapped(jnp.concatenate([first, probe_coef], axis=1), copies)
             away = outward(probe_coef, 2 * copies)
             term_first, term_last = call(
                 functools.partial(term_kernel, level), [square, square_last],
-                couplings, probe_coef, away, theirs_coefs, last, slots=node_slot,
-                specs=[VMEM, VMEM, VMEM, ANY, ANY],
+                couplings, probe_coef, away, last, slots=node_slot, specs=[VMEM, VMEM, VMEM, ANY],
             )
             first = first - swapped(term_first, 2 * copies)
             theirs_first = theirs_coefs[:, :columns] - swapped(term_first, 3 * copies)
             theirs_probe = theirs_coefs[:, columns:]
             term_last = swapped(term_last, 2 * copies)
         else:
-            theirs_probe = swapped(probe_coef, copies)
+            correct = functools.partial(corrected_kernel, level, count == 2)
             if count == 2:
                 fields = [tree_swapped(probe_coef, odd) for odd in (0, 1)]
+                first, term_last, theirs_half = call(
+                    correct, [square, square_last, half.shape],
+                    couplings, *fields, first, swapped(half, copies), slots=node_slot,
+                    specs=[VMEM, VMEM, VMEM, VMEM, ANY], out_specs=[VMEM, VMEM, ANY],
+                    input_output_aliases={5: 2},
+                )
+                theirs_passed = swapped(theirs_half, 1)
             else:
+                theirs_probe = swapped(probe_coef, copies)
                 even = (lax.axis_index("leaf") >> level - 1) & 1 == 0
                 fields = [flat_shift(probe_coef, by) for by in (2 * copies, -2 * copies)]
                 fields = [jnp.where(even, *fields), jnp.where(even, *fields[::-1])]
-            first, term_last = call(
-                functools.partial(corrected_kernel, level, count == 2), [square, square_last],
-                couplings, *fields, first, slots=node_slot,
-            )
+                first, term_last = call(
+                    correct, [square, square_last], couplings, *fields, first, slots=node_slot
+                )
             theirs_first = swapped(first, copies)
         if below is None:
             last = last - term_last
         else:
             (last,) = call(node_last_kernel, [square_last], *below, term_last)
         theirs_last = swapped(last, copies)
-        mine, theirs = (first, last, probe_coef), (theirs_first, theirs_last, theirs_probe)
+        mine = first, last, probe_coef
         (inverse,) = call(
             factor_kernel, [square], first, theirs_first, flops=8 * work if count == 4 else 0, **scratch
         )
@@ -349,15 +389,15 @@
                 inverse, first, theirs_first,
             )
             below = inverse, first, last, theirs_first, theirs_last
-            coefs, first, probe_coef = call(
-                node_kernel, [both, square, (columns, width)],
+            first, probe_coef, half = call(
+                node_kernel, [square, (columns, width), (columns, width // 2)],
                 inverse, first, probe_coef, theirs_first, theirs_probe, last,
                 specs=[VMEM] * 5 + [ANY],
             )
     transfer_bases, top_samples, top_probes = call(
         functools.partial(top_kernel, levels),
         [(1, levels, 2 * columns, columns), (1, columns, width), (1, columns, width)],
-        inverse, *mine, *theirs, *ancestors,
+        inverse, *mine, theirs_first, theirs_last, theirs_half, theirs_passed, *ancestors,
     )
     return (leaf_basis, transfer_bases, top_samples, top_probes)
 

time: 79.3 us -> 74.8 us (0.943)
  Pallas kernels: 25.2 us -> 22.2 us
  waiting for transfers between devices: 19.9 us -> 17.1 us
  starting transfers between devices: 30.3 us -> 31.6 us
    pallas_call x13, Pallas kernels: 25.2 us -> 22.2 us  [call(): pl.pallas_call(kernel, out_shape=outs, in_specs=specs, out_specs=out_spec...]
    ppermute x14 -> x15, waiting for transfers between devices: 19.9 us -> 17.1 us  [permuted(): return lax.ppermute(value, BOTH, pairs)]
    ppermute x14 -> x15, starting transfers between devices: 30.3 us -> 31.6 us  [permuted(): return lax.ppermute(value, BOTH, pairs)]
  transfers between devices with their start and end apart: 14 -> 15, of which waited for: 6 -> 5; matrix products, arithmetic and copies ran while one was open for 0% -> 0% of each run, Pallas kernels for 26% -> 26%
where the time goes in v10:
time: 74.8 us; the launch traced here: 74.5 us
  starting transfers between devices  31.6 us (42%)
  Pallas kernels  22.2 us (30%)
  waiting for transfers between devices  17.1 us (23%)
  local copies, waits for them, and re-layouts  2.66 us (4%)
  between operations  0.89 us (1%)
    ppermute x15, starting transfers between devices, permuted(): return lax.ppermute(value, BOTH, pairs)  31.6 us
    pallas_call x13, Pallas kernels, call(): pl.pallas_call(kernel, out_shape=outs, in_specs=specs, out_specs=out_spec...  22.2 us
    ppermute x15, waiting for transfers between devices, permuted(): return lax.ppermute(value, BOTH, pairs)  17.1 us
    unnamed x12, local copies, waits for them, and re-layouts  2.65 us
  transfers between devices with their start and end apart: 15, of which 5 were waited for; matrix products, arithmetic and copies ran while one was open for 0% of the time, Pallas kernels for 26%

profile of v10, /device:TPU:4, one launch (start us, length us, event | category | flops | bytes accessed | tf_op | source)
XLA Modules:
  0.0 74.5 jit_solution(14213869377545054698)
XLA Ops:
  0.6 5.8 %collective-permute-start = (f32[512,256]{1,0:T(8,128)}, f32[512,256]{1,0:T(8,128)S(1)}, u32[]{:S(2)}, u32[]{:S(2)}) collective-permute-start(f32[512,256]{1,0:T(8,128)} %probes.5), channel_id=1, source_target_pairs={{1,24},{2,25},{3,26},{4,27},{5,28},{6,29},{7,30},{8,0},{9,1},{10,2... | collective-permute-start | bytes 1572872 | tf_op jit(solution)/shard_map/ppermute | solution.py:290
  6.5 1.6 %copy-done = f32[512,2,512]{2,1,0:T(2,128)S(1)} copy-done((f32[512,2,512]{2,1,0:T(2,128)S(1)}, f32[512,2,512]{2,1,0:T(2,128)}, u32[]{:S(2)}) %copy-start) | copy-done | bytes 2097176
  8.1 1.0 %copy-done.3 = f32[512,256]{1,0:T(8,128)S(1)} copy-done((f32[512,256]{1,0:T(8,128)S(1)}, f32[512,256]{1,0:T(8,128)}, u32[]{:S(2)}) %copy-start.3) | copy-done | bytes 524312
  10.0 1.9 %collective-permute-start.2 = (f32[512,128]{1,0:T(8,128)S(1)}, f32[512,128]{1,0:T(8,128)S(1)}, u32[]{:S(2)}, u32[]{:S(2)}) collective-permute-start(f32[512,128]{1,0:T(8,128)S(1)} %shard_map.86), channel_id=1, source_target_pairs={{0,8},{1,9},{2,10},{3,11},{4,12},{5,13},{6,14},{7,15},{8,16},{9,17... | collective-permute-start | bytes 786440 | tf_op jit(solution)/shard_map/ppermute | solution.py:290
  11.9 1.6 %shard_map.84 = (f32[512,256]{1,0:T(8,128)S(1)}, f32[512,128]{1,0:T(8,128)S(1)}) custom-call(f32[4096,128]{1,0:T(8,128)S(1)} %bitcast.6, f32[512,256]{1,0:T(8,128)S(1)} %copy-done.3, f32[512,256]{1,0:T(8,128)S(1)} %copy-done.2), custom_call_target="tpu_custom_call" | custom-call | flops 805306368 | bytes 3932160 | tf_op jit(solution)/shard_map/pallas_call | solution.py:271
  13.6 5.5 %collective-permute-done.following = f32[512,256]{1,0:T(8,128)S(1)} collective-permute-done((f32[512,256]{1,0:T(8,128)}, f32[512,256]{1,0:T(8,128)S(1)}, u32[]{:S(2)}, u32[]{:S(2)}) %collective-permute-start) | collective-permute-done | bytes 524320 | tf_op jit(solution)/shard_map/ppermute | solution.py:290
  19.1 1.2 %shard_map.85 = (f32[512,128]{1,0:T(8,128)S(1)}, f32[512,128]{1,0:T(8,128)S(1)}, f32[512,128]{1,0:T(8,128)S(1)}) custom-call(f32[4096,128]{1,0:T(8,128)S(1)} %bitcast.7, f32[512,256]{1,0:T(8,128)S(1)} %get-tuple-element.26.rest, f32[512,256]{1,0:T(8,128)S(1)} %collective-permute-done.following, ...), custom_call_target="tpu_custom_call", output_to_operand_aliasing={{2}: (3, {})} | custom-call | flops 805306368 | bytes 4194304 | tf_op jit(solution)/shard_map/pallas_call | solution.py:271
  20.3 1.9 %collective-permute-start.1 = (f32[512,128]{1,0:T(8,128)S(1)}, f32[512,128]{1,0:T(8,128)S(1)}, u32[]{:S(2)}, u32[]{:S(2)}) collective-permute-start(f32[512,128]{1,0:T(8,128)S(1)} %get-tuple-element.29), channel_id=1, source_target_pairs={{0,8},{1,9},{2,10},{3,11},{4,12},{5,13},{6,14},{7,15},{8,16},{9,17... | collective-permute-start | bytes 786440 | tf_op jit(solution)/shard_map/ppermute | solution.py:290
  22.2 2.4 %collective-permute-done.2.handed = f32[512,128]{1,0:T(8,128)S(1)} collective-permute-done((f32[512,128]{1,0:T(8,128)S(1)}, f32[512,128]{1,0:T(8,128)S(1)}, u32[]{:S(2)}, u32[]{:S(2)}) %collective-permute-start.2) | collective-permute-done | bytes 262176 | tf_op jit(solution)/shard_map/ppermute | solution.py:290
  24.6 4.3 %shard_map.87 = (f32[512,128]{1,0:T(8,128)S(1)}, f32[128,128]{1,0:T(8,128)S(1)}, f32[128,128]{1,0:T(8,128)S(1)}, f32[128,256]{1,0:T(8,128)S(1)}) custom-call(f32[512,128]{1,0:T(8,128)S(1)} %get-tuple-element.30.rest, f32[512,128]{1,0:T(8,128)S(1)} %collective-permute-done.2.handed, f32[512,256]{1,0:T(8,128)S(1)} %copy-done.4), custom_call_target="tpu_custom_call" | custom-call | flops 805306368 | bytes 1572864 | tf_op jit(solution)/shard_map/pallas_call | solution.py:271
  28.9 2.3 %collective-permute-start.3 = (f32[128,256]{1,0:T(8,128)S(1)}, f32[128,256]{1,0:T(8,128)S(1)}, u32[]{:S(2)}, u32[]{:S(2)}) collective-permute-start(f32[128,256]{1,0:T(8,128)S(1)} %get-tuple-element.35.mine.mine_probes), channel_id=1, source_target_pairs={{1,0},{2,1},{3,2},{4,3},{5,4},{6,5},{7,6},{9,8},{10,9},{11,10},{12... | collective-permute-start | bytes 393224 | tf_op jit(solution)/shard_map/ppermute | solution.py:290
  31.3 2.5 %collective-permute-start.5 = (f32[128,384]{1,0:T(8,128)S(1)}, f32[128,384]{1,0:T(8,128)S(1)}, u32[]{:S(2)}, u32[]{:S(2)}) collective-permute-start(f32[128,384]{1,0:T(8,128)S(1)} %pad_maximum_fusion), channel_id=1, source_target_pairs={{0,8},{1,9},{2,10},{3,11},{4,12},{5,13},{6,14},{7,15},{8,0},{9,1},... | collective-permute-start | bytes 589832 | tf_op jit(solution)/shard_map/ppermute | solution.py:290
  33.8 1.5 %shard_map.88 = (f32[512,128]{1,0:T(8,128)}, f32[128,128]{1,0:T(8,128)S(1)}) custom-call(f32[512,128]{1,0:T(8,128)S(1)} %get-tuple-element.28.rest, f32[512,128]{1,0:T(8,128)S(1)} %collective-permute-done.1.handed, f32[512,128]{1,0:T(8,128)S(1)} %get-tuple-element.31.far, f32[128,128]{1,0:T(8,128)S(1)} %get-tuple-element.32.inverse), custom_call_target="tpu_custom_call" | custom-call | flops 805306368 | bytes 1179648 | tf_op jit(solution)/shard_map/pallas_call | solution.py:271
  36.2 4.4 %collective-permute-start.6 = (f32[128,128]{1,0:T(8,128)S(1)}, f32[128,128]{1,0:T(8,128)S(1)}, u32[]{:S(2)}, u32[]{:S(2)}) collective-permute-start(f32[128,128]{1,0:T(8,128)S(1)} %get-tuple-element.37), channel_id=1, source_target_pairs={{0,24},{1,25},{2,26},{3,27},{4,28},{5,29},{6,30},{7,31},{8,16},{9,... | collective-permute-start | bytes 196616 | tf_op jit(solution)/shard_map/ppermute | solution.py:290
  40.9 2.6 %collective-permute-start.7 = (f32[128,128]{1,0:T(8,128)S(1)}, f32[128,128]{1,0:T(8,128)S(1)}, u32[]{:S(2)}, u32[]{:S(2)}) collective-permute-start(f32[128,128]{1,0:T(8,128)S(1)} %get-tuple-element.38), channel_id=1, source_target_pairs={{0,16},{1,17},{2,18},{3,19},{4,20},{5,21},{6,22},{7,23},{8,24},{9,... | collective-permute-start | bytes 196616 | tf_op jit(solution)/shard_map/ppermute | solution.py:290
  43.6 4.4 %collective-permute-done.4 = f32[128,128]{1,0:T(8,128)S(1)} collective-permute-done((f32[128,128]{1,0:T(8,128)S(1)}, f32[128,128]{1,0:T(8,128)S(1)}, u32[]{:S(2)}, u32[]{:S(2)}) %collective-permute-start.4) | collective-permute-done | bytes 65568 | tf_op jit(solution)/shard_map/ppermute | solution.py:290
  48.0 3.8 %shard_map.90.inverse = f32[128,128]{1,0:T(8,128)S(1)} custom-call(f32[128,128]{1,0:T(8,128)S(1)} %sub.9.mine, f32[128,128]{1,0:T(8,128)S(1)} %slice_subtract_fusion.theirs), custom_call_target="tpu_custom_call" | custom-call | flops 6442450944 | bytes 196608 | tf_op jit(solution)/shard_map/pallas_call | solution.py:271
  52.7 3.1 %collective-permute-start.9 = (f32[128,256]{1,0:T(8,128)S(1)}, f32[128,256]{1,0:T(8,128)S(1)}, u32[]{:S(2)}, u32[]{:S(2)}) collective-permute-start(f32[128,256]{1,0:T(8,128)S(1)} %get-tuple-element.39.refs_2_), channel_id=1, source_target_pairs={{1,2},{2,1},{3,4},{4,3},{5,6},{6,5},{9,10},{10,9},{11,12},{12,11},... | collective-permute-start | bytes 393224 | tf_op jit(solution)/shard_map/ppermute | solution.py:290
  55.9 3.2 %collective-permute-start.12 = (f32[128,128]{1,0:T(8,128)S(1)}, f32[128,128]{1,0:T(8,128)S(1)}, u32[]{:S(2)}, u32[]{:S(2)}) collective-permute-start(f32[128,128]{1,0:T(8,128)S(1)} %sub.11._last.mine_last), channel_id=1, source_target_pairs={{0,8},{1,9},{2,10},{3,11},{4,12},{5,13},{6,14},{7,15},{8,0},{9,1},... | collective-permute-start | bytes 196616 | tf_op jit(solution)/shard_map/ppermute | solution.py:290
  59.0 2.7 %collective-permute-done.10.outs_0_ = f32[128,128]{1,0:T(8,128)S(1)} collective-permute-done((f32[128,128]{1,0:T(8,128)S(1)}, f32[128,128]{1,0:T(8,128)S(1)}, u32[]{:S(2)}, u32[]{:S(2)}) %collective-permute-start.10) | collective-permute-done | bytes 65568 | tf_op jit(solution)/shard_map/ppermute | solution.py:290
  63.3 3.0 %collective-permute-start.13 = (f32[128,128]{1,0:T(8,128)S(1)}, f32[128,128]{1,0:T(8,128)S(1)}, u32[]{:S(2)}, u32[]{:S(2)}) collective-permute-start(f32[128,128]{1,0:T(8,128)S(1)} %shard_map.94.refs_1_), channel_id=1, source_target_pairs={{0,16},{1,17},{2,18},{3,19},{4,20},{5,21},{6,22},{7,23},{8,24},{9,... | collective-permute-start | bytes 196616 | tf_op jit(solution)/shard_map/ppermute | solution.py:290
  66.9 2.0 %collective-permute-done.11.theirs.refs_3_ = f32[128,128]{1,0:T(8,128)S(1)} collective-permute-done((f32[128,128]{1,0:T(8,128)S(1)}, f32[128,128]{1,0:T(8,128)S(1)}, u32[]{:S(2)}, u32[]{:S(2)}) %collective-permute-start.11) | collective-permute-done | bytes 65568 | tf_op jit(solution)/shard_map/ppermute | solution.py:290
  68.9 3.8 %shard_map.93.inverse = f32[128,128]{1,0:T(8,128)S(1)} custom-call(f32[128,128]{1,0:T(8,128)S(1)} %get-tuple-element.42.mine.refs_0_, f32[128,128]{1,0:T(8,128)S(1)} %collective-permute-done.11.theirs.refs_3_), custom_call_target="tpu_custom_call" | custom-call | bytes 196608 | tf_op jit(solution)/shard_map/pallas_call | solution.py:271
  72.7 1.7 %shard_map.96 = (f32[1,2,256,128]{3,2,1,0:T(8,128)}, f32[1,128,256]{2,1,0:T(8,128)}, f32[1,128,256]{2,1,0:T(8,128)}) custom-call(f32[128,128]{1,0:T(8,128)S(1)} %shard_map.93.inverse, f32[128,128]{1,0:T(8,128)S(1)} %get-tuple-element.42.mine.refs_0_, f32[128,128]{1,0:T(8,128)S(1)} %shard_map.94.refs_1_, f32[128,256]{1,0:T(8,128)S(1)} %get-tuple-element.39.refs_2_, ...), custom_call_target="tpu_custom_call" | custom-call | bytes 1245184 | tf_op jit(solution)/shard_map/pallas_call | solution.py:271
  (36 shorter events, 5.3 us)
Async XLA Ops:
  0.6 18.5 %collective-permute-start = (f32[512,256]{1,0:T(8,128)}, f32[512,256]{1,0:T(8,128)S(1)}, u32[]{:S(2)}, u32[]{:S(2)}) collective-permute-start(f32[512,256]{1,0:T(8,128)} %probes.5), channel_id=1, source_target_pairs={{1,24},{2,25},{3,26},{4,27},{5,28},{6,29},{7,30},{8,0},{9,1},{10,2... | collective-permute-start | bytes 1572872 | tf_op jit(solution)/shard_map/ppermute | solution.py:290
  6.5 1.6 %copy-start = (f32[512,2,512]{2,1,0:T(2,128)S(1)}, f32[512,2,512]{2,1,0:T(2,128)}, u32[]{:S(2)}) copy-start(f32[512,2,512]{2,1,0:T(2,128)} %param.7) | copy-start | bytes 6291460
  8.1 1.0 %copy-start.3 = (f32[512,256]{1,0:T(8,128)S(1)}, f32[512,256]{1,0:T(8,128)}, u32[]{:S(2)}) copy-start(f32[512,256]{1,0:T(8,128)} %probes.5) | copy-start | bytes 1572868
  9.1 2.8 %copy-start.2 = (f32[512,256]{1,0:T(8,128)S(1)}, f32[512,256]{1,0:T(8,128)}, u32[]{:S(2)}) copy-start(f32[512,256]{1,0:T(8,128)} %samples.1) | copy-start | bytes 1572868
  10.0 14.6 %collective-permute-start.2 = (f32[512,128]{1,0:T(8,128)S(1)}, f32[512,128]{1,0:T(8,128)S(1)}, u32[]{:S(2)}, u32[]{:S(2)}) collective-permute-start(f32[512,128]{1,0:T(8,128)S(1)} %shard_map.86), channel_id=1, source_target_pairs={{0,8},{1,9},{2,10},{3,11},{4,12},{5,13},{6,14},{7,15},{8,16},{9,17... | collective-permute-start | bytes 786440 | tf_op jit(solution)/shard_map/ppermute | solution.py:290
  13.6 11.1 %copy-start.4 = (f32[512,256]{1,0:T(8,128)S(1)}, f32[512,256]{1,0:T(8,128)}, u32[]{:S(2)}) copy-start(f32[512,256]{1,0:T(8,128)} %probes.5) | copy-start | bytes 1572868
  20.3 13.6 %collective-permute-start.1 = (f32[512,128]{1,0:T(8,128)S(1)}, f32[512,128]{1,0:T(8,128)S(1)}, u32[]{:S(2)}, u32[]{:S(2)}) collective-permute-start(f32[512,128]{1,0:T(8,128)S(1)} %get-tuple-element.29), channel_id=1, source_target_pairs={{0,8},{1,9},{2,10},{3,11},{4,12},{5,13},{6,14},{7,15},{8,16},{9,17... | collective-permute-start | bytes 786440 | tf_op jit(solution)/shard_map/ppermute | solution.py:290
  28.9 6.4 %copy-start.1 = (f32[1,3,2,128,128]{4,3,2,1,0:T(8,128)S(1)}, f32[1,3,2,128,128]{4,3,2,1,0:T(8,128)}, u32[]{:S(2)}) copy-start(f32[1,3,2,128,128]{4,3,2,1,0:T(8,128)} %couplings.3) | copy-start | bytes 1179652
  28.9 6.4 %copy-start.5 = (s32[1,3]{1,0:T(1,128)S(1)}, s32[1,3]{1,0:T(1,128)}, u32[]{:S(2)}) copy-start(s32[1,3]{1,0:T(1,128)} %slots.3) | copy-start | bytes 40
  28.9 6.4 %collective-permute-start.3 = (f32[128,256]{1,0:T(8,128)S(1)}, f32[128,256]{1,0:T(8,128)S(1)}, u32[]{:S(2)}, u32[]{:S(2)}) collective-permute-start(f32[128,256]{1,0:T(8,128)S(1)} %get-tuple-element.35.mine.mine_probes), channel_id=1, source_target_pairs={{1,0},{2,1},{3,2},{4,3},{5,4},{6,5},{7,6},{9,8},{10,9},{11,10},{12... | collective-permute-start | bytes 393224 | tf_op jit(solution)/shard_map/ppermute | solution.py:290
  31.3 9.3 %collective-permute-start.5 = (f32[128,384]{1,0:T(8,128)S(1)}, f32[128,384]{1,0:T(8,128)S(1)}, u32[]{:S(2)}, u32[]{:S(2)}) collective-permute-start(f32[128,384]{1,0:T(8,128)S(1)} %pad_maximum_fusion), channel_id=1, source_target_pairs={{0,8},{1,9},{2,10},{3,11},{4,12},{5,13},{6,14},{7,15},{8,0},{9,1},... | collective-permute-start | bytes 589832 | tf_op jit(solution)/shard_map/ppermute | solution.py:290
  36.2 7.4 %collective-permute-start.6 = (f32[128,128]{1,0:T(8,128)S(1)}, f32[128,128]{1,0:T(8,128)S(1)}, u32[]{:S(2)}, u32[]{:S(2)}) collective-permute-start(f32[128,128]{1,0:T(8,128)S(1)} %get-tuple-element.37), channel_id=1, source_target_pairs={{0,24},{1,25},{2,26},{3,27},{4,28},{5,29},{6,30},{7,31},{8,16},{9,... | collective-permute-start | bytes 196616 | tf_op jit(solution)/shard_map/ppermute | solution.py:290
  40.6 7.5 %collective-permute-start.4 = (f32[128,128]{1,0:T(8,128)S(1)}, f32[128,128]{1,0:T(8,128)S(1)}, u32[]{:S(2)}, u32[]{:S(2)}) collective-permute-start(f32[128,128]{1,0:T(8,128)S(1)} %get-tuple-element.37), channel_id=1, source_target_pairs={{0,16},{1,17},{2,18},{3,19},{4,20},{5,21},{6,22},{7,23},{8,24},{9,... | collective-permute-start | bytes 196616 | tf_op jit(solution)/shard_map/ppermute | solution.py:290
  40.9 10.9 %collective-permute-start.7 = (f32[128,128]{1,0:T(8,128)S(1)}, f32[128,128]{1,0:T(8,128)S(1)}, u32[]{:S(2)}, u32[]{:S(2)}) collective-permute-start(f32[128,128]{1,0:T(8,128)S(1)} %get-tuple-element.38), channel_id=1, source_target_pairs={{0,16},{1,17},{2,18},{3,19},{4,20},{5,21},{6,22},{7,23},{8,24},{9,... | collective-permute-start | bytes 196616 | tf_op jit(solution)/shard_map/ppermute | solution.py:290
  52.6 9.1 %collective-permute-start.8 = (f32[128,256]{1,0:T(8,128)S(1)}, f32[128,256]{1,0:T(8,128)S(1)}, u32[]{:S(2)}, u32[]{:S(2)}) collective-permute-start(f32[128,256]{1,0:T(8,128)S(1)} %get-tuple-element.39.refs_2_), channel_id=1, source_target_pairs={{0,1},{1,0},{2,3},{3,2},{4,5},{5,4},{6,7},{7,6},{8,9},{9,8},{10,11... | collective-permute-start | bytes 393224 | tf_op jit(solution)/shard_map/ppermute | solution.py:290
  52.7 9.0 %collective-permute-start.9 = (f32[128,256]{1,0:T(8,128)S(1)}, f32[128,256]{1,0:T(8,128)S(1)}, u32[]{:S(2)}, u32[]{:S(2)}) collective-permute-start(f32[128,256]{1,0:T(8,128)S(1)} %get-tuple-element.39.refs_2_), channel_id=1, source_target_pairs={{1,2},{2,1},{3,4},{4,3},{5,6},{6,5},{9,10},{10,9},{11,12},{12,11},... | collective-permute-start | bytes 393224 | tf_op jit(solution)/shard_map/ppermute | solution.py:290
  55.8 5.9 %collective-permute-start.10 = (f32[128,128]{1,0:T(8,128)S(1)}, f32[128,128]{1,0:T(8,128)S(1)}, u32[]{:S(2)}, u32[]{:S(2)}) collective-permute-start(f32[128,128]{1,0:T(8,128)S(1)} %get-tuple-element.41), channel_id=1, source_target_pairs={{0,16},{1,17},{2,18},{3,19},{4,20},{5,21},{6,22},{7,23},{8,24},{9,... | collective-permute-start | bytes 196616 | tf_op jit(solution)/shard_map/ppermute | solution.py:290
  55.9 6.8 %collective-permute-start.12 = (f32[128,128]{1,0:T(8,128)S(1)}, f32[128,128]{1,0:T(8,128)S(1)}, u32[]{:S(2)}, u32[]{:S(2)}) collective-permute-start(f32[128,128]{1,0:T(8,128)S(1)} %sub.11._last.mine_last), channel_id=1, source_target_pairs={{0,8},{1,9},{2,10},{3,11},{4,12},{5,13},{6,14},{7,15},{8,0},{9,1},... | collective-permute-start | bytes 196616 | tf_op jit(solution)/shard_map/ppermute | solution.py:290
  62.6 6.3 %collective-permute-start.11 = (f32[128,128]{1,0:T(8,128)S(1)}, f32[128,128]{1,0:T(8,128)S(1)}, u32[]{:S(2)}, u32[]{:S(2)}) collective-permute-start(f32[128,128]{1,0:T(8,128)S(1)} %get-tuple-element.42.mine.refs_0_), channel_id=1, source_target_pairs={{0,16},{1,17},{2,18},{3,19},{4,20},{5,21},{6,22},{7,23},{8,24},{9,... | collective-permute-start | bytes 196616 | tf_op jit(solution)/shard_map/ppermute | solution.py:290
  63.3 9.4 %collective-permute-start.13 = (f32[128,128]{1,0:T(8,128)S(1)}, f32[128,128]{1,0:T(8,128)S(1)}, u32[]{:S(2)}, u32[]{:S(2)}) collective-permute-start(f32[128,128]{1,0:T(8,128)S(1)} %shard_map.94.refs_1_), channel_id=1, source_target_pairs={{0,16},{1,17},{2,18},{3,19},{4,20},{5,21},{6,22},{7,23},{8,24},{9,... | collective-permute-start | bytes 196616 | tf_op jit(solution)/shard_map/ppermute | solution.py:290
  66.2 6.5 %collective-permute-start.14 = (f32[128,128]{1,0:T(8,128)S(1)}, f32[128,128]{1,0:T(8,128)S(1)}, u32[]{:S(2)}, u32[]{:S(2)}) collective-permute-start(f32[128,128]{1,0:T(8,128)S(1)} %get-tuple-element.44.refs_5_), channel_id=1, source_target_pairs={{0,8},{1,9},{2,10},{3,11},{4,12},{5,13},{6,14},{7,15},{8,0},{9,1},... | collective-permute-start | bytes 196616 | tf_op jit(solution)/shard_map/ppermute | solution.py:290

commit v11 on v10

--- a/solution.py
+++ b/solution.py
@@ -183,8 +183,7 @@
     last[...] = term[:, first.shape[1] :]
 
 
-def corrected_kernel(level, trees, slots, couplings, one, two, first, *outs):
-    out_first, out_last = outs[-3:-1] if trees else outs
+def corrected_kernel(level, trees, slots, couplings, one, two, first, out_first, out_last):
     columns = first.shape[1]
     node = member_node(level)
     block = coupling_of(slots, couplings, level, node)
@@ -206,9 +205,9 @@
 def write_basis(level, at, mine, theirs, inverse, bases):
     size = mine.shape[0]
     own = (lax.axis_index("leaf") >> level - 1) & 1
-    for block, half in ((mine, own), (theirs, 1 - own)):
-        rows = pl.ds(pl.multiple_of(half * size, size), size)
-        bases[0, at, rows, :] = dot(block, inverse, 1, 1)
+    block = dot(jnp.concatenate([mine, theirs], axis=0), inverse, 1, 1)
+    bases[0, at, pl.ds(pl.multiple_of(own * size, size), size), :] = block[:size]
+    bases[0, at, pl.ds(pl.multiple_of((1 - own) * size, size), size), :] = block[size:]
 
 
 def basis_kernel(level, inverse, mine, theirs, basis):
@@ -233,9 +232,10 @@
     half[...] = jnp.where(upper, coef[:, columns + width :], coef[:, columns : columns + width])
 
 
-def node_last_kernel(inverse, mine, mine_last, theirs, theirs_last, term, last):
+def node_last_kernel(inverse, mine, mine_last, theirs, theirs_last, term, *refs):
     mine, theirs = mine[...], theirs[...]
     both = dot(mine, mine_last[...], 0, 0) + dot(theirs, theirs_last[...], 0, 0)
+    last = refs[0] if len(refs) == 1 else refs[1]
     last[...] = dot(inverse[...], both) - term[...]
 
 
@@ -353,31 +353,33 @@
             first = first - swapped(term_first, 2 * copies)
             theirs_first = theirs_coefs[:, :columns] - swapped(term_first, 3 * copies)
             theirs_probe = theirs_coefs[:, columns:]
+            first, theirs_first, term_last = lax.optimization_barrier((first, theirs_first, term_last))
             term_last = swapped(term_last, 2 * copies)
         else:
             correct = functools.partial(corrected_kernel, level, count == 2)
             if count == 2:
                 fields = [tree_swapped(probe_coef, odd) for odd in (0, 1)]
-                first, term_last, theirs_half = call(
-                    correct, [square, square_last, half.shape],
-                    couplings, *fields, first, swapped(half, copies), slots=node_slot,
-                    specs=[VMEM, VMEM, VMEM, VMEM, ANY], out_specs=[VMEM, VMEM, ANY],
-                    input_output_aliases={5: 2},
-                )
-                theirs_passed = swapped(theirs_half, 1)
+                theirs_half = swapped(half, copies)
             else:
                 theirs_probe = swapped(probe_coef, copies)
                 even = (lax.axis_index("leaf") >> level - 1) & 1 == 0
                 fields = [flat_shift(probe_coef, by) for by in (2 * copies, -2 * copies)]
                 fields = [jnp.where(even, *fields), jnp.where(even, *fields[::-1])]
-                first, term_last = call(
-                    correct, [square, square_last], couplings, *fields, first, slots=node_slot
-                )
+            first, term_last = call(
+                correct, [square, square_last], couplings, *fields, first, slots=node_slot
+            )
             theirs_first = swapped(first, copies)
         if below is None:
             last = last - term_last
         else:
-            (last,) = call(node_last_kernel, [square_last], *below, term_last)
+            if level < levels:
+                (last,) = call(node_last_kernel, [square_last], *below, term_last)
+            else:
+                last, theirs_half = call(
+                    node_last_kernel, [square_last, half.shape], *below, term_last, theirs_half,
+                    specs=[VMEM] * 6 + [ANY], out_specs=[VMEM, ANY], input_output_aliases={6: 1},
+                )
+                theirs_passed = swapped(theirs_half, 1)
         theirs_last = swapped(last, copies)
         mine = first, last, probe_coef
         (inverse,) = call(

time: 74.8 us -> 75.3 us (level)
  waiting for transfers between devices: 17.1 us -> 19.4 us
  starting transfers between devices: 31.6 us -> 30.1 us
    ppermute x15, waiting for transfers between devices: 17.1 us -> 19.4 us  [permuted(): return lax.ppermute(value, BOTH, pairs)]
    ppermute x15, starting transfers between devices: 31.6 us -> 30.1 us  [permuted(): return lax.ppermute(value, BOTH, pairs)]
  transfers between devices with their start and end apart: 15 -> 15, of which waited for: 5 -> 8; matrix products, arithmetic and copies ran while one was open for 0% -> 0% of each run, Pallas kernels for 26% -> 26%
where the time goes in v11:
time: 75.3 us; the launch traced here: 75 us
  starting transfers between devices  30.1 us (40%)
  Pallas kernels  21.9 us (29%)
  waiting for transfers between devices  19.4 us (26%)
  local copies, waits for them, and re-layouts  2.66 us (4%)
  between operations  0.85 us (1%)
    ppermute x15, starting transfers between devices, permuted(): return lax.ppermute(value, BOTH, pairs)  30.1 us
    pallas_call x13, Pallas kernels, call(): pl.pallas_call(kernel, out_shape=outs, in_specs=specs, out_specs=out_spec...  21.9 us
    ppermute x15, waiting for transfers between devices, permuted(): return lax.ppermute(value, BOTH, pairs)  19.4 us
    unnamed x12, local copies, waits for them, and re-layouts  2.65 us
  transfers between devices with their start and end apart: 15, of which 8 were waited for; matrix products, arithmetic and copies ran while one was open for 0% of the time, Pallas kernels for 26%

profile of v11, /device:TPU:4, one launch (start us, length us, event | category | flops | bytes accessed | tf_op | source)
XLA Modules:
  0.0 75.0 jit_solution(8644117373654767720)
XLA Ops:
  0.6 5.8 %collective-permute-start = (f32[512,256]{1,0:T(8,128)}, f32[512,256]{1,0:T(8,128)S(1)}, u32[]{:S(2)}, u32[]{:S(2)}) collective-permute-start(f32[512,256]{1,0:T(8,128)} %probes.5), channel_id=1, source_target_pairs={{1,24},{2,25},{3,26},{4,27},{5,28},{6,29},{7,30},{8,0},{9,1},{10,2... | collective-permute-start | bytes 1572872 | tf_op jit(solution)/shard_map/ppermute | solution.py:290
  6.5 1.6 %copy-done = f32[512,2,512]{2,1,0:T(2,128)S(1)} copy-done((f32[512,2,512]{2,1,0:T(2,128)S(1)}, f32[512,2,512]{2,1,0:T(2,128)}, u32[]{:S(2)}) %copy-start) | copy-done | bytes 2097176
  10.0 1.9 %collective-permute-start.2 = (f32[512,128]{1,0:T(8,128)S(1)}, f32[512,128]{1,0:T(8,128)S(1)}, u32[]{:S(2)}, u32[]{:S(2)}) collective-permute-start(f32[512,128]{1,0:T(8,128)S(1)} %shard_map.86), channel_id=1, source_target_pairs={{0,8},{1,9},{2,10},{3,11},{4,12},{5,13},{6,14},{7,15},{8,16},{9,17... | collective-permute-start | bytes 786440 | tf_op jit(solution)/shard_map/ppermute | solution.py:290
  11.9 1.6 %shard_map.84 = (f32[512,256]{1,0:T(8,128)S(1)}, f32[512,128]{1,0:T(8,128)S(1)}) custom-call(f32[4096,128]{1,0:T(8,128)S(1)} %bitcast.6, f32[512,256]{1,0:T(8,128)S(1)} %copy-done.3, f32[512,256]{1,0:T(8,128)S(1)} %copy-done.2), custom_call_target="tpu_custom_call" | custom-call | flops 805306368 | bytes 3932160 | tf_op jit(solution)/shard_map/pallas_call | solution.py:271
  13.6 5.5 %collective-permute-done.following = f32[512,256]{1,0:T(8,128)S(1)} collective-permute-done((f32[512,256]{1,0:T(8,128)}, f32[512,256]{1,0:T(8,128)S(1)}, u32[]{:S(2)}, u32[]{:S(2)}) %collective-permute-start) | collective-permute-done | bytes 524320 | tf_op jit(solution)/shard_map/ppermute | solution.py:290
  19.1 1.2 %shard_map.85 = (f32[512,128]{1,0:T(8,128)S(1)}, f32[512,128]{1,0:T(8,128)S(1)}, f32[512,128]{1,0:T(8,128)S(1)}) custom-call(f32[4096,128]{1,0:T(8,128)S(1)} %bitcast.7, f32[512,256]{1,0:T(8,128)S(1)} %get-tuple-element.30.rest, f32[512,256]{1,0:T(8,128)S(1)} %collective-permute-done.following, ...), custom_call_target="tpu_custom_call", output_to_operand_aliasing={{2}: (3, {})} | custom-call | flops 805306368 | bytes 4194304 | tf_op jit(solution)/shard_map/pallas_call | solution.py:271
  20.3 1.9 %collective-permute-start.1 = (f32[512,128]{1,0:T(8,128)S(1)}, f32[512,128]{1,0:T(8,128)S(1)}, u32[]{:S(2)}, u32[]{:S(2)}) collective-permute-start(f32[512,128]{1,0:T(8,128)S(1)} %get-tuple-element.33), channel_id=1, source_target_pairs={{0,8},{1,9},{2,10},{3,11},{4,12},{5,13},{6,14},{7,15},{8,16},{9,17... | collective-permute-start | bytes 786440 | tf_op jit(solution)/shard_map/ppermute | solution.py:290
  22.2 2.4 %collective-permute-done.2.handed = f32[512,128]{1,0:T(8,128)S(1)} collective-permute-done((f32[512,128]{1,0:T(8,128)S(1)}, f32[512,128]{1,0:T(8,128)S(1)}, u32[]{:S(2)}, u32[]{:S(2)}) %collective-permute-start.2) | collective-permute-done | bytes 262176 | tf_op jit(solution)/shard_map/ppermute | solution.py:290
  24.6 4.3 %shard_map.87 = (f32[512,128]{1,0:T(8,128)S(1)}, f32[128,128]{1,0:T(8,128)S(1)}, f32[128,128]{1,0:T(8,128)S(1)}, f32[128,256]{1,0:T(8,128)S(1)}) custom-call(f32[512,128]{1,0:T(8,128)S(1)} %get-tuple-element.34.rest, f32[512,128]{1,0:T(8,128)S(1)} %collective-permute-done.2.handed, f32[512,256]{1,0:T(8,128)S(1)} %copy-done.4), custom_call_target="tpu_custom_call" | custom-call | flops 805306368 | bytes 1572864 | tf_op jit(solution)/shard_map/pallas_call | solution.py:271
  28.9 2.3 %collective-permute-start.3 = (f32[128,256]{1,0:T(8,128)S(1)}, f32[128,256]{1,0:T(8,128)S(1)}, u32[]{:S(2)}, u32[]{:S(2)}) collective-permute-start(f32[128,256]{1,0:T(8,128)S(1)} %get-tuple-element.39.mine.mine_probes), channel_id=1, source_target_pairs={{1,0},{2,1},{3,2},{4,3},{5,4},{6,5},{7,6},{9,8},{10,9},{11,10},{12... | collective-permute-start | bytes 393224 | tf_op jit(solution)/shard_map/ppermute | solution.py:290
  31.3 2.5 %collective-permute-start.5 = (f32[128,384]{1,0:T(8,128)S(1)}, f32[128,384]{1,0:T(8,128)S(1)}, u32[]{:S(2)}, u32[]{:S(2)}) collective-permute-start(f32[128,384]{1,0:T(8,128)S(1)} %pad_maximum_fusion), channel_id=1, source_target_pairs={{0,8},{1,9},{2,10},{3,11},{4,12},{5,13},{6,14},{7,15},{8,0},{9,1},... | collective-permute-start | bytes 589832 | tf_op jit(solution)/shard_map/ppermute | solution.py:290
  33.8 1.5 %shard_map.88 = (f32[512,128]{1,0:T(8,128)}, f32[128,128]{1,0:T(8,128)S(1)}) custom-call(f32[512,128]{1,0:T(8,128)S(1)} %get-tuple-element.32.rest, f32[512,128]{1,0:T(8,128)S(1)} %collective-permute-done.1.handed, f32[512,128]{1,0:T(8,128)S(1)} %get-tuple-element.35.far, f32[128,128]{1,0:T(8,128)S(1)} %get-tuple-element.36.inverse), custom_call_target="tpu_custom_call" | custom-call | flops 805306368 | bytes 1179648 | tf_op jit(solution)/shard_map/pallas_call | solution.py:271
  36.2 4.4 %collective-permute-start.6 = (f32[128,128]{1,0:T(8,128)S(1)}, f32[128,128]{1,0:T(8,128)S(1)}, u32[]{:S(2)}, u32[]{:S(2)}) collective-permute-start(f32[128,128]{1,0:T(8,128)S(1)} %get-tuple-element.41), channel_id=1, source_target_pairs={{0,24},{1,25},{2,26},{3,27},{4,28},{5,29},{6,30},{7,31},{8,16},{9,... | collective-permute-start | bytes 196616 | tf_op jit(solution)/shard_map/ppermute | solution.py:290
  40.9 2.0 %collective-permute-done.6 = f32[128,128]{1,0:T(8,128)S(1)} collective-permute-done((f32[128,128]{1,0:T(8,128)S(1)}, f32[128,128]{1,0:T(8,128)S(1)}, u32[]{:S(2)}, u32[]{:S(2)}) %collective-permute-start.6) | collective-permute-done | bytes 65568 | tf_op jit(solution)/shard_map/ppermute | solution.py:290
  42.9 3.3 %collective-permute-done.4 = f32[128,128]{1,0:T(8,128)S(1)} collective-permute-done((f32[128,128]{1,0:T(8,128)S(1)}, f32[128,128]{1,0:T(8,128)S(1)}, u32[]{:S(2)}, u32[]{:S(2)}) %collective-permute-start.4) | collective-permute-done | bytes 65568 | tf_op jit(solution)/shard_map/ppermute | solution.py:290
  47.1 3.8 %shard_map.90.inverse = f32[128,128]{1,0:T(8,128)S(1)} custom-call(f32[128,128]{1,0:T(8,128)S(1)} %sub.9.mine, f32[128,128]{1,0:T(8,128)S(1)} %slice_subtract_fusion.theirs), custom_call_target="tpu_custom_call" | custom-call | flops 6442450944 | bytes 196608 | tf_op jit(solution)/shard_map/pallas_call | solution.py:271
  50.9 1.3 %collective-permute-done.7 = f32[128,128]{1,0:T(8,128)S(1)} collective-permute-done((f32[128,128]{1,0:T(8,128)S(1)}, f32[128,128]{1,0:T(8,128)S(1)}, u32[]{:S(2)}, u32[]{:S(2)}) %collective-permute-start.7) | collective-permute-done | bytes 65568 | tf_op jit(solution)/shard_map/ppermute | solution.py:290
  53.0 3.6 %collective-permute-start.9 = (f32[128,256]{1,0:T(8,128)S(1)}, f32[128,256]{1,0:T(8,128)S(1)}, u32[]{:S(2)}, u32[]{:S(2)}) collective-permute-start(f32[128,256]{1,0:T(8,128)S(1)} %get-tuple-element.46.refs_2_), channel_id=1, source_target_pairs={{1,2},{2,1},{3,4},{4,3},{5,6},{6,5},{9,10},{10,9},{11,12},{12,11},... | collective-permute-start | bytes 393224 | tf_op jit(solution)/shard_map/ppermute | solution.py:290
  57.3 1.8 %collective-permute-start.11 = (f32[128,128]{1,0:T(8,128)S(1)}, f32[128,128]{1,0:T(8,128)S(1)}, u32[]{:S(2)}, u32[]{:S(2)}) collective-permute-start(f32[128,128]{1,0:T(8,128)S(1)} %sub.11._last.mine_last), channel_id=1, source_target_pairs={{0,8},{1,9},{2,10},{3,11},{4,12},{5,13},{6,14},{7,15},{8,0},{9,1},... | collective-permute-start | bytes 196616 | tf_op jit(solution)/shard_map/ppermute | solution.py:290
  59.2 1.5 %collective-permute-done.9.two = f32[128,256]{1,0:T(8,128)S(1)} collective-permute-done((f32[128,256]{1,0:T(8,128)S(1)}, f32[128,256]{1,0:T(8,128)S(1)}, u32[]{:S(2)}, u32[]{:S(2)}) %collective-permute-start.9) | collective-permute-done | bytes 131104 | tf_op jit(solution)/shard_map/ppermute | solution.py:290
  63.1 2.1 %collective-permute-start.13 = (f32[128,128]{1,0:T(8,128)S(1)}, f32[128,128]{1,0:T(8,128)S(1)}, u32[]{:S(2)}, u32[]{:S(2)}) collective-permute-start(f32[128,128]{1,0:T(8,128)S(1)} %get-tuple-element.51.refs_1_), channel_id=1, source_target_pairs={{0,16},{1,17},{2,18},{3,19},{4,20},{5,21},{6,22},{7,23},{8,24},{9,... | collective-permute-start | bytes 196616 | tf_op jit(solution)/shard_map/ppermute | solution.py:290
  66.4 3.2 %collective-permute-done.10.theirs.refs_3_ = f32[128,128]{1,0:T(8,128)S(1)} collective-permute-done((f32[128,128]{1,0:T(8,128)S(1)}, f32[128,128]{1,0:T(8,128)S(1)}, u32[]{:S(2)}, u32[]{:S(2)}) %collective-permute-start.10) | collective-permute-done | bytes 65568 | tf_op jit(solution)/shard_map/ppermute | solution.py:290
  69.6 3.8 %shard_map.93.inverse = f32[128,128]{1,0:T(8,128)S(1)} custom-call(f32[128,128]{1,0:T(8,128)S(1)} %get-tuple-element.48.mine.refs_0_, f32[128,128]{1,0:T(8,128)S(1)} %collective-permute-done.10.theirs.refs_3_), custom_call_target="tpu_custom_call" | custom-call | bytes 196608 | tf_op jit(solution)/shard_map/pallas_call | solution.py:271
  73.4 1.6 %shard_map.96 = (f32[1,2,256,128]{3,2,1,0:T(8,128)}, f32[1,128,256]{2,1,0:T(8,128)}, f32[1,128,256]{2,1,0:T(8,128)}) custom-call(f32[128,128]{1,0:T(8,128)S(1)} %shard_map.93.inverse, f32[128,128]{1,0:T(8,128)S(1)} %get-tuple-element.48.mine.refs_0_, f32[128,128]{1,0:T(8,128)S(1)} %get-tuple-element.51.refs_1_, f32[128,256]{1,0:T(8,128)S(1)} %get-tuple-element.46.refs_2_, ...), custom_call_target="tpu_custom_call" | custom-call | bytes 1245184 | tf_op jit(solution)/shard_map/pallas_call | solution.py:271
  (36 shorter events, 9.2 us)
Async XLA Ops:
  0.6 18.5 %collective-permute-start = (f32[512,256]{1,0:T(8,128)}, f32[512,256]{1,0:T(8,128)S(1)}, u32[]{:S(2)}, u32[]{:S(2)}) collective-permute-start(f32[512,256]{1,0:T(8,128)} %probes.5), channel_id=1, source_target_pairs={{1,24},{2,25},{3,26},{4,27},{5,28},{6,29},{7,30},{8,0},{9,1},{10,2... | collective-permute-start | bytes 1572872 | tf_op jit(solution)/shard_map/ppermute | solution.py:290
  6.5 1.6 %copy-start = (f32[512,2,512]{2,1,0:T(2,128)S(1)}, f32[512,2,512]{2,1,0:T(2,128)}, u32[]{:S(2)}) copy-start(f32[512,2,512]{2,1,0:T(2,128)} %param.7) | copy-start | bytes 6291460
  8.1 1.0 %copy-start.3 = (f32[512,256]{1,0:T(8,128)S(1)}, f32[512,256]{1,0:T(8,128)}, u32[]{:S(2)}) copy-start(f32[512,256]{1,0:T(8,128)} %probes.5) | copy-start | bytes 1572868
  9.1 2.8 %copy-start.2 = (f32[512,256]{1,0:T(8,128)S(1)}, f32[512,256]{1,0:T(8,128)}, u32[]{:S(2)}) copy-start(f32[512,256]{1,0:T(8,128)} %samples.1) | copy-start | bytes 1572868
  10.0 14.6 %collective-permute-start.2 = (f32[512,128]{1,0:T(8,128)S(1)}, f32[512,128]{1,0:T(8,128)S(1)}, u32[]{:S(2)}, u32[]{:S(2)}) collective-permute-start(f32[512,128]{1,0:T(8,128)S(1)} %shard_map.86), channel_id=1, source_target_pairs={{0,8},{1,9},{2,10},{3,11},{4,12},{5,13},{6,14},{7,15},{8,16},{9,17... | collective-permute-start | bytes 786440 | tf_op jit(solution)/shard_map/ppermute | solution.py:290
  13.6 11.1 %copy-start.4 = (f32[512,256]{1,0:T(8,128)S(1)}, f32[512,256]{1,0:T(8,128)}, u32[]{:S(2)}) copy-start(f32[512,256]{1,0:T(8,128)} %probes.5) | copy-start | bytes 1572868
  20.3 13.6 %collective-permute-start.1 = (f32[512,128]{1,0:T(8,128)S(1)}, f32[512,128]{1,0:T(8,128)S(1)}, u32[]{:S(2)}, u32[]{:S(2)}) collective-permute-start(f32[512,128]{1,0:T(8,128)S(1)} %get-tuple-element.33), channel_id=1, source_target_pairs={{0,8},{1,9},{2,10},{3,11},{4,12},{5,13},{6,14},{7,15},{8,16},{9,17... | collective-permute-start | bytes 786440 | tf_op jit(solution)/shard_map/ppermute | solution.py:290
  28.9 6.4 %copy-start.1 = (f32[1,3,2,128,128]{4,3,2,1,0:T(8,128)S(1)}, f32[1,3,2,128,128]{4,3,2,1,0:T(8,128)}, u32[]{:S(2)}) copy-start(f32[1,3,2,128,128]{4,3,2,1,0:T(8,128)} %couplings.3) | copy-start | bytes 1179652
  28.9 6.4 %copy-start.5 = (s32[1,3]{1,0:T(1,128)S(1)}, s32[1,3]{1,0:T(1,128)}, u32[]{:S(2)}) copy-start(s32[1,3]{1,0:T(1,128)} %slots.3) | copy-start | bytes 40
  28.9 6.4 %collective-permute-start.3 = (f32[128,256]{1,0:T(8,128)S(1)}, f32[128,256]{1,0:T(8,128)S(1)}, u32[]{:S(2)}, u32[]{:S(2)}) collective-permute-start(f32[128,256]{1,0:T(8,128)S(1)} %get-tuple-element.39.mine.mine_probes), channel_id=1, source_target_pairs={{1,0},{2,1},{3,2},{4,3},{5,4},{6,5},{7,6},{9,8},{10,9},{11,10},{12... | collective-permute-start | bytes 393224 | tf_op jit(solution)/shard_map/ppermute | solution.py:290
  31.3 9.3 %collective-permute-start.5 = (f32[128,384]{1,0:T(8,128)S(1)}, f32[128,384]{1,0:T(8,128)S(1)}, u32[]{:S(2)}, u32[]{:S(2)}) collective-permute-start(f32[128,384]{1,0:T(8,128)S(1)} %pad_maximum_fusion), channel_id=1, source_target_pairs={{0,8},{1,9},{2,10},{3,11},{4,12},{5,13},{6,14},{7,15},{8,0},{9,1},... | collective-permute-start | bytes 589832 | tf_op jit(solution)/shard_map/ppermute | solution.py:290
  36.2 6.7 %collective-permute-start.6 = (f32[128,128]{1,0:T(8,128)S(1)}, f32[128,128]{1,0:T(8,128)S(1)}, u32[]{:S(2)}, u32[]{:S(2)}) collective-permute-start(f32[128,128]{1,0:T(8,128)S(1)} %get-tuple-element.41), channel_id=1, source_target_pairs={{0,24},{1,25},{2,26},{3,27},{4,28},{5,29},{6,30},{7,31},{8,16},{9,... | collective-permute-start | bytes 196616 | tf_op jit(solution)/shard_map/ppermute | solution.py:290
  40.6 5.7 %collective-permute-start.4 = (f32[128,128]{1,0:T(8,128)S(1)}, f32[128,128]{1,0:T(8,128)S(1)}, u32[]{:S(2)}, u32[]{:S(2)}) collective-permute-start(f32[128,128]{1,0:T(8,128)S(1)} %get-tuple-element.41), channel_id=1, source_target_pairs={{0,16},{1,17},{2,18},{3,19},{4,20},{5,21},{6,22},{7,23},{8,24},{9,... | collective-permute-start | bytes 196616 | tf_op jit(solution)/shard_map/ppermute | solution.py:290
  46.2 5.9 %collective-permute-start.7 = (f32[128,128]{1,0:T(8,128)S(1)}, f32[128,128]{1,0:T(8,128)S(1)}, u32[]{:S(2)}, u32[]{:S(2)}) collective-permute-start(f32[128,128]{1,0:T(8,128)S(1)} %get-tuple-element.45), channel_id=1, source_target_pairs={{0,16},{1,17},{2,18},{3,19},{4,20},{5,21},{6,22},{7,23},{8,24},{9,... | collective-permute-start | bytes 196616 | tf_op jit(solution)/shard_map/ppermute | solution.py:290
  52.9 6.3 %collective-permute-start.8 = (f32[128,256]{1,0:T(8,128)S(1)}, f32[128,256]{1,0:T(8,128)S(1)}, u32[]{:S(2)}, u32[]{:S(2)}) collective-permute-start(f32[128,256]{1,0:T(8,128)S(1)} %get-tuple-element.46.refs_2_), channel_id=1, source_target_pairs={{0,1},{1,0},{2,3},{3,2},{4,5},{5,4},{6,7},{7,6},{8,9},{9,8},{10,11... | collective-permute-start | bytes 393224 | tf_op jit(solution)/shard_map/ppermute | solution.py:290
  53.0 7.7 %collective-permute-start.9 = (f32[128,256]{1,0:T(8,128)S(1)}, f32[128,256]{1,0:T(8,128)S(1)}, u32[]{:S(2)}, u32[]{:S(2)}) collective-permute-start(f32[128,256]{1,0:T(8,128)S(1)} %get-tuple-element.46.refs_2_), channel_id=1, source_target_pairs={{1,2},{2,1},{3,4},{4,3},{5,6},{6,5},{9,10},{10,9},{11,12},{12,11},... | collective-permute-start | bytes 393224 | tf_op jit(solution)/shard_map/ppermute | solution.py:290
  56.6 5.9 %collective-permute-start.12 = (f32[128,128]{1,0:T(8,128)S(1)}, f32[128,128]{1,0:T(8,128)S(1)}, u32[]{:S(2)}, u32[]{:S(2)}) collective-permute-start(f32[128,128]{1,0:T(8,128)S(1)} %get-tuple-element.50), channel_id=1, source_target_pairs={{0,16},{1,17},{2,18},{3,19},{4,20},{5,21},{6,22},{7,23},{8,24},{9,... | collective-permute-start | bytes 196616 | tf_op jit(solution)/shard_map/ppermute | solution.py:290
  57.3 5.2 %collective-permute-start.11 = (f32[128,128]{1,0:T(8,128)S(1)}, f32[128,128]{1,0:T(8,128)S(1)}, u32[]{:S(2)}, u32[]{:S(2)}) collective-permute-start(f32[128,128]{1,0:T(8,128)S(1)} %sub.11._last.mine_last), channel_id=1, source_target_pairs={{0,8},{1,9},{2,10},{3,11},{4,12},{5,13},{6,14},{7,15},{8,0},{9,1},... | collective-permute-start | bytes 196616 | tf_op jit(solution)/shard_map/ppermute | solution.py:290
  61.6 8.0 %collective-permute-start.10 = (f32[128,128]{1,0:T(8,128)S(1)}, f32[128,128]{1,0:T(8,128)S(1)}, u32[]{:S(2)}, u32[]{:S(2)}) collective-permute-start(f32[128,128]{1,0:T(8,128)S(1)} %get-tuple-element.48.mine.refs_0_), channel_id=1, source_target_pairs={{0,16},{1,17},{2,18},{3,19},{4,20},{5,21},{6,22},{7,23},{8,24},{9,... | collective-permute-start | bytes 196616 | tf_op jit(solution)/shard_map/ppermute | solution.py:290
  63.1 10.3 %collective-permute-start.13 = (f32[128,128]{1,0:T(8,128)S(1)}, f32[128,128]{1,0:T(8,128)S(1)}, u32[]{:S(2)}, u32[]{:S(2)}) collective-permute-start(f32[128,128]{1,0:T(8,128)S(1)} %get-tuple-element.51.refs_1_), channel_id=1, source_target_pairs={{0,16},{1,17},{2,18},{3,19},{4,20},{5,21},{6,22},{7,23},{8,24},{9,... | collective-permute-start | bytes 196616 | tf_op jit(solution)/shard_map/ppermute | solution.py:290
  65.2 8.2 %collective-permute-start.14 = (f32[128,128]{1,0:T(8,128)S(1)}, f32[128,128]{1,0:T(8,128)S(1)}, u32[]{:S(2)}, u32[]{:S(2)}) collective-permute-start(f32[128,128]{1,0:T(8,128)S(1)} %get-tuple-element.52.refs_5_), channel_id=1, source_target_pairs={{0,8},{1,9},{2,10},{3,11},{4,12},{5,13},{6,14},{7,15},{8,0},{9,1},... | collective-permute-start | bytes 196616 | tf_op jit(solution)/shard_map/ppermute | solution.py:290

commit v12 on v11

--- a/solution.py
+++ b/solution.py
@@ -42,53 +42,52 @@
     def columns_of(tile, k):
         return [across_lanes(tile, ROWS * k + n) for n in range(ROWS)]
 
-    def factors(cols, j, step):
+    def factors(u, v, step):
         a, b, c, inverse = step[:4]
-        u, v = cols[j], cols[j + 1]
         return (u * c - v * b) * inverse, (v * a - u * b) * inverse
-
-    def eliminated(tile, cols, j, f, g, step):
-        row, next_row, col_rows = step[4:]
-        for n, (x, y) in enumerate(col_rows, j + 2):
-            cols[n] = cols[n] - (f * x + g * y)
-        return tile - (f * row + g * next_row)
 
     def diagonal(k):
         nonlocal used
-        tile, cols, steps = rows[k], columns_of(rows[k], k), []
+        tile = rows[k]
+        held = scratch.at[pl.ds(used, ROWS * ROWS), :]
+        used += ROWS * ROWS
+        for n, col in enumerate(columns_of(tile, k)):
+            held[pl.ds(ROWS * n, ROWS), :] = col
+        block = {(n, m): row_of(held, ROWS * m + n) for n in range(ROWS) for m in range(n + 1)}
+        steps = []
         pivots = jnp.ones((ROWS, size), jnp.float32)
         for j in range(0, ROWS, 2):
             tile = jnp.where(pair_of(k, j), jnp.where(lane == sub + ROWS * k, 1.0, 0.0), tile)
-            held = scratch.at[pl.ds(used, ROWS * (ROWS - j + 1)), :]
-            used += ROWS * (ROWS - j + 1)
-            for n in range(j, ROWS):
-                held[pl.ds(ROWS * (n - j + 1), ROWS), :] = cols[n]
-            held[pl.ds(0, ROWS), :] = tile
-            a = row_of(held, ROWS + j)
-            b = row_of(held, ROWS + j + 1)
-            c = row_of(held, 2 * ROWS + j + 1)
+            held = scratch.at[pl.ds(used, ROWS), :]
+            used += ROWS
+            held[...] = tile
+            row, next_row = row_of(held, j), row_of(held, j + 1)
+            a, b, c = block[j, j], block[j + 1, j], block[j + 1, j + 1]
             det = a * c - b * b
             inverse = pltpu.reciprocal(det, approx=True)
             inverse_a = pltpu.reciprocal(a, approx=True)
             pivots = jnp.where(sub == j, a, jnp.where(sub == j + 1, det * inverse_a, pivots))
-            col_rows = [
-                (row_of(held, ROWS * (n - j + 1) + j), row_of(held, ROWS * (n - j + 1) + j + 1))
-                for n in range(j + 2, ROWS)
-            ]
-            step = a, b, c, inverse, row_of(held, j), row_of(held, j + 1), col_rows
+            col_rows = [(block[n, j], block[n, j + 1]) for n in range(j + 2, ROWS)]
+            step = a, b, c, inverse, row, next_row, col_rows
             steps.append(step)
-            f, g = factors(cols, j, step)
-            f = jnp.where(sub > j + 1, f, jnp.where(sub == j + 1, b * inverse_a, 0.0))
-            g = jnp.where(sub > j + 1, g, 0.0)
-            tile = eliminated(tile, cols, j, f, g, step)
+            f, g = jnp.where(sub == j + 1, b * inverse_a, 0.0), jnp.zeros((ROWS, size), jnp.float32)
+            for n in range(j + 2, ROWS):
+                f_n, g_n = factors(block[n, j], block[n, j + 1], step)
+                f, g = jnp.where(sub == n, f_n, f), jnp.where(sub == n, g_n, g)
+                for m in range(j + 2, n + 1):
+                    block[n, m] = block[n, m] - (f_n * block[m, j] + g_n * block[m, j + 1])
+            tile = tile - (f * row + g * next_row)
         rows[k] = tile
         return steps, pivots
 
     def below(i, k, steps):
         tile, cols = rows[i], columns_of(rows[i], k)
         for j, step in zip(range(0, ROWS, 2), steps):
-            f, g = factors(cols, j, step)
-            tile = eliminated(jnp.where(pair_of(k, j), 0.0, tile), cols, j, f, g, step)
+            row, next_row, col_rows = step[4:]
+            f, g = factors(cols[j], cols[j + 1], step)
+            for n, (x, y) in enumerate(col_rows, j + 2):
+                cols[n] = cols[n] - (f * x + g * y)
+            tile = jnp.where(pair_of(k, j), 0.0, tile) - (f * row + g * next_row)
         rows[i] = tile
 
     waiting = None
@@ -117,7 +116,7 @@
 
 
 def scratch_rows(size):
-    return size // ROWS * sum(ROWS * (ROWS - j + 1) for j in range(0, ROWS, 2))
+    return size * (ROWS + ROWS // 2)
 
 
 def near_half(view, which, rows, chunks=None):
@@ -353,7 +352,6 @@
             first = first - swapped(term_first, 2 * copies)
             theirs_first = theirs_coefs[:, :columns] - swapped(term_first, 3 * copies)
             theirs_probe = theirs_coefs[:, columns:]
-            first, theirs_first, term_last = lax.optimization_barrier((first, theirs_first, term_last))
             term_last = swapped(term_last, 2 * copies)
         else:
             correct = functools.partial(corrected_kernel, level, count == 2)

time: 75.3 us -> 72.2 us (0.959)
  waiting for transfers between devices: 19.4 us -> 16.1 us
  starting transfers between devices: 30.1 us -> 31.1 us
    ppermute x15, waiting for transfers between devices: 19.4 us -> 16.1 us  [permuted(): return lax.ppermute(value, BOTH, pairs)]
    ppermute x15, starting transfers between devices: 30.1 us -> 31.1 us  [permuted(): return lax.ppermute(value, BOTH, pairs)]
where the time goes in v12:
time: 72.2 us; the launch traced here: 71.9 us
  starting transfers between devices  31.1 us (43%)
  Pallas kernels  21.2 us (29%)
  waiting for transfers between devices  16.1 us (22%)
  local copies, waits for them, and re-layouts  2.66 us (4%)
  between operations  0.88 us (1%)
    ppermute x15, starting transfers between devices, permuted(): return lax.ppermute(value, BOTH, pairs)  31.1 us
    pallas_call x13, Pallas kernels, call(): pl.pallas_call(kernel, out_shape=outs, in_specs=specs, out_specs=out_spec...  21.2 us
    ppermute x15, waiting for transfers between devices, permuted(): return lax.ppermute(value, BOTH, pairs)  16.1 us
    unnamed x12, local copies, waits for them, and re-layouts  2.65 us
  transfers between devices with their start and end apart: 15, of which 8 were waited for; matrix products, arithmetic and copies ran while one was open for 0% of the time, Pallas kernels for 26%

profile of v12, /device:TPU:4, one launch (start us, length us, event | category | flops | bytes accessed | tf_op | source)
XLA Modules:
  0.0 71.9 jit_solution(11689414314821492383)
XLA Ops:
  0.6 5.8 %collective-permute-start = (f32[512,256]{1,0:T(8,128)}, f32[512,256]{1,0:T(8,128)S(1)}, u32[]{:S(2)}, u32[]{:S(2)}) collective-permute-start(f32[512,256]{1,0:T(8,128)} %probes.5), channel_id=1, source_target_pairs={{1,24},{2,25},{3,26},{4,27},{5,28},{6,29},{7,30},{8,0},{9,1},{10,2... | collective-permute-start | bytes 1572872 | tf_op jit(solution)/shard_map/ppermute | solution.py:289
  6.5 1.6 %copy-done = f32[512,2,512]{2,1,0:T(2,128)S(1)} copy-done((f32[512,2,512]{2,1,0:T(2,128)S(1)}, f32[512,2,512]{2,1,0:T(2,128)}, u32[]{:S(2)}) %copy-start) | copy-done | bytes 2097176
  8.1 1.0 %copy-done.3 = f32[512,256]{1,0:T(8,128)S(1)} copy-done((f32[512,256]{1,0:T(8,128)S(1)}, f32[512,256]{1,0:T(8,128)}, u32[]{:S(2)}) %copy-start.3) | copy-done | bytes 524312
  9.1 0.9 %shard_map.86 = f32[512,128]{1,0:T(8,128)S(1)} custom-call(f32[4096,128]{1,0:T(8,128)S(1)} %bitcast.5, f32[512,256]{1,0:T(8,128)S(1)} %copy-done.3), custom_call_target="tpu_custom_call" | custom-call | flops 805306368 | bytes 2883584 | tf_op jit(solution)/shard_map/pallas_call | solution.py:270
  10.0 1.9 %collective-permute-start.2 = (f32[512,128]{1,0:T(8,128)S(1)}, f32[512,128]{1,0:T(8,128)S(1)}, u32[]{:S(2)}, u32[]{:S(2)}) collective-permute-start(f32[512,128]{1,0:T(8,128)S(1)} %shard_map.86), channel_id=1, source_target_pairs={{0,8},{1,9},{2,10},{3,11},{4,12},{5,13},{6,14},{7,15},{8,16},{9,17... | collective-permute-start | bytes 786440 | tf_op jit(solution)/shard_map/ppermute | solution.py:289
  11.9 1.6 %shard_map.84 = (f32[512,256]{1,0:T(8,128)S(1)}, f32[512,128]{1,0:T(8,128)S(1)}) custom-call(f32[4096,128]{1,0:T(8,128)S(1)} %bitcast.6, f32[512,256]{1,0:T(8,128)S(1)} %copy-done.3, f32[512,256]{1,0:T(8,128)S(1)} %copy-done.2), custom_call_target="tpu_custom_call" | custom-call | flops 805306368 | bytes 3932160 | tf_op jit(solution)/shard_map/pallas_call | solution.py:270
  13.6 5.5 %collective-permute-done.following = f32[512,256]{1,0:T(8,128)S(1)} collective-permute-done((f32[512,256]{1,0:T(8,128)}, f32[512,256]{1,0:T(8,128)S(1)}, u32[]{:S(2)}, u32[]{:S(2)}) %collective-permute-start) | collective-permute-done | bytes 524320 | tf_op jit(solution)/shard_map/ppermute | solution.py:289
  19.1 1.2 %shard_map.85 = (f32[512,128]{1,0:T(8,128)S(1)}, f32[512,128]{1,0:T(8,128)S(1)}, f32[512,128]{1,0:T(8,128)S(1)}) custom-call(f32[4096,128]{1,0:T(8,128)S(1)} %bitcast.7, f32[512,256]{1,0:T(8,128)S(1)} %get-tuple-element.27.rest, f32[512,256]{1,0:T(8,128)S(1)} %collective-permute-done.following, ...), custom_call_target="tpu_custom_call", output_to_operand_aliasing={{2}: (3, {})} | custom-call | flops 805306368 | bytes 4194304 | tf_op jit(solution)/shard_map/pallas_call | solution.py:270
  20.3 1.9 %collective-permute-start.1 = (f32[512,128]{1,0:T(8,128)S(1)}, f32[512,128]{1,0:T(8,128)S(1)}, u32[]{:S(2)}, u32[]{:S(2)}) collective-permute-start(f32[512,128]{1,0:T(8,128)S(1)} %get-tuple-element.30), channel_id=1, source_target_pairs={{0,8},{1,9},{2,10},{3,11},{4,12},{5,13},{6,14},{7,15},{8,16},{9,17... | collective-permute-start | bytes 786440 | tf_op jit(solution)/shard_map/ppermute | solution.py:289
  22.2 2.4 %collective-permute-done.2.handed = f32[512,128]{1,0:T(8,128)S(1)} collective-permute-done((f32[512,128]{1,0:T(8,128)S(1)}, f32[512,128]{1,0:T(8,128)S(1)}, u32[]{:S(2)}, u32[]{:S(2)}) %collective-permute-start.2) | collective-permute-done | bytes 262176 | tf_op jit(solution)/shard_map/ppermute | solution.py:289
  24.6 4.0 %shard_map.87 = (f32[512,128]{1,0:T(8,128)S(1)}, f32[128,128]{1,0:T(8,128)S(1)}, f32[128,128]{1,0:T(8,128)S(1)}, f32[128,256]{1,0:T(8,128)S(1)}) custom-call(f32[512,128]{1,0:T(8,128)S(1)} %get-tuple-element.31.rest, f32[512,128]{1,0:T(8,128)S(1)} %collective-permute-done.2.handed, f32[512,256]{1,0:T(8,128)S(1)} %copy-done.4), custom_call_target="tpu_custom_call" | custom-call | flops 805306368 | bytes 1572864 | tf_op jit(solution)/shard_map/pallas_call | solution.py:270
  28.7 2.3 %collective-permute-start.3 = (f32[128,256]{1,0:T(8,128)S(1)}, f32[128,256]{1,0:T(8,128)S(1)}, u32[]{:S(2)}, u32[]{:S(2)}) collective-permute-start(f32[128,256]{1,0:T(8,128)S(1)} %get-tuple-element.36.mine.mine_probes), channel_id=1, source_target_pairs={{1,0},{2,1},{3,2},{4,3},{5,4},{6,5},{7,6},{9,8},{10,9},{11,10},{12... | collective-permute-start | bytes 393224 | tf_op jit(solution)/shard_map/ppermute | solution.py:289
  31.1 2.5 %collective-permute-start.5 = (f32[128,384]{1,0:T(8,128)S(1)}, f32[128,384]{1,0:T(8,128)S(1)}, u32[]{:S(2)}, u32[]{:S(2)}) collective-permute-start(f32[128,384]{1,0:T(8,128)S(1)} %pad_maximum_fusion), channel_id=1, source_target_pairs={{0,8},{1,9},{2,10},{3,11},{4,12},{5,13},{6,14},{7,15},{8,0},{9,1},... | collective-permute-start | bytes 589832 | tf_op jit(solution)/shard_map/ppermute | solution.py:289
  33.7 1.5 %shard_map.88 = (f32[512,128]{1,0:T(8,128)}, f32[128,128]{1,0:T(8,128)S(1)}) custom-call(f32[512,128]{1,0:T(8,128)S(1)} %get-tuple-element.29.rest, f32[512,128]{1,0:T(8,128)S(1)} %collective-permute-done.1.handed, f32[512,128]{1,0:T(8,128)S(1)} %get-tuple-element.32.far, f32[128,128]{1,0:T(8,128)S(1)} %get-tuple-element.33.inverse), custom_call_target="tpu_custom_call" | custom-call | flops 805306368 | bytes 1179648 | tf_op jit(solution)/shard_map/pallas_call | solution.py:270
  36.0 4.3 %collective-permute-start.6 = (f32[128,128]{1,0:T(8,128)S(1)}, f32[128,128]{1,0:T(8,128)S(1)}, u32[]{:S(2)}, u32[]{:S(2)}) collective-permute-start(f32[128,128]{1,0:T(8,128)S(1)} %get-tuple-element.38), channel_id=1, source_target_pairs={{0,24},{1,25},{2,26},{3,27},{4,28},{5,29},{6,30},{7,31},{8,16},{9,... | collective-permute-start | bytes 196616 | tf_op jit(solution)/shard_map/ppermute | solution.py:289
  40.7 2.6 %collective-permute-start.7 = (f32[128,128]{1,0:T(8,128)S(1)}, f32[128,128]{1,0:T(8,128)S(1)}, u32[]{:S(2)}, u32[]{:S(2)}) collective-permute-start(f32[128,128]{1,0:T(8,128)S(1)} %get-tuple-element.39), channel_id=1, source_target_pairs={{0,16},{1,17},{2,18},{3,19},{4,20},{5,21},{6,22},{7,23},{8,24},{9,... | collective-permute-start | bytes 196616 | tf_op jit(solution)/shard_map/ppermute | solution.py:289
  43.4 4.4 %collective-permute-done.4 = f32[128,128]{1,0:T(8,128)S(1)} collective-permute-done((f32[128,128]{1,0:T(8,128)S(1)}, f32[128,128]{1,0:T(8,128)S(1)}, u32[]{:S(2)}, u32[]{:S(2)}) %collective-permute-start.4) | collective-permute-done | bytes 65568 | tf_op jit(solution)/shard_map/ppermute | solution.py:289
  47.8 3.5 %shard_map.90.inverse = f32[128,128]{1,0:T(8,128)S(1)} custom-call(f32[128,128]{1,0:T(8,128)S(1)} %sub.9.mine, f32[128,128]{1,0:T(8,128)S(1)} %slice_subtract_fusion.theirs), custom_call_target="tpu_custom_call" | custom-call | flops 6442450944 | bytes 196608 | tf_op jit(solution)/shard_map/pallas_call | solution.py:270
  52.2 3.1 %collective-permute-start.9 = (f32[128,256]{1,0:T(8,128)S(1)}, f32[128,256]{1,0:T(8,128)S(1)}, u32[]{:S(2)}, u32[]{:S(2)}) collective-permute-start(f32[128,256]{1,0:T(8,128)S(1)} %get-tuple-element.40.refs_2_), channel_id=1, source_target_pairs={{1,2},{2,1},{3,4},{4,3},{5,6},{6,5},{9,10},{10,9},{11,12},{12,11},... | collective-permute-start | bytes 393224 | tf_op jit(solution)/shard_map/ppermute | solution.py:289
  55.4 3.2 %collective-permute-start.11 = (f32[128,128]{1,0:T(8,128)S(1)}, f32[128,128]{1,0:T(8,128)S(1)}, u32[]{:S(2)}, u32[]{:S(2)}) collective-permute-start(f32[128,128]{1,0:T(8,128)S(1)} %sub.11._last.mine_last), channel_id=1, source_target_pairs={{0,8},{1,9},{2,10},{3,11},{4,12},{5,13},{6,14},{7,15},{8,0},{9,1},... | collective-permute-start | bytes 196616 | tf_op jit(solution)/shard_map/ppermute | solution.py:289
  62.1 1.9 %collective-permute-start.13 = (f32[128,128]{1,0:T(8,128)S(1)}, f32[128,128]{1,0:T(8,128)S(1)}, u32[]{:S(2)}, u32[]{:S(2)}) collective-permute-start(f32[128,128]{1,0:T(8,128)S(1)} %get-tuple-element.45.refs_1_), channel_id=1, source_target_pairs={{0,16},{1,17},{2,18},{3,19},{4,20},{5,21},{6,22},{7,23},{8,24},{9,... | collective-permute-start | bytes 196616 | tf_op jit(solution)/shard_map/ppermute | solution.py:289
  65.1 1.7 %collective-permute-done.10.theirs.refs_3_ = f32[128,128]{1,0:T(8,128)S(1)} collective-permute-done((f32[128,128]{1,0:T(8,128)S(1)}, f32[128,128]{1,0:T(8,128)S(1)}, u32[]{:S(2)}, u32[]{:S(2)}) %collective-permute-start.10) | collective-permute-done | bytes 65568 | tf_op jit(solution)/shard_map/ppermute | solution.py:289
  66.8 3.5 %shard_map.93.inverse = f32[128,128]{1,0:T(8,128)S(1)} custom-call(f32[128,128]{1,0:T(8,128)S(1)} %get-tuple-element.42.mine.refs_0_, f32[128,128]{1,0:T(8,128)S(1)} %collective-permute-done.10.theirs.refs_3_), custom_call_target="tpu_custom_call" | custom-call | bytes 196608 | tf_op jit(solution)/shard_map/pallas_call | solution.py:270
  70.3 1.6 %shard_map.96 = (f32[1,2,256,128]{3,2,1,0:T(8,128)}, f32[1,128,256]{2,1,0:T(8,128)}, f32[1,128,256]{2,1,0:T(8,128)}) custom-call(f32[128,128]{1,0:T(8,128)S(1)} %shard_map.93.inverse, f32[128,128]{1,0:T(8,128)S(1)} %get-tuple-element.42.mine.refs_0_, f32[128,128]{1,0:T(8,128)S(1)} %get-tuple-element.45.refs_1_, f32[128,256]{1,0:T(8,128)S(1)} %get-tuple-element.40.refs_2_, ...), custom_call_target="tpu_custom_call" | custom-call | bytes 1245184 | tf_op jit(solution)/shard_map/pallas_call | solution.py:270
  (36 shorter events, 6.9 us)
Async XLA Ops:
  0.6 18.5 %collective-permute-start = (f32[512,256]{1,0:T(8,128)}, f32[512,256]{1,0:T(8,128)S(1)}, u32[]{:S(2)}, u32[]{:S(2)}) collective-permute-start(f32[512,256]{1,0:T(8,128)} %probes.5), channel_id=1, source_target_pairs={{1,24},{2,25},{3,26},{4,27},{5,28},{6,29},{7,30},{8,0},{9,1},{10,2... | collective-permute-start | bytes 1572872 | tf_op jit(solution)/shard_map/ppermute | solution.py:289
  6.5 1.6 %copy-start = (f32[512,2,512]{2,1,0:T(2,128)S(1)}, f32[512,2,512]{2,1,0:T(2,128)}, u32[]{:S(2)}) copy-start(f32[512,2,512]{2,1,0:T(2,128)} %param.7) | copy-start | bytes 6291460
  8.1 1.0 %copy-start.3 = (f32[512,256]{1,0:T(8,128)S(1)}, f32[512,256]{1,0:T(8,128)}, u32[]{:S(2)}) copy-start(f32[512,256]{1,0:T(8,128)} %probes.5) | copy-start | bytes 1572868
  9.1 2.8 %copy-start.2 = (f32[512,256]{1,0:T(8,128)S(1)}, f32[512,256]{1,0:T(8,128)}, u32[]{:S(2)}) copy-start(f32[512,256]{1,0:T(8,128)} %samples.1) | copy-start | bytes 1572868
  10.0 14.6 %collective-permute-start.2 = (f32[512,128]{1,0:T(8,128)S(1)}, f32[512,128]{1,0:T(8,128)S(1)}, u32[]{:S(2)}, u32[]{:S(2)}) collective-permute-start(f32[512,128]{1,0:T(8,128)S(1)} %shard_map.86), channel_id=1, source_target_pairs={{0,8},{1,9},{2,10},{3,11},{4,12},{5,13},{6,14},{7,15},{8,16},{9,17... | collective-permute-start | bytes 786440 | tf_op jit(solution)/shard_map/ppermute | solution.py:289
  13.6 11.1 %copy-start.4 = (f32[512,256]{1,0:T(8,128)S(1)}, f32[512,256]{1,0:T(8,128)}, u32[]{:S(2)}) copy-start(f32[512,256]{1,0:T(8,128)} %probes.5) | copy-start | bytes 1572868
  20.3 13.4 %collective-permute-start.1 = (f32[512,128]{1,0:T(8,128)S(1)}, f32[512,128]{1,0:T(8,128)S(1)}, u32[]{:S(2)}, u32[]{:S(2)}) collective-permute-start(f32[512,128]{1,0:T(8,128)S(1)} %get-tuple-element.30), channel_id=1, source_target_pairs={{0,8},{1,9},{2,10},{3,11},{4,12},{5,13},{6,14},{7,15},{8,16},{9,17... | collective-permute-start | bytes 786440 | tf_op jit(solution)/shard_map/ppermute | solution.py:289
  28.7 6.5 %copy-start.1 = (f32[1,3,2,128,128]{4,3,2,1,0:T(8,128)S(1)}, f32[1,3,2,128,128]{4,3,2,1,0:T(8,128)}, u32[]{:S(2)}) copy-start(f32[1,3,2,128,128]{4,3,2,1,0:T(8,128)} %couplings.3) | copy-start | bytes 1179652
  28.7 6.4 %copy-start.5 = (s32[1,3]{1,0:T(1,128)S(1)}, s32[1,3]{1,0:T(1,128)}, u32[]{:S(2)}) copy-start(s32[1,3]{1,0:T(1,128)} %slots.3) | copy-start | bytes 40
  28.7 6.4 %collective-permute-start.3 = (f32[128,256]{1,0:T(8,128)S(1)}, f32[128,256]{1,0:T(8,128)S(1)}, u32[]{:S(2)}, u32[]{:S(2)}) collective-permute-start(f32[128,256]{1,0:T(8,128)S(1)} %get-tuple-element.36.mine.mine_probes), channel_id=1, source_target_pairs={{1,0},{2,1},{3,2},{4,3},{5,4},{6,5},{7,6},{9,8},{10,9},{11,10},{12... | collective-permute-start | bytes 393224 | tf_op jit(solution)/shard_map/ppermute | solution.py:289
  31.1 9.3 %collective-permute-start.5 = (f32[128,384]{1,0:T(8,128)S(1)}, f32[128,384]{1,0:T(8,128)S(1)}, u32[]{:S(2)}, u32[]{:S(2)}) collective-permute-start(f32[128,384]{1,0:T(8,128)S(1)} %pad_maximum_fusion), channel_id=1, source_target_pairs={{0,8},{1,9},{2,10},{3,11},{4,12},{5,13},{6,14},{7,15},{8,0},{9,1},... | collective-permute-start | bytes 589832 | tf_op jit(solution)/shard_map/ppermute | solution.py:289
  36.0 7.4 %collective-permute-start.6 = (f32[128,128]{1,0:T(8,128)S(1)}, f32[128,128]{1,0:T(8,128)S(1)}, u32[]{:S(2)}, u32[]{:S(2)}) collective-permute-start(f32[128,128]{1,0:T(8,128)S(1)} %get-tuple-element.38), channel_id=1, source_target_pairs={{0,24},{1,25},{2,26},{3,27},{4,28},{5,29},{6,30},{7,31},{8,16},{9,... | collective-permute-start | bytes 196616 | tf_op jit(solution)/shard_map/ppermute | solution.py:289
  40.3 7.5 %collective-permute-start.4 = (f32[128,128]{1,0:T(8,128)S(1)}, f32[128,128]{1,0:T(8,128)S(1)}, u32[]{:S(2)}, u32[]{:S(2)}) collective-permute-start(f32[128,128]{1,0:T(8,128)S(1)} %get-tuple-element.38), channel_id=1, source_target_pairs={{0,16},{1,17},{2,18},{3,19},{4,20},{5,21},{6,22},{7,23},{8,24},{9,... | collective-permute-start | bytes 196616 | tf_op jit(solution)/shard_map/ppermute | solution.py:289
  40.7 10.6 %collective-permute-start.7 = (f32[128,128]{1,0:T(8,128)S(1)}, f32[128,128]{1,0:T(8,128)S(1)}, u32[]{:S(2)}, u32[]{:S(2)}) collective-permute-start(f32[128,128]{1,0:T(8,128)S(1)} %get-tuple-element.39), channel_id=1, source_target_pairs={{0,16},{1,17},{2,18},{3,19},{4,20},{5,21},{6,22},{7,23},{8,24},{9,... | collective-permute-start | bytes 196616 | tf_op jit(solution)/shard_map/ppermute | solution.py:289
  52.1 6.4 %collective-permute-start.8 = (f32[128,256]{1,0:T(8,128)S(1)}, f32[128,256]{1,0:T(8,128)S(1)}, u32[]{:S(2)}, u32[]{:S(2)}) collective-permute-start(f32[128,256]{1,0:T(8,128)S(1)} %get-tuple-element.40.refs_2_), channel_id=1, source_target_pairs={{0,1},{1,0},{2,3},{3,2},{4,5},{5,4},{6,7},{7,6},{8,9},{9,8},{10,11... | collective-permute-start | bytes 393224 | tf_op jit(solution)/shard_map/ppermute | solution.py:289
  52.2 7.2 %collective-permute-start.9 = (f32[128,256]{1,0:T(8,128)S(1)}, f32[128,256]{1,0:T(8,128)S(1)}, u32[]{:S(2)}, u32[]{:S(2)}) collective-permute-start(f32[128,256]{1,0:T(8,128)S(1)} %get-tuple-element.40.refs_2_), channel_id=1, source_target_pairs={{1,2},{2,1},{3,4},{4,3},{5,6},{6,5},{9,10},{10,9},{11,12},{12,11},... | collective-permute-start | bytes 393224 | tf_op jit(solution)/shard_map/ppermute | solution.py:289
  55.3 5.9 %collective-permute-start.12 = (f32[128,128]{1,0:T(8,128)S(1)}, f32[128,128]{1,0:T(8,128)S(1)}, u32[]{:S(2)}, u32[]{:S(2)}) collective-permute-start(f32[128,128]{1,0:T(8,128)S(1)} %get-tuple-element.44), channel_id=1, source_target_pairs={{0,16},{1,17},{2,18},{3,19},{4,20},{5,21},{6,22},{7,23},{8,24},{9,... | collective-permute-start | bytes 196616 | tf_op jit(solution)/shard_map/ppermute | solution.py:289
  55.4 6.1 %collective-permute-start.11 = (f32[128,128]{1,0:T(8,128)S(1)}, f32[128,128]{1,0:T(8,128)S(1)}, u32[]{:S(2)}, u32[]{:S(2)}) collective-permute-start(f32[128,128]{1,0:T(8,128)S(1)} %sub.11._last.mine_last), channel_id=1, source_target_pairs={{0,8},{1,9},{2,10},{3,11},{4,12},{5,13},{6,14},{7,15},{8,0},{9,1},... | collective-permute-start | bytes 196616 | tf_op jit(solution)/shard_map/ppermute | solution.py:289
  60.3 6.5 %collective-permute-start.10 = (f32[128,128]{1,0:T(8,128)S(1)}, f32[128,128]{1,0:T(8,128)S(1)}, u32[]{:S(2)}, u32[]{:S(2)}) collective-permute-start(f32[128,128]{1,0:T(8,128)S(1)} %get-tuple-element.42.mine.refs_0_), channel_id=1, source_target_pairs={{0,16},{1,17},{2,18},{3,19},{4,20},{5,21},{6,22},{7,23},{8,24},{9,... | collective-permute-start | bytes 196616 | tf_op jit(solution)/shard_map/ppermute | solution.py:289
  62.1 8.2 %collective-permute-start.13 = (f32[128,128]{1,0:T(8,128)S(1)}, f32[128,128]{1,0:T(8,128)S(1)}, u32[]{:S(2)}, u32[]{:S(2)}) collective-permute-start(f32[128,128]{1,0:T(8,128)S(1)} %get-tuple-element.45.refs_1_), channel_id=1, source_target_pairs={{0,16},{1,17},{2,18},{3,19},{4,20},{5,21},{6,22},{7,23},{8,24},{9,... | collective-permute-start | bytes 196616 | tf_op jit(solution)/shard_map/ppermute | solution.py:289
  63.9 6.4 %collective-permute-start.14 = (f32[128,128]{1,0:T(8,128)S(1)}, f32[128,128]{1,0:T(8,128)S(1)}, u32[]{:S(2)}, u32[]{:S(2)}) collective-permute-start(f32[128,128]{1,0:T(8,128)S(1)} %get-tuple-element.46.refs_5_), channel_id=1, source_target_pairs={{0,8},{1,9},{2,10},{3,11},{4,12},{5,13},{6,14},{7,15},{8,0},{9,1},... | collective-permute-start | bytes 196616 | tf_op jit(solution)/shard_map/ppermute | solution.py:289

commit v13 on v12

--- a/solution.py
+++ b/solution.py
@@ -171,15 +171,14 @@
     return lax.axis_index("leaf") >> level - 1
 
 
-def term_kernel(level, slots, couplings, mine, away, _last, first, last):
+def term_kernel(level, at, slots, couplings, mine, away, out):
     node = member_node(level)
     block = coupling_of(slots, couplings, level, node ^ 2)
     outer = (node == 0) | (node == 3)
-    main = jnp.where(outer, mine[...], away[...])
-    other = jnp.where(outer, away[...], mine[...])
-    term = dot(jnp.concatenate([block, block.T], axis=1), jnp.concatenate([main, other], axis=0))
-    first[...] = term[:, : first.shape[1]]
-    last[...] = term[:, first.shape[1] :]
+    cols = slice(at, at + out.shape[1])
+    main = jnp.where(outer, mine[:, cols], away[:, cols])
+    other = jnp.where(outer, away[:, cols], mine[:, cols])
+    out[...] = dot(jnp.concatenate([block, block.T], axis=1), jnp.concatenate([main, other], axis=0))
 
 
 def corrected_kernel(level, trees, slots, couplings, one, two, first, out_first, out_last):
@@ -333,9 +332,10 @@
         leaf_kernel, [tall, square, square, (columns, width)], rest_first, handed, probes,
         flops=work, **scratch,
     )
-    leaf_basis, last = call(
-        leaf_last_kernel, [tall, square_last], rest_last, handed_last, far, inverse, flops=work
-    )
+    if subtree != 4:
+        leaf_basis, last = call(
+            leaf_last_kernel, [tall, square_last], rest_last, handed_last, far, inverse, flops=work
+        )
 
     ancestors = []
     below = None
@@ -345,18 +345,34 @@
         if count == 4:
             theirs_coefs = swapped(jnp.concatenate([first, probe_coef], axis=1), copies)
             away = outward(probe_coef, 2 * copies)
-            term_first, term_last = call(
-                functools.partial(term_kernel, level), [square, square_last],
-                couplings, probe_coef, away, last, slots=node_slot, specs=[VMEM, VMEM, VMEM, ANY],
-            )
-            first = first - swapped(term_first, 2 * copies)
-            theirs_first = theirs_coefs[:, :columns] - swapped(term_first, 3 * copies)
+            if level == 1:
+                away, handed_last = lax.optimization_barrier((away, handed_last))
+            (term_first,) = call(
+                functools.partial(term_kernel, level, 0), [square], couplings, probe_coef, away,
+                slots=node_slot,
+            )
+            (term_last,) = call(
+                functools.partial(term_kernel, level, columns), [square_last],
+                couplings, probe_coef, away, slots=node_slot,
+            )
+            if level == 1:
+                leaf_basis, last = call(
+                    leaf_last_kernel, [tall, square_last], rest_last, handed_last, far, inverse,
+                    flops=work,
+                )
+            term_first, term_twin = swapped(term_first, 2 * copies), swapped(term_first, 3 * copies)
+            term_first, term_twin, theirs_coefs, last = lax.optimization_barrier(
+                (term_first, term_twin, theirs_coefs, last)
+            )
+            first = first - term_first
+            theirs_first = theirs_coefs[:, :columns] - term_twin
             theirs_probe = theirs_coefs[:, columns:]
             term_last = swapped(term_last, 2 * copies)
         else:
             correct = functools.partial(corrected_kernel, level, count == 2)
             if count == 2:
                 fields = [tree_swapped(probe_coef, odd) for odd in (0, 1)]
+                *fields, ancestors[-1] = lax.optimization_barrier((*fields, ancestors[-1]))
                 theirs_half = swapped(half, copies)
             else:
                 theirs_probe = swapped(probe_coef, copies)

time: 72.2 us -> 71.9 us (level)
  waiting for transfers between devices: 16.1 us -> 11.4 us
  starting transfers between devices: 31.1 us -> 34.6 us
  Pallas kernels: 21.2 us -> 22 us
    ppermute x15, waiting for transfers between devices: 16.1 us -> 11.4 us  [permuted(): return lax.ppermute(value, BOTH, pairs)]
    ppermute x15, starting transfers between devices: 31.1 us -> 34.6 us  [permuted(): return lax.ppermute(value, BOTH, pairs)]
    pallas_call x13 -> x14, Pallas kernels: 21.2 us -> 22 us  [call(): pl.pallas_call(kernel, out_shape=outs, in_specs=specs, out_specs=out_spec...]
  transfers between devices with their start and end apart: 15 -> 15, of which waited for: 8 -> 5; matrix products, arithmetic and copies ran while one was open for 0% -> 0% of each run, Pallas kernels for 26% -> 28%
where the time goes in v13:
time: 71.9 us; the launch traced here: 71.6 us
  starting transfers between devices  34.6 us (48%)
  Pallas kernels  22 us (31%)
  waiting for transfers between devices  11.4 us (16%)
  local copies, waits for them, and re-layouts  2.66 us (4%)
  between operations  0.88 us (1%)
    ppermute x15, starting transfers between devices, permuted(): return lax.ppermute(value, BOTH, pairs)  34.6 us
    pallas_call x14, Pallas kernels, call(): pl.pallas_call(kernel, out_shape=outs, in_specs=specs, out_specs=out_spec...  22 us
    ppermute x15, waiting for transfers between devices, permuted(): return lax.ppermute(value, BOTH, pairs)  11.4 us
    unnamed x12, local copies, waits for them, and re-layouts  2.65 us
  transfers between devices with their start and end apart: 15, of which 5 were waited for; matrix products, arithmetic and copies ran while one was open for 0% of the time, Pallas kernels for 28%

profile of v13, /device:TPU:4, one launch (start us, length us, event | category | flops | bytes accessed | tf_op | source)
XLA Modules:
  0.0 71.6 jit_solution(9745532512481264711)
XLA Ops:
  0.6 5.8 %collective-permute-start = (f32[512,256]{1,0:T(8,128)}, f32[512,256]{1,0:T(8,128)S(1)}, u32[]{:S(2)}, u32[]{:S(2)}) collective-permute-start(f32[512,256]{1,0:T(8,128)} %probes.5), channel_id=1, source_target_pairs={{1,24},{2,25},{3,26},{4,27},{5,28},{6,29},{7,30},{8,0},{9,1},{10,2... | collective-permute-start | bytes 1572872 | tf_op jit(solution)/shard_map/ppermute | solution.py:288
  6.5 1.6 %copy-done = f32[512,2,512]{2,1,0:T(2,128)S(1)} copy-done((f32[512,2,512]{2,1,0:T(2,128)S(1)}, f32[512,2,512]{2,1,0:T(2,128)}, u32[]{:S(2)}) %copy-start) | copy-done | bytes 2097176
  8.1 1.0 %copy-done.3 = f32[512,256]{1,0:T(8,128)S(1)} copy-done((f32[512,256]{1,0:T(8,128)S(1)}, f32[512,256]{1,0:T(8,128)}, u32[]{:S(2)}) %copy-start.3) | copy-done | bytes 524312
  10.0 1.9 %collective-permute-start.1 = (f32[512,128]{1,0:T(8,128)S(1)}, f32[512,128]{1,0:T(8,128)S(1)}, u32[]{:S(2)}, u32[]{:S(2)}) collective-permute-start(f32[512,128]{1,0:T(8,128)S(1)} %shard_map.86), channel_id=1, source_target_pairs={{0,8},{1,9},{2,10},{3,11},{4,12},{5,13},{6,14},{7,15},{8,16},{9,17... | collective-permute-start | bytes 786440 | tf_op jit(solution)/shard_map/ppermute | solution.py:288
  11.9 1.6 %shard_map.84 = (f32[512,256]{1,0:T(8,128)S(1)}, f32[512,128]{1,0:T(8,128)S(1)}) custom-call(f32[4096,128]{1,0:T(8,128)S(1)} %bitcast.6, f32[512,256]{1,0:T(8,128)S(1)} %copy-done.3, f32[512,256]{1,0:T(8,128)S(1)} %copy-done.2), custom_call_target="tpu_custom_call" | custom-call | flops 805306368 | bytes 3932160 | tf_op jit(solution)/shard_map/pallas_call | solution.py:269
  13.6 5.5 %collective-permute-done.following = f32[512,256]{1,0:T(8,128)S(1)} collective-permute-done((f32[512,256]{1,0:T(8,128)}, f32[512,256]{1,0:T(8,128)S(1)}, u32[]{:S(2)}, u32[]{:S(2)}) %collective-permute-start) | collective-permute-done | bytes 524320 | tf_op jit(solution)/shard_map/ppermute | solution.py:288
  19.1 1.2 %shard_map.85 = (f32[512,128]{1,0:T(8,128)S(1)}, f32[512,128]{1,0:T(8,128)S(1)}, f32[512,128]{1,0:T(8,128)S(1)}) custom-call(f32[4096,128]{1,0:T(8,128)S(1)} %bitcast.7, f32[512,256]{1,0:T(8,128)S(1)} %get-tuple-element.34.rest, f32[512,256]{1,0:T(8,128)S(1)} %collective-permute-done.following, ...), custom_call_target="tpu_custom_call", output_to_operand_aliasing={{2}: (3, {})} | custom-call | flops 805306368 | bytes 4194304 | tf_op jit(solution)/shard_map/pallas_call | solution.py:269
  20.3 2.1 %collective-permute-start.3 = (f32[512,128]{1,0:T(8,128)S(1)}, f32[512,128]{1,0:T(8,128)S(1)}, u32[]{:S(2)}, u32[]{:S(2)}) collective-permute-start(f32[512,128]{1,0:T(8,128)S(1)} %get-tuple-element.39), channel_id=1, source_target_pairs={{0,8},{1,9},{2,10},{3,11},{4,12},{5,13},{6,14},{7,15},{8,16},{9,17... | collective-permute-start | bytes 786440 | tf_op jit(solution)/shard_map/ppermute | solution.py:288
  22.3 2.3 %collective-permute-done.1.handed = f32[512,128]{1,0:T(8,128)S(1)} collective-permute-done((f32[512,128]{1,0:T(8,128)S(1)}, f32[512,128]{1,0:T(8,128)S(1)}, u32[]{:S(2)}, u32[]{:S(2)}) %collective-permute-start.1) | collective-permute-done | bytes 262176 | tf_op jit(solution)/shard_map/ppermute | solution.py:288
  24.6 4.0 %shard_map.87 = (f32[512,128]{1,0:T(8,128)S(1)}, f32[128,128]{1,0:T(8,128)S(1)}, f32[128,128]{1,0:T(8,128)S(1)}, f32[128,256]{1,0:T(8,128)S(1)}) custom-call(f32[512,128]{1,0:T(8,128)S(1)} %get-tuple-element.37.rest, f32[512,128]{1,0:T(8,128)S(1)} %collective-permute-done.1.handed, f32[512,256]{1,0:T(8,128)S(1)} %copy-done.4), custom_call_target="tpu_custom_call" | custom-call | flops 805306368 | bytes 1572864 | tf_op jit(solution)/shard_map/pallas_call | solution.py:269
  28.7 2.2 %collective-permute-start.2 = (f32[128,256]{1,0:T(8,128)S(1)}, f32[128,256]{1,0:T(8,128)S(1)}, u32[]{:S(2)}, u32[]{:S(2)}) collective-permute-start(f32[128,256]{1,0:T(8,128)S(1)} %get-tuple-element.38.mine.mine_probes), channel_id=1, source_target_pairs={{1,0},{2,1},{3,2},{4,3},{5,4},{6,5},{7,6},{9,8},{10,9},{11,10},{12... | collective-permute-start | bytes 393224 | tf_op jit(solution)/shard_map/ppermute | solution.py:288
  30.9 2.5 %collective-permute-start.6 = (f32[128,384]{1,0:T(8,128)S(1)}, f32[128,384]{1,0:T(8,128)S(1)}, u32[]{:S(2)}, u32[]{:S(2)}) collective-permute-start(f32[128,384]{1,0:T(8,128)S(1)} %pad_maximum_fusion), channel_id=1, source_target_pairs={{0,8},{1,9},{2,10},{3,11},{4,12},{5,13},{6,14},{7,15},{8,0},{9,1},... | collective-permute-start | bytes 589832 | tf_op jit(solution)/shard_map/ppermute | solution.py:288
  34.7 4.6 %collective-permute-start.4 = (f32[128,128]{1,0:T(8,128)S(1)}, f32[128,128]{1,0:T(8,128)S(1)}, u32[]{:S(2)}, u32[]{:S(2)}) collective-permute-start(f32[128,128]{1,0:T(8,128)S(1)} %shard_map.89), channel_id=1, source_target_pairs={{0,16},{1,17},{2,18},{3,19},{4,20},{5,21},{6,22},{7,23},{8,24},{9,... | collective-permute-start | bytes 196616 | tf_op jit(solution)/shard_map/ppermute | solution.py:288
  39.4 0.9 %collective-permute-start.5 = (f32[128,128]{1,0:T(8,128)S(1)}, f32[128,128]{1,0:T(8,128)S(1)}, u32[]{:S(2)}, u32[]{:S(2)}) collective-permute-start(f32[128,128]{1,0:T(8,128)S(1)} %shard_map.89), channel_id=1, source_target_pairs={{0,24},{1,25},{2,26},{3,27},{4,28},{5,29},{6,30},{7,31},{8,16},{9,... | collective-permute-start | bytes 196616 | tf_op jit(solution)/shard_map/ppermute | solution.py:288
  41.1 2.0 %collective-permute-start.7 = (f32[128,128]{1,0:T(8,128)S(1)}, f32[128,128]{1,0:T(8,128)S(1)}, u32[]{:S(2)}, u32[]{:S(2)}) collective-permute-start(f32[128,128]{1,0:T(8,128)S(1)} %shard_map.91), channel_id=1, source_target_pairs={{0,16},{1,17},{2,18},{3,19},{4,20},{5,21},{6,22},{7,23},{8,24},{9,... | collective-permute-start | bytes 196616 | tf_op jit(solution)/shard_map/ppermute | solution.py:288
  43.1 1.5 %shard_map.88 = (f32[512,128]{1,0:T(8,128)}, f32[128,128]{1,0:T(8,128)S(1)}) custom-call(f32[512,128]{1,0:T(8,128)S(1)} %get-tuple-element.36.rest, f32[512,128]{1,0:T(8,128)S(1)} %collective-permute-done.3.handed, f32[512,128]{1,0:T(8,128)S(1)} %get-tuple-element.41.far, f32[128,128]{1,0:T(8,128)S(1)} %get-tuple-element.42.inverse), custom_call_target="tpu_custom_call" | custom-call | flops 805306368 | bytes 1179648 | tf_op jit(solution)/shard_map/pallas_call | solution.py:269
  45.6 3.5 %shard_map.90.inverse = f32[128,128]{1,0:T(8,128)S(1)} custom-call(f32[128,128]{1,0:T(8,128)S(1)} %sub.9.mine, f32[128,128]{1,0:T(8,128)S(1)} %slice_subtract_fusion.theirs), custom_call_target="tpu_custom_call" | custom-call | flops 6442450944 | bytes 196608 | tf_op jit(solution)/shard_map/pallas_call | solution.py:269
  50.0 2.8 %collective-permute-start.9 = (f32[128,256]{1,0:T(8,128)S(1)}, f32[128,256]{1,0:T(8,128)S(1)}, u32[]{:S(2)}, u32[]{:S(2)}) collective-permute-start(f32[128,256]{1,0:T(8,128)S(1)} %get-tuple-element.51.refs_2_), channel_id=1, source_target_pairs={{1,2},{2,1},{3,4},{4,3},{5,6},{6,5},{9,10},{10,9},{11,12},{12,11},... | collective-permute-start | bytes 393224 | tf_op jit(solution)/shard_map/ppermute | solution.py:288
  52.8 4.1 %collective-permute-start.12 = (f32[128,128]{1,0:T(8,128)S(1)}, f32[128,128]{1,0:T(8,128)S(1)}, u32[]{:S(2)}, u32[]{:S(2)}) collective-permute-start(f32[128,128]{1,0:T(8,128)S(1)} %get-tuple-element.57), channel_id=1, source_target_pairs={{0,16},{1,17},{2,18},{3,19},{4,20},{5,21},{6,22},{7,23},{8,24},{9,... | collective-permute-start | bytes 196616 | tf_op jit(solution)/shard_map/ppermute | solution.py:288
  58.6 3.3 %collective-permute-start.10 = (f32[128,128]{1,0:T(8,128)S(1)}, f32[128,128]{1,0:T(8,128)S(1)}, u32[]{:S(2)}, u32[]{:S(2)}) collective-permute-start(f32[128,128]{1,0:T(8,128)S(1)} %get-tuple-element.55.mine.refs_0_), channel_id=1, source_target_pairs={{0,16},{1,17},{2,18},{3,19},{4,20},{5,21},{6,22},{7,23},{8,24},{9,... | collective-permute-start | bytes 196616 | tf_op jit(solution)/shard_map/ppermute | solution.py:288
  62.7 1.5 %collective-permute-start.14 = (f32[128,128]{1,0:T(8,128)S(1)}, f32[128,128]{1,0:T(8,128)S(1)}, u32[]{:S(2)}, u32[]{:S(2)}) collective-permute-start(f32[128,128]{1,0:T(8,128)S(1)} %get-tuple-element.59.refs_5_), channel_id=1, source_target_pairs={{0,8},{1,9},{2,10},{3,11},{4,12},{5,13},{6,14},{7,15},{8,0},{9,1},... | collective-permute-start | bytes 196616 | tf_op jit(solution)/shard_map/ppermute | solution.py:288
  64.2 2.2 %collective-permute-done.10.theirs.refs_3_ = f32[128,128]{1,0:T(8,128)S(1)} collective-permute-done((f32[128,128]{1,0:T(8,128)S(1)}, f32[128,128]{1,0:T(8,128)S(1)}, u32[]{:S(2)}, u32[]{:S(2)}) %collective-permute-start.10) | collective-permute-done | bytes 65568 | tf_op jit(solution)/shard_map/ppermute | solution.py:288
  66.4 3.5 %shard_map.95.inverse = f32[128,128]{1,0:T(8,128)S(1)} custom-call(f32[128,128]{1,0:T(8,128)S(1)} %get-tuple-element.55.mine.refs_0_, f32[128,128]{1,0:T(8,128)S(1)} %collective-permute-done.10.theirs.refs_3_), custom_call_target="tpu_custom_call" | custom-call | bytes 196608 | tf_op jit(solution)/shard_map/pallas_call | solution.py:269
  70.0 1.6 %shard_map.97 = (f32[1,2,256,128]{3,2,1,0:T(8,128)}, f32[1,128,256]{2,1,0:T(8,128)}, f32[1,128,256]{2,1,0:T(8,128)}) custom-call(f32[128,128]{1,0:T(8,128)S(1)} %shard_map.95.inverse, f32[128,128]{1,0:T(8,128)S(1)} %get-tuple-element.55.mine.refs_0_, f32[128,128]{1,0:T(8,128)S(1)} %get-tuple-element.58.refs_1_, f32[128,256]{1,0:T(8,128)S(1)} %get-tuple-element.51.refs_2_, ...), custom_call_target="tpu_custom_call" | custom-call | bytes 1245184 | tf_op jit(solution)/shard_map/pallas_call | solution.py:269
  (37 shorter events, 7.4 us)
Async XLA Ops:
  0.6 18.5 %collective-permute-start = (f32[512,256]{1,0:T(8,128)}, f32[512,256]{1,0:T(8,128)S(1)}, u32[]{:S(2)}, u32[]{:S(2)}) collective-permute-start(f32[512,256]{1,0:T(8,128)} %probes.5), channel_id=1, source_target_pairs={{1,24},{2,25},{3,26},{4,27},{5,28},{6,29},{7,30},{8,0},{9,1},{10,2... | collective-permute-start | bytes 1572872 | tf_op jit(solution)/shard_map/ppermute | solution.py:288
  6.5 1.6 %copy-start = (f32[512,2,512]{2,1,0:T(2,128)S(1)}, f32[512,2,512]{2,1,0:T(2,128)}, u32[]{:S(2)}) copy-start(f32[512,2,512]{2,1,0:T(2,128)} %param.7) | copy-start | bytes 6291460
  8.1 1.0 %copy-start.3 = (f32[512,256]{1,0:T(8,128)S(1)}, f32[512,256]{1,0:T(8,128)}, u32[]{:S(2)}) copy-start(f32[512,256]{1,0:T(8,128)} %probes.5) | copy-start | bytes 1572868
  9.1 2.8 %copy-start.2 = (f32[512,256]{1,0:T(8,128)S(1)}, f32[512,256]{1,0:T(8,128)}, u32[]{:S(2)}) copy-start(f32[512,256]{1,0:T(8,128)} %samples.1) | copy-start | bytes 1572868
  10.0 14.6 %collective-permute-start.1 = (f32[512,128]{1,0:T(8,128)S(1)}, f32[512,128]{1,0:T(8,128)S(1)}, u32[]{:S(2)}, u32[]{:S(2)}) collective-permute-start(f32[512,128]{1,0:T(8,128)S(1)} %shard_map.86), channel_id=1, source_target_pairs={{0,8},{1,9},{2,10},{3,11},{4,12},{5,13},{6,14},{7,15},{8,16},{9,17... | collective-permute-start | bytes 786440 | tf_op jit(solution)/shard_map/ppermute | solution.py:288
  13.6 11.1 %copy-start.4 = (f32[512,256]{1,0:T(8,128)S(1)}, f32[512,256]{1,0:T(8,128)}, u32[]{:S(2)}) copy-start(f32[512,256]{1,0:T(8,128)} %probes.5) | copy-start | bytes 1572868
  20.3 13.6 %copy-start.1 = (f32[1,3,2,128,128]{4,3,2,1,0:T(8,128)S(1)}, f32[1,3,2,128,128]{4,3,2,1,0:T(8,128)}, u32[]{:S(2)}) copy-start(f32[1,3,2,128,128]{4,3,2,1,0:T(8,128)} %couplings.5) | copy-start | bytes 1179652
  20.3 13.6 %copy-start.5 = (s32[1,3]{1,0:T(1,128)S(1)}, s32[1,3]{1,0:T(1,128)}, u32[]{:S(2)}) copy-start(s32[1,3]{1,0:T(1,128)} %slots.5) | copy-start | bytes 40
  20.3 13.6 %collective-permute-start.3 = (f32[512,128]{1,0:T(8,128)S(1)}, f32[512,128]{1,0:T(8,128)S(1)}, u32[]{:S(2)}, u32[]{:S(2)}) collective-permute-start(f32[512,128]{1,0:T(8,128)S(1)} %get-tuple-element.39), channel_id=1, source_target_pairs={{0,8},{1,9},{2,10},{3,11},{4,12},{5,13},{6,14},{7,15},{8,16},{9,17... | collective-permute-start | bytes 786440 | tf_op jit(solution)/shard_map/ppermute | solution.py:288
  28.7 4.8 %collective-permute-start.2 = (f32[128,256]{1,0:T(8,128)S(1)}, f32[128,256]{1,0:T(8,128)S(1)}, u32[]{:S(2)}, u32[]{:S(2)}) collective-permute-start(f32[128,256]{1,0:T(8,128)S(1)} %get-tuple-element.38.mine.mine_probes), channel_id=1, source_target_pairs={{1,0},{2,1},{3,2},{4,3},{5,4},{6,5},{7,6},{9,8},{10,9},{11,10},{12... | collective-permute-start | bytes 393224 | tf_op jit(solution)/shard_map/ppermute | solution.py:288
  30.9 13.7 %collective-permute-start.6 = (f32[128,384]{1,0:T(8,128)S(1)}, f32[128,384]{1,0:T(8,128)S(1)}, u32[]{:S(2)}, u32[]{:S(2)}) collective-permute-start(f32[128,384]{1,0:T(8,128)S(1)} %pad_maximum_fusion), channel_id=1, source_target_pairs={{0,8},{1,9},{2,10},{3,11},{4,12},{5,13},{6,14},{7,15},{8,0},{9,1},... | collective-permute-start | bytes 589832 | tf_op jit(solution)/shard_map/ppermute | solution.py:288
  34.7 9.9 %collective-permute-start.4 = (f32[128,128]{1,0:T(8,128)S(1)}, f32[128,128]{1,0:T(8,128)S(1)}, u32[]{:S(2)}, u32[]{:S(2)}) collective-permute-start(f32[128,128]{1,0:T(8,128)S(1)} %shard_map.89), channel_id=1, source_target_pairs={{0,16},{1,17},{2,18},{3,19},{4,20},{5,21},{6,22},{7,23},{8,24},{9,... | collective-permute-start | bytes 196616 | tf_op jit(solution)/shard_map/ppermute | solution.py:288
  39.4 6.2 %collective-permute-start.5 = (f32[128,128]{1,0:T(8,128)S(1)}, f32[128,128]{1,0:T(8,128)S(1)}, u32[]{:S(2)}, u32[]{:S(2)}) collective-permute-start(f32[128,128]{1,0:T(8,128)S(1)} %shard_map.89), channel_id=1, source_target_pairs={{0,24},{1,25},{2,26},{3,27},{4,28},{5,29},{6,30},{7,31},{8,16},{9,... | collective-permute-start | bytes 196616 | tf_op jit(solution)/shard_map/ppermute | solution.py:288
  41.1 8.0 %collective-permute-start.7 = (f32[128,128]{1,0:T(8,128)S(1)}, f32[128,128]{1,0:T(8,128)S(1)}, u32[]{:S(2)}, u32[]{:S(2)}) collective-permute-start(f32[128,128]{1,0:T(8,128)S(1)} %shard_map.91), channel_id=1, source_target_pairs={{0,16},{1,17},{2,18},{3,19},{4,20},{5,21},{6,22},{7,23},{8,24},{9,... | collective-permute-start | bytes 196616 | tf_op jit(solution)/shard_map/ppermute | solution.py:288
  49.9 7.8 %collective-permute-start.8 = (f32[128,256]{1,0:T(8,128)S(1)}, f32[128,256]{1,0:T(8,128)S(1)}, u32[]{:S(2)}, u32[]{:S(2)}) collective-permute-start(f32[128,256]{1,0:T(8,128)S(1)} %get-tuple-element.51.refs_2_), channel_id=1, source_target_pairs={{0,1},{1,0},{2,3},{3,2},{4,5},{5,4},{6,7},{7,6},{8,9},{9,8},{10,11... | collective-permute-start | bytes 393224 | tf_op jit(solution)/shard_map/ppermute | solution.py:288
  50.0 7.7 %collective-permute-start.9 = (f32[128,256]{1,0:T(8,128)S(1)}, f32[128,256]{1,0:T(8,128)S(1)}, u32[]{:S(2)}, u32[]{:S(2)}) collective-permute-start(f32[128,256]{1,0:T(8,128)S(1)} %get-tuple-element.51.refs_2_), channel_id=1, source_target_pairs={{1,2},{2,1},{3,4},{4,3},{5,6},{6,5},{9,10},{10,9},{11,12},{12,11},... | collective-permute-start | bytes 393224 | tf_op jit(solution)/shard_map/ppermute | solution.py:288
  52.8 9.1 %collective-permute-start.12 = (f32[128,128]{1,0:T(8,128)S(1)}, f32[128,128]{1,0:T(8,128)S(1)}, u32[]{:S(2)}, u32[]{:S(2)}) collective-permute-start(f32[128,128]{1,0:T(8,128)S(1)} %get-tuple-element.57), channel_id=1, source_target_pairs={{0,16},{1,17},{2,18},{3,19},{4,20},{5,21},{6,22},{7,23},{8,24},{9,... | collective-permute-start | bytes 196616 | tf_op jit(solution)/shard_map/ppermute | solution.py:288
  56.9 5.0 %collective-permute-start.11 = (f32[128,128]{1,0:T(8,128)S(1)}, f32[128,128]{1,0:T(8,128)S(1)}, u32[]{:S(2)}, u32[]{:S(2)}) collective-permute-start(f32[128,128]{1,0:T(8,128)S(1)} %sub.11._last.mine_last), channel_id=1, source_target_pairs={{0,8},{1,9},{2,10},{3,11},{4,12},{5,13},{6,14},{7,15},{8,0},{9,1},... | collective-permute-start | bytes 196616 | tf_op jit(solution)/shard_map/ppermute | solution.py:288
  58.6 7.8 %collective-permute-start.10 = (f32[128,128]{1,0:T(8,128)S(1)}, f32[128,128]{1,0:T(8,128)S(1)}, u32[]{:S(2)}, u32[]{:S(2)}) collective-permute-start(f32[128,128]{1,0:T(8,128)S(1)} %get-tuple-element.55.mine.refs_0_), channel_id=1, source_target_pairs={{0,16},{1,17},{2,18},{3,19},{4,20},{5,21},{6,22},{7,23},{8,24},{9,... | collective-permute-start | bytes 196616 | tf_op jit(solution)/shard_map/ppermute | solution.py:288
  62.4 7.5 %collective-permute-start.13 = (f32[128,128]{1,0:T(8,128)S(1)}, f32[128,128]{1,0:T(8,128)S(1)}, u32[]{:S(2)}, u32[]{:S(2)}) collective-permute-start(f32[128,128]{1,0:T(8,128)S(1)} %get-tuple-element.58.refs_1_), channel_id=1, source_target_pairs={{0,16},{1,17},{2,18},{3,19},{4,20},{5,21},{6,22},{7,23},{8,24},{9,... | collective-permute-start | bytes 196616 | tf_op jit(solution)/shard_map/ppermute | solution.py:288
  62.7 7.3 %collective-permute-start.14 = (f32[128,128]{1,0:T(8,128)S(1)}, f32[128,128]{1,0:T(8,128)S(1)}, u32[]{:S(2)}, u32[]{:S(2)}) collective-permute-start(f32[128,128]{1,0:T(8,128)S(1)} %get-tuple-element.59.refs_5_), channel_id=1, source_target_pairs={{0,8},{1,9},{2,10},{3,11},{4,12},{5,13},{6,14},{7,15},{8,0},{9,1},... | collective-permute-start | bytes 196616 | tf_op jit(solution)/shard_map/ppermute | solution.py:288

commit v14 on v13

--- a/solution.py
+++ b/solution.py
@@ -147,13 +147,12 @@
     columns = far.shape[1]
     block = rest[...] - handed[...]
     far[...] = block
-    gram = dot(block, block, 0, 0)
-    cross = dot(block, probes[...], 0, 0)
-    factor = inverse_factor(gram, scratch)
+    products = dot(block, jnp.concatenate([block, probes[...]], axis=1), 0, 0)
+    factor = inverse_factor(products[:, :columns], scratch)
     inverse[...] = factor
-    coef = dot(factor, jnp.concatenate([gram, cross], axis=1))
+    coef = dot(factor, products)
+    probe_coef[...] = coef[:, columns:]
     sample_coef[...] = coef[:, :columns]
-    probe_coef[...] = coef[:, columns:]
 
 
 def leaf_last_kernel(rest, handed, far, inverse, basis, sample_coef):
@@ -200,57 +199,72 @@
     inverse[...] = inverse_factor(gram, scratch)
 
 
-def write_basis(level, at, mine, theirs, inverse, bases):
+def basis_of(level, mine, theirs, inverse, out):
     size = mine.shape[0]
     own = (lax.axis_index("leaf") >> level - 1) & 1
     block = dot(jnp.concatenate([mine, theirs], axis=0), inverse, 1, 1)
-    bases[0, at, pl.ds(pl.multiple_of(own * size, size), size), :] = block[:size]
-    bases[0, at, pl.ds(pl.multiple_of((1 - own) * size, size), size), :] = block[size:]
+    out[pl.ds(pl.multiple_of(own * size, size), size), :] = block[:size]
+    out[pl.ds(pl.multiple_of((1 - own) * size, size), size), :] = block[size:]
 
 
 def basis_kernel(level, inverse, mine, theirs, basis):
-    write_basis(level, 0, mine[...], theirs[...], inverse[...], basis)
-
-
-def level_coefs(inverse, mine, theirs):
-    own = jnp.concatenate(mine, axis=1)
-    sibling = jnp.concatenate(theirs, axis=1)
-    size = inverse.shape[0]
+    basis_of(level, mine[...], theirs[...], inverse[...], basis)
+
+
+def level_products(inverse, size, own, sibling):
+    own, sibling = jnp.concatenate(own, axis=1), jnp.concatenate(sibling, axis=1)
     both = jnp.concatenate([own, sibling], axis=0)
     return dot(inverse, dot(both[:, :size], both, 0, 0))
 
 
-def node_kernel(inverse, mine, mine_probes, theirs, theirs_probes, _last, first, probe_coef, half):
-    columns = first.shape[1]
-    coef = level_coefs(inverse[...], (mine[...], mine_probes[...]), (theirs[...], theirs_probes[...]))
-    first[...] = coef[:, :columns]
-    probe_coef[...] = coef[:, columns:]
+def node_first_kernel(inverse, mine, theirs, first):
+    both = jnp.concatenate([mine[...], theirs[...]], axis=0)
+    first[...] = dot(inverse[...], dot(both, both, 0, 0))
+
+
+def node_kernel(inverse, mine, theirs, mine_probes, theirs_probes, _last, probe_coef, half):
+    nodes = jnp.concatenate([mine[...], theirs[...]], axis=0)
+    probes = jnp.concatenate([mine_probes[...], theirs_probes[...]], axis=0)
+    coef = dot(inverse[...], dot(nodes, probes, 0, 0))
+    probe_coef[...] = coef
     width = half.shape[1]
     upper = lax.axis_index("leaf") & 1 == 1
-    half[...] = jnp.where(upper, coef[:, columns + width :], coef[:, columns : columns + width])
+    half[...] = jnp.where(upper, coef[:, width:], coef[:, :width])
 
 
 def node_last_kernel(inverse, mine, mine_last, theirs, theirs_last, term, *refs):
-    mine, theirs = mine[...], theirs[...]
-    both = dot(mine, mine_last[...], 0, 0) + dot(theirs, theirs_last[...], 0, 0)
+    nodes = jnp.concatenate([mine[...], theirs[...]], axis=0)
+    both = jnp.concatenate([mine_last[...], theirs_last[...]], axis=0)
     last = refs[0] if len(refs) == 1 else refs[1]
-    last[...] = dot(inverse[...], both) - term[...]
+    last[...] = dot(inverse[...], dot(nodes, both, 0, 0)) - term[...]
 
 
 def top_kernel(level, inverse, *refs):
+    mine, theirs, (half, passed) = refs[:3], refs[3:5], refs[5:7]
+    earlier, (bases, samples, probe_coef, basis, coefs, done) = refs[7:-6], refs[-6:]
+    copies = [
+        pltpu.make_async_copy(one, bases.at[0, at], done.at[at]) for at, one in enumerate(earlier)
+    ]
+    for copy in copies:
+        copy.start()
     factor = inverse[...]
-    earlier, (bases, samples, probe_coef) = refs[7:-3], refs[-3:]
-    mine, theirs, (half, passed) = [r[...] for r in refs[:3]], [r[...] for r in refs[3:5]], refs[5:7]
+    mine, theirs = [ref[...] for ref in mine], [ref[...] for ref in theirs]
+    basis_of(level, mine[0], theirs[0], factor, basis)
+    at = len(earlier)
+    copies.append(pltpu.make_async_copy(basis, bases.at[0, at], done.at[at]))
+    copies[-1].start()
     upper = lax.axis_index("leaf") & 1 == 1
     theirs.append(jnp.where(upper, passed[...], half[...]))
     theirs.append(jnp.where(upper, half[...], passed[...]))
-    coef = level_coefs(factor, mine, theirs)
+    coef = level_products(factor, factor.shape[0], mine, theirs)
     width = samples.shape[2]
-    samples[0] = coef[:, :width]
-    probe_coef[0] = coef[:, width:]
-    for at, done in enumerate(earlier):
-        bases[0, at] = done[0, 0]
-    write_basis(level, len(earlier), mine[0], theirs[0], factor, bases)
+    coefs[0] = coef[:, :width]
+    coefs[1] = coef[:, width:]
+    for at, out in enumerate((samples, probe_coef)):
+        copies.append(pltpu.make_async_copy(coefs.at[at], out.at[0], done.at[level + at]))
+        copies[-1].start()
+    for copy in copies:
+        copy.wait()
 
 
 VMEM = pl.BlockSpec(memory_space=pltpu.VMEM)
@@ -351,15 +365,16 @@
                 functools.partial(term_kernel, level, 0), [square], couplings, probe_coef, away,
                 slots=node_slot,
             )
-            (term_last,) = call(
-                functools.partial(term_kernel, level, columns), [square_last],
-                couplings, probe_coef, away, slots=node_slot,
-            )
             if level == 1:
                 leaf_basis, last = call(
                     leaf_last_kernel, [tall, square_last], rest_last, handed_last, far, inverse,
                     flops=work,
                 )
+            away, last = lax.optimization_barrier((away, last))
+            (term_last,) = call(
+                functools.partial(term_kernel, level, columns), [square_last],
+                couplings, probe_coef, away, slots=node_slot,
+            )
             term_first, term_twin = swapped(term_first, 2 * copies), swapped(term_first, 3 * copies)
             term_first, term_twin, theirs_coefs, last = lax.optimization_barrier(
                 (term_first, term_twin, theirs_coefs, last)
@@ -395,25 +410,31 @@
                 )
                 theirs_passed = swapped(theirs_half, 1)
         theirs_last = swapped(last, copies)
-        mine = first, last, probe_coef
         (inverse,) = call(
             factor_kernel, [square], first, theirs_first, flops=8 * work if count == 4 else 0, **scratch
         )
         if level < levels:
             ancestors += call(
-                functools.partial(basis_kernel, level), [(1, 1, 2 * columns, columns)],
+                functools.partial(basis_kernel, level), [(2 * columns, columns)],
                 inverse, first, theirs_first,
             )
             below = inverse, first, last, theirs_first, theirs_last
-            first, probe_coef, half = call(
-                node_kernel, [square, (columns, width), (columns, width // 2)],
-                inverse, first, probe_coef, theirs_first, theirs_probe, last,
+            probe_coef, half = call(
+                node_kernel, [(columns, width), (columns, width // 2)],
+                inverse, first, theirs_first, probe_coef, theirs_probe, last,
                 specs=[VMEM] * 5 + [ANY],
             )
+            (first,) = call(node_first_kernel, [square], inverse, first, theirs_first)
     transfer_bases, top_samples, top_probes = call(
         functools.partial(top_kernel, levels),
         [(1, levels, 2 * columns, columns), (1, columns, width), (1, columns, width)],
-        inverse, *mine, theirs_first, theirs_last, theirs_half, theirs_passed, *ancestors,
+        inverse, first, last, probe_coef, theirs_first, theirs_last, theirs_half, theirs_passed,
+        *ancestors, out_specs=[ANY] * 3,
+        scratch_shapes=[
+            pltpu.VMEM((2 * columns, columns), jnp.float32),
+            pltpu.VMEM((2, columns, width), jnp.float32),
+            pltpu.SemaphoreType.DMA((levels + 2,)),
+        ],
     )
     return (leaf_basis, transfer_bases, top_samples, top_probes)
 

time: 71.9 us -> 71 us (0.987)
  the two profiles are of different devices: /device:TPU:4 before, /device:TPU:28 now
where the time goes in v14:
time: 71 us; the launch traced here: 70.7 us
  starting transfers between devices  25.9 us (36%)
  Pallas kernels  22.7 us (32%)
  waiting for transfers between devices  18.2 us (26%)
  local copies, waits for them, and re-layouts  2.66 us (4%)
  between operations  1.07 us (2%)
    ppermute x15, starting transfers between devices, permuted(): return lax.ppermute(value, BOTH, pairs)  25.9 us
    pallas_call x15, Pallas kernels, call(): pl.pallas_call(kernel, out_shape=outs, in_specs=specs, out_specs=out_spec...  22.7 us
    ppermute x15, waiting for transfers between devices, permuted(): return lax.ppermute(value, BOTH, pairs)  18.2 us
    unnamed x12, local copies, waits for them, and re-layouts  2.65 us
  transfers between devices with their start and end apart: 15, of which 6 were waited for; matrix products, arithmetic and copies ran while one was open for 0% of the time, Pallas kernels for 29%

profile of v14, /device:TPU:28, one launch (start us, length us, event | category | flops | bytes accessed | tf_op | source)
XLA Modules:
  0.0 70.7 jit_solution(8239068817307953414)
XLA Ops:
  0.6 2.4 %collective-permute-start = (f32[512,256]{1,0:T(8,128)}, f32[512,256]{1,0:T(8,128)S(1)}, u32[]{:S(2)}, u32[]{:S(2)}) collective-permute-start(f32[512,256]{1,0:T(8,128)} %probes.5), channel_id=1, source_target_pairs={{1,24},{2,25},{3,26},{4,27},{5,28},{6,29},{7,30},{8,0},{9,1},{10,2... | collective-permute-start | bytes 1572872 | tf_op jit(solution)/shard_map/ppermute | solution.py:302
  3.0 1.6 %copy-done = f32[512,2,512]{2,1,0:T(2,128)S(1)} copy-done((f32[512,2,512]{2,1,0:T(2,128)S(1)}, f32[512,2,512]{2,1,0:T(2,128)}, u32[]{:S(2)}) %copy-start) | copy-done | bytes 2097176
  4.6 1.0 %copy-done.3 = f32[512,256]{1,0:T(8,128)S(1)} copy-done((f32[512,256]{1,0:T(8,128)S(1)}, f32[512,256]{1,0:T(8,128)}, u32[]{:S(2)}) %copy-start.3) | copy-done | bytes 524312
  6.5 5.0 %collective-permute-start.1 = (f32[512,128]{1,0:T(8,128)S(1)}, f32[512,128]{1,0:T(8,128)S(1)}, u32[]{:S(2)}, u32[]{:S(2)}) collective-permute-start(f32[512,128]{1,0:T(8,128)S(1)} %shard_map.86), channel_id=1, source_target_pairs={{0,8},{1,9},{2,10},{3,11},{4,12},{5,13},{6,14},{7,15},{8,16},{9,17... | collective-permute-start | bytes 786440 | tf_op jit(solution)/shard_map/ppermute | solution.py:302
  11.5 1.6 %shard_map.84 = (f32[512,256]{1,0:T(8,128)S(1)}, f32[512,128]{1,0:T(8,128)S(1)}) custom-call(f32[4096,128]{1,0:T(8,128)S(1)} %bitcast.6, f32[512,256]{1,0:T(8,128)S(1)} %copy-done.3, f32[512,256]{1,0:T(8,128)S(1)} %copy-done.2), custom_call_target="tpu_custom_call" | custom-call | flops 805306368 | bytes 3932160 | tf_op jit(solution)/shard_map/pallas_call | solution.py:283
  13.2 4.9 %collective-permute-done.following = f32[512,256]{1,0:T(8,128)S(1)} collective-permute-done((f32[512,256]{1,0:T(8,128)}, f32[512,256]{1,0:T(8,128)S(1)}, u32[]{:S(2)}, u32[]{:S(2)}) %collective-permute-start) | collective-permute-done | bytes 524320 | tf_op jit(solution)/shard_map/ppermute | solution.py:302
  18.0 1.2 %shard_map.85 = (f32[512,128]{1,0:T(8,128)S(1)}, f32[512,128]{1,0:T(8,128)S(1)}, f32[512,128]{1,0:T(8,128)S(1)}) custom-call(f32[4096,128]{1,0:T(8,128)S(1)} %bitcast.7, f32[512,256]{1,0:T(8,128)S(1)} %get-tuple-element.35.rest, f32[512,256]{1,0:T(8,128)S(1)} %collective-permute-done.following, ...), custom_call_target="tpu_custom_call", output_to_operand_aliasing={{2}: (3, {})} | custom-call | flops 805306368 | bytes 4194304 | tf_op jit(solution)/shard_map/pallas_call | solution.py:283
  19.2 2.1 %collective-permute-start.3 = (f32[512,128]{1,0:T(8,128)S(1)}, f32[512,128]{1,0:T(8,128)S(1)}, u32[]{:S(2)}, u32[]{:S(2)}) collective-permute-start(f32[512,128]{1,0:T(8,128)S(1)} %get-tuple-element.40), channel_id=1, source_target_pairs={{0,8},{1,9},{2,10},{3,11},{4,12},{5,13},{6,14},{7,15},{8,16},{9,17... | collective-permute-start | bytes 786440 | tf_op jit(solution)/shard_map/ppermute | solution.py:302
  21.3 3.1 %collective-permute-done.1.handed = f32[512,128]{1,0:T(8,128)S(1)} collective-permute-done((f32[512,128]{1,0:T(8,128)S(1)}, f32[512,128]{1,0:T(8,128)S(1)}, u32[]{:S(2)}, u32[]{:S(2)}) %collective-permute-start.1) | collective-permute-done | bytes 262176 | tf_op jit(solution)/shard_map/ppermute | solution.py:302
  24.4 4.2 %shard_map.87 = (f32[512,128]{1,0:T(8,128)S(1)}, f32[128,128]{1,0:T(8,128)S(1)}, f32[128,128]{1,0:T(8,128)S(1)}, f32[128,256]{1,0:T(8,128)S(1)}) custom-call(f32[512,128]{1,0:T(8,128)S(1)} %get-tuple-element.38.rest, f32[512,128]{1,0:T(8,128)S(1)} %collective-permute-done.1.handed, f32[512,256]{1,0:T(8,128)S(1)} %copy-done.4), custom_call_target="tpu_custom_call" | custom-call | flops 805306368 | bytes 1572864 | tf_op jit(solution)/shard_map/pallas_call | solution.py:283
  28.6 1.9 %collective-permute-start.2 = (f32[128,256]{1,0:T(8,128)S(1)}, f32[128,256]{1,0:T(8,128)S(1)}, u32[]{:S(2)}, u32[]{:S(2)}) collective-permute-start(f32[128,256]{1,0:T(8,128)S(1)} %get-tuple-element.39.mine.mine_probes), channel_id=1, source_target_pairs={{1,0},{2,1},{3,2},{4,3},{5,4},{6,5},{7,6},{9,8},{10,9},{11,10},{12... | collective-permute-start | bytes 393224 | tf_op jit(solution)/shard_map/ppermute | solution.py:302
  31.3 4.5 %collective-permute-done.2.away = f32[128,256]{1,0:T(8,128)S(1)} collective-permute-done((f32[128,256]{1,0:T(8,128)S(1)}, f32[128,256]{1,0:T(8,128)S(1)}, u32[]{:S(2)}, u32[]{:S(2)}) %collective-permute-start.2) | collective-permute-done | bytes 131104 | tf_op jit(solution)/shard_map/ppermute | solution.py:302
  36.8 3.0 %collective-permute-start.5 = (f32[128,128]{1,0:T(8,128)S(1)}, f32[128,128]{1,0:T(8,128)S(1)}, u32[]{:S(2)}, u32[]{:S(2)}) collective-permute-start(f32[128,128]{1,0:T(8,128)S(1)} %shard_map.89), channel_id=1, source_target_pairs={{0,24},{1,25},{2,26},{3,27},{4,28},{5,29},{6,30},{7,31},{8,16},{9,... | collective-permute-start | bytes 196616 | tf_op jit(solution)/shard_map/ppermute | solution.py:302
  39.8 1.5 %shard_map.88 = (f32[512,128]{1,0:T(8,128)}, f32[128,128]{1,0:T(8,128)S(1)}) custom-call(f32[512,128]{1,0:T(8,128)S(1)} %get-tuple-element.37.rest, f32[512,128]{1,0:T(8,128)S(1)} %collective-permute-done.3.handed, f32[512,128]{1,0:T(8,128)S(1)} %get-tuple-element.42.far, f32[128,128]{1,0:T(8,128)S(1)} %get-tuple-element.43.inverse), custom_call_target="tpu_custom_call" | custom-call | flops 805306368 | bytes 1179648 | tf_op jit(solution)/shard_map/pallas_call | solution.py:283
  42.2 2.2 %collective-permute-done.4 = f32[128,128]{1,0:T(8,128)S(1)} collective-permute-done((f32[128,128]{1,0:T(8,128)S(1)}, f32[128,128]{1,0:T(8,128)S(1)}, u32[]{:S(2)}, u32[]{:S(2)}) %collective-permute-start.4) | collective-permute-done | bytes 65568 | tf_op jit(solution)/shard_map/ppermute | solution.py:302
  44.4 3.5 %shard_map.90.inverse = f32[128,128]{1,0:T(8,128)S(1)} custom-call(f32[128,128]{1,0:T(8,128)S(1)} %sub.9.mine, f32[128,128]{1,0:T(8,128)S(1)} %slice_subtract_fusion.theirs), custom_call_target="tpu_custom_call" | custom-call | flops 6442450944 | bytes 196608 | tf_op jit(solution)/shard_map/pallas_call | solution.py:283
  48.8 2.6 %collective-permute-start.9 = (f32[128,256]{1,0:T(8,128)S(1)}, f32[128,256]{1,0:T(8,128)S(1)}, u32[]{:S(2)}, u32[]{:S(2)}) collective-permute-start(f32[128,256]{1,0:T(8,128)S(1)} %get-tuple-element.54.refs_2_), channel_id=1, source_target_pairs={{1,2},{2,1},{3,4},{4,3},{5,6},{6,5},{9,10},{10,9},{11,12},{12,11},... | collective-permute-start | bytes 393224 | tf_op jit(solution)/shard_map/ppermute | solution.py:302
  51.5 2.0 %collective-permute-start.12 = (f32[128,128]{1,0:T(8,128)S(1)}, f32[128,128]{1,0:T(8,128)S(1)}, u32[]{:S(2)}, u32[]{:S(2)}) collective-permute-start(f32[128,128]{1,0:T(8,128)S(1)} %get-tuple-element.59), channel_id=1, source_target_pairs={{0,16},{1,17},{2,18},{3,19},{4,20},{5,21},{6,22},{7,23},{8,24},{9,... | collective-permute-start | bytes 196616 | tf_op jit(solution)/shard_map/ppermute | solution.py:302
  56.9 2.1 %collective-permute-start.10 = (f32[128,128]{1,0:T(8,128)S(1)}, f32[128,128]{1,0:T(8,128)S(1)}, u32[]{:S(2)}, u32[]{:S(2)}) collective-permute-start(f32[128,128]{1,0:T(8,128)S(1)} %get-tuple-element.57.mine.refs_0_), channel_id=1, source_target_pairs={{0,16},{1,17},{2,18},{3,19},{4,20},{5,21},{6,22},{7,23},{8,24},{9,... | collective-permute-start | bytes 196616 | tf_op jit(solution)/shard_map/ppermute | solution.py:302
  59.5 1.2 %collective-permute-start.13 = (f32[128,128]{1,0:T(8,128)S(1)}, f32[128,128]{1,0:T(8,128)S(1)}, u32[]{:S(2)}, u32[]{:S(2)}) collective-permute-start(f32[128,128]{1,0:T(8,128)S(1)} %get-tuple-element.60.refs_1_), channel_id=1, source_target_pairs={{0,16},{1,17},{2,18},{3,19},{4,20},{5,21},{6,22},{7,23},{8,24},{9,... | collective-permute-start | bytes 196616 | tf_op jit(solution)/shard_map/ppermute | solution.py:302
  60.7 2.0 %collective-permute-start.14 = (f32[128,128]{1,0:T(8,128)S(1)}, f32[128,128]{1,0:T(8,128)S(1)}, u32[]{:S(2)}, u32[]{:S(2)}) collective-permute-start(f32[128,128]{1,0:T(8,128)S(1)} %get-tuple-element.61.refs_5_), channel_id=1, source_target_pairs={{0,8},{1,9},{2,10},{3,11},{4,12},{5,13},{6,14},{7,15},{8,0},{9,1},... | collective-permute-start | bytes 196616 | tf_op jit(solution)/shard_map/ppermute | solution.py:302
  62.7 2.7 %collective-permute-done.10.theirs.refs_3_ = f32[128,128]{1,0:T(8,128)S(1)} collective-permute-done((f32[128,128]{1,0:T(8,128)S(1)}, f32[128,128]{1,0:T(8,128)S(1)}, u32[]{:S(2)}, u32[]{:S(2)}) %collective-permute-start.10) | collective-permute-done | bytes 65568 | tf_op jit(solution)/shard_map/ppermute | solution.py:302
  65.4 3.5 %shard_map.96.inverse = f32[128,128]{1,0:T(8,128)S(1)} custom-call(f32[128,128]{1,0:T(8,128)S(1)} %get-tuple-element.57.mine.refs_0_, f32[128,128]{1,0:T(8,128)S(1)} %collective-permute-done.10.theirs.refs_3_), custom_call_target="tpu_custom_call" | custom-call | bytes 196608 | tf_op jit(solution)/shard_map/pallas_call | solution.py:283
  68.9 1.6 %shard_map.98 = (f32[1,2,256,128]{3,2,1,0:T(8,128)}, f32[1,128,256]{2,1,0:T(8,128)}, f32[1,128,256]{2,1,0:T(8,128)}) custom-call(f32[128,128]{1,0:T(8,128)S(1)} %shard_map.96.inverse, f32[128,128]{1,0:T(8,128)S(1)} %get-tuple-element.57.mine.refs_0_, f32[128,128]{1,0:T(8,128)S(1)} %get-tuple-element.60.refs_1_, f32[128,256]{1,0:T(8,128)S(1)} %get-tuple-element.54.refs_2_, ...), custom_call_target="tpu_custom_call" | custom-call | bytes 1245184 | tf_op jit(solution)/shard_map/pallas_call | solution.py:283
  (38 shorter events, 8.3 us)
Async XLA Ops:
  0.6 17.4 %collective-permute-start = (f32[512,256]{1,0:T(8,128)}, f32[512,256]{1,0:T(8,128)S(1)}, u32[]{:S(2)}, u32[]{:S(2)}) collective-permute-start(f32[512,256]{1,0:T(8,128)} %probes.5), channel_id=1, source_target_pairs={{1,24},{2,25},{3,26},{4,27},{5,28},{6,29},{7,30},{8,0},{9,1},{10,2... | collective-permute-start | bytes 1572872 | tf_op jit(solution)/shard_map/ppermute | solution.py:302
  3.0 1.6 %copy-start = (f32[512,2,512]{2,1,0:T(2,128)S(1)}, f32[512,2,512]{2,1,0:T(2,128)}, u32[]{:S(2)}) copy-start(f32[512,2,512]{2,1,0:T(2,128)} %param.7) | copy-start | bytes 6291460
  4.6 1.0 %copy-start.3 = (f32[512,256]{1,0:T(8,128)S(1)}, f32[512,256]{1,0:T(8,128)}, u32[]{:S(2)}) copy-start(f32[512,256]{1,0:T(8,128)} %probes.5) | copy-start | bytes 1572868
  5.6 5.9 %copy-start.2 = (f32[512,256]{1,0:T(8,128)S(1)}, f32[512,256]{1,0:T(8,128)}, u32[]{:S(2)}) copy-start(f32[512,256]{1,0:T(8,128)} %samples.1) | copy-start | bytes 1572868
  6.5 17.9 %collective-permute-start.1 = (f32[512,128]{1,0:T(8,128)S(1)}, f32[512,128]{1,0:T(8,128)S(1)}, u32[]{:S(2)}, u32[]{:S(2)}) collective-permute-start(f32[512,128]{1,0:T(8,128)S(1)} %shard_map.86), channel_id=1, source_target_pairs={{0,8},{1,9},{2,10},{3,11},{4,12},{5,13},{6,14},{7,15},{8,16},{9,17... | collective-permute-start | bytes 786440 | tf_op jit(solution)/shard_map/ppermute | solution.py:302
  13.2 11.2 %copy-start.4 = (f32[512,256]{1,0:T(8,128)S(1)}, f32[512,256]{1,0:T(8,128)}, u32[]{:S(2)}) copy-start(f32[512,256]{1,0:T(8,128)} %probes.5) | copy-start | bytes 1572868
  19.2 16.6 %copy-start.1 = (f32[1,3,2,128,128]{4,3,2,1,0:T(8,128)S(1)}, f32[1,3,2,128,128]{4,3,2,1,0:T(8,128)}, u32[]{:S(2)}) copy-start(f32[1,3,2,128,128]{4,3,2,1,0:T(8,128)} %couplings.5) | copy-start | bytes 1179652
  19.2 16.6 %copy-start.5 = (s32[1,3]{1,0:T(1,128)S(1)}, s32[1,3]{1,0:T(1,128)}, u32[]{:S(2)}) copy-start(s32[1,3]{1,0:T(1,128)} %slots.5) | copy-start | bytes 40
  19.2 16.6 %collective-permute-start.3 = (f32[512,128]{1,0:T(8,128)S(1)}, f32[512,128]{1,0:T(8,128)S(1)}, u32[]{:S(2)}, u32[]{:S(2)}) collective-permute-start(f32[512,128]{1,0:T(8,128)S(1)} %get-tuple-element.40), channel_id=1, source_target_pairs={{0,8},{1,9},{2,10},{3,11},{4,12},{5,13},{6,14},{7,15},{8,16},{9,17... | collective-permute-start | bytes 786440 | tf_op jit(solution)/shard_map/ppermute | solution.py:302
  28.6 7.2 %collective-permute-start.2 = (f32[128,256]{1,0:T(8,128)S(1)}, f32[128,256]{1,0:T(8,128)S(1)}, u32[]{:S(2)}, u32[]{:S(2)}) collective-permute-start(f32[128,256]{1,0:T(8,128)S(1)} %get-tuple-element.39.mine.mine_probes), channel_id=1, source_target_pairs={{1,0},{2,1},{3,2},{4,3},{5,4},{6,5},{7,6},{9,8},{10,9},{11,10},{12... | collective-permute-start | bytes 393224 | tf_op jit(solution)/shard_map/ppermute | solution.py:302
  30.6 11.6 %collective-permute-start.6 = (f32[128,384]{1,0:T(8,128)S(1)}, f32[128,384]{1,0:T(8,128)S(1)}, u32[]{:S(2)}, u32[]{:S(2)}) collective-permute-start(f32[128,384]{1,0:T(8,128)S(1)} %pad_maximum_fusion), channel_id=1, source_target_pairs={{0,8},{1,9},{2,10},{3,11},{4,12},{5,13},{6,14},{7,15},{8,0},{9,1},... | collective-permute-start | bytes 589832 | tf_op jit(solution)/shard_map/ppermute | solution.py:302
  36.7 7.7 %collective-permute-start.4 = (f32[128,128]{1,0:T(8,128)S(1)}, f32[128,128]{1,0:T(8,128)S(1)}, u32[]{:S(2)}, u32[]{:S(2)}) collective-permute-start(f32[128,128]{1,0:T(8,128)S(1)} %shard_map.89), channel_id=1, source_target_pairs={{0,16},{1,17},{2,18},{3,19},{4,20},{5,21},{6,22},{7,23},{8,24},{9,... | collective-permute-start | bytes 196616 | tf_op jit(solution)/shard_map/ppermute | solution.py:302
  36.8 7.6 %collective-permute-start.5 = (f32[128,128]{1,0:T(8,128)S(1)}, f32[128,128]{1,0:T(8,128)S(1)}, u32[]{:S(2)}, u32[]{:S(2)}) collective-permute-start(f32[128,128]{1,0:T(8,128)S(1)} %shard_map.89), channel_id=1, source_target_pairs={{0,24},{1,25},{2,26},{3,27},{4,28},{5,29},{6,30},{7,31},{8,16},{9,... | collective-permute-start | bytes 196616 | tf_op jit(solution)/shard_map/ppermute | solution.py:302
  42.1 5.9 %collective-permute-start.7 = (f32[128,128]{1,0:T(8,128)S(1)}, f32[128,128]{1,0:T(8,128)S(1)}, u32[]{:S(2)}, u32[]{:S(2)}) collective-permute-start(f32[128,128]{1,0:T(8,128)S(1)} %shard_map.91), channel_id=1, source_target_pairs={{0,16},{1,17},{2,18},{3,19},{4,20},{5,21},{6,22},{7,23},{8,24},{9,... | collective-permute-start | bytes 196616 | tf_op jit(solution)/shard_map/ppermute | solution.py:302
  48.7 6.4 %collective-permute-start.8 = (f32[128,256]{1,0:T(8,128)S(1)}, f32[128,256]{1,0:T(8,128)S(1)}, u32[]{:S(2)}, u32[]{:S(2)}) collective-permute-start(f32[128,256]{1,0:T(8,128)S(1)} %get-tuple-element.54.refs_2_), channel_id=1, source_target_pairs={{0,1},{1,0},{2,3},{3,2},{4,5},{5,4},{6,7},{7,6},{8,9},{9,8},{10,11... | collective-permute-start | bytes 393224 | tf_op jit(solution)/shard_map/ppermute | solution.py:302
  48.8 7.2 %collective-permute-start.9 = (f32[128,256]{1,0:T(8,128)S(1)}, f32[128,256]{1,0:T(8,128)S(1)}, u32[]{:S(2)}, u32[]{:S(2)}) collective-permute-start(f32[128,256]{1,0:T(8,128)S(1)} %get-tuple-element.54.refs_2_), channel_id=1, source_target_pairs={{1,2},{2,1},{3,4},{4,3},{5,6},{6,5},{9,10},{10,9},{11,12},{12,11},... | collective-permute-start | bytes 393224 | tf_op jit(solution)/shard_map/ppermute | solution.py:302
  51.5 7.5 %collective-permute-start.12 = (f32[128,128]{1,0:T(8,128)S(1)}, f32[128,128]{1,0:T(8,128)S(1)}, u32[]{:S(2)}, u32[]{:S(2)}) collective-permute-start(f32[128,128]{1,0:T(8,128)S(1)} %get-tuple-element.59), channel_id=1, source_target_pairs={{0,16},{1,17},{2,18},{3,19},{4,20},{5,21},{6,22},{7,23},{8,24},{9,... | collective-permute-start | bytes 196616 | tf_op jit(solution)/shard_map/ppermute | solution.py:302
  53.5 5.5 %collective-permute-start.11 = (f32[128,128]{1,0:T(8,128)S(1)}, f32[128,128]{1,0:T(8,128)S(1)}, u32[]{:S(2)}, u32[]{:S(2)}) collective-permute-start(f32[128,128]{1,0:T(8,128)S(1)} %sub.11._last.mine_last), channel_id=1, source_target_pairs={{0,8},{1,9},{2,10},{3,11},{4,12},{5,13},{6,14},{7,15},{8,0},{9,1},... | collective-permute-start | bytes 196616 | tf_op jit(solution)/shard_map/ppermute | solution.py:302
  56.9 8.5 %collective-permute-start.10 = (f32[128,128]{1,0:T(8,128)S(1)}, f32[128,128]{1,0:T(8,128)S(1)}, u32[]{:S(2)}, u32[]{:S(2)}) collective-permute-start(f32[128,128]{1,0:T(8,128)S(1)} %get-tuple-element.57.mine.refs_0_), channel_id=1, source_target_pairs={{0,16},{1,17},{2,18},{3,19},{4,20},{5,21},{6,22},{7,23},{8,24},{9,... | collective-permute-start | bytes 196616 | tf_op jit(solution)/shard_map/ppermute | solution.py:302
  59.5 9.4 %collective-permute-start.13 = (f32[128,128]{1,0:T(8,128)S(1)}, f32[128,128]{1,0:T(8,128)S(1)}, u32[]{:S(2)}, u32[]{:S(2)}) collective-permute-start(f32[128,128]{1,0:T(8,128)S(1)} %get-tuple-element.60.refs_1_), channel_id=1, source_target_pairs={{0,16},{1,17},{2,18},{3,19},{4,20},{5,21},{6,22},{7,23},{8,24},{9,... | collective-permute-start | bytes 196616 | tf_op jit(solution)/shard_map/ppermute | solution.py:302
  60.7 8.2 %collective-permute-start.14 = (f32[128,128]{1,0:T(8,128)S(1)}, f32[128,128]{1,0:T(8,128)S(1)}, u32[]{:S(2)}, u32[]{:S(2)}) collective-permute-start(f32[128,128]{1,0:T(8,128)S(1)} %get-tuple-element.61.refs_5_), channel_id=1, source_target_pairs={{0,8},{1,9},{2,10},{3,11},{4,12},{5,13},{6,14},{7,15},{8,0},{9,1},... | collective-permute-start | bytes 196616 | tf_op jit(solution)/shard_map/ppermute | solution.py:302

commit v15 on v14

--- a/solution.py
+++ b/solution.py
@@ -186,7 +186,7 @@
     block = coupling_of(slots, couplings, level, node)
     main, other = one[...], two[...]
     if trees:
-        straight = (lax.axis_index("clusters") ^ node) & 1 == 1
+        straight = (lax.axis_index("clusters") ^ node) & 1 == 0
         main, other = jnp.where(straight, main, other), jnp.where(straight, other, main)
     term = dot(jnp.concatenate([block, block.T], axis=1), jnp.concatenate([main, other], axis=0))
     out_first[...] = first[...] - term[:, :columns]
@@ -386,7 +386,7 @@
         else:
             correct = functools.partial(corrected_kernel, level, count == 2)
             if count == 2:
-                fields = [tree_swapped(probe_coef, odd) for odd in (0, 1)]
+                fields = [tree_swapped(probe_coef, odd) for odd in (1, 0)]
                 *fields, ancestors[-1] = lax.optimization_barrier((*fields, ancestors[-1]))
                 theirs_half = swapped(half, copies)
             else:

time: 71 us -> 71.1 us (level)
  the two profiles are of different devices: /device:TPU:28 before, /device:TPU:4 now
where the time goes in v15:
time: 71.1 us; the launch traced here: 70.6 us
  starting transfers between devices  32.5 us (46%)
  Pallas kernels  22.7 us (32%)
  waiting for transfers between devices  11.6 us (16%)
  local copies, waits for them, and re-layouts  2.66 us (4%)
  between operations  1.03 us (1%)
    ppermute x15, starting transfers between devices, permuted(): return lax.ppermute(value, BOTH, pairs)  32.5 us
    pallas_call x15, Pallas kernels, call(): pl.pallas_call(kernel, out_shape=outs, in_specs=specs, out_specs=out_spec...  22.7 us
    ppermute x15, waiting for transfers between devices, permuted(): return lax.ppermute(value, BOTH, pairs)  11.6 us
    unnamed x12, local copies, waits for them, and re-layouts  2.65 us
  transfers between devices with their start and end apart: 15, of which 6 were waited for; matrix products, arithmetic and copies ran while one was open for 0% of the time, Pallas kernels for 29%

profile of v15, /device:TPU:4, one launch (start us, length us, event | category | flops | bytes accessed | tf_op | source)
XLA Modules:
  0.0 70.6 jit_solution(16000334542271193577)
XLA Ops:
  0.6 5.8 %collective-permute-start = (f32[512,256]{1,0:T(8,128)}, f32[512,256]{1,0:T(8,128)S(1)}, u32[]{:S(2)}, u32[]{:S(2)}) collective-permute-start(f32[512,256]{1,0:T(8,128)} %probes.5), channel_id=1, source_target_pairs={{1,24},{2,25},{3,26},{4,27},{5,28},{6,29},{7,30},{8,0},{9,1},{10,2... | collective-permute-start | bytes 1572872 | tf_op jit(solution)/shard_map/ppermute | solution.py:302
  6.5 1.6 %copy-done = f32[512,2,512]{2,1,0:T(2,128)S(1)} copy-done((f32[512,2,512]{2,1,0:T(2,128)S(1)}, f32[512,2,512]{2,1,0:T(2,128)}, u32[]{:S(2)}) %copy-start) | copy-done | bytes 2097176
  8.1 1.0 %copy-done.3 = f32[512,256]{1,0:T(8,128)S(1)} copy-done((f32[512,256]{1,0:T(8,128)S(1)}, f32[512,256]{1,0:T(8,128)}, u32[]{:S(2)}) %copy-start.3) | copy-done | bytes 524312
  10.0 1.9 %collective-permute-start.1 = (f32[512,128]{1,0:T(8,128)S(1)}, f32[512,128]{1,0:T(8,128)S(1)}, u32[]{:S(2)}, u32[]{:S(2)}) collective-permute-start(f32[512,128]{1,0:T(8,128)S(1)} %shard_map.86), channel_id=1, source_target_pairs={{0,8},{1,9},{2,10},{3,11},{4,12},{5,13},{6,14},{7,15},{8,16},{9,17... | collective-permute-start | bytes 786440 | tf_op jit(solution)/shard_map/ppermute | solution.py:302
  11.9 1.6 %shard_map.84 = (f32[512,256]{1,0:T(8,128)S(1)}, f32[512,128]{1,0:T(8,128)S(1)}) custom-call(f32[4096,128]{1,0:T(8,128)S(1)} %bitcast.6, f32[512,256]{1,0:T(8,128)S(1)} %copy-done.3, f32[512,256]{1,0:T(8,128)S(1)} %copy-done.2), custom_call_target="tpu_custom_call" | custom-call | flops 805306368 | bytes 3932160 | tf_op jit(solution)/shard_map/pallas_call | solution.py:283
  13.6 5.5 %collective-permute-done.following = f32[512,256]{1,0:T(8,128)S(1)} collective-permute-done((f32[512,256]{1,0:T(8,128)}, f32[512,256]{1,0:T(8,128)S(1)}, u32[]{:S(2)}, u32[]{:S(2)}) %collective-permute-start) | collective-permute-done | bytes 524320 | tf_op jit(solution)/shard_map/ppermute | solution.py:302
  19.1 1.2 %shard_map.85 = (f32[512,128]{1,0:T(8,128)S(1)}, f32[512,128]{1,0:T(8,128)S(1)}, f32[512,128]{1,0:T(8,128)S(1)}) custom-call(f32[4096,128]{1,0:T(8,128)S(1)} %bitcast.7, f32[512,256]{1,0:T(8,128)S(1)} %get-tuple-element.35.rest, f32[512,256]{1,0:T(8,128)S(1)} %collective-permute-done.following, ...), custom_call_target="tpu_custom_call", output_to_operand_aliasing={{2}: (3, {})} | custom-call | flops 805306368 | bytes 4194304 | tf_op jit(solution)/shard_map/pallas_call | solution.py:283
  20.3 2.1 %collective-permute-start.3 = (f32[512,128]{1,0:T(8,128)S(1)}, f32[512,128]{1,0:T(8,128)S(1)}, u32[]{:S(2)}, u32[]{:S(2)}) collective-permute-start(f32[512,128]{1,0:T(8,128)S(1)} %get-tuple-element.40), channel_id=1, source_target_pairs={{0,8},{1,9},{2,10},{3,11},{4,12},{5,13},{6,14},{7,15},{8,16},{9,17... | collective-permute-start | bytes 786440 | tf_op jit(solution)/shard_map/ppermute | solution.py:302
  22.3 2.3 %collective-permute-done.1.handed = f32[512,128]{1,0:T(8,128)S(1)} collective-permute-done((f32[512,128]{1,0:T(8,128)S(1)}, f32[512,128]{1,0:T(8,128)S(1)}, u32[]{:S(2)}, u32[]{:S(2)}) %collective-permute-start.1) | collective-permute-done | bytes 262176 | tf_op jit(solution)/shard_map/ppermute | solution.py:302
  24.6 4.2 %shard_map.87 = (f32[512,128]{1,0:T(8,128)S(1)}, f32[128,128]{1,0:T(8,128)S(1)}, f32[128,128]{1,0:T(8,128)S(1)}, f32[128,256]{1,0:T(8,128)S(1)}) custom-call(f32[512,128]{1,0:T(8,128)S(1)} %get-tuple-element.38.rest, f32[512,128]{1,0:T(8,128)S(1)} %collective-permute-done.1.handed, f32[512,256]{1,0:T(8,128)S(1)} %copy-done.4), custom_call_target="tpu_custom_call" | custom-call | flops 805306368 | bytes 1572864 | tf_op jit(solution)/shard_map/pallas_call | solution.py:283
  28.8 2.2 %collective-permute-start.2 = (f32[128,256]{1,0:T(8,128)S(1)}, f32[128,256]{1,0:T(8,128)S(1)}, u32[]{:S(2)}, u32[]{:S(2)}) collective-permute-start(f32[128,256]{1,0:T(8,128)S(1)} %get-tuple-element.39.mine.mine_probes), channel_id=1, source_target_pairs={{1,0},{2,1},{3,2},{4,3},{5,4},{6,5},{7,6},{9,8},{10,9},{11,10},{12... | collective-permute-start | bytes 393224 | tf_op jit(solution)/shard_map/ppermute | solution.py:302
  31.1 2.5 %collective-permute-start.6 = (f32[128,384]{1,0:T(8,128)S(1)}, f32[128,384]{1,0:T(8,128)S(1)}, u32[]{:S(2)}, u32[]{:S(2)}) collective-permute-start(f32[128,384]{1,0:T(8,128)S(1)} %pad_maximum_fusion), channel_id=1, source_target_pairs={{0,8},{1,9},{2,10},{3,11},{4,12},{5,13},{6,14},{7,15},{8,0},{9,1},... | collective-permute-start | bytes 589832 | tf_op jit(solution)/shard_map/ppermute | solution.py:302
  34.7 4.9 %collective-permute-start.4 = (f32[128,128]{1,0:T(8,128)S(1)}, f32[128,128]{1,0:T(8,128)S(1)}, u32[]{:S(2)}, u32[]{:S(2)}) collective-permute-start(f32[128,128]{1,0:T(8,128)S(1)} %shard_map.89), channel_id=1, source_target_pairs={{0,16},{1,17},{2,18},{3,19},{4,20},{5,21},{6,22},{7,23},{8,24},{9,... | collective-permute-start | bytes 196616 | tf_op jit(solution)/shard_map/ppermute | solution.py:302
  40.4 1.5 %shard_map.88 = (f32[512,128]{1,0:T(8,128)}, f32[128,128]{1,0:T(8,128)S(1)}) custom-call(f32[512,128]{1,0:T(8,128)S(1)} %get-tuple-element.37.rest, f32[512,128]{1,0:T(8,128)S(1)} %collective-permute-done.3.handed, f32[512,128]{1,0:T(8,128)S(1)} %get-tuple-element.42.far, f32[128,128]{1,0:T(8,128)S(1)} %get-tuple-element.43.inverse), custom_call_target="tpu_custom_call" | custom-call | flops 805306368 | bytes 1179648 | tf_op jit(solution)/shard_map/pallas_call | solution.py:283
  42.8 2.0 %collective-permute-start.7 = (f32[128,128]{1,0:T(8,128)S(1)}, f32[128,128]{1,0:T(8,128)S(1)}, u32[]{:S(2)}, u32[]{:S(2)}) collective-permute-start(f32[128,128]{1,0:T(8,128)S(1)} %shard_map.91), channel_id=1, source_target_pairs={{0,16},{1,17},{2,18},{3,19},{4,20},{5,21},{6,22},{7,23},{8,24},{9,... | collective-permute-start | bytes 196616 | tf_op jit(solution)/shard_map/ppermute | solution.py:302
  44.8 1.1 %collective-permute-done.5 = f32[128,128]{1,0:T(8,128)S(1)} collective-permute-done((f32[128,128]{1,0:T(8,128)S(1)}, f32[128,128]{1,0:T(8,128)S(1)}, u32[]{:S(2)}, u32[]{:S(2)}) %collective-permute-start.5) | collective-permute-done | bytes 65568 | tf_op jit(solution)/shard_map/ppermute | solution.py:302
  45.9 3.5 %shard_map.90.inverse = f32[128,128]{1,0:T(8,128)S(1)} custom-call(f32[128,128]{1,0:T(8,128)S(1)} %sub.9.mine, f32[128,128]{1,0:T(8,128)S(1)} %slice_subtract_fusion.theirs), custom_call_target="tpu_custom_call" | custom-call | flops 6442450944 | bytes 196608 | tf_op jit(solution)/shard_map/pallas_call | solution.py:283
  50.2 2.2 %collective-permute-start.8 = (f32[128,256]{1,0:T(8,128)S(1)}, f32[128,256]{1,0:T(8,128)S(1)}, u32[]{:S(2)}, u32[]{:S(2)}) collective-permute-start(f32[128,256]{1,0:T(8,128)S(1)} %get-tuple-element.54.refs_2_), channel_id=1, source_target_pairs={{1,2},{2,1},{3,4},{4,3},{5,6},{6,5},{9,10},{10,9},{11,12},{12,11},... | collective-permute-start | bytes 393224 | tf_op jit(solution)/shard_map/ppermute | solution.py:302
  52.9 2.5 %collective-permute-start.12 = (f32[128,128]{1,0:T(8,128)S(1)}, f32[128,128]{1,0:T(8,128)S(1)}, u32[]{:S(2)}, u32[]{:S(2)}) collective-permute-start(f32[128,128]{1,0:T(8,128)S(1)} %get-tuple-element.59), channel_id=1, source_target_pairs={{0,16},{1,17},{2,18},{3,19},{4,20},{5,21},{6,22},{7,23},{8,24},{9,... | collective-permute-start | bytes 196616 | tf_op jit(solution)/shard_map/ppermute | solution.py:302
  58.3 2.9 %collective-permute-start.10 = (f32[128,128]{1,0:T(8,128)S(1)}, f32[128,128]{1,0:T(8,128)S(1)}, u32[]{:S(2)}, u32[]{:S(2)}) collective-permute-start(f32[128,128]{1,0:T(8,128)S(1)} %get-tuple-element.57.mine.refs_0_), channel_id=1, source_target_pairs={{0,16},{1,17},{2,18},{3,19},{4,20},{5,21},{6,22},{7,23},{8,24},{9,... | collective-permute-start | bytes 196616 | tf_op jit(solution)/shard_map/ppermute | solution.py:302
  61.9 1.3 %collective-permute-start.14 = (f32[128,128]{1,0:T(8,128)S(1)}, f32[128,128]{1,0:T(8,128)S(1)}, u32[]{:S(2)}, u32[]{:S(2)}) collective-permute-start(f32[128,128]{1,0:T(8,128)S(1)} %get-tuple-element.61.refs_5_), channel_id=1, source_target_pairs={{0,8},{1,9},{2,10},{3,11},{4,12},{5,13},{6,14},{7,15},{8,0},{9,1},... | collective-permute-start | bytes 196616 | tf_op jit(solution)/shard_map/ppermute | solution.py:302
  63.2 2.0 %collective-permute-done.10.theirs.refs_3_ = f32[128,128]{1,0:T(8,128)S(1)} collective-permute-done((f32[128,128]{1,0:T(8,128)S(1)}, f32[128,128]{1,0:T(8,128)S(1)}, u32[]{:S(2)}, u32[]{:S(2)}) %collective-permute-start.10) | collective-permute-done | bytes 65568 | tf_op jit(solution)/shard_map/ppermute | solution.py:302
  65.3 3.5 %shard_map.96.inverse = f32[128,128]{1,0:T(8,128)S(1)} custom-call(f32[128,128]{1,0:T(8,128)S(1)} %get-tuple-element.57.mine.refs_0_, f32[128,128]{1,0:T(8,128)S(1)} %collective-permute-done.10.theirs.refs_3_), custom_call_target="tpu_custom_call" | custom-call | bytes 196608 | tf_op jit(solution)/shard_map/pallas_call | solution.py:283
  68.8 1.6 %shard_map.98 = (f32[1,2,256,128]{3,2,1,0:T(8,128)}, f32[1,128,256]{2,1,0:T(8,128)}, f32[1,128,256]{2,1,0:T(8,128)}) custom-call(f32[128,128]{1,0:T(8,128)S(1)} %shard_map.96.inverse, f32[128,128]{1,0:T(8,128)S(1)} %get-tuple-element.57.mine.refs_0_, f32[128,128]{1,0:T(8,128)S(1)} %get-tuple-element.60.refs_1_, f32[128,256]{1,0:T(8,128)S(1)} %get-tuple-element.54.refs_2_, ...), custom_call_target="tpu_custom_call" | custom-call | bytes 1245184 | tf_op jit(solution)/shard_map/pallas_call | solution.py:283
  (38 shorter events, 8.5 us)
Async XLA Ops:
  0.6 18.5 %collective-permute-start = (f32[512,256]{1,0:T(8,128)}, f32[512,256]{1,0:T(8,128)S(1)}, u32[]{:S(2)}, u32[]{:S(2)}) collective-permute-start(f32[512,256]{1,0:T(8,128)} %probes.5), channel_id=1, source_target_pairs={{1,24},{2,25},{3,26},{4,27},{5,28},{6,29},{7,30},{8,0},{9,1},{10,2... | collective-permute-start | bytes 1572872 | tf_op jit(solution)/shard_map/ppermute | solution.py:302
  6.5 1.6 %copy-start = (f32[512,2,512]{2,1,0:T(2,128)S(1)}, f32[512,2,512]{2,1,0:T(2,128)}, u32[]{:S(2)}) copy-start(f32[512,2,512]{2,1,0:T(2,128)} %param.7) | copy-start | bytes 6291460
  8.1 1.0 %copy-start.3 = (f32[512,256]{1,0:T(8,128)S(1)}, f32[512,256]{1,0:T(8,128)}, u32[]{:S(2)}) copy-start(f32[512,256]{1,0:T(8,128)} %probes.5) | copy-start | bytes 1572868
  9.1 2.8 %copy-start.2 = (f32[512,256]{1,0:T(8,128)S(1)}, f32[512,256]{1,0:T(8,128)}, u32[]{:S(2)}) copy-start(f32[512,256]{1,0:T(8,128)} %samples.1) | copy-start | bytes 1572868
  10.0 14.6 %collective-permute-start.1 = (f32[512,128]{1,0:T(8,128)S(1)}, f32[512,128]{1,0:T(8,128)S(1)}, u32[]{:S(2)}, u32[]{:S(2)}) collective-permute-start(f32[512,128]{1,0:T(8,128)S(1)} %shard_map.86), channel_id=1, source_target_pairs={{0,8},{1,9},{2,10},{3,11},{4,12},{5,13},{6,14},{7,15},{8,16},{9,17... | collective-permute-start | bytes 786440 | tf_op jit(solution)/shard_map/ppermute | solution.py:302
  13.6 11.1 %copy-start.4 = (f32[512,256]{1,0:T(8,128)S(1)}, f32[512,256]{1,0:T(8,128)}, u32[]{:S(2)}) copy-start(f32[512,256]{1,0:T(8,128)} %probes.5) | copy-start | bytes 1572868
  20.3 13.6 %copy-start.1 = (f32[1,3,2,128,128]{4,3,2,1,0:T(8,128)S(1)}, f32[1,3,2,128,128]{4,3,2,1,0:T(8,128)}, u32[]{:S(2)}) copy-start(f32[1,3,2,128,128]{4,3,2,1,0:T(8,128)} %couplings.5) | copy-start | bytes 1179652
  20.3 13.6 %copy-start.5 = (s32[1,3]{1,0:T(1,128)S(1)}, s32[1,3]{1,0:T(1,128)}, u32[]{:S(2)}) copy-start(s32[1,3]{1,0:T(1,128)} %slots.5) | copy-start | bytes 40
  20.3 13.5 %collective-permute-start.3 = (f32[512,128]{1,0:T(8,128)S(1)}, f32[512,128]{1,0:T(8,128)S(1)}, u32[]{:S(2)}, u32[]{:S(2)}) collective-permute-start(f32[512,128]{1,0:T(8,128)S(1)} %get-tuple-element.40), channel_id=1, source_target_pairs={{0,8},{1,9},{2,10},{3,11},{4,12},{5,13},{6,14},{7,15},{8,16},{9,17... | collective-permute-start | bytes 786440 | tf_op jit(solution)/shard_map/ppermute | solution.py:302
  28.8 4.8 %collective-permute-start.2 = (f32[128,256]{1,0:T(8,128)S(1)}, f32[128,256]{1,0:T(8,128)S(1)}, u32[]{:S(2)}, u32[]{:S(2)}) collective-permute-start(f32[128,256]{1,0:T(8,128)S(1)} %get-tuple-element.39.mine.mine_probes), channel_id=1, source_target_pairs={{1,0},{2,1},{3,2},{4,3},{5,4},{6,5},{7,6},{9,8},{10,9},{11,10},{12... | collective-permute-start | bytes 393224 | tf_op jit(solution)/shard_map/ppermute | solution.py:302
  31.1 13.7 %collective-permute-start.6 = (f32[128,384]{1,0:T(8,128)S(1)}, f32[128,384]{1,0:T(8,128)S(1)}, u32[]{:S(2)}, u32[]{:S(2)}) collective-permute-start(f32[128,384]{1,0:T(8,128)S(1)} %pad_maximum_fusion), channel_id=1, source_target_pairs={{0,8},{1,9},{2,10},{3,11},{4,12},{5,13},{6,14},{7,15},{8,0},{9,1},... | collective-permute-start | bytes 589832 | tf_op jit(solution)/shard_map/ppermute | solution.py:302
  34.7 10.1 %collective-permute-start.4 = (f32[128,128]{1,0:T(8,128)S(1)}, f32[128,128]{1,0:T(8,128)S(1)}, u32[]{:S(2)}, u32[]{:S(2)}) collective-permute-start(f32[128,128]{1,0:T(8,128)S(1)} %shard_map.89), channel_id=1, source_target_pairs={{0,16},{1,17},{2,18},{3,19},{4,20},{5,21},{6,22},{7,23},{8,24},{9,... | collective-permute-start | bytes 196616 | tf_op jit(solution)/shard_map/ppermute | solution.py:302
  39.5 6.3 %collective-permute-start.5 = (f32[128,128]{1,0:T(8,128)S(1)}, f32[128,128]{1,0:T(8,128)S(1)}, u32[]{:S(2)}, u32[]{:S(2)}) collective-permute-start(f32[128,128]{1,0:T(8,128)S(1)} %shard_map.89), channel_id=1, source_target_pairs={{0,24},{1,25},{2,26},{3,27},{4,28},{5,29},{6,30},{7,31},{8,16},{9,... | collective-permute-start | bytes 196616 | tf_op jit(solution)/shard_map/ppermute | solution.py:302
  42.8 6.7 %collective-permute-start.7 = (f32[128,128]{1,0:T(8,128)S(1)}, f32[128,128]{1,0:T(8,128)S(1)}, u32[]{:S(2)}, u32[]{:S(2)}) collective-permute-start(f32[128,128]{1,0:T(8,128)S(1)} %shard_map.91), channel_id=1, source_target_pairs={{0,16},{1,17},{2,18},{3,19},{4,20},{5,21},{6,22},{7,23},{8,24},{9,... | collective-permute-start | bytes 196616 | tf_op jit(solution)/shard_map/ppermute | solution.py:302
  50.2 7.2 %collective-permute-start.8 = (f32[128,256]{1,0:T(8,128)S(1)}, f32[128,256]{1,0:T(8,128)S(1)}, u32[]{:S(2)}, u32[]{:S(2)}) collective-permute-start(f32[128,256]{1,0:T(8,128)S(1)} %get-tuple-element.54.refs_2_), channel_id=1, source_target_pairs={{1,2},{2,1},{3,4},{4,3},{5,6},{6,5},{9,10},{10,9},{11,12},{12,11},... | collective-permute-start | bytes 393224 | tf_op jit(solution)/shard_map/ppermute | solution.py:302
  52.5 4.9 %collective-permute-start.9 = (f32[128,256]{1,0:T(8,128)S(1)}, f32[128,256]{1,0:T(8,128)S(1)}, u32[]{:S(2)}, u32[]{:S(2)}) collective-permute-start(f32[128,256]{1,0:T(8,128)S(1)} %get-tuple-element.54.refs_2_), channel_id=1, source_target_pairs={{0,1},{1,0},{2,3},{3,2},{4,5},{5,4},{6,7},{7,6},{8,9},{9,8},{10,11... | collective-permute-start | bytes 393224 | tf_op jit(solution)/shard_map/ppermute | solution.py:302
  52.9 8.3 %collective-permute-start.12 = (f32[128,128]{1,0:T(8,128)S(1)}, f32[128,128]{1,0:T(8,128)S(1)}, u32[]{:S(2)}, u32[]{:S(2)}) collective-permute-start(f32[128,128]{1,0:T(8,128)S(1)} %get-tuple-element.59), channel_id=1, source_target_pairs={{0,16},{1,17},{2,18},{3,19},{4,20},{5,21},{6,22},{7,23},{8,24},{9,... | collective-permute-start | bytes 196616 | tf_op jit(solution)/shard_map/ppermute | solution.py:302
  55.4 5.8 %collective-permute-start.11 = (f32[128,128]{1,0:T(8,128)S(1)}, f32[128,128]{1,0:T(8,128)S(1)}, u32[]{:S(2)}, u32[]{:S(2)}) collective-permute-start(f32[128,128]{1,0:T(8,128)S(1)} %sub.11._last.mine_last), channel_id=1, source_target_pairs={{0,8},{1,9},{2,10},{3,11},{4,12},{5,13},{6,14},{7,15},{8,0},{9,1},... | collective-permute-start | bytes 196616 | tf_op jit(solution)/shard_map/ppermute | solution.py:302
  58.3 7.0 %collective-permute-start.10 = (f32[128,128]{1,0:T(8,128)S(1)}, f32[128,128]{1,0:T(8,128)S(1)}, u32[]{:S(2)}, u32[]{:S(2)}) collective-permute-start(f32[128,128]{1,0:T(8,128)S(1)} %get-tuple-element.57.mine.refs_0_), channel_id=1, source_target_pairs={{0,16},{1,17},{2,18},{3,19},{4,20},{5,21},{6,22},{7,23},{8,24},{9,... | collective-permute-start | bytes 196616 | tf_op jit(solution)/shard_map/ppermute | solution.py:302
  61.8 7.0 %collective-permute-start.13 = (f32[128,128]{1,0:T(8,128)S(1)}, f32[128,128]{1,0:T(8,128)S(1)}, u32[]{:S(2)}, u32[]{:S(2)}) collective-permute-start(f32[128,128]{1,0:T(8,128)S(1)} %get-tuple-element.60.refs_1_), channel_id=1, source_target_pairs={{0,16},{1,17},{2,18},{3,19},{4,20},{5,21},{6,22},{7,23},{8,24},{9,... | collective-permute-start | bytes 196616 | tf_op jit(solution)/shard_map/ppermute | solution.py:302
  61.9 6.9 %collective-permute-start.14 = (f32[128,128]{1,0:T(8,128)S(1)}, f32[128,128]{1,0:T(8,128)S(1)}, u32[]{:S(2)}, u32[]{:S(2)}) collective-permute-start(f32[128,128]{1,0:T(8,128)S(1)} %get-tuple-element.61.refs_5_), channel_id=1, source_target_pairs={{0,8},{1,9},{2,10},{3,11},{4,12},{5,13},{6,14},{7,15},{8,0},{9,1},... | collective-permute-start | bytes 196616 | tf_op jit(solution)/shard_map/ppermute | solution.py:302

commit v16 on v15

--- a/solution.py
+++ b/solution.py
@@ -160,35 +160,38 @@
     sample_coef[...] = dot(basis[...], rest[...] - handed[...], 0, 0)
 
 
-def coupling_of(slots, couplings, level, node):
-    subtree = lax.axis_size("leaf")
-    index = subtree - (subtree >> level - 1) + (node >> 1)
-    return couplings[0, slots[0, index], node & 1]
-
-
 def member_node(level):
     return lax.axis_index("leaf") >> level - 1
 
 
-def term_kernel(level, at, slots, couplings, mine, away, out):
+def pick_kernel(slots, couplings, *blocks):
+    subtree = lax.axis_size("leaf")
+    for at, out in enumerate(blocks):
+        level = at + 1
+        node = member_node(level)
+        if subtree >> at == 4:
+            node = node ^ 2
+        index = subtree - (subtree >> at) + (node >> 1)
+        block = couplings[0, slots[0, index], node & 1]
+        out[...] = jnp.concatenate([block, block.T], axis=1)
+
+
+def term_kernel(level, at, block, mine, away, out):
     node = member_node(level)
-    block = coupling_of(slots, couplings, level, node ^ 2)
     outer = (node == 0) | (node == 3)
     cols = slice(at, at + out.shape[1])
     main = jnp.where(outer, mine[:, cols], away[:, cols])
     other = jnp.where(outer, away[:, cols], mine[:, cols])
-    out[...] = dot(jnp.concatenate([block, block.T], axis=1), jnp.concatenate([main, other], axis=0))
-
-
-def corrected_kernel(level, trees, slots, couplings, one, two, first, out_first, out_last):
+    out[...] = dot(block[...], jnp.concatenate([main, other], axis=0))
+
+
+def corrected_kernel(level, trees, block, one, two, first, out_first, out_last):
     columns = first.shape[1]
-    node = member_node(level)
-    block = coupling_of(slots, couplings, level, node)
     main, other = one[...], two[...]
     if trees:
-        straight = (lax.axis_index("clusters") ^ node) & 1 == 0
+        straight = (lax.axis_index("clusters") ^ member_node(level)) & 1 == 0
         main, other = jnp.where(straight, main, other), jnp.where(straight, other, main)
-    term = dot(jnp.concatenate([block, block.T], axis=1), jnp.concatenate([main, other], axis=0))
+    term = dot(block[...], jnp.concatenate([main, other], axis=0))
     out_first[...] = first[...] - term[:, :columns]
     out_last[...] = term[:, columns:]
 
@@ -222,10 +225,13 @@
     first[...] = dot(inverse[...], dot(both, both, 0, 0))
 
 
-def node_kernel(inverse, mine, theirs, mine_probes, theirs_probes, _last, probe_coef, half):
+def node_kernel(mine, theirs, mine_probes, theirs_probes, inverse, probe_coef, half, scratch):
     nodes = jnp.concatenate([mine[...], theirs[...]], axis=0)
     probes = jnp.concatenate([mine_probes[...], theirs_probes[...]], axis=0)
-    coef = dot(inverse[...], dot(nodes, probes, 0, 0))
+    cross = dot(nodes, probes, 0, 0)
+    factor = inverse_factor(dot(nodes, nodes, 0, 0), scratch)
+    inverse[...] = factor
+    coef = dot(factor, cross)
     probe_coef[...] = coef
     width = half.shape[1]
     upper = lax.axis_index("leaf") & 1 == 1
@@ -333,6 +339,8 @@
     following = flat_shift(probes, -1)
     (handed,) = call(handed_kernel, [tall], near, probes, flops=work)
     handed = flat_shift(handed, 1)
+    blocks = call(pick_kernel, [(columns, 2 * columns)] * levels, couplings, slots=node_slot)
+    following, *blocks = lax.optimization_barrier((following, *blocks))
     rest, handed_last = call(
         rest_kernel, [(rows, width), tall_last], near, probes, samples, flops=work
     )
@@ -362,8 +370,7 @@
             if level == 1:
                 away, handed_last = lax.optimization_barrier((away, handed_last))
             (term_first,) = call(
-                functools.partial(term_kernel, level, 0), [square], couplings, probe_coef, away,
-                slots=node_slot,
+                functools.partial(term_kernel, level, 0), [square], blocks[level - 1], probe_coef, away
             )
             if level == 1:
                 leaf_basis, last = call(
@@ -373,7 +380,7 @@
             away, last = lax.optimization_barrier((away, last))
             (term_last,) = call(
                 functools.partial(term_kernel, level, columns), [square_last],
-                couplings, probe_coef, away, slots=node_slot,
+                blocks[level - 1], probe_coef, away,
             )
             term_first, term_twin = swapped(term_first, 2 * copies), swapped(term_first, 3 * copies)
             term_first, term_twin, theirs_coefs, last = lax.optimization_barrier(
@@ -395,7 +402,7 @@
                 fields = [flat_shift(probe_coef, by) for by in (2 * copies, -2 * copies)]
                 fields = [jnp.where(even, *fields), jnp.where(even, *fields[::-1])]
             first, term_last = call(
-                correct, [square, square_last], couplings, *fields, first, slots=node_slot
+                correct, [square, square_last], blocks[level - 1], *fields, first
             )
             theirs_first = swapped(first, copies)
         if below is None:
@@ -410,20 +417,19 @@
                 )
                 theirs_passed = swapped(theirs_half, 1)
         theirs_last = swapped(last, copies)
-        (inverse,) = call(
-            factor_kernel, [square], first, theirs_first, flops=8 * work if count == 4 else 0, **scratch
-        )
-        if level < levels:
+        if level == levels:
+            (inverse,) = call(factor_kernel, [square], first, theirs_first, **scratch)
+        else:
+            inverse, probe_coef, half = call(
+                node_kernel, [square, (columns, width), (columns, width // 2)],
+                first, theirs_first, probe_coef, theirs_probe, flops=8 * work, **scratch,
+            )
+            probe_coef, half, last = lax.optimization_barrier((probe_coef, half, last))
             ancestors += call(
                 functools.partial(basis_kernel, level), [(2 * columns, columns)],
                 inverse, first, theirs_first,
             )
             below = inverse, first, last, theirs_first, theirs_last
-            probe_coef, half = call(
-                node_kernel, [(columns, width), (columns, width // 2)],
-                inverse, first, theirs_first, probe_coef, theirs_probe, last,
-                specs=[VMEM] * 5 + [ANY],
-            )
             (first,) = call(node_first_kernel, [square], inverse, first, theirs_first)
     transfer_bases, top_samples, top_probes = call(
         functools.partial(top_kernel, levels),

time: 71.1 us -> 70.7 us (level)
  waiting for transfers between devices: 11.6 us -> 9.46 us
  Pallas kernels: 22.7 us -> 21.4 us
  starting transfers between devices: 32.5 us -> 33.8 us
  local copies, waits for them, and re-layouts: 2.66 us -> 3.64 us
    ppermute x15, waiting for transfers between devices: 11.6 us -> 9.46 us  [permuted(): return lax.ppermute(value, BOTH, pairs)]
    ppermute x15, starting transfers between devices: 32.5 us -> 33.8 us  [permuted(): return lax.ppermute(value, BOTH, pairs)]
    pallas_call x15, Pallas kernels: 22.7 us -> 21.4 us  [call(): pl.pallas_call(kernel, out_shape=outs, in_specs=specs, out_specs=out_spec...]
    unnamed x12 -> x14, local copies, waits for them, and re-layouts: 2.65 us -> 3.63 us
  transfers between devices with their start and end apart: 15 -> 15, of which waited for: 6 -> 5; matrix products, arithmetic and copies ran while one was open for 0% -> 0% of each run, Pallas kernels for 29% -> 29%
where the time goes in v16:
time: 70.7 us; the launch traced here: 69.5 us
  starting transfers between devices  33.8 us (48%)
  Pallas kernels  21.4 us (30%)
  waiting for transfers between devices  9.46 us (13%)
  local copies, waits for them, and re-layouts  3.64 us (5%)
  between operations  1.05 us (1%)
    ppermute x15, starting transfers between devices, permuted(): return lax.ppermute(value, BOTH, pairs)  33.8 us
    pallas_call x15, Pallas kernels, call(): pl.pallas_call(kernel, out_shape=outs, in_specs=specs, out_specs=out_spec...  21.4 us
    ppermute x15, waiting for transfers between devices, permuted(): return lax.ppermute(value, BOTH, pairs)  9.46 us
    unnamed x14, local copies, waits for them, and re-layouts  3.63 us
  transfers between devices with their start and end apart: 15, of which 5 were waited for; matrix products, arithmetic and copies ran while one was open for 0% of the time, Pallas kernels for 29%

profile of v16, /device:TPU:4, one launch (start us, length us, event | category | flops | bytes accessed | tf_op | source)
XLA Modules:
  0.0 69.5 jit_solution(11577635035815605691)
XLA Ops:
  0.6 5.8 %collective-permute-start = (f32[512,256]{1,0:T(8,128)}, f32[512,256]{1,0:T(8,128)S(1)}, u32[]{:S(2)}, u32[]{:S(2)}) collective-permute-start(f32[512,256]{1,0:T(8,128)} %probes.5), channel_id=1, source_target_pairs={{1,24},{2,25},{3,26},{4,27},{5,28},{6,29},{7,30},{8,0},{9,1},{10,2... | collective-permute-start | bytes 1572872 | tf_op jit(solution)/shard_map/ppermute | solution.py:308
  6.5 1.6 %copy-done = f32[512,2,512]{2,1,0:T(2,128)S(1)} copy-done((f32[512,2,512]{2,1,0:T(2,128)S(1)}, f32[512,2,512]{2,1,0:T(2,128)}, u32[]{:S(2)}) %copy-start) | copy-done | bytes 2097176
  8.1 1.0 %copy-done.3 = f32[512,256]{1,0:T(8,128)S(1)} copy-done((f32[512,256]{1,0:T(8,128)S(1)}, f32[512,256]{1,0:T(8,128)}, u32[]{:S(2)}) %copy-start.3) | copy-done | bytes 524312
  10.0 1.9 %collective-permute-start.1 = (f32[512,128]{1,0:T(8,128)S(1)}, f32[512,128]{1,0:T(8,128)S(1)}, u32[]{:S(2)}, u32[]{:S(2)}) collective-permute-start(f32[512,128]{1,0:T(8,128)S(1)} %shard_map.87), channel_id=1, source_target_pairs={{0,8},{1,9},{2,10},{3,11},{4,12},{5,13},{6,14},{7,15},{8,16},{9,17... | collective-permute-start | bytes 786440 | tf_op jit(solution)/shard_map/ppermute | solution.py:308
  12.0 1.0 %copy-done.5 = f32[1,3,2,128,128]{4,3,2,1,0:T(8,128)S(1)} copy-done((f32[1,3,2,128,128]{4,3,2,1,0:T(8,128)S(1)}, f32[1,3,2,128,128]{4,3,2,1,0:T(8,128)}, u32[]{:S(2)}) %copy-start.5) | copy-done | bytes 393240
  13.6 1.6 %shard_map.84 = (f32[512,256]{1,0:T(8,128)S(1)}, f32[512,128]{1,0:T(8,128)S(1)}) custom-call(f32[4096,128]{1,0:T(8,128)S(1)} %bitcast.6, f32[512,256]{1,0:T(8,128)S(1)} %copy-done.3, f32[512,256]{1,0:T(8,128)S(1)} %copy-done.2), custom_call_target="tpu_custom_call" | custom-call | flops 805306368 | bytes 3932160 | tf_op jit(solution)/shard_map/pallas_call | solution.py:289
  15.3 3.9 %collective-permute-done.following = f32[512,256]{1,0:T(8,128)S(1)} collective-permute-done((f32[512,256]{1,0:T(8,128)}, f32[512,256]{1,0:T(8,128)S(1)}, u32[]{:S(2)}, u32[]{:S(2)}) %collective-permute-start) | collective-permute-done | bytes 524320 | tf_op jit(solution)/shard_map/ppermute | solution.py:308
  19.1 1.2 %shard_map.86 = (f32[512,128]{1,0:T(8,128)S(1)}, f32[512,128]{1,0:T(8,128)S(1)}, f32[512,128]{1,0:T(8,128)S(1)}) custom-call(f32[4096,128]{1,0:T(8,128)S(1)} %bitcast.7, f32[512,256]{1,0:T(8,128)S(1)} %get-tuple-element.44.rest, f32[512,256]{1,0:T(8,128)S(1)} %collective-permute-done.following, ...), custom_call_target="tpu_custom_call", output_to_operand_aliasing={{2}: (3, {})} | custom-call | flops 805306368 | bytes 4194304 | tf_op jit(solution)/shard_map/pallas_call | solution.py:289
  20.3 1.9 %collective-permute-start.3 = (f32[512,128]{1,0:T(8,128)S(1)}, f32[512,128]{1,0:T(8,128)S(1)}, u32[]{:S(2)}, u32[]{:S(2)}) collective-permute-start(f32[512,128]{1,0:T(8,128)S(1)} %get-tuple-element.52), channel_id=1, source_target_pairs={{0,8},{1,9},{2,10},{3,11},{4,12},{5,13},{6,14},{7,15},{8,16},{9,17... | collective-permute-start | bytes 786440 | tf_op jit(solution)/shard_map/ppermute | solution.py:308
  22.2 2.4 %collective-permute-done.1.handed = f32[512,128]{1,0:T(8,128)S(1)} collective-permute-done((f32[512,128]{1,0:T(8,128)S(1)}, f32[512,128]{1,0:T(8,128)S(1)}, u32[]{:S(2)}, u32[]{:S(2)}) %collective-permute-start.1) | collective-permute-done | bytes 262176 | tf_op jit(solution)/shard_map/ppermute | solution.py:308
  24.6 4.2 %shard_map.88 = (f32[512,128]{1,0:T(8,128)S(1)}, f32[128,128]{1,0:T(8,128)S(1)}, f32[128,128]{1,0:T(8,128)S(1)}, f32[128,256]{1,0:T(8,128)S(1)}) custom-call(f32[512,128]{1,0:T(8,128)S(1)} %get-tuple-element.50.rest, f32[512,128]{1,0:T(8,128)S(1)} %collective-permute-done.1.handed, f32[512,256]{1,0:T(8,128)S(1)} %copy-done.4), custom_call_target="tpu_custom_call" | custom-call | flops 805306368 | bytes 1572864 | tf_op jit(solution)/shard_map/pallas_call | solution.py:289
  28.9 2.2 %collective-permute-start.2 = (f32[128,256]{1,0:T(8,128)S(1)}, f32[128,256]{1,0:T(8,128)S(1)}, u32[]{:S(2)}, u32[]{:S(2)}) collective-permute-start(f32[128,256]{1,0:T(8,128)S(1)} %get-tuple-element.51.mine.mine_probes), channel_id=1, source_target_pairs={{1,0},{2,1},{3,2},{4,3},{5,4},{6,5},{7,6},{9,8},{10,9},{11,10},{12... | collective-permute-start | bytes 393224 | tf_op jit(solution)/shard_map/ppermute | solution.py:308
  31.1 2.5 %collective-permute-start.6 = (f32[128,384]{1,0:T(8,128)S(1)}, f32[128,384]{1,0:T(8,128)S(1)}, u32[]{:S(2)}, u32[]{:S(2)}) collective-permute-start(f32[128,384]{1,0:T(8,128)S(1)} %pad_maximum_fusion), channel_id=1, source_target_pairs={{0,8},{1,9},{2,10},{3,11},{4,12},{5,13},{6,14},{7,15},{8,0},{9,1},... | collective-permute-start | bytes 589832 | tf_op jit(solution)/shard_map/ppermute | solution.py:308
  33.9 5.0 %collective-permute-start.4 = (f32[128,128]{1,0:T(8,128)S(1)}, f32[128,128]{1,0:T(8,128)S(1)}, u32[]{:S(2)}, u32[]{:S(2)}) collective-permute-start(f32[128,128]{1,0:T(8,128)S(1)} %shard_map.90), channel_id=1, source_target_pairs={{0,16},{1,17},{2,18},{3,19},{4,20},{5,21},{6,22},{7,23},{8,24},{9,... | collective-permute-start | bytes 196616 | tf_op jit(solution)/shard_map/ppermute | solution.py:308
  39.8 1.5 %shard_map.89 = (f32[512,128]{1,0:T(8,128)}, f32[128,128]{1,0:T(8,128)S(1)}) custom-call(f32[512,128]{1,0:T(8,128)S(1)} %get-tuple-element.49.rest, f32[512,128]{1,0:T(8,128)S(1)} %collective-permute-done.3.handed, f32[512,128]{1,0:T(8,128)S(1)} %get-tuple-element.54.far, f32[128,128]{1,0:T(8,128)S(1)} %get-tuple-element.55.inverse), custom_call_target="tpu_custom_call" | custom-call | flops 805306368 | bytes 1179648 | tf_op jit(solution)/shard_map/pallas_call | solution.py:289
  41.6 2.0 %collective-permute-start.7 = (f32[128,128]{1,0:T(8,128)S(1)}, f32[128,128]{1,0:T(8,128)S(1)}, u32[]{:S(2)}, u32[]{:S(2)}) collective-permute-start(f32[128,128]{1,0:T(8,128)S(1)} %shard_map.92), channel_id=1, source_target_pairs={{0,16},{1,17},{2,18},{3,19},{4,20},{5,21},{6,22},{7,23},{8,24},{9,... | collective-permute-start | bytes 196616 | tf_op jit(solution)/shard_map/ppermute | solution.py:308
  43.6 1.8 %collective-permute-done.4 = f32[128,128]{1,0:T(8,128)S(1)} collective-permute-done((f32[128,128]{1,0:T(8,128)S(1)}, f32[128,128]{1,0:T(8,128)S(1)}, u32[]{:S(2)}, u32[]{:S(2)}) %collective-permute-start.4) | collective-permute-done | bytes 65568 | tf_op jit(solution)/shard_map/ppermute | solution.py:308
  45.5 4.1 %shard_map.91 = (f32[128,128]{1,0:T(8,128)S(1)}, f32[128,256]{1,0:T(8,128)S(1)}, f32[128,128]{1,0:T(8,128)S(1)}) custom-call(f32[128,128]{1,0:T(8,128)S(1)} %sub.9.mine, f32[128,128]{1,0:T(8,128)S(1)} %slice_subtract_fusion.theirs, f32[128,256]{1,0:T(8,128)S(1)} %get-tuple-element.51.mine.mine_probes, f32[128,256]{1,0:T(8,128)S(1)} %slice.7.theirs_probes), custom_call_target="tpu_custom_call" | custom-call | flops 6442450944 | bytes 655360 | tf_op jit(solution)/shard_map/pallas_call | solution.py:289
  49.6 2.1 %collective-permute-start.8 = (f32[128,256]{1,0:T(8,128)S(1)}, f32[128,256]{1,0:T(8,128)S(1)}, u32[]{:S(2)}, u32[]{:S(2)}) collective-permute-start(f32[128,256]{1,0:T(8,128)S(1)} %get-tuple-element.70.refs_2_), channel_id=1, source_target_pairs={{1,2},{2,1},{3,4},{4,3},{5,6},{6,5},{9,10},{10,9},{11,12},{12,11},... | collective-permute-start | bytes 393224 | tf_op jit(solution)/shard_map/ppermute | solution.py:308
  52.1 2.5 %collective-permute-start.12 = (f32[128,128]{1,0:T(8,128)S(1)}, f32[128,128]{1,0:T(8,128)S(1)}, u32[]{:S(2)}, u32[]{:S(2)}) collective-permute-start(f32[128,128]{1,0:T(8,128)S(1)} %get-tuple-element.77), channel_id=1, source_target_pairs={{0,16},{1,17},{2,18},{3,19},{4,20},{5,21},{6,22},{7,23},{8,24},{9,... | collective-permute-start | bytes 196616 | tf_op jit(solution)/shard_map/ppermute | solution.py:308
  57.1 3.5 %collective-permute-start.10 = (f32[128,128]{1,0:T(8,128)S(1)}, f32[128,128]{1,0:T(8,128)S(1)}, u32[]{:S(2)}, u32[]{:S(2)}) collective-permute-start(f32[128,128]{1,0:T(8,128)S(1)} %get-tuple-element.74.mine.refs_0_), channel_id=1, source_target_pairs={{0,16},{1,17},{2,18},{3,19},{4,20},{5,21},{6,22},{7,23},{8,24},{9,... | collective-permute-start | bytes 196616 | tf_op jit(solution)/shard_map/ppermute | solution.py:308
  62.1 1.3 %collective-permute-start.14 = (f32[128,128]{1,0:T(8,128)S(1)}, f32[128,128]{1,0:T(8,128)S(1)}, u32[]{:S(2)}, u32[]{:S(2)}) collective-permute-start(f32[128,128]{1,0:T(8,128)S(1)} %get-tuple-element.79.refs_5_), channel_id=1, source_target_pairs={{0,8},{1,9},{2,10},{3,11},{4,12},{5,13},{6,14},{7,15},{8,0},{9,1},... | collective-permute-start | bytes 196616 | tf_op jit(solution)/shard_map/ppermute | solution.py:308
  64.2 3.5 %shard_map.96.inverse = f32[128,128]{1,0:T(8,128)S(1)} custom-call(f32[128,128]{1,0:T(8,128)S(1)} %get-tuple-element.74.mine.refs_0_, f32[128,128]{1,0:T(8,128)S(1)} %collective-permute-done.10.theirs.refs_3_), custom_call_target="tpu_custom_call" | custom-call | bytes 196608 | tf_op jit(solution)/shard_map/pallas_call | solution.py:289
  67.7 1.6 %shard_map.98 = (f32[1,2,256,128]{3,2,1,0:T(8,128)}, f32[1,128,256]{2,1,0:T(8,128)}, f32[1,128,256]{2,1,0:T(8,128)}) custom-call(f32[128,128]{1,0:T(8,128)S(1)} %shard_map.96.inverse, f32[128,128]{1,0:T(8,128)S(1)} %get-tuple-element.74.mine.refs_0_, f32[128,128]{1,0:T(8,128)S(1)} %get-tuple-element.78.refs_1_, f32[128,256]{1,0:T(8,128)S(1)} %get-tuple-element.70.refs_2_, ...), custom_call_target="tpu_custom_call" | custom-call | bytes 1245184 | tf_op jit(solution)/shard_map/pallas_call | solution.py:289
  (40 shorter events, 8.3 us)
Async XLA Ops:
  0.6 11.3 %copy-start.6 = (s32[1,3]{1,0:T(1,128)S(1)}, s32[1,3]{1,0:T(1,128)}, u32[]{:S(2)}) copy-start(s32[1,3]{1,0:T(1,128)} %slots.1) | copy-start | bytes 40
  0.6 18.5 %collective-permute-start = (f32[512,256]{1,0:T(8,128)}, f32[512,256]{1,0:T(8,128)S(1)}, u32[]{:S(2)}, u32[]{:S(2)}) collective-permute-start(f32[512,256]{1,0:T(8,128)} %probes.5), channel_id=1, source_target_pairs={{1,24},{2,25},{3,26},{4,27},{5,28},{6,29},{7,30},{8,0},{9,1},{10,2... | collective-permute-start | bytes 1572872 | tf_op jit(solution)/shard_map/ppermute | solution.py:308
  6.5 1.6 %copy-start = (f32[512,2,512]{2,1,0:T(2,128)S(1)}, f32[512,2,512]{2,1,0:T(2,128)}, u32[]{:S(2)}) copy-start(f32[512,2,512]{2,1,0:T(2,128)} %param.7) | copy-start | bytes 6291460
  8.1 1.0 %copy-start.3 = (f32[512,256]{1,0:T(8,128)S(1)}, f32[512,256]{1,0:T(8,128)}, u32[]{:S(2)}) copy-start(f32[512,256]{1,0:T(8,128)} %probes.5) | copy-start | bytes 1572868
  9.1 4.5 %copy-start.1 = (f32[512,2,512]{2,1,0:T(2,128)S(1)}, f32[512,2,512]{2,1,0:T(2,128)}, u32[]{:S(2)}) copy-start(f32[512,2,512]{2,1,0:T(2,128)} %param.7) | copy-start | bytes 6291460
  9.1 4.5 %copy-start.2 = (f32[512,256]{1,0:T(8,128)S(1)}, f32[512,256]{1,0:T(8,128)}, u32[]{:S(2)}) copy-start(f32[512,256]{1,0:T(8,128)} %samples.1) | copy-start | bytes 1572868
  10.0 14.6 %collective-permute-start.1 = (f32[512,128]{1,0:T(8,128)S(1)}, f32[512,128]{1,0:T(8,128)S(1)}, u32[]{:S(2)}, u32[]{:S(2)}) collective-permute-start(f32[512,128]{1,0:T(8,128)S(1)} %shard_map.87), channel_id=1, source_target_pairs={{0,8},{1,9},{2,10},{3,11},{4,12},{5,13},{6,14},{7,15},{8,16},{9,17... | collective-permute-start | bytes 786440 | tf_op jit(solution)/shard_map/ppermute | solution.py:308
  11.9 1.0 %copy-start.5 = (f32[1,3,2,128,128]{4,3,2,1,0:T(8,128)S(1)}, f32[1,3,2,128,128]{4,3,2,1,0:T(8,128)}, u32[]{:S(2)}) copy-start(f32[1,3,2,128,128]{4,3,2,1,0:T(8,128)} %couplings.1) | copy-start | bytes 1179652
  15.2 9.4 %copy-start.4 = (f32[512,256]{1,0:T(8,128)S(1)}, f32[512,256]{1,0:T(8,128)}, u32[]{:S(2)}) copy-start(f32[512,256]{1,0:T(8,128)} %probes.5) | copy-start | bytes 1572868
  20.3 13.4 %collective-permute-start.3 = (f32[512,128]{1,0:T(8,128)S(1)}, f32[512,128]{1,0:T(8,128)S(1)}, u32[]{:S(2)}, u32[]{:S(2)}) collective-permute-start(f32[512,128]{1,0:T(8,128)S(1)} %get-tuple-element.52), channel_id=1, source_target_pairs={{0,8},{1,9},{2,10},{3,11},{4,12},{5,13},{6,14},{7,15},{8,16},{9,17... | collective-permute-start | bytes 786440 | tf_op jit(solution)/shard_map/ppermute | solution.py:308
  28.9 4.8 %collective-permute-start.2 = (f32[128,256]{1,0:T(8,128)S(1)}, f32[128,256]{1,0:T(8,128)S(1)}, u32[]{:S(2)}, u32[]{:S(2)}) collective-permute-start(f32[128,256]{1,0:T(8,128)S(1)} %get-tuple-element.51.mine.mine_probes), channel_id=1, source_target_pairs={{1,0},{2,1},{3,2},{4,3},{5,4},{6,5},{7,6},{9,8},{10,9},{11,10},{12... | collective-permute-start | bytes 393224 | tf_op jit(solution)/shard_map/ppermute | solution.py:308
  31.1 12.5 %collective-permute-start.6 = (f32[128,384]{1,0:T(8,128)S(1)}, f32[128,384]{1,0:T(8,128)S(1)}, u32[]{:S(2)}, u32[]{:S(2)}) collective-permute-start(f32[128,384]{1,0:T(8,128)S(1)} %pad_maximum_fusion), channel_id=1, source_target_pairs={{0,8},{1,9},{2,10},{3,11},{4,12},{5,13},{6,14},{7,15},{8,0},{9,1},... | collective-permute-start | bytes 589832 | tf_op jit(solution)/shard_map/ppermute | solution.py:308
  33.9 11.5 %collective-permute-start.4 = (f32[128,128]{1,0:T(8,128)S(1)}, f32[128,128]{1,0:T(8,128)S(1)}, u32[]{:S(2)}, u32[]{:S(2)}) collective-permute-start(f32[128,128]{1,0:T(8,128)S(1)} %shard_map.90), channel_id=1, source_target_pairs={{0,16},{1,17},{2,18},{3,19},{4,20},{5,21},{6,22},{7,23},{8,24},{9,... | collective-permute-start | bytes 196616 | tf_op jit(solution)/shard_map/ppermute | solution.py:308
  38.9 6.5 %collective-permute-start.5 = (f32[128,128]{1,0:T(8,128)S(1)}, f32[128,128]{1,0:T(8,128)S(1)}, u32[]{:S(2)}, u32[]{:S(2)}) collective-permute-start(f32[128,128]{1,0:T(8,128)S(1)} %shard_map.90), channel_id=1, source_target_pairs={{0,24},{1,25},{2,26},{3,27},{4,28},{5,29},{6,30},{7,31},{8,16},{9,... | collective-permute-start | bytes 196616 | tf_op jit(solution)/shard_map/ppermute | solution.py:308
  41.6 8.0 %collective-permute-start.7 = (f32[128,128]{1,0:T(8,128)S(1)}, f32[128,128]{1,0:T(8,128)S(1)}, u32[]{:S(2)}, u32[]{:S(2)}) collective-permute-start(f32[128,128]{1,0:T(8,128)S(1)} %shard_map.92), channel_id=1, source_target_pairs={{0,16},{1,17},{2,18},{3,19},{4,20},{5,21},{6,22},{7,23},{8,24},{9,... | collective-permute-start | bytes 196616 | tf_op jit(solution)/shard_map/ppermute | solution.py:308
  49.6 7.2 %collective-permute-start.8 = (f32[128,256]{1,0:T(8,128)S(1)}, f32[128,256]{1,0:T(8,128)S(1)}, u32[]{:S(2)}, u32[]{:S(2)}) collective-permute-start(f32[128,256]{1,0:T(8,128)S(1)} %get-tuple-element.70.refs_2_), channel_id=1, source_target_pairs={{1,2},{2,1},{3,4},{4,3},{5,6},{6,5},{9,10},{10,9},{11,12},{12,11},... | collective-permute-start | bytes 393224 | tf_op jit(solution)/shard_map/ppermute | solution.py:308
  51.7 5.1 %collective-permute-start.9 = (f32[128,256]{1,0:T(8,128)S(1)}, f32[128,256]{1,0:T(8,128)S(1)}, u32[]{:S(2)}, u32[]{:S(2)}) collective-permute-start(f32[128,256]{1,0:T(8,128)S(1)} %get-tuple-element.70.refs_2_), channel_id=1, source_target_pairs={{0,1},{1,0},{2,3},{3,2},{4,5},{5,4},{6,7},{7,6},{8,9},{9,8},{10,11... | collective-permute-start | bytes 393224 | tf_op jit(solution)/shard_map/ppermute | solution.py:308
  52.1 8.4 %collective-permute-start.12 = (f32[128,128]{1,0:T(8,128)S(1)}, f32[128,128]{1,0:T(8,128)S(1)}, u32[]{:S(2)}, u32[]{:S(2)}) collective-permute-start(f32[128,128]{1,0:T(8,128)S(1)} %get-tuple-element.77), channel_id=1, source_target_pairs={{0,16},{1,17},{2,18},{3,19},{4,20},{5,21},{6,22},{7,23},{8,24},{9,... | collective-permute-start | bytes 196616 | tf_op jit(solution)/shard_map/ppermute | solution.py:308
  54.6 5.9 %collective-permute-start.11 = (f32[128,128]{1,0:T(8,128)S(1)}, f32[128,128]{1,0:T(8,128)S(1)}, u32[]{:S(2)}, u32[]{:S(2)}) collective-permute-start(f32[128,128]{1,0:T(8,128)S(1)} %sub.11.mine_last), channel_id=1, source_target_pairs={{0,8},{1,9},{2,10},{3,11},{4,12},{5,13},{6,14},{7,15},{8,0},{9,1},... | collective-permute-start | bytes 196616 | tf_op jit(solution)/shard_map/ppermute | solution.py:308
  57.1 7.1 %collective-permute-start.10 = (f32[128,128]{1,0:T(8,128)S(1)}, f32[128,128]{1,0:T(8,128)S(1)}, u32[]{:S(2)}, u32[]{:S(2)}) collective-permute-start(f32[128,128]{1,0:T(8,128)S(1)} %get-tuple-element.74.mine.refs_0_), channel_id=1, source_target_pairs={{0,16},{1,17},{2,18},{3,19},{4,20},{5,21},{6,22},{7,23},{8,24},{9,... | collective-permute-start | bytes 196616 | tf_op jit(solution)/shard_map/ppermute | solution.py:308
  61.1 6.6 %collective-permute-start.13 = (f32[128,128]{1,0:T(8,128)S(1)}, f32[128,128]{1,0:T(8,128)S(1)}, u32[]{:S(2)}, u32[]{:S(2)}) collective-permute-start(f32[128,128]{1,0:T(8,128)S(1)} %get-tuple-element.78.refs_1_), channel_id=1, source_target_pairs={{0,16},{1,17},{2,18},{3,19},{4,20},{5,21},{6,22},{7,23},{8,24},{9,... | collective-permute-start | bytes 196616 | tf_op jit(solution)/shard_map/ppermute | solution.py:308
  62.1 5.7 %collective-permute-start.14 = (f32[128,128]{1,0:T(8,128)S(1)}, f32[128,128]{1,0:T(8,128)S(1)}, u32[]{:S(2)}, u32[]{:S(2)}) collective-permute-start(f32[128,128]{1,0:T(8,128)S(1)} %get-tuple-element.79.refs_5_), channel_id=1, source_target_pairs={{0,8},{1,9},{2,10},{3,11},{4,12},{5,13},{6,14},{7,15},{8,0},{9,1},... | collective-permute-start | bytes 196616 | tf_op jit(solution)/shard_map/ppermute | solution.py:308

commit v17 on v16

--- a/solution.py
+++ b/solution.py
@@ -166,22 +166,29 @@
 
 def pick_kernel(slots, couplings, *blocks):
     subtree = lax.axis_size("leaf")
-    for at, out in enumerate(blocks):
-        level = at + 1
+    levels = subtree.bit_length() - 1
+    for level, out in zip([*range(1, levels + 1), levels - 1], blocks):
         node = member_node(level)
-        if subtree >> at == 4:
+        if out is blocks[-1]:
             node = node ^ 2
-        index = subtree - (subtree >> at) + (node >> 1)
+        index = subtree - (subtree >> level - 1) + (node >> 1)
         block = couplings[0, slots[0, index], node & 1]
         out[...] = jnp.concatenate([block, block.T], axis=1)
 
 
-def term_kernel(level, at, block, mine, away, out):
+def quad_kernel(level, block, inner, outer, coef, out):
+    node = member_node(level)
+    inside = (node == 1) | (node == 2)
+    main = jnp.where(inside, inner[...], outer[...])
+    other = jnp.where(inside, outer[...], inner[...])
+    out[...] = coef[...] - dot(block[...], jnp.concatenate([main, other], axis=0))
+
+
+def term_kernel(level, block, mine, away, out):
     node = member_node(level)
     outer = (node == 0) | (node == 3)
-    cols = slice(at, at + out.shape[1])
-    main = jnp.where(outer, mine[:, cols], away[:, cols])
-    other = jnp.where(outer, away[:, cols], mine[:, cols])
+    main = jnp.where(outer, mine[...], away[...])
+    other = jnp.where(outer, away[...], mine[...])
     out[...] = dot(block[...], jnp.concatenate([main, other], axis=0))
 
 
@@ -321,6 +328,12 @@
     return permuted(value, lambda tree, member: (tree - 1 if member < half else tree + 1, member))
 
 
+def outer_swapped(value, half):
+    return permuted(
+        value, lambda tree, member: (tree - 1 if member < half else tree + 1, member ^ half)
+    )
+
+
 def tree_swapped(value, odd):
     return permuted(value, lambda tree, member: (tree + 1 if tree & 1 == odd else tree - 1, member))
 
@@ -339,7 +352,7 @@
     following = flat_shift(probes, -1)
     (handed,) = call(handed_kernel, [tall], near, probes, flops=work)
     handed = flat_shift(handed, 1)
-    blocks = call(pick_kernel, [(columns, 2 * columns)] * levels, couplings, slots=node_slot)
+    blocks = call(pick_kernel, [(columns, 2 * columns)] * (levels + 1), couplings, slots=node_slot)
     following, *blocks = lax.optimization_barrier((following, *blocks))
     rest, handed_last = call(
         rest_kernel, [(rows, width), tall_last], near, probes, samples, flops=work
@@ -365,31 +378,27 @@
         copies = 2 ** (level - 1)
         count = subtree // copies
         if count == 4:
-            theirs_coefs = swapped(jnp.concatenate([first, probe_coef], axis=1), copies)
-            away = outward(probe_coef, 2 * copies)
+            probe_first, probe_last = probe_coef[:, :columns], probe_coef[:, columns:]
+            inner = swapped(probe_first, 2 * copies)
+            outer = outer_swapped(probe_first, 2 * copies)
+            away = outward(probe_last, 2 * copies)
+            theirs_probe = swapped(probe_coef, copies)
             if level == 1:
-                away, handed_last = lax.optimization_barrier((away, handed_last))
-            (term_first,) = call(
-                functools.partial(term_kernel, level, 0), [square], blocks[level - 1], probe_coef, away
-            )
-            if level == 1:
+                inner, handed_last = lax.optimization_barrier((inner, handed_last))
                 leaf_basis, last = call(
                     leaf_last_kernel, [tall, square_last], rest_last, handed_last, far, inverse,
                     flops=work,
                 )
-            away, last = lax.optimization_barrier((away, last))
+                inner, outer, last = lax.optimization_barrier((inner, outer, last))
+            (first,) = call(
+                functools.partial(quad_kernel, level), [square], blocks[level - 1], inner, outer, first
+            )
+            away, first = lax.optimization_barrier((away, first))
             (term_last,) = call(
-                functools.partial(term_kernel, level, columns), [square_last],
-                blocks[level - 1], probe_coef, away,
+                functools.partial(term_kernel, level), [square_last], blocks[-1], probe_last, away
             )
-            term_first, term_twin = swapped(term_first, 2 * copies), swapped(term_first, 3 * copies)
-            term_first, term_twin, theirs_coefs, last = lax.optimization_barrier(
-                (term_first, term_twin, theirs_coefs, last)
-            )
-            first = first - term_first
-            theirs_first = theirs_coefs[:, :columns] - term_twin
-            theirs_probe = theirs_coefs[:, columns:]
             term_last = swapped(term_last, 2 * copies)
+            theirs_first = swapped(first, copies)
         else:
             correct = functools.partial(corrected_kernel, level, count == 2)
             if count == 2:

time: 70.7 us -> 71.3 us (level); the launches traced: 69.5 us -> 70.9 us
  waiting for transfers between devices: 9.46 us -> 13.4 us
  starting transfers between devices: 33.8 us -> 31.3 us
    ppermute x15 -> x16, waiting for transfers between devices: 9.46 us -> 13.4 us  [permuted(): return lax.ppermute(value, BOTH, pairs)]
    ppermute x15 -> x16, starting transfers between devices: 33.8 us -> 31.3 us  [permuted(): return lax.ppermute(value, BOTH, pairs)]
  transfers between devices with their start and end apart: 15 -> 16, of which waited for: 5 -> 6; matrix products, arithmetic and copies ran while one was open for 0% -> 0% of each run, Pallas kernels for 29% -> 28%
where the time goes in v17:
time: 71.3 us; the launch traced here: 70.9 us
  starting transfers between devices  31.3 us (44%)
  Pallas kernels  21.5 us (30%)
  waiting for transfers between devices  13.4 us (19%)
  local copies, waits for them, and re-layouts  3.65 us (5%)
  between operations  1.07 us (2%)
    ppermute x16, starting transfers between devices, permuted(): return lax.ppermute(value, BOTH, pairs)  31.3 us
    pallas_call x15, Pallas kernels, call(): pl.pallas_call(kernel, out_shape=outs, in_specs=specs, out_specs=out_spec...  21.5 us
    ppermute x16, waiting for transfers between devices, permuted(): return lax.ppermute(value, BOTH, pairs)  13.4 us
    unnamed x14, local copies, waits for them, and re-layouts  3.63 us
  transfers between devices with their start and end apart: 16, of which 6 were waited for; matrix products, arithmetic and copies ran while one was open for 0% of the time, Pallas kernels for 28%

profile of v17, /device:TPU:4, one launch (start us, length us, event | category | flops | bytes accessed | tf_op | source)
XLA Modules:
  0.0 70.9 jit_solution(4312511380419770026)
XLA Ops:
  0.6 5.8 %collective-permute-start = (f32[512,256]{1,0:T(8,128)}, f32[512,256]{1,0:T(8,128)S(1)}, u32[]{:S(2)}, u32[]{:S(2)}) collective-permute-start(f32[512,256]{1,0:T(8,128)} %probes.5), channel_id=1, source_target_pairs={{1,24},{2,25},{3,26},{4,27},{5,28},{6,29},{7,30},{8,0},{9,1},{10,2... | collective-permute-start | bytes 1572872 | tf_op jit(solution)/shard_map/ppermute | solution.py:315
  6.5 1.6 %copy-done = f32[512,2,512]{2,1,0:T(2,128)S(1)} copy-done((f32[512,2,512]{2,1,0:T(2,128)S(1)}, f32[512,2,512]{2,1,0:T(2,128)}, u32[]{:S(2)}) %copy-start) | copy-done | bytes 2097176
  10.0 1.9 %collective-permute-start.1 = (f32[512,128]{1,0:T(8,128)S(1)}, f32[512,128]{1,0:T(8,128)S(1)}, u32[]{:S(2)}, u32[]{:S(2)}) collective-permute-start(f32[512,128]{1,0:T(8,128)S(1)} %shard_map.87), channel_id=1, source_target_pairs={{0,8},{1,9},{2,10},{3,11},{4,12},{5,13},{6,14},{7,15},{8,16},{9,17... | collective-permute-start | bytes 786440 | tf_op jit(solution)/shard_map/ppermute | solution.py:315
  13.6 1.6 %shard_map.84 = (f32[512,256]{1,0:T(8,128)S(1)}, f32[512,128]{1,0:T(8,128)S(1)}) custom-call(f32[4096,128]{1,0:T(8,128)S(1)} %bitcast.6, f32[512,256]{1,0:T(8,128)S(1)} %copy-done.3, f32[512,256]{1,0:T(8,128)S(1)} %copy-done.2), custom_call_target="tpu_custom_call" | custom-call | flops 805306368 | bytes 3932160 | tf_op jit(solution)/shard_map/pallas_call | solution.py:296
  15.3 3.8 %collective-permute-done.following = f32[512,256]{1,0:T(8,128)S(1)} collective-permute-done((f32[512,256]{1,0:T(8,128)}, f32[512,256]{1,0:T(8,128)S(1)}, u32[]{:S(2)}, u32[]{:S(2)}) %collective-permute-start) | collective-permute-done | bytes 524320 | tf_op jit(solution)/shard_map/ppermute | solution.py:315
  20.3 1.9 %collective-permute-start.3 = (f32[512,128]{1,0:T(8,128)S(1)}, f32[512,128]{1,0:T(8,128)S(1)}, u32[]{:S(2)}, u32[]{:S(2)}) collective-permute-start(f32[512,128]{1,0:T(8,128)S(1)} %get-tuple-element.54), channel_id=1, source_target_pairs={{0,8},{1,9},{2,10},{3,11},{4,12},{5,13},{6,14},{7,15},{8,16},{9,17... | collective-permute-start | bytes 786440 | tf_op jit(solution)/shard_map/ppermute | solution.py:315
  22.2 2.4 %collective-permute-done.1.handed = f32[512,128]{1,0:T(8,128)S(1)} collective-permute-done((f32[512,128]{1,0:T(8,128)S(1)}, f32[512,128]{1,0:T(8,128)S(1)}, u32[]{:S(2)}, u32[]{:S(2)}) %collective-permute-start.1) | collective-permute-done | bytes 262176 | tf_op jit(solution)/shard_map/ppermute | solution.py:315
  24.6 4.2 %shard_map.88 = (f32[512,128]{1,0:T(8,128)S(1)}, f32[128,128]{1,0:T(8,128)S(1)}, f32[128,128]{1,0:T(8,128)S(1)}, f32[128,256]{1,0:T(8,128)S(1)}) custom-call(f32[512,128]{1,0:T(8,128)S(1)} %get-tuple-element.52.rest, f32[512,128]{1,0:T(8,128)S(1)} %collective-permute-done.1.handed, f32[512,256]{1,0:T(8,128)S(1)} %copy-done.4), custom_call_target="tpu_custom_call" | custom-call | flops 805306368 | bytes 1572864 | tf_op jit(solution)/shard_map/pallas_call | solution.py:296
  28.9 2.6 %collective-permute-start.2 = (f32[128,128]{1,0:T(8,128)S(1)}, f32[128,128]{1,0:T(8,128)S(1)}, u32[]{:S(2)}, u32[]{:S(2)}) collective-permute-start(f32[128,128]{1,0:T(8,128)S(1)} %get-tuple-element.87), channel_id=1, source_target_pairs={{0,16},{1,17},{2,18},{3,19},{4,20},{5,21},{6,22},{7,23},{8,24},{9,... | collective-permute-start | bytes 196616 | tf_op jit(solution)/shard_map/ppermute | solution.py:315
  31.5 2.6 %collective-permute-start.5 = (f32[128,128]{1,0:T(8,128)S(1)}, f32[128,128]{1,0:T(8,128)S(1)}, u32[]{:S(2)}, u32[]{:S(2)}) collective-permute-start(f32[128,128]{1,0:T(8,128)S(1)} %get-tuple-element.87), channel_id=1, source_target_pairs={{1,16},{2,17},{3,18},{4,19},{5,20},{6,21},{7,22},{9,24},{10,25},{1... | collective-permute-start | bytes 196616 | tf_op jit(solution)/shard_map/ppermute | solution.py:315
  34.1 1.6 %collective-permute-start.7 = (f32[128,256]{1,0:T(8,128)S(1)}, f32[128,256]{1,0:T(8,128)S(1)}, u32[]{:S(2)}, u32[]{:S(2)}) collective-permute-start(f32[128,256]{1,0:T(8,128)S(1)} %get-tuple-element.53.mine_probes), channel_id=1, source_target_pairs={{0,8},{1,9},{2,10},{3,11},{4,12},{5,13},{6,14},{7,15},{8,0},{9,1},... | collective-permute-start | bytes 393224 | tf_op jit(solution)/shard_map/ppermute | solution.py:315
  35.8 2.4 %collective-permute-start.4 = (f32[128,128]{1,0:T(8,128)S(1)}, f32[128,128]{1,0:T(8,128)S(1)}, u32[]{:S(2)}, u32[]{:S(2)}) collective-permute-start(f32[128,128]{1,0:T(8,128)S(1)} %get-tuple-element.86.mine), channel_id=1, source_target_pairs={{1,0},{2,1},{3,2},{4,3},{5,4},{6,5},{7,6},{9,8},{10,9},{11,10},{12... | collective-permute-start | bytes 196616 | tf_op jit(solution)/shard_map/ppermute | solution.py:315
  38.2 1.5 %shard_map.89 = (f32[512,128]{1,0:T(8,128)}, f32[128,128]{1,0:T(8,128)S(1)}) custom-call(f32[512,128]{1,0:T(8,128)S(1)} %get-tuple-element.51.rest, f32[512,128]{1,0:T(8,128)S(1)} %collective-permute-done.3.handed, f32[512,128]{1,0:T(8,128)S(1)} %get-tuple-element.56.far, f32[128,128]{1,0:T(8,128)S(1)} %get-tuple-element.57.inverse), custom_call_target="tpu_custom_call" | custom-call | flops 805306368 | bytes 1179648 | tf_op jit(solution)/shard_map/pallas_call | solution.py:296
  39.7 1.2 %collective-permute-done.5.outer = f32[128,128]{1,0:T(8,128)S(1)} collective-permute-done((f32[128,128]{1,0:T(8,128)S(1)}, f32[128,128]{1,0:T(8,128)S(1)}, u32[]{:S(2)}, u32[]{:S(2)}) %collective-permute-start.5) | collective-permute-done | bytes 65568 | tf_op jit(solution)/shard_map/ppermute | solution.py:315
  42.5 2.0 %collective-permute-start.8 = (f32[128,128]{1,0:T(8,128)S(1)}, f32[128,128]{1,0:T(8,128)S(1)}, u32[]{:S(2)}, u32[]{:S(2)}) collective-permute-start(f32[128,128]{1,0:T(8,128)S(1)} %shard_map.92), channel_id=1, source_target_pairs={{0,16},{1,17},{2,18},{3,19},{4,20},{5,21},{6,22},{7,23},{8,24},{9,... | collective-permute-start | bytes 196616 | tf_op jit(solution)/shard_map/ppermute | solution.py:315
  44.5 1.9 %collective-permute-done.6.theirs = f32[128,128]{1,0:T(8,128)S(1)} collective-permute-done((f32[128,128]{1,0:T(8,128)S(1)}, f32[128,128]{1,0:T(8,128)S(1)}, u32[]{:S(2)}, u32[]{:S(2)}) %collective-permute-start.6) | collective-permute-done | bytes 65568 | tf_op jit(solution)/shard_map/ppermute | solution.py:315
  46.4 4.1 %shard_map.91 = (f32[128,128]{1,0:T(8,128)S(1)}, f32[128,256]{1,0:T(8,128)S(1)}, f32[128,128]{1,0:T(8,128)S(1)}) custom-call(f32[128,128]{1,0:T(8,128)S(1)} %shard_map.90.mine, f32[128,128]{1,0:T(8,128)S(1)} %collective-permute-done.6.theirs, f32[128,256]{1,0:T(8,128)S(1)} %get-tuple-element.53.mine_probes, f32[128,256]{1,0:T(8,128)S(1)} %collective-permute-done.7.theirs_probes), custom_call_target="tpu_custom_call" | custom-call | flops 6442450944 | bytes 655360 | tf_op jit(solution)/shard_map/pallas_call | solution.py:296
  50.6 2.1 %collective-permute-start.9 = (f32[128,256]{1,0:T(8,128)S(1)}, f32[128,256]{1,0:T(8,128)S(1)}, u32[]{:S(2)}, u32[]{:S(2)}) collective-permute-start(f32[128,256]{1,0:T(8,128)S(1)} %get-tuple-element.72.refs_2_), channel_id=1, source_target_pairs={{1,2},{2,1},{3,4},{4,3},{5,6},{6,5},{9,10},{10,9},{11,12},{12,11},... | collective-permute-start | bytes 393224 | tf_op jit(solution)/shard_map/ppermute | solution.py:315
  52.7 2.1 %collective-permute-start.13 = (f32[128,128]{1,0:T(8,128)S(1)}, f32[128,128]{1,0:T(8,128)S(1)}, u32[]{:S(2)}, u32[]{:S(2)}) collective-permute-start(f32[128,128]{1,0:T(8,128)S(1)} %get-tuple-element.79), channel_id=1, source_target_pairs={{0,16},{1,17},{2,18},{3,19},{4,20},{5,21},{6,22},{7,23},{8,24},{9,... | collective-permute-start | bytes 196616 | tf_op jit(solution)/shard_map/ppermute | solution.py:315
  56.6 1.2 %collective-permute-done.9.one = f32[128,256]{1,0:T(8,128)S(1)} collective-permute-done((f32[128,256]{1,0:T(8,128)S(1)}, f32[128,256]{1,0:T(8,128)S(1)}, u32[]{:S(2)}, u32[]{:S(2)}) %collective-permute-start.9) | collective-permute-done | bytes 131104 | tf_op jit(solution)/shard_map/ppermute | solution.py:315
  58.1 1.9 %collective-permute-start.11 = (f32[128,128]{1,0:T(8,128)S(1)}, f32[128,128]{1,0:T(8,128)S(1)}, u32[]{:S(2)}, u32[]{:S(2)}) collective-permute-start(f32[128,128]{1,0:T(8,128)S(1)} %get-tuple-element.76.mine.refs_0_), channel_id=1, source_target_pairs={{0,16},{1,17},{2,18},{3,19},{4,20},{5,21},{6,22},{7,23},{8,24},{9,... | collective-permute-start | bytes 196616 | tf_op jit(solution)/shard_map/ppermute | solution.py:315
  62.9 2.8 %collective-permute-done.11.theirs.refs_3_ = f32[128,128]{1,0:T(8,128)S(1)} collective-permute-done((f32[128,128]{1,0:T(8,128)S(1)}, f32[128,128]{1,0:T(8,128)S(1)}, u32[]{:S(2)}, u32[]{:S(2)}) %collective-permute-start.11) | collective-permute-done | bytes 65568 | tf_op jit(solution)/shard_map/ppermute | solution.py:315
  65.6 3.5 %shard_map.96.inverse = f32[128,128]{1,0:T(8,128)S(1)} custom-call(f32[128,128]{1,0:T(8,128)S(1)} %get-tuple-element.76.mine.refs_0_, f32[128,128]{1,0:T(8,128)S(1)} %collective-permute-done.11.theirs.refs_3_), custom_call_target="tpu_custom_call" | custom-call | bytes 196608 | tf_op jit(solution)/shard_map/pallas_call | solution.py:296
  69.2 1.6 %shard_map.98 = (f32[1,2,256,128]{3,2,1,0:T(8,128)}, f32[1,128,256]{2,1,0:T(8,128)}, f32[1,128,256]{2,1,0:T(8,128)}) custom-call(f32[128,128]{1,0:T(8,128)S(1)} %shard_map.96.inverse, f32[128,128]{1,0:T(8,128)S(1)} %get-tuple-element.76.mine.refs_0_, f32[128,128]{1,0:T(8,128)S(1)} %get-tuple-element.80.refs_1_, f32[128,256]{1,0:T(8,128)S(1)} %get-tuple-element.72.refs_2_, ...), custom_call_target="tpu_custom_call" | custom-call | bytes 1245184 | tf_op jit(solution)/shard_map/pallas_call | solution.py:296
  (39 shorter events, 11.3 us)
Async XLA Ops:
  0.6 11.3 %copy-start.6 = (s32[1,3]{1,0:T(1,128)S(1)}, s32[1,3]{1,0:T(1,128)}, u32[]{:S(2)}) copy-start(s32[1,3]{1,0:T(1,128)} %slots.1) | copy-start | bytes 40
  0.6 18.5 %collective-permute-start = (f32[512,256]{1,0:T(8,128)}, f32[512,256]{1,0:T(8,128)S(1)}, u32[]{:S(2)}, u32[]{:S(2)}) collective-permute-start(f32[512,256]{1,0:T(8,128)} %probes.5), channel_id=1, source_target_pairs={{1,24},{2,25},{3,26},{4,27},{5,28},{6,29},{7,30},{8,0},{9,1},{10,2... | collective-permute-start | bytes 1572872 | tf_op jit(solution)/shard_map/ppermute | solution.py:315
  6.5 1.6 %copy-start = (f32[512,2,512]{2,1,0:T(2,128)S(1)}, f32[512,2,512]{2,1,0:T(2,128)}, u32[]{:S(2)}) copy-start(f32[512,2,512]{2,1,0:T(2,128)} %param.7) | copy-start | bytes 6291460
  8.1 1.0 %copy-start.3 = (f32[512,256]{1,0:T(8,128)S(1)}, f32[512,256]{1,0:T(8,128)}, u32[]{:S(2)}) copy-start(f32[512,256]{1,0:T(8,128)} %probes.5) | copy-start | bytes 1572868
  9.1 4.5 %copy-start.1 = (f32[512,2,512]{2,1,0:T(2,128)S(1)}, f32[512,2,512]{2,1,0:T(2,128)}, u32[]{:S(2)}) copy-start(f32[512,2,512]{2,1,0:T(2,128)} %param.7) | copy-start | bytes 6291460
  9.1 4.5 %copy-start.2 = (f32[512,256]{1,0:T(8,128)S(1)}, f32[512,256]{1,0:T(8,128)}, u32[]{:S(2)}) copy-start(f32[512,256]{1,0:T(8,128)} %samples.1) | copy-start | bytes 1572868
  10.0 14.6 %collective-permute-start.1 = (f32[512,128]{1,0:T(8,128)S(1)}, f32[512,128]{1,0:T(8,128)S(1)}, u32[]{:S(2)}, u32[]{:S(2)}) collective-permute-start(f32[512,128]{1,0:T(8,128)S(1)} %shard_map.87), channel_id=1, source_target_pairs={{0,8},{1,9},{2,10},{3,11},{4,12},{5,13},{6,14},{7,15},{8,16},{9,17... | collective-permute-start | bytes 786440 | tf_op jit(solution)/shard_map/ppermute | solution.py:315
  11.9 1.0 %copy-start.5 = (f32[1,3,2,128,128]{4,3,2,1,0:T(8,128)S(1)}, f32[1,3,2,128,128]{4,3,2,1,0:T(8,128)}, u32[]{:S(2)}) copy-start(f32[1,3,2,128,128]{4,3,2,1,0:T(8,128)} %couplings.1) | copy-start | bytes 1179652
  15.3 9.4 %copy-start.4 = (f32[512,256]{1,0:T(8,128)S(1)}, f32[512,256]{1,0:T(8,128)}, u32[]{:S(2)}) copy-start(f32[512,256]{1,0:T(8,128)} %probes.5) | copy-start | bytes 1572868
  20.3 17.9 %collective-permute-start.3 = (f32[512,128]{1,0:T(8,128)S(1)}, f32[512,128]{1,0:T(8,128)S(1)}, u32[]{:S(2)}, u32[]{:S(2)}) collective-permute-start(f32[512,128]{1,0:T(8,128)S(1)} %get-tuple-element.54), channel_id=1, source_target_pairs={{0,8},{1,9},{2,10},{3,11},{4,12},{5,13},{6,14},{7,15},{8,16},{9,17... | collective-permute-start | bytes 786440 | tf_op jit(solution)/shard_map/ppermute | solution.py:315
  28.9 9.3 %collective-permute-start.2 = (f32[128,128]{1,0:T(8,128)S(1)}, f32[128,128]{1,0:T(8,128)S(1)}, u32[]{:S(2)}, u32[]{:S(2)}) collective-permute-start(f32[128,128]{1,0:T(8,128)S(1)} %get-tuple-element.87), channel_id=1, source_target_pairs={{0,16},{1,17},{2,18},{3,19},{4,20},{5,21},{6,22},{7,23},{8,24},{9,... | collective-permute-start | bytes 196616 | tf_op jit(solution)/shard_map/ppermute | solution.py:315
  31.5 9.4 %collective-permute-start.5 = (f32[128,128]{1,0:T(8,128)S(1)}, f32[128,128]{1,0:T(8,128)S(1)}, u32[]{:S(2)}, u32[]{:S(2)}) collective-permute-start(f32[128,128]{1,0:T(8,128)S(1)} %get-tuple-element.87), channel_id=1, source_target_pairs={{1,16},{2,17},{3,18},{4,19},{5,20},{6,21},{7,22},{9,24},{10,25},{1... | collective-permute-start | bytes 196616 | tf_op jit(solution)/shard_map/ppermute | solution.py:315
  34.1 10.3 %collective-permute-start.7 = (f32[128,256]{1,0:T(8,128)S(1)}, f32[128,256]{1,0:T(8,128)S(1)}, u32[]{:S(2)}, u32[]{:S(2)}) collective-permute-start(f32[128,256]{1,0:T(8,128)S(1)} %get-tuple-element.53.mine_probes), channel_id=1, source_target_pairs={{0,8},{1,9},{2,10},{3,11},{4,12},{5,13},{6,14},{7,15},{8,0},{9,1},... | collective-permute-start | bytes 393224 | tf_op jit(solution)/shard_map/ppermute | solution.py:315
  35.8 5.4 %collective-permute-start.4 = (f32[128,128]{1,0:T(8,128)S(1)}, f32[128,128]{1,0:T(8,128)S(1)}, u32[]{:S(2)}, u32[]{:S(2)}) collective-permute-start(f32[128,128]{1,0:T(8,128)S(1)} %get-tuple-element.86.mine), channel_id=1, source_target_pairs={{1,0},{2,1},{3,2},{4,3},{5,4},{6,5},{7,6},{9,8},{10,9},{11,10},{12... | collective-permute-start | bytes 196616 | tf_op jit(solution)/shard_map/ppermute | solution.py:315
  41.2 5.2 %collective-permute-start.6 = (f32[128,128]{1,0:T(8,128)S(1)}, f32[128,128]{1,0:T(8,128)S(1)}, u32[]{:S(2)}, u32[]{:S(2)}) collective-permute-start(f32[128,128]{1,0:T(8,128)S(1)} %shard_map.90.mine), channel_id=1, source_target_pairs={{0,8},{1,9},{2,10},{3,11},{4,12},{5,13},{6,14},{7,15},{8,0},{9,1},... | collective-permute-start | bytes 196616 | tf_op jit(solution)/shard_map/ppermute | solution.py:315
  42.5 8.0 %collective-permute-start.8 = (f32[128,128]{1,0:T(8,128)S(1)}, f32[128,128]{1,0:T(8,128)S(1)}, u32[]{:S(2)}, u32[]{:S(2)}) collective-permute-start(f32[128,128]{1,0:T(8,128)S(1)} %shard_map.92), channel_id=1, source_target_pairs={{0,16},{1,17},{2,18},{3,19},{4,20},{5,21},{6,22},{7,23},{8,24},{9,... | collective-permute-start | bytes 196616 | tf_op jit(solution)/shard_map/ppermute | solution.py:315
  50.5 6.0 %collective-permute-start.10 = (f32[128,256]{1,0:T(8,128)S(1)}, f32[128,256]{1,0:T(8,128)S(1)}, u32[]{:S(2)}, u32[]{:S(2)}) collective-permute-start(f32[128,256]{1,0:T(8,128)S(1)} %get-tuple-element.72.refs_2_), channel_id=1, source_target_pairs={{0,1},{1,0},{2,3},{3,2},{4,5},{5,4},{6,7},{7,6},{8,9},{9,8},{10,11... | collective-permute-start | bytes 393224 | tf_op jit(solution)/shard_map/ppermute | solution.py:315
  50.6 7.2 %collective-permute-start.9 = (f32[128,256]{1,0:T(8,128)S(1)}, f32[128,256]{1,0:T(8,128)S(1)}, u32[]{:S(2)}, u32[]{:S(2)}) collective-permute-start(f32[128,256]{1,0:T(8,128)S(1)} %get-tuple-element.72.refs_2_), channel_id=1, source_target_pairs={{1,2},{2,1},{3,4},{4,3},{5,6},{6,5},{9,10},{10,9},{11,12},{12,11},... | collective-permute-start | bytes 393224 | tf_op jit(solution)/shard_map/ppermute | solution.py:315
  52.7 7.3 %collective-permute-start.13 = (f32[128,128]{1,0:T(8,128)S(1)}, f32[128,128]{1,0:T(8,128)S(1)}, u32[]{:S(2)}, u32[]{:S(2)}) collective-permute-start(f32[128,128]{1,0:T(8,128)S(1)} %get-tuple-element.79), channel_id=1, source_target_pairs={{0,16},{1,17},{2,18},{3,19},{4,20},{5,21},{6,22},{7,23},{8,24},{9,... | collective-permute-start | bytes 196616 | tf_op jit(solution)/shard_map/ppermute | solution.py:315
  54.8 5.3 %collective-permute-start.12 = (f32[128,128]{1,0:T(8,128)S(1)}, f32[128,128]{1,0:T(8,128)S(1)}, u32[]{:S(2)}, u32[]{:S(2)}) collective-permute-start(f32[128,128]{1,0:T(8,128)S(1)} %sub.3.mine_last), channel_id=1, source_target_pairs={{0,8},{1,9},{2,10},{3,11},{4,12},{5,13},{6,14},{7,15},{8,0},{9,1},... | collective-permute-start | bytes 196616 | tf_op jit(solution)/shard_map/ppermute | solution.py:315
  58.1 7.5 %collective-permute-start.11 = (f32[128,128]{1,0:T(8,128)S(1)}, f32[128,128]{1,0:T(8,128)S(1)}, u32[]{:S(2)}, u32[]{:S(2)}) collective-permute-start(f32[128,128]{1,0:T(8,128)S(1)} %get-tuple-element.76.mine.refs_0_), channel_id=1, source_target_pairs={{0,16},{1,17},{2,18},{3,19},{4,20},{5,21},{6,22},{7,23},{8,24},{9,... | collective-permute-start | bytes 196616 | tf_op jit(solution)/shard_map/ppermute | solution.py:315
  60.6 8.5 %collective-permute-start.14 = (f32[128,128]{1,0:T(8,128)S(1)}, f32[128,128]{1,0:T(8,128)S(1)}, u32[]{:S(2)}, u32[]{:S(2)}) collective-permute-start(f32[128,128]{1,0:T(8,128)S(1)} %get-tuple-element.80.refs_1_), channel_id=1, source_target_pairs={{0,16},{1,17},{2,18},{3,19},{4,20},{5,21},{6,22},{7,23},{8,24},{9,... | collective-permute-start | bytes 196616 | tf_op jit(solution)/shard_map/ppermute | solution.py:315
  61.7 7.4 %collective-permute-start.15 = (f32[128,128]{1,0:T(8,128)S(1)}, f32[128,128]{1,0:T(8,128)S(1)}, u32[]{:S(2)}, u32[]{:S(2)}) collective-permute-start(f32[128,128]{1,0:T(8,128)S(1)} %get-tuple-element.81.refs_5_), channel_id=1, source_target_pairs={{0,8},{1,9},{2,10},{3,11},{4,12},{5,13},{6,14},{7,15},{8,0},{9,1},... | collective-permute-start | bytes 196616 | tf_op jit(solution)/shard_map/ppermute | solution.py:315

commit v18 on v17

--- a/solution.py
+++ b/solution.py
@@ -393,7 +393,7 @@
             (first,) = call(
                 functools.partial(quad_kernel, level), [square], blocks[level - 1], inner, outer, first
             )
-            away, first = lax.optimization_barrier((away, first))
+            away, _ = lax.optimization_barrier((away, first))
             (term_last,) = call(
                 functools.partial(term_kernel, level), [square_last], blocks[-1], probe_last, away
             )
@@ -425,7 +425,10 @@
                     specs=[VMEM] * 6 + [ANY], out_specs=[VMEM, ANY], input_output_aliases={6: 1},
                 )
                 theirs_passed = swapped(theirs_half, 1)
-        theirs_last = swapped(last, copies)
+        leaving = last
+        if level == levels:
+            theirs_first, leaving = lax.optimization_barrier((theirs_first, last))
+        theirs_last = swapped(leaving, copies)
         if level == levels:
             (inverse,) = call(factor_kernel, [square], first, theirs_first, **scratch)
         else:

time: 71.3 us -> 71.4 us (level)
  starting transfers between devices: 31.3 us -> 32.4 us
  waiting for transfers between devices: 13.4 us -> 12.4 us
    ppermute x16, starting transfers between devices: 31.3 us -> 32.4 us  [permuted(): return lax.ppermute(value, BOTH, pairs)]
    ppermute x16, waiting for transfers between devices: 13.4 us -> 12.4 us  [permuted(): return lax.ppermute(value, BOTH, pairs)]
where the time goes in v18:
time: 71.4 us; the launch traced here: 71 us
  starting transfers between devices  32.4 us (45%)
  Pallas kernels  21.5 us (30%)
  waiting for transfers between devices  12.4 us (17%)
  local copies, waits for them, and re-layouts  3.65 us (5%)
  between operations  1.06 us (1%)
    ppermute x16, starting transfers between devices, permuted(): return lax.ppermute(value, BOTH, pairs)  32.4 us
    pallas_call x15, Pallas kernels, call(): pl.pallas_call(kernel, out_shape=outs, in_specs=specs, out_specs=out_spec...  21.5 us
    ppermute x16, waiting for transfers between devices, permuted(): return lax.ppermute(value, BOTH, pairs)  12.4 us
    unnamed x14, local copies, waits for them, and re-layouts  3.63 us
  transfers between devices with their start and end apart: 16, of which 6 were waited for; matrix products, arithmetic and copies ran while one was open for 0% of the time, Pallas kernels for 28%

profile of v18, /device:TPU:4, one launch (start us, length us, event | category | flops | bytes accessed | tf_op | source)
XLA Modules:
  0.0 71.0 jit_solution(4528851209724823064)
XLA Ops:
  0.6 5.8 %collective-permute-start = (f32[512,256]{1,0:T(8,128)}, f32[512,256]{1,0:T(8,128)S(1)}, u32[]{:S(2)}, u32[]{:S(2)}) collective-permute-start(f32[512,256]{1,0:T(8,128)} %probes.5), channel_id=1, source_target_pairs={{1,24},{2,25},{3,26},{4,27},{5,28},{6,29},{7,30},{8,0},{9,1},{10,2... | collective-permute-start | bytes 1572872 | tf_op jit(solution)/shard_map/ppermute | solution.py:315
  6.5 1.6 %copy-done = f32[512,2,512]{2,1,0:T(2,128)S(1)} copy-done((f32[512,2,512]{2,1,0:T(2,128)S(1)}, f32[512,2,512]{2,1,0:T(2,128)}, u32[]{:S(2)}) %copy-start) | copy-done | bytes 2097176
  10.0 1.9 %collective-permute-start.1 = (f32[512,128]{1,0:T(8,128)S(1)}, f32[512,128]{1,0:T(8,128)S(1)}, u32[]{:S(2)}, u32[]{:S(2)}) collective-permute-start(f32[512,128]{1,0:T(8,128)S(1)} %shard_map.87), channel_id=1, source_target_pairs={{0,8},{1,9},{2,10},{3,11},{4,12},{5,13},{6,14},{7,15},{8,16},{9,17... | collective-permute-start | bytes 786440 | tf_op jit(solution)/shard_map/ppermute | solution.py:315
  13.6 1.6 %shard_map.84 = (f32[512,256]{1,0:T(8,128)S(1)}, f32[512,128]{1,0:T(8,128)S(1)}) custom-call(f32[4096,128]{1,0:T(8,128)S(1)} %bitcast.6, f32[512,256]{1,0:T(8,128)S(1)} %copy-done.3, f32[512,256]{1,0:T(8,128)S(1)} %copy-done.2), custom_call_target="tpu_custom_call" | custom-call | flops 805306368 | bytes 3932160 | tf_op jit(solution)/shard_map/pallas_call | solution.py:296
  15.3 3.8 %collective-permute-done.following = f32[512,256]{1,0:T(8,128)S(1)} collective-permute-done((f32[512,256]{1,0:T(8,128)}, f32[512,256]{1,0:T(8,128)S(1)}, u32[]{:S(2)}, u32[]{:S(2)}) %collective-permute-start) | collective-permute-done | bytes 524320 | tf_op jit(solution)/shard_map/ppermute | solution.py:315
  20.3 1.9 %collective-permute-start.3 = (f32[512,128]{1,0:T(8,128)S(1)}, f32[512,128]{1,0:T(8,128)S(1)}, u32[]{:S(2)}, u32[]{:S(2)}) collective-permute-start(f32[512,128]{1,0:T(8,128)S(1)} %get-tuple-element.55), channel_id=1, source_target_pairs={{0,8},{1,9},{2,10},{3,11},{4,12},{5,13},{6,14},{7,15},{8,16},{9,17... | collective-permute-start | bytes 786440 | tf_op jit(solution)/shard_map/ppermute | solution.py:315
  22.2 2.4 %collective-permute-done.1.handed = f32[512,128]{1,0:T(8,128)S(1)} collective-permute-done((f32[512,128]{1,0:T(8,128)S(1)}, f32[512,128]{1,0:T(8,128)S(1)}, u32[]{:S(2)}, u32[]{:S(2)}) %collective-permute-start.1) | collective-permute-done | bytes 262176 | tf_op jit(solution)/shard_map/ppermute | solution.py:315
  24.6 4.2 %shard_map.88 = (f32[512,128]{1,0:T(8,128)S(1)}, f32[128,128]{1,0:T(8,128)S(1)}, f32[128,128]{1,0:T(8,128)S(1)}, f32[128,256]{1,0:T(8,128)S(1)}) custom-call(f32[512,128]{1,0:T(8,128)S(1)} %get-tuple-element.53.rest, f32[512,128]{1,0:T(8,128)S(1)} %collective-permute-done.1.handed, f32[512,256]{1,0:T(8,128)S(1)} %copy-done.4), custom_call_target="tpu_custom_call" | custom-call | flops 805306368 | bytes 1572864 | tf_op jit(solution)/shard_map/pallas_call | solution.py:296
  28.9 2.6 %collective-permute-start.2 = (f32[128,128]{1,0:T(8,128)S(1)}, f32[128,128]{1,0:T(8,128)S(1)}, u32[]{:S(2)}, u32[]{:S(2)}) collective-permute-start(f32[128,128]{1,0:T(8,128)S(1)} %get-tuple-element.89), channel_id=1, source_target_pairs={{0,16},{1,17},{2,18},{3,19},{4,20},{5,21},{6,22},{7,23},{8,24},{9,... | collective-permute-start | bytes 196616 | tf_op jit(solution)/shard_map/ppermute | solution.py:315
  31.5 2.6 %collective-permute-start.4 = (f32[128,128]{1,0:T(8,128)S(1)}, f32[128,128]{1,0:T(8,128)S(1)}, u32[]{:S(2)}, u32[]{:S(2)}) collective-permute-start(f32[128,128]{1,0:T(8,128)S(1)} %get-tuple-element.89), channel_id=1, source_target_pairs={{1,16},{2,17},{3,18},{4,19},{5,20},{6,21},{7,22},{9,24},{10,25},{1... | collective-permute-start | bytes 196616 | tf_op jit(solution)/shard_map/ppermute | solution.py:315
  34.1 1.6 %collective-permute-start.6 = (f32[128,256]{1,0:T(8,128)S(1)}, f32[128,256]{1,0:T(8,128)S(1)}, u32[]{:S(2)}, u32[]{:S(2)}) collective-permute-start(f32[128,256]{1,0:T(8,128)S(1)} %get-tuple-element.54.mine_probes), channel_id=1, source_target_pairs={{0,8},{1,9},{2,10},{3,11},{4,12},{5,13},{6,14},{7,15},{8,0},{9,1},... | collective-permute-start | bytes 393224 | tf_op jit(solution)/shard_map/ppermute | solution.py:315
  35.8 2.4 %collective-permute-start.7 = (f32[128,128]{1,0:T(8,128)S(1)}, f32[128,128]{1,0:T(8,128)S(1)}, u32[]{:S(2)}, u32[]{:S(2)}) collective-permute-start(f32[128,128]{1,0:T(8,128)S(1)} %get-tuple-element.88.mine), channel_id=1, source_target_pairs={{1,0},{2,1},{3,2},{4,3},{5,4},{6,5},{7,6},{9,8},{10,9},{11,10},{12... | collective-permute-start | bytes 196616 | tf_op jit(solution)/shard_map/ppermute | solution.py:315
  38.2 1.5 %shard_map.89 = (f32[512,128]{1,0:T(8,128)}, f32[128,128]{1,0:T(8,128)S(1)}) custom-call(f32[512,128]{1,0:T(8,128)S(1)} %get-tuple-element.52.rest, f32[512,128]{1,0:T(8,128)S(1)} %collective-permute-done.3.handed, f32[512,128]{1,0:T(8,128)S(1)} %get-tuple-element.57.far, f32[128,128]{1,0:T(8,128)S(1)} %get-tuple-element.58.inverse), custom_call_target="tpu_custom_call" | custom-call | flops 805306368 | bytes 1179648 | tf_op jit(solution)/shard_map/pallas_call | solution.py:296
  42.5 1.4 %collective-permute-start.8 = (f32[128,128]{1,0:T(8,128)S(1)}, f32[128,128]{1,0:T(8,128)S(1)}, u32[]{:S(2)}, u32[]{:S(2)}) collective-permute-start(f32[128,128]{1,0:T(8,128)S(1)} %shard_map.92), channel_id=1, source_target_pairs={{0,16},{1,17},{2,18},{3,19},{4,20},{5,21},{6,22},{7,23},{8,24},{9,... | collective-permute-start | bytes 196616 | tf_op jit(solution)/shard_map/ppermute | solution.py:315
  43.9 1.6 %collective-permute-done.5.theirs = f32[128,128]{1,0:T(8,128)S(1)} collective-permute-done((f32[128,128]{1,0:T(8,128)S(1)}, f32[128,128]{1,0:T(8,128)S(1)}, u32[]{:S(2)}, u32[]{:S(2)}) %collective-permute-start.5) | collective-permute-done | bytes 65568 | tf_op jit(solution)/shard_map/ppermute | solution.py:315
  45.5 4.1 %shard_map.91 = (f32[128,128]{1,0:T(8,128)S(1)}, f32[128,256]{1,0:T(8,128)S(1)}, f32[128,128]{1,0:T(8,128)S(1)}) custom-call(f32[128,128]{1,0:T(8,128)S(1)} %shard_map.90.mine, f32[128,128]{1,0:T(8,128)S(1)} %collective-permute-done.5.theirs, f32[128,256]{1,0:T(8,128)S(1)} %get-tuple-element.54.mine_probes, f32[128,256]{1,0:T(8,128)S(1)} %collective-permute-done.6.theirs_probes), custom_call_target="tpu_custom_call" | custom-call | flops 6442450944 | bytes 655360 | tf_op jit(solution)/shard_map/pallas_call | solution.py:296
  49.7 2.4 %collective-permute-start.9 = (f32[128,256]{1,0:T(8,128)S(1)}, f32[128,256]{1,0:T(8,128)S(1)}, u32[]{:S(2)}, u32[]{:S(2)}) collective-permute-start(f32[128,256]{1,0:T(8,128)S(1)} %get-tuple-element.72.refs_2_), channel_id=1, source_target_pairs={{1,2},{2,1},{3,4},{4,3},{5,6},{6,5},{9,10},{10,9},{11,12},{12,11},... | collective-permute-start | bytes 393224 | tf_op jit(solution)/shard_map/ppermute | solution.py:315
  52.1 1.4 %collective-permute-start.12 = (f32[128,128]{1,0:T(8,128)S(1)}, f32[128,128]{1,0:T(8,128)S(1)}, u32[]{:S(2)}, u32[]{:S(2)}) collective-permute-start(f32[128,128]{1,0:T(8,128)S(1)} %sub.3.mine_last), channel_id=1, source_target_pairs={{0,8},{1,9},{2,10},{3,11},{4,12},{5,13},{6,14},{7,15},{8,0},{9,1},... | collective-permute-start | bytes 196616 | tf_op jit(solution)/shard_map/ppermute | solution.py:315
  53.4 1.8 %collective-permute-start.13 = (f32[128,128]{1,0:T(8,128)S(1)}, f32[128,128]{1,0:T(8,128)S(1)}, u32[]{:S(2)}, u32[]{:S(2)}) collective-permute-start(f32[128,128]{1,0:T(8,128)S(1)} %get-tuple-element.79), channel_id=1, source_target_pairs={{0,16},{1,17},{2,18},{3,19},{4,20},{5,21},{6,22},{7,23},{8,24},{9,... | collective-permute-start | bytes 196616 | tf_op jit(solution)/shard_map/ppermute | solution.py:315
  57.2 2.8 %collective-permute-start.11 = (f32[128,128]{1,0:T(8,128)S(1)}, f32[128,128]{1,0:T(8,128)S(1)}, u32[]{:S(2)}, u32[]{:S(2)}) collective-permute-start(f32[128,128]{1,0:T(8,128)S(1)} %get-tuple-element.76.mine.refs_0_), channel_id=1, source_target_pairs={{0,16},{1,17},{2,18},{3,19},{4,20},{5,21},{6,22},{7,23},{8,24},{9,... | collective-permute-start | bytes 196616 | tf_op jit(solution)/shard_map/ppermute | solution.py:315
  60.8 2.5 %collective-permute-done.11.theirs.refs_3_ = f32[128,128]{1,0:T(8,128)S(1)} collective-permute-done((f32[128,128]{1,0:T(8,128)S(1)}, f32[128,128]{1,0:T(8,128)S(1)}, u32[]{:S(2)}, u32[]{:S(2)}) %collective-permute-start.11) | collective-permute-done | bytes 65568 | tf_op jit(solution)/shard_map/ppermute | solution.py:315
  63.3 2.4 %collective-permute-start.14 = (f32[128,128]{1,0:T(8,128)S(1)}, f32[128,128]{1,0:T(8,128)S(1)}, u32[]{:S(2)}, u32[]{:S(2)}) collective-permute-start(f32[128,128]{1,0:T(8,128)S(1)} %get-tuple-element.82.refs_1_), channel_id=1, source_target_pairs={{0,16},{1,17},{2,18},{3,19},{4,20},{5,21},{6,22},{7,23},{8,24},{9,... | collective-permute-start | bytes 196616 | tf_op jit(solution)/shard_map/ppermute | solution.py:315
  65.7 3.5 %shard_map.97.inverse = f32[128,128]{1,0:T(8,128)S(1)} custom-call(f32[128,128]{1,0:T(8,128)S(1)} %get-tuple-element.76.mine.refs_0_, f32[128,128]{1,0:T(8,128)S(1)} %collective-permute-done.11.theirs.refs_3_), custom_call_target="tpu_custom_call" | custom-call | bytes 196608 | tf_op jit(solution)/shard_map/pallas_call | solution.py:296
  69.3 1.6 %shard_map.98 = (f32[1,2,256,128]{3,2,1,0:T(8,128)}, f32[1,128,256]{2,1,0:T(8,128)}, f32[1,128,256]{2,1,0:T(8,128)}) custom-call(f32[128,128]{1,0:T(8,128)S(1)} %shard_map.97.inverse, f32[128,128]{1,0:T(8,128)S(1)} %get-tuple-element.76.mine.refs_0_, f32[128,128]{1,0:T(8,128)S(1)} %get-tuple-element.82.refs_1_, f32[128,256]{1,0:T(8,128)S(1)} %get-tuple-element.72.refs_2_, ...), custom_call_target="tpu_custom_call" | custom-call | bytes 1245184 | tf_op jit(solution)/shard_map/pallas_call | solution.py:296
  (39 shorter events, 10.5 us)
Async XLA Ops:
  0.6 11.3 %copy-start.6 = (s32[1,3]{1,0:T(1,128)S(1)}, s32[1,3]{1,0:T(1,128)}, u32[]{:S(2)}) copy-start(s32[1,3]{1,0:T(1,128)} %slots.1) | copy-start | bytes 40
  0.6 18.5 %collective-permute-start = (f32[512,256]{1,0:T(8,128)}, f32[512,256]{1,0:T(8,128)S(1)}, u32[]{:S(2)}, u32[]{:S(2)}) collective-permute-start(f32[512,256]{1,0:T(8,128)} %probes.5), channel_id=1, source_target_pairs={{1,24},{2,25},{3,26},{4,27},{5,28},{6,29},{7,30},{8,0},{9,1},{10,2... | collective-permute-start | bytes 1572872 | tf_op jit(solution)/shard_map/ppermute | solution.py:315
  6.5 1.6 %copy-start = (f32[512,2,512]{2,1,0:T(2,128)S(1)}, f32[512,2,512]{2,1,0:T(2,128)}, u32[]{:S(2)}) copy-start(f32[512,2,512]{2,1,0:T(2,128)} %param.7) | copy-start | bytes 6291460
  8.1 1.0 %copy-start.3 = (f32[512,256]{1,0:T(8,128)S(1)}, f32[512,256]{1,0:T(8,128)}, u32[]{:S(2)}) copy-start(f32[512,256]{1,0:T(8,128)} %probes.5) | copy-start | bytes 1572868
  9.1 4.5 %copy-start.1 = (f32[512,2,512]{2,1,0:T(2,128)S(1)}, f32[512,2,512]{2,1,0:T(2,128)}, u32[]{:S(2)}) copy-start(f32[512,2,512]{2,1,0:T(2,128)} %param.7) | copy-start | bytes 6291460
  9.1 4.5 %copy-start.2 = (f32[512,256]{1,0:T(8,128)S(1)}, f32[512,256]{1,0:T(8,128)}, u32[]{:S(2)}) copy-start(f32[512,256]{1,0:T(8,128)} %samples.1) | copy-start | bytes 1572868
  10.0 14.6 %collective-permute-start.1 = (f32[512,128]{1,0:T(8,128)S(1)}, f32[512,128]{1,0:T(8,128)S(1)}, u32[]{:S(2)}, u32[]{:S(2)}) collective-permute-start(f32[512,128]{1,0:T(8,128)S(1)} %shard_map.87), channel_id=1, source_target_pairs={{0,8},{1,9},{2,10},{3,11},{4,12},{5,13},{6,14},{7,15},{8,16},{9,17... | collective-permute-start | bytes 786440 | tf_op jit(solution)/shard_map/ppermute | solution.py:315
  11.9 1.0 %copy-start.5 = (f32[1,3,2,128,128]{4,3,2,1,0:T(8,128)S(1)}, f32[1,3,2,128,128]{4,3,2,1,0:T(8,128)}, u32[]{:S(2)}) copy-start(f32[1,3,2,128,128]{4,3,2,1,0:T(8,128)} %couplings.1) | copy-start | bytes 1179652
  15.3 9.4 %copy-start.4 = (f32[512,256]{1,0:T(8,128)S(1)}, f32[512,256]{1,0:T(8,128)}, u32[]{:S(2)}) copy-start(f32[512,256]{1,0:T(8,128)} %probes.5) | copy-start | bytes 1572868
  20.3 17.9 %collective-permute-start.3 = (f32[512,128]{1,0:T(8,128)S(1)}, f32[512,128]{1,0:T(8,128)S(1)}, u32[]{:S(2)}, u32[]{:S(2)}) collective-permute-start(f32[512,128]{1,0:T(8,128)S(1)} %get-tuple-element.55), channel_id=1, source_target_pairs={{0,8},{1,9},{2,10},{3,11},{4,12},{5,13},{6,14},{7,15},{8,16},{9,17... | collective-permute-start | bytes 786440 | tf_op jit(solution)/shard_map/ppermute | solution.py:315
  28.9 9.3 %collective-permute-start.2 = (f32[128,128]{1,0:T(8,128)S(1)}, f32[128,128]{1,0:T(8,128)S(1)}, u32[]{:S(2)}, u32[]{:S(2)}) collective-permute-start(f32[128,128]{1,0:T(8,128)S(1)} %get-tuple-element.89), channel_id=1, source_target_pairs={{0,16},{1,17},{2,18},{3,19},{4,20},{5,21},{6,22},{7,23},{8,24},{9,... | collective-permute-start | bytes 196616 | tf_op jit(solution)/shard_map/ppermute | solution.py:315
  31.5 9.4 %collective-permute-start.4 = (f32[128,128]{1,0:T(8,128)S(1)}, f32[128,128]{1,0:T(8,128)S(1)}, u32[]{:S(2)}, u32[]{:S(2)}) collective-permute-start(f32[128,128]{1,0:T(8,128)S(1)} %get-tuple-element.89), channel_id=1, source_target_pairs={{1,16},{2,17},{3,18},{4,19},{5,20},{6,21},{7,22},{9,24},{10,25},{1... | collective-permute-start | bytes 196616 | tf_op jit(solution)/shard_map/ppermute | solution.py:315
  34.1 9.7 %collective-permute-start.6 = (f32[128,256]{1,0:T(8,128)S(1)}, f32[128,256]{1,0:T(8,128)S(1)}, u32[]{:S(2)}, u32[]{:S(2)}) collective-permute-start(f32[128,256]{1,0:T(8,128)S(1)} %get-tuple-element.54.mine_probes), channel_id=1, source_target_pairs={{0,8},{1,9},{2,10},{3,11},{4,12},{5,13},{6,14},{7,15},{8,0},{9,1},... | collective-permute-start | bytes 393224 | tf_op jit(solution)/shard_map/ppermute | solution.py:315
  35.8 6.4 %collective-permute-start.7 = (f32[128,128]{1,0:T(8,128)S(1)}, f32[128,128]{1,0:T(8,128)S(1)}, u32[]{:S(2)}, u32[]{:S(2)}) collective-permute-start(f32[128,128]{1,0:T(8,128)S(1)} %get-tuple-element.88.mine), channel_id=1, source_target_pairs={{1,0},{2,1},{3,2},{4,3},{5,4},{6,5},{7,6},{9,8},{10,9},{11,10},{12... | collective-permute-start | bytes 196616 | tf_op jit(solution)/shard_map/ppermute | solution.py:315
  41.2 4.3 %collective-permute-start.5 = (f32[128,128]{1,0:T(8,128)S(1)}, f32[128,128]{1,0:T(8,128)S(1)}, u32[]{:S(2)}, u32[]{:S(2)}) collective-permute-start(f32[128,128]{1,0:T(8,128)S(1)} %shard_map.90.mine), channel_id=1, source_target_pairs={{0,8},{1,9},{2,10},{3,11},{4,12},{5,13},{6,14},{7,15},{8,0},{9,1},... | collective-permute-start | bytes 196616 | tf_op jit(solution)/shard_map/ppermute | solution.py:315
  42.5 7.1 %collective-permute-start.8 = (f32[128,128]{1,0:T(8,128)S(1)}, f32[128,128]{1,0:T(8,128)S(1)}, u32[]{:S(2)}, u32[]{:S(2)}) collective-permute-start(f32[128,128]{1,0:T(8,128)S(1)} %shard_map.92), channel_id=1, source_target_pairs={{0,16},{1,17},{2,18},{3,19},{4,20},{5,21},{6,22},{7,23},{8,24},{9,... | collective-permute-start | bytes 196616 | tf_op jit(solution)/shard_map/ppermute | solution.py:315
  49.6 6.5 %collective-permute-start.10 = (f32[128,256]{1,0:T(8,128)S(1)}, f32[128,256]{1,0:T(8,128)S(1)}, u32[]{:S(2)}, u32[]{:S(2)}) collective-permute-start(f32[128,256]{1,0:T(8,128)S(1)} %get-tuple-element.72.refs_2_), channel_id=1, source_target_pairs={{0,1},{1,0},{2,3},{3,2},{4,5},{5,4},{6,7},{7,6},{8,9},{9,8},{10,11... | collective-permute-start | bytes 393224 | tf_op jit(solution)/shard_map/ppermute | solution.py:315
  49.7 7.2 %collective-permute-start.9 = (f32[128,256]{1,0:T(8,128)S(1)}, f32[128,256]{1,0:T(8,128)S(1)}, u32[]{:S(2)}, u32[]{:S(2)}) collective-permute-start(f32[128,256]{1,0:T(8,128)S(1)} %get-tuple-element.72.refs_2_), channel_id=1, source_target_pairs={{1,2},{2,1},{3,4},{4,3},{5,6},{6,5},{9,10},{10,9},{11,12},{12,11},... | collective-permute-start | bytes 393224 | tf_op jit(solution)/shard_map/ppermute | solution.py:315
  52.1 7.9 %collective-permute-start.12 = (f32[128,128]{1,0:T(8,128)S(1)}, f32[128,128]{1,0:T(8,128)S(1)}, u32[]{:S(2)}, u32[]{:S(2)}) collective-permute-start(f32[128,128]{1,0:T(8,128)S(1)} %sub.3.mine_last), channel_id=1, source_target_pairs={{0,8},{1,9},{2,10},{3,11},{4,12},{5,13},{6,14},{7,15},{8,0},{9,1},... | collective-permute-start | bytes 196616 | tf_op jit(solution)/shard_map/ppermute | solution.py:315
  53.4 6.5 %collective-permute-start.13 = (f32[128,128]{1,0:T(8,128)S(1)}, f32[128,128]{1,0:T(8,128)S(1)}, u32[]{:S(2)}, u32[]{:S(2)}) collective-permute-start(f32[128,128]{1,0:T(8,128)S(1)} %get-tuple-element.79), channel_id=1, source_target_pairs={{0,16},{1,17},{2,18},{3,19},{4,20},{5,21},{6,22},{7,23},{8,24},{9,... | collective-permute-start | bytes 196616 | tf_op jit(solution)/shard_map/ppermute | solution.py:315
  57.2 6.2 %collective-permute-start.11 = (f32[128,128]{1,0:T(8,128)S(1)}, f32[128,128]{1,0:T(8,128)S(1)}, u32[]{:S(2)}, u32[]{:S(2)}) collective-permute-start(f32[128,128]{1,0:T(8,128)S(1)} %get-tuple-element.76.mine.refs_0_), channel_id=1, source_target_pairs={{0,16},{1,17},{2,18},{3,19},{4,20},{5,21},{6,22},{7,23},{8,24},{9,... | collective-permute-start | bytes 196616 | tf_op jit(solution)/shard_map/ppermute | solution.py:315
  60.5 8.7 %collective-permute-start.15 = (f32[128,128]{1,0:T(8,128)S(1)}, f32[128,128]{1,0:T(8,128)S(1)}, u32[]{:S(2)}, u32[]{:S(2)}) collective-permute-start(f32[128,128]{1,0:T(8,128)S(1)} %get-tuple-element.83.refs_5_), channel_id=1, source_target_pairs={{0,8},{1,9},{2,10},{3,11},{4,12},{5,13},{6,14},{7,15},{8,0},{9,1},... | collective-permute-start | bytes 196616 | tf_op jit(solution)/shard_map/ppermute | solution.py:315
  63.3 5.9 %collective-permute-start.14 = (f32[128,128]{1,0:T(8,128)S(1)}, f32[128,128]{1,0:T(8,128)S(1)}, u32[]{:S(2)}, u32[]{:S(2)}) collective-permute-start(f32[128,128]{1,0:T(8,128)S(1)} %get-tuple-element.82.refs_1_), channel_id=1, source_target_pairs={{0,16},{1,17},{2,18},{3,19},{4,20},{5,21},{6,22},{7,23},{8,24},{9,... | collective-permute-start | bytes 196616 | tf_op jit(solution)/shard_map/ppermute | solution.py:315

commit v19 on v17

--- a/solution.py
+++ b/solution.py
@@ -9,7 +9,7 @@
 
 HIGHEST = lax.Precision.HIGHEST
 ROWS = 8
-GROUP = 4
+GROUP = 8
 BOTH = ("leaf", "clusters")
 
 
@@ -36,8 +36,8 @@
     scaled = [None] * blocks
     used = 0
 
-    def pair_of(k, j):
-        return (lane == ROWS * k + j) | (lane == ROWS * k + j + 1)
+    def panel_lanes(k):
+        return (lane >= ROWS * k) & (lane < ROWS * (k + 1))
 
     def columns_of(tile, k):
         return [across_lanes(tile, ROWS * k + n) for n in range(ROWS)]
@@ -54,10 +54,10 @@
         for n, col in enumerate(columns_of(tile, k)):
             held[pl.ds(ROWS * n, ROWS), :] = col
         block = {(n, m): row_of(held, ROWS * m + n) for n in range(ROWS) for m in range(n + 1)}
+        tile = jnp.where(panel_lanes(k), jnp.where(lane == sub + ROWS * k, 1.0, 0.0), tile)
         steps = []
         pivots = jnp.ones((ROWS, size), jnp.float32)
         for j in range(0, ROWS, 2):
-            tile = jnp.where(pair_of(k, j), jnp.where(lane == sub + ROWS * k, 1.0, 0.0), tile)
             held = scratch.at[pl.ds(used, ROWS), :]
             used += ROWS
             held[...] = tile
@@ -81,13 +81,14 @@
         return steps, pivots
 
     def below(i, k, steps):
-        tile, cols = rows[i], columns_of(rows[i], k)
+        cols = columns_of(rows[i], k)
+        tile = jnp.where(panel_lanes(k), 0.0, rows[i])
         for j, step in zip(range(0, ROWS, 2), steps):
             row, next_row, col_rows = step[4:]
             f, g = factors(cols[j], cols[j + 1], step)
             for n, (x, y) in enumerate(col_rows, j + 2):
                 cols[n] = cols[n] - (f * x + g * y)
-            tile = jnp.where(pair_of(k, j), 0.0, tile) - (f * row + g * next_row)
+            tile = tile - (f * row + g * next_row)
         rows[i] = tile
 
     waiting = None
@@ -393,7 +394,7 @@
             (first,) = call(
                 functools.partial(quad_kernel, level), [square], blocks[level - 1], inner, outer, first
             )
-            away, first = lax.optimization_barrier((away, first))
+            away, _ = lax.optimization_barrier((away, first))
             (term_last,) = call(
                 functools.partial(term_kernel, level), [square_last], blocks[-1], probe_last, away
             )

time: 71.3 us -> 70.1 us (0.983)
  Pallas kernels: 21.5 us -> 20.2 us
    pallas_call x15, Pallas kernels: 21.5 us -> 20.2 us  [call(): pl.pallas_call(kernel, out_shape=outs, in_specs=specs, out_specs=out_spec...]
  transfers between devices with their start and end apart: 16 -> 16, of which waited for: 6 -> 6; matrix products, arithmetic and copies ran while one was open for 0% -> 0% of each run, Pallas kernels for 28% -> 27%
where the time goes in v19:
time: 70.1 us; the launch traced here: 69.7 us
  starting transfers between devices  31.7 us (45%)
  Pallas kernels  20.2 us (29%)
  waiting for transfers between devices  13.1 us (19%)
  local copies, waits for them, and re-layouts  3.65 us (5%)
  between operations  1.06 us (2%)
    ppermute x16, starting transfers between devices, permuted(): return lax.ppermute(value, BOTH, pairs)  31.7 us
    pallas_call x15, Pallas kernels, call(): pl.pallas_call(kernel, out_shape=outs, in_specs=specs, out_specs=out_spec...  20.2 us
    ppermute x16, waiting for transfers between devices, permuted(): return lax.ppermute(value, BOTH, pairs)  13.1 us
    unnamed x14, local copies, waits for them, and re-layouts  3.63 us
  transfers between devices with their start and end apart: 16, of which 6 were waited for; matrix products, arithmetic and copies ran while one was open for 0% of the time, Pallas kernels for 27%

profile of v19, /device:TPU:4, one launch (start us, length us, event | category | flops | bytes accessed | tf_op | source)
XLA Modules:
  0.0 69.7 jit_solution(7194509048024963974)
XLA Ops:
  0.6 5.8 %collective-permute-start = (f32[512,256]{1,0:T(8,128)}, f32[512,256]{1,0:T(8,128)S(1)}, u32[]{:S(2)}, u32[]{:S(2)}) collective-permute-start(f32[512,256]{1,0:T(8,128)} %probes.5), channel_id=1, source_target_pairs={{1,24},{2,25},{3,26},{4,27},{5,28},{6,29},{7,30},{8,0},{9,1},{10,2... | collective-permute-start | bytes 1572872 | tf_op jit(solution)/shard_map/ppermute | solution.py:316
  6.5 1.6 %copy-done = f32[512,2,512]{2,1,0:T(2,128)S(1)} copy-done((f32[512,2,512]{2,1,0:T(2,128)S(1)}, f32[512,2,512]{2,1,0:T(2,128)}, u32[]{:S(2)}) %copy-start) | copy-done | bytes 2097176
  10.0 1.9 %collective-permute-start.1 = (f32[512,128]{1,0:T(8,128)S(1)}, f32[512,128]{1,0:T(8,128)S(1)}, u32[]{:S(2)}, u32[]{:S(2)}) collective-permute-start(f32[512,128]{1,0:T(8,128)S(1)} %shard_map.87), channel_id=1, source_target_pairs={{0,8},{1,9},{2,10},{3,11},{4,12},{5,13},{6,14},{7,15},{8,16},{9,17... | collective-permute-start | bytes 786440 | tf_op jit(solution)/shard_map/ppermute | solution.py:316
  13.6 1.6 %shard_map.84 = (f32[512,256]{1,0:T(8,128)S(1)}, f32[512,128]{1,0:T(8,128)S(1)}) custom-call(f32[4096,128]{1,0:T(8,128)S(1)} %bitcast.6, f32[512,256]{1,0:T(8,128)S(1)} %copy-done.3, f32[512,256]{1,0:T(8,128)S(1)} %copy-done.2), custom_call_target="tpu_custom_call" | custom-call | flops 805306368 | bytes 3932160 | tf_op jit(solution)/shard_map/pallas_call | solution.py:297
  15.3 3.8 %collective-permute-done.following = f32[512,256]{1,0:T(8,128)S(1)} collective-permute-done((f32[512,256]{1,0:T(8,128)}, f32[512,256]{1,0:T(8,128)S(1)}, u32[]{:S(2)}, u32[]{:S(2)}) %collective-permute-start) | collective-permute-done | bytes 524320 | tf_op jit(solution)/shard_map/ppermute | solution.py:316
  19.1 1.2 %shard_map.86 = (f32[512,128]{1,0:T(8,128)S(1)}, f32[512,128]{1,0:T(8,128)S(1)}, f32[512,128]{1,0:T(8,128)S(1)}) custom-call(f32[4096,128]{1,0:T(8,128)S(1)} %bitcast.7, f32[512,256]{1,0:T(8,128)S(1)} %get-tuple-element.44.rest, f32[512,256]{1,0:T(8,128)S(1)} %collective-permute-done.following, ...), custom_call_target="tpu_custom_call", output_to_operand_aliasing={{2}: (3, {})} | custom-call | flops 805306368 | bytes 4194304 | tf_op jit(solution)/shard_map/pallas_call | solution.py:297
  20.3 1.9 %collective-permute-start.3 = (f32[512,128]{1,0:T(8,128)S(1)}, f32[512,128]{1,0:T(8,128)S(1)}, u32[]{:S(2)}, u32[]{:S(2)}) collective-permute-start(f32[512,128]{1,0:T(8,128)S(1)} %get-tuple-element.53), channel_id=1, source_target_pairs={{0,8},{1,9},{2,10},{3,11},{4,12},{5,13},{6,14},{7,15},{8,16},{9,17... | collective-permute-start | bytes 786440 | tf_op jit(solution)/shard_map/ppermute | solution.py:316
  22.2 2.4 %collective-permute-done.1.handed = f32[512,128]{1,0:T(8,128)S(1)} collective-permute-done((f32[512,128]{1,0:T(8,128)S(1)}, f32[512,128]{1,0:T(8,128)S(1)}, u32[]{:S(2)}, u32[]{:S(2)}) %collective-permute-start.1) | collective-permute-done | bytes 262176 | tf_op jit(solution)/shard_map/ppermute | solution.py:316
  24.6 3.8 %shard_map.88 = (f32[512,128]{1,0:T(8,128)S(1)}, f32[128,128]{1,0:T(8,128)S(1)}, f32[128,128]{1,0:T(8,128)S(1)}, f32[128,256]{1,0:T(8,128)S(1)}) custom-call(f32[512,128]{1,0:T(8,128)S(1)} %get-tuple-element.51.rest, f32[512,128]{1,0:T(8,128)S(1)} %collective-permute-done.1.handed, f32[512,256]{1,0:T(8,128)S(1)} %copy-done.4), custom_call_target="tpu_custom_call" | custom-call | flops 805306368 | bytes 1572864 | tf_op jit(solution)/shard_map/pallas_call | solution.py:297
  28.4 2.6 %collective-permute-start.2 = (f32[128,128]{1,0:T(8,128)S(1)}, f32[128,128]{1,0:T(8,128)S(1)}, u32[]{:S(2)}, u32[]{:S(2)}) collective-permute-start(f32[128,128]{1,0:T(8,128)S(1)} %get-tuple-element.85), channel_id=1, source_target_pairs={{0,16},{1,17},{2,18},{3,19},{4,20},{5,21},{6,22},{7,23},{8,24},{9,... | collective-permute-start | bytes 196616 | tf_op jit(solution)/shard_map/ppermute | solution.py:316
  31.0 2.6 %collective-permute-start.4 = (f32[128,128]{1,0:T(8,128)S(1)}, f32[128,128]{1,0:T(8,128)S(1)}, u32[]{:S(2)}, u32[]{:S(2)}) collective-permute-start(f32[128,128]{1,0:T(8,128)S(1)} %get-tuple-element.85), channel_id=1, source_target_pairs={{1,16},{2,17},{3,18},{4,19},{5,20},{6,21},{7,22},{9,24},{10,25},{1... | collective-permute-start | bytes 196616 | tf_op jit(solution)/shard_map/ppermute | solution.py:316
  33.7 1.6 %collective-permute-start.6 = (f32[128,256]{1,0:T(8,128)S(1)}, f32[128,256]{1,0:T(8,128)S(1)}, u32[]{:S(2)}, u32[]{:S(2)}) collective-permute-start(f32[128,256]{1,0:T(8,128)S(1)} %get-tuple-element.52.mine_probes), channel_id=1, source_target_pairs={{0,8},{1,9},{2,10},{3,11},{4,12},{5,13},{6,14},{7,15},{8,0},{9,1},... | collective-permute-start | bytes 393224 | tf_op jit(solution)/shard_map/ppermute | solution.py:316
  35.3 2.6 %collective-permute-start.7 = (f32[128,128]{1,0:T(8,128)S(1)}, f32[128,128]{1,0:T(8,128)S(1)}, u32[]{:S(2)}, u32[]{:S(2)}) collective-permute-start(f32[128,128]{1,0:T(8,128)S(1)} %get-tuple-element.84.mine), channel_id=1, source_target_pairs={{1,0},{2,1},{3,2},{4,3},{5,4},{6,5},{7,6},{9,8},{10,9},{11,10},{12... | collective-permute-start | bytes 196616 | tf_op jit(solution)/shard_map/ppermute | solution.py:316
  37.9 1.5 %shard_map.89 = (f32[512,128]{1,0:T(8,128)}, f32[128,128]{1,0:T(8,128)S(1)}) custom-call(f32[512,128]{1,0:T(8,128)S(1)} %get-tuple-element.50.rest, f32[512,128]{1,0:T(8,128)S(1)} %collective-permute-done.3.handed, f32[512,128]{1,0:T(8,128)S(1)} %get-tuple-element.55.far, f32[128,128]{1,0:T(8,128)S(1)} %get-tuple-element.56.inverse), custom_call_target="tpu_custom_call" | custom-call | flops 805306368 | bytes 1179648 | tf_op jit(solution)/shard_map/pallas_call | solution.py:297
  42.0 1.4 %collective-permute-start.8 = (f32[128,128]{1,0:T(8,128)S(1)}, f32[128,128]{1,0:T(8,128)S(1)}, u32[]{:S(2)}, u32[]{:S(2)}) collective-permute-start(f32[128,128]{1,0:T(8,128)S(1)} %shard_map.92), channel_id=1, source_target_pairs={{0,16},{1,17},{2,18},{3,19},{4,20},{5,21},{6,22},{7,23},{8,24},{9,... | collective-permute-start | bytes 196616 | tf_op jit(solution)/shard_map/ppermute | solution.py:316
  43.4 1.6 %collective-permute-done.5.theirs = f32[128,128]{1,0:T(8,128)S(1)} collective-permute-done((f32[128,128]{1,0:T(8,128)S(1)}, f32[128,128]{1,0:T(8,128)S(1)}, u32[]{:S(2)}, u32[]{:S(2)}) %collective-permute-start.5) | collective-permute-done | bytes 65568 | tf_op jit(solution)/shard_map/ppermute | solution.py:316
  45.0 3.6 %shard_map.91 = (f32[128,128]{1,0:T(8,128)S(1)}, f32[128,256]{1,0:T(8,128)S(1)}, f32[128,128]{1,0:T(8,128)S(1)}) custom-call(f32[128,128]{1,0:T(8,128)S(1)} %shard_map.90.mine, f32[128,128]{1,0:T(8,128)S(1)} %collective-permute-done.5.theirs, f32[128,256]{1,0:T(8,128)S(1)} %get-tuple-element.52.mine_probes, f32[128,256]{1,0:T(8,128)S(1)} %collective-permute-done.6.theirs_probes), custom_call_target="tpu_custom_call" | custom-call | flops 6442450944 | bytes 655360 | tf_op jit(solution)/shard_map/pallas_call | solution.py:297
  48.7 2.7 %collective-permute-start.9 = (f32[128,256]{1,0:T(8,128)S(1)}, f32[128,256]{1,0:T(8,128)S(1)}, u32[]{:S(2)}, u32[]{:S(2)}) collective-permute-start(f32[128,256]{1,0:T(8,128)S(1)} %get-tuple-element.70.refs_2_), channel_id=1, source_target_pairs={{1,2},{2,1},{3,4},{4,3},{5,6},{6,5},{9,10},{10,9},{11,12},{12,11},... | collective-permute-start | bytes 393224 | tf_op jit(solution)/shard_map/ppermute | solution.py:316
  51.4 2.6 %collective-permute-start.13 = (f32[128,128]{1,0:T(8,128)S(1)}, f32[128,128]{1,0:T(8,128)S(1)}, u32[]{:S(2)}, u32[]{:S(2)}) collective-permute-start(f32[128,128]{1,0:T(8,128)S(1)} %get-tuple-element.77), channel_id=1, source_target_pairs={{0,16},{1,17},{2,18},{3,19},{4,20},{5,21},{6,22},{7,23},{8,24},{9,... | collective-permute-start | bytes 196616 | tf_op jit(solution)/shard_map/ppermute | solution.py:316
  56.2 3.0 %collective-permute-start.11 = (f32[128,128]{1,0:T(8,128)S(1)}, f32[128,128]{1,0:T(8,128)S(1)}, u32[]{:S(2)}, u32[]{:S(2)}) collective-permute-start(f32[128,128]{1,0:T(8,128)S(1)} %get-tuple-element.74.mine.refs_0_), channel_id=1, source_target_pairs={{0,16},{1,17},{2,18},{3,19},{4,20},{5,21},{6,22},{7,23},{8,24},{9,... | collective-permute-start | bytes 196616 | tf_op jit(solution)/shard_map/ppermute | solution.py:316
  59.8 1.6 %collective-permute-start.15 = (f32[128,128]{1,0:T(8,128)S(1)}, f32[128,128]{1,0:T(8,128)S(1)}, u32[]{:S(2)}, u32[]{:S(2)}) collective-permute-start(f32[128,128]{1,0:T(8,128)S(1)} %get-tuple-element.79.refs_5_), channel_id=1, source_target_pairs={{0,8},{1,9},{2,10},{3,11},{4,12},{5,13},{6,14},{7,15},{8,0},{9,1},... | collective-permute-start | bytes 196616 | tf_op jit(solution)/shard_map/ppermute | solution.py:316
  61.4 3.3 %collective-permute-done.11.theirs.refs_3_ = f32[128,128]{1,0:T(8,128)S(1)} collective-permute-done((f32[128,128]{1,0:T(8,128)S(1)}, f32[128,128]{1,0:T(8,128)S(1)}, u32[]{:S(2)}, u32[]{:S(2)}) %collective-permute-start.11) | collective-permute-done | bytes 65568 | tf_op jit(solution)/shard_map/ppermute | solution.py:316
  64.8 3.2 %shard_map.96.inverse = f32[128,128]{1,0:T(8,128)S(1)} custom-call(f32[128,128]{1,0:T(8,128)S(1)} %get-tuple-element.74.mine.refs_0_, f32[128,128]{1,0:T(8,128)S(1)} %collective-permute-done.11.theirs.refs_3_), custom_call_target="tpu_custom_call" | custom-call | bytes 196608 | tf_op jit(solution)/shard_map/pallas_call | solution.py:297
  68.0 1.6 %shard_map.98 = (f32[1,2,256,128]{3,2,1,0:T(8,128)}, f32[1,128,256]{2,1,0:T(8,128)}, f32[1,128,256]{2,1,0:T(8,128)}) custom-call(f32[128,128]{1,0:T(8,128)S(1)} %shard_map.96.inverse, f32[128,128]{1,0:T(8,128)S(1)} %get-tuple-element.74.mine.refs_0_, f32[128,128]{1,0:T(8,128)S(1)} %get-tuple-element.78.refs_1_, f32[128,256]{1,0:T(8,128)S(1)} %get-tuple-element.70.refs_2_, ...), custom_call_target="tpu_custom_call" | custom-call | bytes 1245184 | tf_op jit(solution)/shard_map/pallas_call | solution.py:297
  (39 shorter events, 9.1 us)
Async XLA Ops:
  0.6 11.3 %copy-start.6 = (s32[1,3]{1,0:T(1,128)S(1)}, s32[1,3]{1,0:T(1,128)}, u32[]{:S(2)}) copy-start(s32[1,3]{1,0:T(1,128)} %slots.1) | copy-start | bytes 40
  0.6 18.5 %collective-permute-start = (f32[512,256]{1,0:T(8,128)}, f32[512,256]{1,0:T(8,128)S(1)}, u32[]{:S(2)}, u32[]{:S(2)}) collective-permute-start(f32[512,256]{1,0:T(8,128)} %probes.5), channel_id=1, source_target_pairs={{1,24},{2,25},{3,26},{4,27},{5,28},{6,29},{7,30},{8,0},{9,1},{10,2... | collective-permute-start | bytes 1572872 | tf_op jit(solution)/shard_map/ppermute | solution.py:316
  6.5 1.6 %copy-start = (f32[512,2,512]{2,1,0:T(2,128)S(1)}, f32[512,2,512]{2,1,0:T(2,128)}, u32[]{:S(2)}) copy-start(f32[512,2,512]{2,1,0:T(2,128)} %param.7) | copy-start | bytes 6291460
  8.1 1.0 %copy-start.3 = (f32[512,256]{1,0:T(8,128)S(1)}, f32[512,256]{1,0:T(8,128)}, u32[]{:S(2)}) copy-start(f32[512,256]{1,0:T(8,128)} %probes.5) | copy-start | bytes 1572868
  9.1 4.5 %copy-start.1 = (f32[512,2,512]{2,1,0:T(2,128)S(1)}, f32[512,2,512]{2,1,0:T(2,128)}, u32[]{:S(2)}) copy-start(f32[512,2,512]{2,1,0:T(2,128)} %param.7) | copy-start | bytes 6291460
  9.1 4.5 %copy-start.2 = (f32[512,256]{1,0:T(8,128)S(1)}, f32[512,256]{1,0:T(8,128)}, u32[]{:S(2)}) copy-start(f32[512,256]{1,0:T(8,128)} %samples.1) | copy-start | bytes 1572868
  10.0 14.6 %collective-permute-start.1 = (f32[512,128]{1,0:T(8,128)S(1)}, f32[512,128]{1,0:T(8,128)S(1)}, u32[]{:S(2)}, u32[]{:S(2)}) collective-permute-start(f32[512,128]{1,0:T(8,128)S(1)} %shard_map.87), channel_id=1, source_target_pairs={{0,8},{1,9},{2,10},{3,11},{4,12},{5,13},{6,14},{7,15},{8,16},{9,17... | collective-permute-start | bytes 786440 | tf_op jit(solution)/shard_map/ppermute | solution.py:316
  11.9 1.0 %copy-start.5 = (f32[1,3,2,128,128]{4,3,2,1,0:T(8,128)S(1)}, f32[1,3,2,128,128]{4,3,2,1,0:T(8,128)}, u32[]{:S(2)}) copy-start(f32[1,3,2,128,128]{4,3,2,1,0:T(8,128)} %couplings.1) | copy-start | bytes 1179652
  15.3 9.4 %copy-start.4 = (f32[512,256]{1,0:T(8,128)S(1)}, f32[512,256]{1,0:T(8,128)}, u32[]{:S(2)}) copy-start(f32[512,256]{1,0:T(8,128)} %probes.5) | copy-start | bytes 1572868
  20.3 17.6 %collective-permute-start.3 = (f32[512,128]{1,0:T(8,128)S(1)}, f32[512,128]{1,0:T(8,128)S(1)}, u32[]{:S(2)}, u32[]{:S(2)}) collective-permute-start(f32[512,128]{1,0:T(8,128)S(1)} %get-tuple-element.53), channel_id=1, source_target_pairs={{0,8},{1,9},{2,10},{3,11},{4,12},{5,13},{6,14},{7,15},{8,16},{9,17... | collective-permute-start | bytes 786440 | tf_op jit(solution)/shard_map/ppermute | solution.py:316
  28.4 9.5 %collective-permute-start.2 = (f32[128,128]{1,0:T(8,128)S(1)}, f32[128,128]{1,0:T(8,128)S(1)}, u32[]{:S(2)}, u32[]{:S(2)}) collective-permute-start(f32[128,128]{1,0:T(8,128)S(1)} %get-tuple-element.85), channel_id=1, source_target_pairs={{0,16},{1,17},{2,18},{3,19},{4,20},{5,21},{6,22},{7,23},{8,24},{9,... | collective-permute-start | bytes 196616 | tf_op jit(solution)/shard_map/ppermute | solution.py:316
  31.0 9.4 %collective-permute-start.4 = (f32[128,128]{1,0:T(8,128)S(1)}, f32[128,128]{1,0:T(8,128)S(1)}, u32[]{:S(2)}, u32[]{:S(2)}) collective-permute-start(f32[128,128]{1,0:T(8,128)S(1)} %get-tuple-element.85), channel_id=1, source_target_pairs={{1,16},{2,17},{3,18},{4,19},{5,20},{6,21},{7,22},{9,24},{10,25},{1... | collective-permute-start | bytes 196616 | tf_op jit(solution)/shard_map/ppermute | solution.py:316
  33.7 9.8 %collective-permute-start.6 = (f32[128,256]{1,0:T(8,128)S(1)}, f32[128,256]{1,0:T(8,128)S(1)}, u32[]{:S(2)}, u32[]{:S(2)}) collective-permute-start(f32[128,256]{1,0:T(8,128)S(1)} %get-tuple-element.52.mine_probes), channel_id=1, source_target_pairs={{0,8},{1,9},{2,10},{3,11},{4,12},{5,13},{6,14},{7,15},{8,0},{9,1},... | collective-permute-start | bytes 393224 | tf_op jit(solution)/shard_map/ppermute | solution.py:316
  35.3 6.4 %collective-permute-start.7 = (f32[128,128]{1,0:T(8,128)S(1)}, f32[128,128]{1,0:T(8,128)S(1)}, u32[]{:S(2)}, u32[]{:S(2)}) collective-permute-start(f32[128,128]{1,0:T(8,128)S(1)} %get-tuple-element.84.mine), channel_id=1, source_target_pairs={{1,0},{2,1},{3,2},{4,3},{5,4},{6,5},{7,6},{9,8},{10,9},{11,10},{12... | collective-permute-start | bytes 196616 | tf_op jit(solution)/shard_map/ppermute | solution.py:316
  40.7 4.3 %collective-permute-start.5 = (f32[128,128]{1,0:T(8,128)S(1)}, f32[128,128]{1,0:T(8,128)S(1)}, u32[]{:S(2)}, u32[]{:S(2)}) collective-permute-start(f32[128,128]{1,0:T(8,128)S(1)} %shard_map.90.mine), channel_id=1, source_target_pairs={{0,8},{1,9},{2,10},{3,11},{4,12},{5,13},{6,14},{7,15},{8,0},{9,1},... | collective-permute-start | bytes 196616 | tf_op jit(solution)/shard_map/ppermute | solution.py:316
  42.0 6.6 %collective-permute-start.8 = (f32[128,128]{1,0:T(8,128)S(1)}, f32[128,128]{1,0:T(8,128)S(1)}, u32[]{:S(2)}, u32[]{:S(2)}) collective-permute-start(f32[128,128]{1,0:T(8,128)S(1)} %shard_map.92), channel_id=1, source_target_pairs={{0,16},{1,17},{2,18},{3,19},{4,20},{5,21},{6,22},{7,23},{8,24},{9,... | collective-permute-start | bytes 196616 | tf_op jit(solution)/shard_map/ppermute | solution.py:316
  48.6 6.4 %collective-permute-start.10 = (f32[128,256]{1,0:T(8,128)S(1)}, f32[128,256]{1,0:T(8,128)S(1)}, u32[]{:S(2)}, u32[]{:S(2)}) collective-permute-start(f32[128,256]{1,0:T(8,128)S(1)} %get-tuple-element.70.refs_2_), channel_id=1, source_target_pairs={{0,1},{1,0},{2,3},{3,2},{4,5},{5,4},{6,7},{7,6},{8,9},{9,8},{10,11... | collective-permute-start | bytes 393224 | tf_op jit(solution)/shard_map/ppermute | solution.py:316
  48.7 7.2 %collective-permute-start.9 = (f32[128,256]{1,0:T(8,128)S(1)}, f32[128,256]{1,0:T(8,128)S(1)}, u32[]{:S(2)}, u32[]{:S(2)}) collective-permute-start(f32[128,256]{1,0:T(8,128)S(1)} %get-tuple-element.70.refs_2_), channel_id=1, source_target_pairs={{1,2},{2,1},{3,4},{4,3},{5,6},{6,5},{9,10},{10,9},{11,12},{12,11},... | collective-permute-start | bytes 393224 | tf_op jit(solution)/shard_map/ppermute | solution.py:316
  51.4 7.7 %collective-permute-start.13 = (f32[128,128]{1,0:T(8,128)S(1)}, f32[128,128]{1,0:T(8,128)S(1)}, u32[]{:S(2)}, u32[]{:S(2)}) collective-permute-start(f32[128,128]{1,0:T(8,128)S(1)} %get-tuple-element.77), channel_id=1, source_target_pairs={{0,16},{1,17},{2,18},{3,19},{4,20},{5,21},{6,22},{7,23},{8,24},{9,... | collective-permute-start | bytes 196616 | tf_op jit(solution)/shard_map/ppermute | solution.py:316
  54.0 5.1 %collective-permute-start.12 = (f32[128,128]{1,0:T(8,128)S(1)}, f32[128,128]{1,0:T(8,128)S(1)}, u32[]{:S(2)}, u32[]{:S(2)}) collective-permute-start(f32[128,128]{1,0:T(8,128)S(1)} %sub.3.mine_last), channel_id=1, source_target_pairs={{0,8},{1,9},{2,10},{3,11},{4,12},{5,13},{6,14},{7,15},{8,0},{9,1},... | collective-permute-start | bytes 196616 | tf_op jit(solution)/shard_map/ppermute | solution.py:316
  56.2 8.6 %collective-permute-start.11 = (f32[128,128]{1,0:T(8,128)S(1)}, f32[128,128]{1,0:T(8,128)S(1)}, u32[]{:S(2)}, u32[]{:S(2)}) collective-permute-start(f32[128,128]{1,0:T(8,128)S(1)} %get-tuple-element.74.mine.refs_0_), channel_id=1, source_target_pairs={{0,16},{1,17},{2,18},{3,19},{4,20},{5,21},{6,22},{7,23},{8,24},{9,... | collective-permute-start | bytes 196616 | tf_op jit(solution)/shard_map/ppermute | solution.py:316
  59.7 8.2 %collective-permute-start.14 = (f32[128,128]{1,0:T(8,128)S(1)}, f32[128,128]{1,0:T(8,128)S(1)}, u32[]{:S(2)}, u32[]{:S(2)}) collective-permute-start(f32[128,128]{1,0:T(8,128)S(1)} %get-tuple-element.78.refs_1_), channel_id=1, source_target_pairs={{0,16},{1,17},{2,18},{3,19},{4,20},{5,21},{6,22},{7,23},{8,24},{9,... | collective-permute-start | bytes 196616 | tf_op jit(solution)/shard_map/ppermute | solution.py:316
  59.8 8.1 %collective-permute-start.15 = (f32[128,128]{1,0:T(8,128)S(1)}, f32[128,128]{1,0:T(8,128)S(1)}, u32[]{:S(2)}, u32[]{:S(2)}) collective-permute-start(f32[128,128]{1,0:T(8,128)S(1)} %get-tuple-element.79.refs_5_), channel_id=1, source_target_pairs={{0,8},{1,9},{2,10},{3,11},{4,12},{5,13},{6,14},{7,15},{8,0},{9,1},... | collective-permute-start | bytes 196616 | tf_op jit(solution)/shard_map/ppermute | solution.py:316

commit v20 on v19

--- a/solution.py
+++ b/solution.py
@@ -9,7 +9,7 @@
 
 HIGHEST = lax.Precision.HIGHEST
 ROWS = 8
-GROUP = 8
+GROUP = 16
 BOTH = ("leaf", "clusters")
 
 
@@ -80,12 +80,18 @@
         rows[k] = tile
         return steps, pivots
 
+    def scaled_factors(u, v, step):
+        a, b, c, inverse = step[:4]
+        a, b, c = a * inverse, b * inverse, c * inverse
+        return u * c - v * b, v * a - u * b
+
     def below(i, k, steps):
         cols = columns_of(rows[i], k)
         tile = jnp.where(panel_lanes(k), 0.0, rows[i])
         for j, step in zip(range(0, ROWS, 2), steps):
             row, next_row, col_rows = step[4:]
-            f, g = factors(cols[j], cols[j + 1], step)
+            ratios = factors if i == k + 1 else scaled_factors
+            f, g = ratios(cols[j], cols[j + 1], step)
             for n, (x, y) in enumerate(col_rows, j + 2):
                 cols[n] = cols[n] - (f * x + g * y)
             tile = tile - (f * row + g * next_row)
@@ -148,10 +154,11 @@
     columns = far.shape[1]
     block = rest[...] - handed[...]
     far[...] = block
-    products = dot(block, jnp.concatenate([block, probes[...]], axis=1), 0, 0)
-    factor = inverse_factor(products[:, :columns], scratch)
+    gram = dot(block, block, 0, 0)
+    cross = dot(block, probes[...], 0, 0)
+    factor = inverse_factor(gram, scratch)
     inverse[...] = factor
-    coef = dot(factor, products)
+    coef = dot(factor, jnp.concatenate([gram, cross], axis=1))
     probe_coef[...] = coef[:, columns:]
     sample_coef[...] = coef[:, :columns]
 

time: 70.1 us -> 70.1 us (level)
  no operation moved by 1% of the time
where the time goes in v20:
time: 70.1 us; the launch traced here: 69.7 us
  starting transfers between devices  31.7 us (45%)
  Pallas kernels  20.2 us (29%)
  waiting for transfers between devices  13.1 us (19%)
  local copies, waits for them, and re-layouts  3.65 us (5%)
  between operations  1.05 us (1%)
    ppermute x16, starting transfers between devices, permuted(): return lax.ppermute(value, BOTH, pairs)  31.7 us
    pallas_call x15, Pallas kernels, call(): pl.pallas_call(kernel, out_shape=outs, in_specs=specs, out_specs=out_spec...  20.2 us
    ppermute x16, waiting for transfers between devices, permuted(): return lax.ppermute(value, BOTH, pairs)  13.1 us
    unnamed x14, local copies, waits for them, and re-layouts  3.63 us
  transfers between devices with their start and end apart: 16, of which 6 were waited for; matrix products, arithmetic and copies ran while one was open for 0% of the time, Pallas kernels for 27%

profile of v20, /device:TPU:4, one launch (start us, length us, event | category | flops | bytes accessed | tf_op | source)
XLA Modules:
  0.0 69.7 jit_solution(17131771939006245961)
XLA Ops:
  0.6 5.8 %collective-permute-start = (f32[512,256]{1,0:T(8,128)}, f32[512,256]{1,0:T(8,128)S(1)}, u32[]{:S(2)}, u32[]{:S(2)}) collective-permute-start(f32[512,256]{1,0:T(8,128)} %probes.5), channel_id=1, source_target_pairs={{1,24},{2,25},{3,26},{4,27},{5,28},{6,29},{7,30},{8,0},{9,1},{10,2... | collective-permute-start | bytes 1572872 | tf_op jit(solution)/shard_map/ppermute | solution.py:323
  6.5 1.6 %copy-done = f32[512,2,512]{2,1,0:T(2,128)S(1)} copy-done((f32[512,2,512]{2,1,0:T(2,128)S(1)}, f32[512,2,512]{2,1,0:T(2,128)}, u32[]{:S(2)}) %copy-start) | copy-done | bytes 2097176
  10.0 1.9 %collective-permute-start.1 = (f32[512,128]{1,0:T(8,128)S(1)}, f32[512,128]{1,0:T(8,128)S(1)}, u32[]{:S(2)}, u32[]{:S(2)}) collective-permute-start(f32[512,128]{1,0:T(8,128)S(1)} %shard_map.87), channel_id=1, source_target_pairs={{0,8},{1,9},{2,10},{3,11},{4,12},{5,13},{6,14},{7,15},{8,16},{9,17... | collective-permute-start | bytes 786440 | tf_op jit(solution)/shard_map/ppermute | solution.py:323
  13.6 1.6 %shard_map.84 = (f32[512,256]{1,0:T(8,128)S(1)}, f32[512,128]{1,0:T(8,128)S(1)}) custom-call(f32[4096,128]{1,0:T(8,128)S(1)} %bitcast.6, f32[512,256]{1,0:T(8,128)S(1)} %copy-done.3, f32[512,256]{1,0:T(8,128)S(1)} %copy-done.2), custom_call_target="tpu_custom_call" | custom-call | flops 805306368 | bytes 3932160 | tf_op jit(solution)/shard_map/pallas_call | solution.py:304
  15.3 3.8 %collective-permute-done.following = f32[512,256]{1,0:T(8,128)S(1)} collective-permute-done((f32[512,256]{1,0:T(8,128)}, f32[512,256]{1,0:T(8,128)S(1)}, u32[]{:S(2)}, u32[]{:S(2)}) %collective-permute-start) | collective-permute-done | bytes 524320 | tf_op jit(solution)/shard_map/ppermute | solution.py:323
  19.1 1.2 %shard_map.86 = (f32[512,128]{1,0:T(8,128)S(1)}, f32[512,128]{1,0:T(8,128)S(1)}, f32[512,128]{1,0:T(8,128)S(1)}) custom-call(f32[4096,128]{1,0:T(8,128)S(1)} %bitcast.7, f32[512,256]{1,0:T(8,128)S(1)} %get-tuple-element.44.rest, f32[512,256]{1,0:T(8,128)S(1)} %collective-permute-done.following, ...), custom_call_target="tpu_custom_call", output_to_operand_aliasing={{2}: (3, {})} | custom-call | flops 805306368 | bytes 4194304 | tf_op jit(solution)/shard_map/pallas_call | solution.py:304
  20.3 1.9 %collective-permute-start.3 = (f32[512,128]{1,0:T(8,128)S(1)}, f32[512,128]{1,0:T(8,128)S(1)}, u32[]{:S(2)}, u32[]{:S(2)}) collective-permute-start(f32[512,128]{1,0:T(8,128)S(1)} %get-tuple-element.53), channel_id=1, source_target_pairs={{0,8},{1,9},{2,10},{3,11},{4,12},{5,13},{6,14},{7,15},{8,16},{9,17... | collective-permute-start | bytes 786440 | tf_op jit(solution)/shard_map/ppermute | solution.py:323
  22.2 2.4 %collective-permute-done.1.handed = f32[512,128]{1,0:T(8,128)S(1)} collective-permute-done((f32[512,128]{1,0:T(8,128)S(1)}, f32[512,128]{1,0:T(8,128)S(1)}, u32[]{:S(2)}, u32[]{:S(2)}) %collective-permute-start.1) | collective-permute-done | bytes 262176 | tf_op jit(solution)/shard_map/ppermute | solution.py:323
  24.6 3.8 %shard_map.88 = (f32[512,128]{1,0:T(8,128)S(1)}, f32[128,128]{1,0:T(8,128)S(1)}, f32[128,128]{1,0:T(8,128)S(1)}, f32[128,256]{1,0:T(8,128)S(1)}) custom-call(f32[512,128]{1,0:T(8,128)S(1)} %get-tuple-element.51.rest, f32[512,128]{1,0:T(8,128)S(1)} %collective-permute-done.1.handed, f32[512,256]{1,0:T(8,128)S(1)} %copy-done.4), custom_call_target="tpu_custom_call" | custom-call | flops 805306368 | bytes 1572864 | tf_op jit(solution)/shard_map/pallas_call | solution.py:304
  28.4 2.6 %collective-permute-start.2 = (f32[128,128]{1,0:T(8,128)S(1)}, f32[128,128]{1,0:T(8,128)S(1)}, u32[]{:S(2)}, u32[]{:S(2)}) collective-permute-start(f32[128,128]{1,0:T(8,128)S(1)} %get-tuple-element.85), channel_id=1, source_target_pairs={{0,16},{1,17},{2,18},{3,19},{4,20},{5,21},{6,22},{7,23},{8,24},{9,... | collective-permute-start | bytes 196616 | tf_op jit(solution)/shard_map/ppermute | solution.py:323
  31.0 2.6 %collective-permute-start.4 = (f32[128,128]{1,0:T(8,128)S(1)}, f32[128,128]{1,0:T(8,128)S(1)}, u32[]{:S(2)}, u32[]{:S(2)}) collective-permute-start(f32[128,128]{1,0:T(8,128)S(1)} %get-tuple-element.85), channel_id=1, source_target_pairs={{1,16},{2,17},{3,18},{4,19},{5,20},{6,21},{7,22},{9,24},{10,25},{1... | collective-permute-start | bytes 196616 | tf_op jit(solution)/shard_map/ppermute | solution.py:323
  33.7 1.6 %collective-permute-start.6 = (f32[128,256]{1,0:T(8,128)S(1)}, f32[128,256]{1,0:T(8,128)S(1)}, u32[]{:S(2)}, u32[]{:S(2)}) collective-permute-start(f32[128,256]{1,0:T(8,128)S(1)} %get-tuple-element.52.mine_probes), channel_id=1, source_target_pairs={{0,8},{1,9},{2,10},{3,11},{4,12},{5,13},{6,14},{7,15},{8,0},{9,1},... | collective-permute-start | bytes 393224 | tf_op jit(solution)/shard_map/ppermute | solution.py:323
  35.3 2.6 %collective-permute-start.7 = (f32[128,128]{1,0:T(8,128)S(1)}, f32[128,128]{1,0:T(8,128)S(1)}, u32[]{:S(2)}, u32[]{:S(2)}) collective-permute-start(f32[128,128]{1,0:T(8,128)S(1)} %get-tuple-element.84.mine), channel_id=1, source_target_pairs={{1,0},{2,1},{3,2},{4,3},{5,4},{6,5},{7,6},{9,8},{10,9},{11,10},{12... | collective-permute-start | bytes 196616 | tf_op jit(solution)/shard_map/ppermute | solution.py:323
  37.9 1.5 %shard_map.89 = (f32[512,128]{1,0:T(8,128)}, f32[128,128]{1,0:T(8,128)S(1)}) custom-call(f32[512,128]{1,0:T(8,128)S(1)} %get-tuple-element.50.rest, f32[512,128]{1,0:T(8,128)S(1)} %collective-permute-done.3.handed, f32[512,128]{1,0:T(8,128)S(1)} %get-tuple-element.55.far, f32[128,128]{1,0:T(8,128)S(1)} %get-tuple-element.56.inverse), custom_call_target="tpu_custom_call" | custom-call | flops 805306368 | bytes 1179648 | tf_op jit(solution)/shard_map/pallas_call | solution.py:304
  42.0 1.4 %collective-permute-start.8 = (f32[128,128]{1,0:T(8,128)S(1)}, f32[128,128]{1,0:T(8,128)S(1)}, u32[]{:S(2)}, u32[]{:S(2)}) collective-permute-start(f32[128,128]{1,0:T(8,128)S(1)} %shard_map.92), channel_id=1, source_target_pairs={{0,16},{1,17},{2,18},{3,19},{4,20},{5,21},{6,22},{7,23},{8,24},{9,... | collective-permute-start | bytes 196616 | tf_op jit(solution)/shard_map/ppermute | solution.py:323
  43.4 1.6 %collective-permute-done.5.theirs = f32[128,128]{1,0:T(8,128)S(1)} collective-permute-done((f32[128,128]{1,0:T(8,128)S(1)}, f32[128,128]{1,0:T(8,128)S(1)}, u32[]{:S(2)}, u32[]{:S(2)}) %collective-permute-start.5) | collective-permute-done | bytes 65568 | tf_op jit(solution)/shard_map/ppermute | solution.py:323
  45.0 3.6 %shard_map.91 = (f32[128,128]{1,0:T(8,128)S(1)}, f32[128,256]{1,0:T(8,128)S(1)}, f32[128,128]{1,0:T(8,128)S(1)}) custom-call(f32[128,128]{1,0:T(8,128)S(1)} %shard_map.90.mine, f32[128,128]{1,0:T(8,128)S(1)} %collective-permute-done.5.theirs, f32[128,256]{1,0:T(8,128)S(1)} %get-tuple-element.52.mine_probes, f32[128,256]{1,0:T(8,128)S(1)} %collective-permute-done.6.theirs_probes), custom_call_target="tpu_custom_call" | custom-call | flops 6442450944 | bytes 655360 | tf_op jit(solution)/shard_map/pallas_call | solution.py:304
  48.7 2.7 %collective-permute-start.9 = (f32[128,256]{1,0:T(8,128)S(1)}, f32[128,256]{1,0:T(8,128)S(1)}, u32[]{:S(2)}, u32[]{:S(2)}) collective-permute-start(f32[128,256]{1,0:T(8,128)S(1)} %get-tuple-element.70.refs_2_), channel_id=1, source_target_pairs={{1,2},{2,1},{3,4},{4,3},{5,6},{6,5},{9,10},{10,9},{11,12},{12,11},... | collective-permute-start | bytes 393224 | tf_op jit(solution)/shard_map/ppermute | solution.py:323
  51.4 2.6 %collective-permute-start.13 = (f32[128,128]{1,0:T(8,128)S(1)}, f32[128,128]{1,0:T(8,128)S(1)}, u32[]{:S(2)}, u32[]{:S(2)}) collective-permute-start(f32[128,128]{1,0:T(8,128)S(1)} %get-tuple-element.77), channel_id=1, source_target_pairs={{0,16},{1,17},{2,18},{3,19},{4,20},{5,21},{6,22},{7,23},{8,24},{9,... | collective-permute-start | bytes 196616 | tf_op jit(solution)/shard_map/ppermute | solution.py:323
  56.2 3.0 %collective-permute-start.11 = (f32[128,128]{1,0:T(8,128)S(1)}, f32[128,128]{1,0:T(8,128)S(1)}, u32[]{:S(2)}, u32[]{:S(2)}) collective-permute-start(f32[128,128]{1,0:T(8,128)S(1)} %get-tuple-element.74.mine.refs_0_), channel_id=1, source_target_pairs={{0,16},{1,17},{2,18},{3,19},{4,20},{5,21},{6,22},{7,23},{8,24},{9,... | collective-permute-start | bytes 196616 | tf_op jit(solution)/shard_map/ppermute | solution.py:323
  59.9 1.6 %collective-permute-start.15 = (f32[128,128]{1,0:T(8,128)S(1)}, f32[128,128]{1,0:T(8,128)S(1)}, u32[]{:S(2)}, u32[]{:S(2)}) collective-permute-start(f32[128,128]{1,0:T(8,128)S(1)} %get-tuple-element.79.refs_5_), channel_id=1, source_target_pairs={{0,8},{1,9},{2,10},{3,11},{4,12},{5,13},{6,14},{7,15},{8,0},{9,1},... | collective-permute-start | bytes 196616 | tf_op jit(solution)/shard_map/ppermute | solution.py:323
  61.5 3.3 %collective-permute-done.11.theirs.refs_3_ = f32[128,128]{1,0:T(8,128)S(1)} collective-permute-done((f32[128,128]{1,0:T(8,128)S(1)}, f32[128,128]{1,0:T(8,128)S(1)}, u32[]{:S(2)}, u32[]{:S(2)}) %collective-permute-start.11) | collective-permute-done | bytes 65568 | tf_op jit(solution)/shard_map/ppermute | solution.py:323
  64.8 3.1 %shard_map.96.inverse = f32[128,128]{1,0:T(8,128)S(1)} custom-call(f32[128,128]{1,0:T(8,128)S(1)} %get-tuple-element.74.mine.refs_0_, f32[128,128]{1,0:T(8,128)S(1)} %collective-permute-done.11.theirs.refs_3_), custom_call_target="tpu_custom_call" | custom-call | bytes 196608 | tf_op jit(solution)/shard_map/pallas_call | solution.py:304
  68.0 1.6 %shard_map.98 = (f32[1,2,256,128]{3,2,1,0:T(8,128)}, f32[1,128,256]{2,1,0:T(8,128)}, f32[1,128,256]{2,1,0:T(8,128)}) custom-call(f32[128,128]{1,0:T(8,128)S(1)} %shard_map.96.inverse, f32[128,128]{1,0:T(8,128)S(1)} %get-tuple-element.74.mine.refs_0_, f32[128,128]{1,0:T(8,128)S(1)} %get-tuple-element.78.refs_1_, f32[128,256]{1,0:T(8,128)S(1)} %get-tuple-element.70.refs_2_, ...), custom_call_target="tpu_custom_call" | custom-call | bytes 1245184 | tf_op jit(solution)/shard_map/pallas_call | solution.py:304
  (39 shorter events, 9.1 us)
Async XLA Ops:
  0.6 11.3 %copy-start.6 = (s32[1,3]{1,0:T(1,128)S(1)}, s32[1,3]{1,0:T(1,128)}, u32[]{:S(2)}) copy-start(s32[1,3]{1,0:T(1,128)} %slots.1) | copy-start | bytes 40
  0.6 18.5 %collective-permute-start = (f32[512,256]{1,0:T(8,128)}, f32[512,256]{1,0:T(8,128)S(1)}, u32[]{:S(2)}, u32[]{:S(2)}) collective-permute-start(f32[512,256]{1,0:T(8,128)} %probes.5), channel_id=1, source_target_pairs={{1,24},{2,25},{3,26},{4,27},{5,28},{6,29},{7,30},{8,0},{9,1},{10,2... | collective-permute-start | bytes 1572872 | tf_op jit(solution)/shard_map/ppermute | solution.py:323
  6.5 1.6 %copy-start = (f32[512,2,512]{2,1,0:T(2,128)S(1)}, f32[512,2,512]{2,1,0:T(2,128)}, u32[]{:S(2)}) copy-start(f32[512,2,512]{2,1,0:T(2,128)} %param.7) | copy-start | bytes 6291460
  8.1 1.0 %copy-start.3 = (f32[512,256]{1,0:T(8,128)S(1)}, f32[512,256]{1,0:T(8,128)}, u32[]{:S(2)}) copy-start(f32[512,256]{1,0:T(8,128)} %probes.5) | copy-start | bytes 1572868
  9.1 4.5 %copy-start.1 = (f32[512,2,512]{2,1,0:T(2,128)S(1)}, f32[512,2,512]{2,1,0:T(2,128)}, u32[]{:S(2)}) copy-start(f32[512,2,512]{2,1,0:T(2,128)} %param.7) | copy-start | bytes 6291460
  9.1 4.5 %copy-start.2 = (f32[512,256]{1,0:T(8,128)S(1)}, f32[512,256]{1,0:T(8,128)}, u32[]{:S(2)}) copy-start(f32[512,256]{1,0:T(8,128)} %samples.1) | copy-start | bytes 1572868
  10.0 14.6 %collective-permute-start.1 = (f32[512,128]{1,0:T(8,128)S(1)}, f32[512,128]{1,0:T(8,128)S(1)}, u32[]{:S(2)}, u32[]{:S(2)}) collective-permute-start(f32[512,128]{1,0:T(8,128)S(1)} %shard_map.87), channel_id=1, source_target_pairs={{0,8},{1,9},{2,10},{3,11},{4,12},{5,13},{6,14},{7,15},{8,16},{9,17... | collective-permute-start | bytes 786440 | tf_op jit(solution)/shard_map/ppermute | solution.py:323
  11.9 1.0 %copy-start.5 = (f32[1,3,2,128,128]{4,3,2,1,0:T(8,128)S(1)}, f32[1,3,2,128,128]{4,3,2,1,0:T(8,128)}, u32[]{:S(2)}) copy-start(f32[1,3,2,128,128]{4,3,2,1,0:T(8,128)} %couplings.1) | copy-start | bytes 1179652
  15.3 9.4 %copy-start.4 = (f32[512,256]{1,0:T(8,128)S(1)}, f32[512,256]{1,0:T(8,128)}, u32[]{:S(2)}) copy-start(f32[512,256]{1,0:T(8,128)} %probes.5) | copy-start | bytes 1572868
  20.3 17.7 %collective-permute-start.3 = (f32[512,128]{1,0:T(8,128)S(1)}, f32[512,128]{1,0:T(8,128)S(1)}, u32[]{:S(2)}, u32[]{:S(2)}) collective-permute-start(f32[512,128]{1,0:T(8,128)S(1)} %get-tuple-element.53), channel_id=1, source_target_pairs={{0,8},{1,9},{2,10},{3,11},{4,12},{5,13},{6,14},{7,15},{8,16},{9,17... | collective-permute-start | bytes 786440 | tf_op jit(solution)/shard_map/ppermute | solution.py:323
  28.4 9.5 %collective-permute-start.2 = (f32[128,128]{1,0:T(8,128)S(1)}, f32[128,128]{1,0:T(8,128)S(1)}, u32[]{:S(2)}, u32[]{:S(2)}) collective-permute-start(f32[128,128]{1,0:T(8,128)S(1)} %get-tuple-element.85), channel_id=1, source_target_pairs={{0,16},{1,17},{2,18},{3,19},{4,20},{5,21},{6,22},{7,23},{8,24},{9,... | collective-permute-start | bytes 196616 | tf_op jit(solution)/shard_map/ppermute | solution.py:323
  31.0 9.4 %collective-permute-start.4 = (f32[128,128]{1,0:T(8,128)S(1)}, f32[128,128]{1,0:T(8,128)S(1)}, u32[]{:S(2)}, u32[]{:S(2)}) collective-permute-start(f32[128,128]{1,0:T(8,128)S(1)} %get-tuple-element.85), channel_id=1, source_target_pairs={{1,16},{2,17},{3,18},{4,19},{5,20},{6,21},{7,22},{9,24},{10,25},{1... | collective-permute-start | bytes 196616 | tf_op jit(solution)/shard_map/ppermute | solution.py:323
  33.7 9.8 %collective-permute-start.6 = (f32[128,256]{1,0:T(8,128)S(1)}, f32[128,256]{1,0:T(8,128)S(1)}, u32[]{:S(2)}, u32[]{:S(2)}) collective-permute-start(f32[128,256]{1,0:T(8,128)S(1)} %get-tuple-element.52.mine_probes), channel_id=1, source_target_pairs={{0,8},{1,9},{2,10},{3,11},{4,12},{5,13},{6,14},{7,15},{8,0},{9,1},... | collective-permute-start | bytes 393224 | tf_op jit(solution)/shard_map/ppermute | solution.py:323
  35.3 6.4 %collective-permute-start.7 = (f32[128,128]{1,0:T(8,128)S(1)}, f32[128,128]{1,0:T(8,128)S(1)}, u32[]{:S(2)}, u32[]{:S(2)}) collective-permute-start(f32[128,128]{1,0:T(8,128)S(1)} %get-tuple-element.84.mine), channel_id=1, source_target_pairs={{1,0},{2,1},{3,2},{4,3},{5,4},{6,5},{7,6},{9,8},{10,9},{11,10},{12... | collective-permute-start | bytes 196616 | tf_op jit(solution)/shard_map/ppermute | solution.py:323
  40.7 4.3 %collective-permute-start.5 = (f32[128,128]{1,0:T(8,128)S(1)}, f32[128,128]{1,0:T(8,128)S(1)}, u32[]{:S(2)}, u32[]{:S(2)}) collective-permute-start(f32[128,128]{1,0:T(8,128)S(1)} %shard_map.90.mine), channel_id=1, source_target_pairs={{0,8},{1,9},{2,10},{3,11},{4,12},{5,13},{6,14},{7,15},{8,0},{9,1},... | collective-permute-start | bytes 196616 | tf_op jit(solution)/shard_map/ppermute | solution.py:323
  42.0 6.6 %collective-permute-start.8 = (f32[128,128]{1,0:T(8,128)S(1)}, f32[128,128]{1,0:T(8,128)S(1)}, u32[]{:S(2)}, u32[]{:S(2)}) collective-permute-start(f32[128,128]{1,0:T(8,128)S(1)} %shard_map.92), channel_id=1, source_target_pairs={{0,16},{1,17},{2,18},{3,19},{4,20},{5,21},{6,22},{7,23},{8,24},{9,... | collective-permute-start | bytes 196616 | tf_op jit(solution)/shard_map/ppermute | solution.py:323
  48.7 6.3 %collective-permute-start.10 = (f32[128,256]{1,0:T(8,128)S(1)}, f32[128,256]{1,0:T(8,128)S(1)}, u32[]{:S(2)}, u32[]{:S(2)}) collective-permute-start(f32[128,256]{1,0:T(8,128)S(1)} %get-tuple-element.70.refs_2_), channel_id=1, source_target_pairs={{0,1},{1,0},{2,3},{3,2},{4,5},{5,4},{6,7},{7,6},{8,9},{9,8},{10,11... | collective-permute-start | bytes 393224 | tf_op jit(solution)/shard_map/ppermute | solution.py:323
  48.7 7.2 %collective-permute-start.9 = (f32[128,256]{1,0:T(8,128)S(1)}, f32[128,256]{1,0:T(8,128)S(1)}, u32[]{:S(2)}, u32[]{:S(2)}) collective-permute-start(f32[128,256]{1,0:T(8,128)S(1)} %get-tuple-element.70.refs_2_), channel_id=1, source_target_pairs={{1,2},{2,1},{3,4},{4,3},{5,6},{6,5},{9,10},{10,9},{11,12},{12,11},... | collective-permute-start | bytes 393224 | tf_op jit(solution)/shard_map/ppermute | solution.py:323
  51.4 7.8 %collective-permute-start.13 = (f32[128,128]{1,0:T(8,128)S(1)}, f32[128,128]{1,0:T(8,128)S(1)}, u32[]{:S(2)}, u32[]{:S(2)}) collective-permute-start(f32[128,128]{1,0:T(8,128)S(1)} %get-tuple-element.77), channel_id=1, source_target_pairs={{0,16},{1,17},{2,18},{3,19},{4,20},{5,21},{6,22},{7,23},{8,24},{9,... | collective-permute-start | bytes 196616 | tf_op jit(solution)/shard_map/ppermute | solution.py:323
  54.1 5.1 %collective-permute-start.12 = (f32[128,128]{1,0:T(8,128)S(1)}, f32[128,128]{1,0:T(8,128)S(1)}, u32[]{:S(2)}, u32[]{:S(2)}) collective-permute-start(f32[128,128]{1,0:T(8,128)S(1)} %sub.3.mine_last), channel_id=1, source_target_pairs={{0,8},{1,9},{2,10},{3,11},{4,12},{5,13},{6,14},{7,15},{8,0},{9,1},... | collective-permute-start | bytes 196616 | tf_op jit(solution)/shard_map/ppermute | solution.py:323
  56.2 8.6 %collective-permute-start.11 = (f32[128,128]{1,0:T(8,128)S(1)}, f32[128,128]{1,0:T(8,128)S(1)}, u32[]{:S(2)}, u32[]{:S(2)}) collective-permute-start(f32[128,128]{1,0:T(8,128)S(1)} %get-tuple-element.74.mine.refs_0_), channel_id=1, source_target_pairs={{0,16},{1,17},{2,18},{3,19},{4,20},{5,21},{6,22},{7,23},{8,24},{9,... | collective-permute-start | bytes 196616 | tf_op jit(solution)/shard_map/ppermute | solution.py:323
  59.8 8.2 %collective-permute-start.14 = (f32[128,128]{1,0:T(8,128)S(1)}, f32[128,128]{1,0:T(8,128)S(1)}, u32[]{:S(2)}, u32[]{:S(2)}) collective-permute-start(f32[128,128]{1,0:T(8,128)S(1)} %get-tuple-element.78.refs_1_), channel_id=1, source_target_pairs={{0,16},{1,17},{2,18},{3,19},{4,20},{5,21},{6,22},{7,23},{8,24},{9,... | collective-permute-start | bytes 196616 | tf_op jit(solution)/shard_map/ppermute | solution.py:323
  59.9 8.1 %collective-permute-start.15 = (f32[128,128]{1,0:T(8,128)S(1)}, f32[128,128]{1,0:T(8,128)S(1)}, u32[]{:S(2)}, u32[]{:S(2)}) collective-permute-start(f32[128,128]{1,0:T(8,128)S(1)} %get-tuple-element.79.refs_5_), channel_id=1, source_target_pairs={{0,8},{1,9},{2,10},{3,11},{4,12},{5,13},{6,14},{7,15},{8,0},{9,1},... | collective-permute-start | bytes 196616 | tf_op jit(solution)/shard_map/ppermute | solution.py:323

commit v21 on v19

--- a/solution.py
+++ b/solution.py
@@ -148,10 +148,11 @@
     columns = far.shape[1]
     block = rest[...] - handed[...]
     far[...] = block
-    products = dot(block, jnp.concatenate([block, probes[...]], axis=1), 0, 0)
-    factor = inverse_factor(products[:, :columns], scratch)
+    gram = dot(block, block, 0, 0)
+    cross = dot(block, probes[...], 0, 0)
+    factor = inverse_factor(gram, scratch)
     inverse[...] = factor
-    coef = dot(factor, products)
+    coef = dot(factor, jnp.concatenate([gram, cross], axis=1))
     probe_coef[...] = coef[:, columns:]
     sample_coef[...] = coef[:, :columns]
 
@@ -177,7 +178,7 @@
         out[...] = jnp.concatenate([block, block.T], axis=1)
 
 
-def quad_kernel(level, block, inner, outer, coef, out):
+def quad_kernel(level, block, outer, inner, coef, out):
     node = member_node(level)
     inside = (node == 1) | (node == 2)
     main = jnp.where(inside, inner[...], outer[...])
@@ -380,19 +381,19 @@
         count = subtree // copies
         if count == 4:
             probe_first, probe_last = probe_coef[:, :columns], probe_coef[:, columns:]
+            outer = outer_swapped(probe_first, 2 * copies)
             inner = swapped(probe_first, 2 * copies)
-            outer = outer_swapped(probe_first, 2 * copies)
             away = outward(probe_last, 2 * copies)
             theirs_probe = swapped(probe_coef, copies)
             if level == 1:
-                inner, handed_last = lax.optimization_barrier((inner, handed_last))
+                outer, handed_last = lax.optimization_barrier((outer, handed_last))
                 leaf_basis, last = call(
                     leaf_last_kernel, [tall, square_last], rest_last, handed_last, far, inverse,
                     flops=work,
                 )
-                inner, outer, last = lax.optimization_barrier((inner, outer, last))
+                outer, inner, last = lax.optimization_barrier((outer, inner, last))
             (first,) = call(
-                functools.partial(quad_kernel, level), [square], blocks[level - 1], inner, outer, first
+                functools.partial(quad_kernel, level), [square], blocks[level - 1], outer, inner, first
             )
             away, _ = lax.optimization_barrier((away, first))
             (term_last,) = call(

time: 70.1 us -> 70.5 us (level)
  starting transfers between devices: 31.7 us -> 35.2 us
  waiting for transfers between devices: 13.1 us -> 10.1 us
    ppermute x16, starting transfers between devices: 31.7 us -> 35.2 us  [permuted(): return lax.ppermute(value, BOTH, pairs)]
    ppermute x16, waiting for transfers between devices: 13.1 us -> 10.1 us  [permuted(): return lax.ppermute(value, BOTH, pairs)]
  transfers between devices with their start and end apart: 16 -> 16, of which waited for: 6 -> 6; matrix products, arithmetic and copies ran while one was open for 0% -> 0% of each run, Pallas kernels for 27% -> 26%
where the time goes in v21:
time: 70.5 us; the launch traced here: 70.1 us
  starting transfers between devices  35.2 us (50%)
  Pallas kernels  20.1 us (29%)
  waiting for transfers between devices  10.1 us (14%)
  local copies, waits for them, and re-layouts  3.65 us (5%)
  between operations  1.06 us (2%)
    ppermute x16, starting transfers between devices, permuted(): return lax.ppermute(value, BOTH, pairs)  35.2 us
    pallas_call x15, Pallas kernels, call(): pl.pallas_call(kernel, out_shape=outs, in_specs=specs, out_specs=out_spec...  20.1 us
    ppermute x16, waiting for transfers between devices, permuted(): return lax.ppermute(value, BOTH, pairs)  10.1 us
    unnamed x14, local copies, waits for them, and re-layouts  3.63 us
  transfers between devices with their start and end apart: 16, of which 6 were waited for; matrix products, arithmetic and copies ran while one was open for 0% of the time, Pallas kernels for 26%

profile of v21, /device:TPU:4, one launch (start us, length us, event | category | flops | bytes accessed | tf_op | source)
XLA Modules:
  0.0 70.1 jit_solution(2683711605027028722)
XLA Ops:
  0.6 5.8 %collective-permute-start = (f32[512,256]{1,0:T(8,128)}, f32[512,256]{1,0:T(8,128)S(1)}, u32[]{:S(2)}, u32[]{:S(2)}) collective-permute-start(f32[512,256]{1,0:T(8,128)} %probes.5), channel_id=1, source_target_pairs={{1,24},{2,25},{3,26},{4,27},{5,28},{6,29},{7,30},{8,0},{9,1},{10,2... | collective-permute-start | bytes 1572872 | tf_op jit(solution)/shard_map/ppermute | solution.py:317
  6.5 1.6 %copy-done = f32[512,2,512]{2,1,0:T(2,128)S(1)} copy-done((f32[512,2,512]{2,1,0:T(2,128)S(1)}, f32[512,2,512]{2,1,0:T(2,128)}, u32[]{:S(2)}) %copy-start) | copy-done | bytes 2097176
  8.1 1.0 %copy-done.3 = f32[512,256]{1,0:T(8,128)S(1)} copy-done((f32[512,256]{1,0:T(8,128)S(1)}, f32[512,256]{1,0:T(8,128)}, u32[]{:S(2)}) %copy-start.3) | copy-done | bytes 524312
  10.0 1.9 %collective-permute-start.1 = (f32[512,128]{1,0:T(8,128)S(1)}, f32[512,128]{1,0:T(8,128)S(1)}, u32[]{:S(2)}, u32[]{:S(2)}) collective-permute-start(f32[512,128]{1,0:T(8,128)S(1)} %shard_map.87), channel_id=1, source_target_pairs={{0,8},{1,9},{2,10},{3,11},{4,12},{5,13},{6,14},{7,15},{8,16},{9,17... | collective-permute-start | bytes 786440 | tf_op jit(solution)/shard_map/ppermute | solution.py:317
  13.6 1.6 %shard_map.84 = (f32[512,256]{1,0:T(8,128)S(1)}, f32[512,128]{1,0:T(8,128)S(1)}) custom-call(f32[4096,128]{1,0:T(8,128)S(1)} %bitcast.6, f32[512,256]{1,0:T(8,128)S(1)} %copy-done.3, f32[512,256]{1,0:T(8,128)S(1)} %copy-done.2), custom_call_target="tpu_custom_call" | custom-call | flops 805306368 | bytes 3932160 | tf_op jit(solution)/shard_map/pallas_call | solution.py:298
  15.3 3.8 %collective-permute-done.following = f32[512,256]{1,0:T(8,128)S(1)} collective-permute-done((f32[512,256]{1,0:T(8,128)}, f32[512,256]{1,0:T(8,128)S(1)}, u32[]{:S(2)}, u32[]{:S(2)}) %collective-permute-start) | collective-permute-done | bytes 524320 | tf_op jit(solution)/shard_map/ppermute | solution.py:317
  19.1 1.2 %shard_map.86 = (f32[512,128]{1,0:T(8,128)S(1)}, f32[512,128]{1,0:T(8,128)S(1)}, f32[512,128]{1,0:T(8,128)S(1)}) custom-call(f32[4096,128]{1,0:T(8,128)S(1)} %bitcast.7, f32[512,256]{1,0:T(8,128)S(1)} %get-tuple-element.44.rest, f32[512,256]{1,0:T(8,128)S(1)} %collective-permute-done.following, ...), custom_call_target="tpu_custom_call", output_to_operand_aliasing={{2}: (3, {})} | custom-call | flops 805306368 | bytes 4194304 | tf_op jit(solution)/shard_map/pallas_call | solution.py:298
  20.3 1.9 %collective-permute-start.3 = (f32[512,128]{1,0:T(8,128)S(1)}, f32[512,128]{1,0:T(8,128)S(1)}, u32[]{:S(2)}, u32[]{:S(2)}) collective-permute-start(f32[512,128]{1,0:T(8,128)S(1)} %get-tuple-element.53), channel_id=1, source_target_pairs={{0,8},{1,9},{2,10},{3,11},{4,12},{5,13},{6,14},{7,15},{8,16},{9,17... | collective-permute-start | bytes 786440 | tf_op jit(solution)/shard_map/ppermute | solution.py:317
  22.2 2.4 %collective-permute-done.1.handed = f32[512,128]{1,0:T(8,128)S(1)} collective-permute-done((f32[512,128]{1,0:T(8,128)S(1)}, f32[512,128]{1,0:T(8,128)S(1)}, u32[]{:S(2)}, u32[]{:S(2)}) %collective-permute-start.1) | collective-permute-done | bytes 262176 | tf_op jit(solution)/shard_map/ppermute | solution.py:317
  24.6 3.7 %shard_map.88 = (f32[512,128]{1,0:T(8,128)S(1)}, f32[128,128]{1,0:T(8,128)S(1)}, f32[128,128]{1,0:T(8,128)S(1)}, f32[128,256]{1,0:T(8,128)S(1)}) custom-call(f32[512,128]{1,0:T(8,128)S(1)} %get-tuple-element.51.rest, f32[512,128]{1,0:T(8,128)S(1)} %collective-permute-done.1.handed, f32[512,256]{1,0:T(8,128)S(1)} %copy-done.4), custom_call_target="tpu_custom_call" | custom-call | flops 805306368 | bytes 1572864 | tf_op jit(solution)/shard_map/pallas_call | solution.py:298
  28.3 5.2 %collective-permute-start.2 = (f32[128,128]{1,0:T(8,128)S(1)}, f32[128,128]{1,0:T(8,128)S(1)}, u32[]{:S(2)}, u32[]{:S(2)}) collective-permute-start(f32[128,128]{1,0:T(8,128)S(1)} %get-tuple-element.85), channel_id=1, source_target_pairs={{1,16},{2,17},{3,18},{4,19},{5,20},{6,21},{7,22},{9,24},{10,25},{1... | collective-permute-start | bytes 196616 | tf_op jit(solution)/shard_map/ppermute | solution.py:317
  33.6 1.2 %collective-permute-start.6 = (f32[128,256]{1,0:T(8,128)S(1)}, f32[128,256]{1,0:T(8,128)S(1)}, u32[]{:S(2)}, u32[]{:S(2)}) collective-permute-start(f32[128,256]{1,0:T(8,128)S(1)} %get-tuple-element.52.mine_probes), channel_id=1, source_target_pairs={{0,8},{1,9},{2,10},{3,11},{4,12},{5,13},{6,14},{7,15},{8,0},{9,1},... | collective-permute-start | bytes 393224 | tf_op jit(solution)/shard_map/ppermute | solution.py:317
  34.8 4.5 %collective-permute-start.7 = (f32[128,128]{1,0:T(8,128)S(1)}, f32[128,128]{1,0:T(8,128)S(1)}, u32[]{:S(2)}, u32[]{:S(2)}) collective-permute-start(f32[128,128]{1,0:T(8,128)S(1)} %get-tuple-element.84.mine), channel_id=1, source_target_pairs={{1,0},{2,1},{3,2},{4,3},{5,4},{6,5},{7,6},{9,8},{10,9},{11,10},{12... | collective-permute-start | bytes 196616 | tf_op jit(solution)/shard_map/ppermute | solution.py:317
  39.4 1.5 %shard_map.89 = (f32[512,128]{1,0:T(8,128)}, f32[128,128]{1,0:T(8,128)S(1)}) custom-call(f32[512,128]{1,0:T(8,128)S(1)} %get-tuple-element.50.rest, f32[512,128]{1,0:T(8,128)S(1)} %collective-permute-done.3.handed, f32[512,128]{1,0:T(8,128)S(1)} %get-tuple-element.55.far, f32[128,128]{1,0:T(8,128)S(1)} %get-tuple-element.56.inverse), custom_call_target="tpu_custom_call" | custom-call | flops 805306368 | bytes 1179648 | tf_op jit(solution)/shard_map/pallas_call | solution.py:298
  41.7 2.7 %collective-permute-start.8 = (f32[128,128]{1,0:T(8,128)S(1)}, f32[128,128]{1,0:T(8,128)S(1)}, u32[]{:S(2)}, u32[]{:S(2)}) collective-permute-start(f32[128,128]{1,0:T(8,128)S(1)} %shard_map.92), channel_id=1, source_target_pairs={{0,16},{1,17},{2,18},{3,19},{4,20},{5,21},{6,22},{7,23},{8,24},{9,... | collective-permute-start | bytes 196616 | tf_op jit(solution)/shard_map/ppermute | solution.py:317
  45.5 3.6 %shard_map.91 = (f32[128,128]{1,0:T(8,128)S(1)}, f32[128,256]{1,0:T(8,128)S(1)}, f32[128,128]{1,0:T(8,128)S(1)}) custom-call(f32[128,128]{1,0:T(8,128)S(1)} %shard_map.90.mine, f32[128,128]{1,0:T(8,128)S(1)} %collective-permute-done.5.theirs, f32[128,256]{1,0:T(8,128)S(1)} %get-tuple-element.52.mine_probes, f32[128,256]{1,0:T(8,128)S(1)} %collective-permute-done.6.theirs_probes), custom_call_target="tpu_custom_call" | custom-call | flops 6442450944 | bytes 655360 | tf_op jit(solution)/shard_map/pallas_call | solution.py:298
  49.2 2.4 %collective-permute-start.9 = (f32[128,256]{1,0:T(8,128)S(1)}, f32[128,256]{1,0:T(8,128)S(1)}, u32[]{:S(2)}, u32[]{:S(2)}) collective-permute-start(f32[128,256]{1,0:T(8,128)S(1)} %get-tuple-element.70.refs_2_), channel_id=1, source_target_pairs={{1,2},{2,1},{3,4},{4,3},{5,6},{6,5},{9,10},{10,9},{11,12},{12,11},... | collective-permute-start | bytes 393224 | tf_op jit(solution)/shard_map/ppermute | solution.py:317
  51.6 1.9 %collective-permute-start.13 = (f32[128,128]{1,0:T(8,128)S(1)}, f32[128,128]{1,0:T(8,128)S(1)}, u32[]{:S(2)}, u32[]{:S(2)}) collective-permute-start(f32[128,128]{1,0:T(8,128)S(1)} %get-tuple-element.77), channel_id=1, source_target_pairs={{0,16},{1,17},{2,18},{3,19},{4,20},{5,21},{6,22},{7,23},{8,24},{9,... | collective-permute-start | bytes 196616 | tf_op jit(solution)/shard_map/ppermute | solution.py:317
  53.5 3.2 %collective-permute-start.12 = (f32[128,128]{1,0:T(8,128)S(1)}, f32[128,128]{1,0:T(8,128)S(1)}, u32[]{:S(2)}, u32[]{:S(2)}) collective-permute-start(f32[128,128]{1,0:T(8,128)S(1)} %sub.3.mine_last), channel_id=1, source_target_pairs={{0,8},{1,9},{2,10},{3,11},{4,12},{5,13},{6,14},{7,15},{8,0},{9,1},... | collective-permute-start | bytes 196616 | tf_op jit(solution)/shard_map/ppermute | solution.py:317
  59.5 2.0 %collective-permute-start.14 = (f32[128,128]{1,0:T(8,128)S(1)}, f32[128,128]{1,0:T(8,128)S(1)}, u32[]{:S(2)}, u32[]{:S(2)}) collective-permute-start(f32[128,128]{1,0:T(8,128)S(1)} %get-tuple-element.78.refs_1_), channel_id=1, source_target_pairs={{0,16},{1,17},{2,18},{3,19},{4,20},{5,21},{6,22},{7,23},{8,24},{9,... | collective-permute-start | bytes 196616 | tf_op jit(solution)/shard_map/ppermute | solution.py:317
  61.5 1.6 %collective-permute-start.15 = (f32[128,128]{1,0:T(8,128)S(1)}, f32[128,128]{1,0:T(8,128)S(1)}, u32[]{:S(2)}, u32[]{:S(2)}) collective-permute-start(f32[128,128]{1,0:T(8,128)S(1)} %get-tuple-element.79.refs_5_), channel_id=1, source_target_pairs={{0,8},{1,9},{2,10},{3,11},{4,12},{5,13},{6,14},{7,15},{8,0},{9,1},... | collective-permute-start | bytes 196616 | tf_op jit(solution)/shard_map/ppermute | solution.py:317
  63.1 2.1 %collective-permute-done.11.theirs.refs_3_ = f32[128,128]{1,0:T(8,128)S(1)} collective-permute-done((f32[128,128]{1,0:T(8,128)S(1)}, f32[128,128]{1,0:T(8,128)S(1)}, u32[]{:S(2)}, u32[]{:S(2)}) %collective-permute-start.11) | collective-permute-done | bytes 65568 | tf_op jit(solution)/shard_map/ppermute | solution.py:317
  65.2 3.2 %shard_map.96.inverse = f32[128,128]{1,0:T(8,128)S(1)} custom-call(f32[128,128]{1,0:T(8,128)S(1)} %get-tuple-element.74.mine.refs_0_, f32[128,128]{1,0:T(8,128)S(1)} %collective-permute-done.11.theirs.refs_3_), custom_call_target="tpu_custom_call" | custom-call | bytes 196608 | tf_op jit(solution)/shard_map/pallas_call | solution.py:298
  68.4 1.6 %shard_map.98 = (f32[1,2,256,128]{3,2,1,0:T(8,128)}, f32[1,128,256]{2,1,0:T(8,128)}, f32[1,128,256]{2,1,0:T(8,128)}) custom-call(f32[128,128]{1,0:T(8,128)S(1)} %shard_map.96.inverse, f32[128,128]{1,0:T(8,128)S(1)} %get-tuple-element.74.mine.refs_0_, f32[128,128]{1,0:T(8,128)S(1)} %get-tuple-element.78.refs_1_, f32[128,256]{1,0:T(8,128)S(1)} %get-tuple-element.70.refs_2_, ...), custom_call_target="tpu_custom_call" | custom-call | bytes 1245184 | tf_op jit(solution)/shard_map/pallas_call | solution.py:298
  (39 shorter events, 7.4 us)
Async XLA Ops:
  0.6 11.3 %copy-start.6 = (s32[1,3]{1,0:T(1,128)S(1)}, s32[1,3]{1,0:T(1,128)}, u32[]{:S(2)}) copy-start(s32[1,3]{1,0:T(1,128)} %slots.1) | copy-start | bytes 40
  0.6 18.5 %collective-permute-start = (f32[512,256]{1,0:T(8,128)}, f32[512,256]{1,0:T(8,128)S(1)}, u32[]{:S(2)}, u32[]{:S(2)}) collective-permute-start(f32[512,256]{1,0:T(8,128)} %probes.5), channel_id=1, source_target_pairs={{1,24},{2,25},{3,26},{4,27},{5,28},{6,29},{7,30},{8,0},{9,1},{10,2... | collective-permute-start | bytes 1572872 | tf_op jit(solution)/shard_map/ppermute | solution.py:317
  6.5 1.6 %copy-start = (f32[512,2,512]{2,1,0:T(2,128)S(1)}, f32[512,2,512]{2,1,0:T(2,128)}, u32[]{:S(2)}) copy-start(f32[512,2,512]{2,1,0:T(2,128)} %param.7) | copy-start | bytes 6291460
  8.1 1.0 %copy-start.3 = (f32[512,256]{1,0:T(8,128)S(1)}, f32[512,256]{1,0:T(8,128)}, u32[]{:S(2)}) copy-start(f32[512,256]{1,0:T(8,128)} %probes.5) | copy-start | bytes 1572868
  9.1 4.5 %copy-start.1 = (f32[512,2,512]{2,1,0:T(2,128)S(1)}, f32[512,2,512]{2,1,0:T(2,128)}, u32[]{:S(2)}) copy-start(f32[512,2,512]{2,1,0:T(2,128)} %param.7) | copy-start | bytes 6291460
  9.1 4.5 %copy-start.2 = (f32[512,256]{1,0:T(8,128)S(1)}, f32[512,256]{1,0:T(8,128)}, u32[]{:S(2)}) copy-start(f32[512,256]{1,0:T(8,128)} %samples.1) | copy-start | bytes 1572868
  10.0 14.6 %collective-permute-start.1 = (f32[512,128]{1,0:T(8,128)S(1)}, f32[512,128]{1,0:T(8,128)S(1)}, u32[]{:S(2)}, u32[]{:S(2)}) collective-permute-start(f32[512,128]{1,0:T(8,128)S(1)} %shard_map.87), channel_id=1, source_target_pairs={{0,8},{1,9},{2,10},{3,11},{4,12},{5,13},{6,14},{7,15},{8,16},{9,17... | collective-permute-start | bytes 786440 | tf_op jit(solution)/shard_map/ppermute | solution.py:317
  11.9 1.0 %copy-start.5 = (f32[1,3,2,128,128]{4,3,2,1,0:T(8,128)S(1)}, f32[1,3,2,128,128]{4,3,2,1,0:T(8,128)}, u32[]{:S(2)}) copy-start(f32[1,3,2,128,128]{4,3,2,1,0:T(8,128)} %couplings.1) | copy-start | bytes 1179652
  15.3 9.4 %copy-start.4 = (f32[512,256]{1,0:T(8,128)S(1)}, f32[512,256]{1,0:T(8,128)}, u32[]{:S(2)}) copy-start(f32[512,256]{1,0:T(8,128)} %probes.5) | copy-start | bytes 1572868
  20.3 19.1 %collective-permute-start.3 = (f32[512,128]{1,0:T(8,128)S(1)}, f32[512,128]{1,0:T(8,128)S(1)}, u32[]{:S(2)}, u32[]{:S(2)}) collective-permute-start(f32[512,128]{1,0:T(8,128)S(1)} %get-tuple-element.53), channel_id=1, source_target_pairs={{0,8},{1,9},{2,10},{3,11},{4,12},{5,13},{6,14},{7,15},{8,16},{9,17... | collective-permute-start | bytes 786440 | tf_op jit(solution)/shard_map/ppermute | solution.py:317
  28.3 11.0 %collective-permute-start.2 = (f32[128,128]{1,0:T(8,128)S(1)}, f32[128,128]{1,0:T(8,128)S(1)}, u32[]{:S(2)}, u32[]{:S(2)}) collective-permute-start(f32[128,128]{1,0:T(8,128)S(1)} %get-tuple-element.85), channel_id=1, source_target_pairs={{1,16},{2,17},{3,18},{4,19},{5,20},{6,21},{7,22},{9,24},{10,25},{1... | collective-permute-start | bytes 196616 | tf_op jit(solution)/shard_map/ppermute | solution.py:317
  33.5 7.3 %collective-permute-start.4 = (f32[128,128]{1,0:T(8,128)S(1)}, f32[128,128]{1,0:T(8,128)S(1)}, u32[]{:S(2)}, u32[]{:S(2)}) collective-permute-start(f32[128,128]{1,0:T(8,128)S(1)} %get-tuple-element.85), channel_id=1, source_target_pairs={{0,16},{1,17},{2,18},{3,19},{4,20},{5,21},{6,22},{7,23},{8,24},{9,... | collective-permute-start | bytes 196616 | tf_op jit(solution)/shard_map/ppermute | solution.py:317
  33.6 10.9 %collective-permute-start.6 = (f32[128,256]{1,0:T(8,128)S(1)}, f32[128,256]{1,0:T(8,128)S(1)}, u32[]{:S(2)}, u32[]{:S(2)}) collective-permute-start(f32[128,256]{1,0:T(8,128)S(1)} %get-tuple-element.52.mine_probes), channel_id=1, source_target_pairs={{0,8},{1,9},{2,10},{3,11},{4,12},{5,13},{6,14},{7,15},{8,0},{9,1},... | collective-permute-start | bytes 393224 | tf_op jit(solution)/shard_map/ppermute | solution.py:317
  34.8 6.7 %collective-permute-start.7 = (f32[128,128]{1,0:T(8,128)S(1)}, f32[128,128]{1,0:T(8,128)S(1)}, u32[]{:S(2)}, u32[]{:S(2)}) collective-permute-start(f32[128,128]{1,0:T(8,128)S(1)} %get-tuple-element.84.mine), channel_id=1, source_target_pairs={{1,0},{2,1},{3,2},{4,3},{5,4},{6,5},{7,6},{9,8},{10,9},{11,10},{12... | collective-permute-start | bytes 196616 | tf_op jit(solution)/shard_map/ppermute | solution.py:317
  41.1 4.3 %collective-permute-start.5 = (f32[128,128]{1,0:T(8,128)S(1)}, f32[128,128]{1,0:T(8,128)S(1)}, u32[]{:S(2)}, u32[]{:S(2)}) collective-permute-start(f32[128,128]{1,0:T(8,128)S(1)} %shard_map.90.mine), channel_id=1, source_target_pairs={{0,8},{1,9},{2,10},{3,11},{4,12},{5,13},{6,14},{7,15},{8,0},{9,1},... | collective-permute-start | bytes 196616 | tf_op jit(solution)/shard_map/ppermute | solution.py:317
  41.7 7.3 %collective-permute-start.8 = (f32[128,128]{1,0:T(8,128)S(1)}, f32[128,128]{1,0:T(8,128)S(1)}, u32[]{:S(2)}, u32[]{:S(2)}) collective-permute-start(f32[128,128]{1,0:T(8,128)S(1)} %shard_map.92), channel_id=1, source_target_pairs={{0,16},{1,17},{2,18},{3,19},{4,20},{5,21},{6,22},{7,23},{8,24},{9,... | collective-permute-start | bytes 196616 | tf_op jit(solution)/shard_map/ppermute | solution.py:317
  49.1 8.5 %collective-permute-start.10 = (f32[128,256]{1,0:T(8,128)S(1)}, f32[128,256]{1,0:T(8,128)S(1)}, u32[]{:S(2)}, u32[]{:S(2)}) collective-permute-start(f32[128,256]{1,0:T(8,128)S(1)} %get-tuple-element.70.refs_2_), channel_id=1, source_target_pairs={{0,1},{1,0},{2,3},{3,2},{4,5},{5,4},{6,7},{7,6},{8,9},{9,8},{10,11... | collective-permute-start | bytes 393224 | tf_op jit(solution)/shard_map/ppermute | solution.py:317
  49.2 8.4 %collective-permute-start.9 = (f32[128,256]{1,0:T(8,128)S(1)}, f32[128,256]{1,0:T(8,128)S(1)}, u32[]{:S(2)}, u32[]{:S(2)}) collective-permute-start(f32[128,256]{1,0:T(8,128)S(1)} %get-tuple-element.70.refs_2_), channel_id=1, source_target_pairs={{1,2},{2,1},{3,4},{4,3},{5,6},{6,5},{9,10},{10,9},{11,12},{12,11},... | collective-permute-start | bytes 393224 | tf_op jit(solution)/shard_map/ppermute | solution.py:317
  51.6 6.7 %collective-permute-start.13 = (f32[128,128]{1,0:T(8,128)S(1)}, f32[128,128]{1,0:T(8,128)S(1)}, u32[]{:S(2)}, u32[]{:S(2)}) collective-permute-start(f32[128,128]{1,0:T(8,128)S(1)} %get-tuple-element.77), channel_id=1, source_target_pairs={{0,16},{1,17},{2,18},{3,19},{4,20},{5,21},{6,22},{7,23},{8,24},{9,... | collective-permute-start | bytes 196616 | tf_op jit(solution)/shard_map/ppermute | solution.py:317
  53.5 5.5 %collective-permute-start.12 = (f32[128,128]{1,0:T(8,128)S(1)}, f32[128,128]{1,0:T(8,128)S(1)}, u32[]{:S(2)}, u32[]{:S(2)}) collective-permute-start(f32[128,128]{1,0:T(8,128)S(1)} %sub.3.mine_last), channel_id=1, source_target_pairs={{0,8},{1,9},{2,10},{3,11},{4,12},{5,13},{6,14},{7,15},{8,0},{9,1},... | collective-permute-start | bytes 196616 | tf_op jit(solution)/shard_map/ppermute | solution.py:317
  57.9 7.3 %collective-permute-start.11 = (f32[128,128]{1,0:T(8,128)S(1)}, f32[128,128]{1,0:T(8,128)S(1)}, u32[]{:S(2)}, u32[]{:S(2)}) collective-permute-start(f32[128,128]{1,0:T(8,128)S(1)} %get-tuple-element.74.mine.refs_0_), channel_id=1, source_target_pairs={{0,16},{1,17},{2,18},{3,19},{4,20},{5,21},{6,22},{7,23},{8,24},{9,... | collective-permute-start | bytes 196616 | tf_op jit(solution)/shard_map/ppermute | solution.py:317
  59.5 8.9 %collective-permute-start.14 = (f32[128,128]{1,0:T(8,128)S(1)}, f32[128,128]{1,0:T(8,128)S(1)}, u32[]{:S(2)}, u32[]{:S(2)}) collective-permute-start(f32[128,128]{1,0:T(8,128)S(1)} %get-tuple-element.78.refs_1_), channel_id=1, source_target_pairs={{0,16},{1,17},{2,18},{3,19},{4,20},{5,21},{6,22},{7,23},{8,24},{9,... | collective-permute-start | bytes 196616 | tf_op jit(solution)/shard_map/ppermute | solution.py:317
  61.5 6.9 %collective-permute-start.15 = (f32[128,128]{1,0:T(8,128)S(1)}, f32[128,128]{1,0:T(8,128)S(1)}, u32[]{:S(2)}, u32[]{:S(2)}) collective-permute-start(f32[128,128]{1,0:T(8,128)S(1)} %get-tuple-element.79.refs_5_), channel_id=1, source_target_pairs={{0,8},{1,9},{2,10},{3,11},{4,12},{5,13},{6,14},{7,15},{8,0},{9,1},... | collective-permute-start | bytes 196616 | tf_op jit(solution)/shard_map/ppermute | solution.py:317

commit v22 on v19

--- a/solution.py
+++ b/solution.py
@@ -33,6 +33,12 @@
     sub = lax.broadcasted_iota(jnp.int32, (ROWS, size), 0)
     lane = lax.broadcasted_iota(jnp.int32, (ROWS, size), 1)
     rows = [gram[ROWS * i : ROWS * (i + 1), :] for i in range(blocks)]
+    diagonals = [jnp.where(lane == sub + ROWS * i, rows[i], 0.0) for i in range(blocks)]
+    norms = lax.rsqrt(jnp.sum(functools.reduce(jnp.add, diagonals), axis=0, keepdims=True))
+    norms = jnp.broadcast_to(norms, (ROWS, size))
+    for i in range(blocks):
+        own = jnp.sum(jnp.where(lane == sub + ROWS * i, norms, 0.0), axis=1, keepdims=True)
+        rows[i] = rows[i] * norms * own
     scaled = [None] * blocks
     used = 0
 
@@ -112,7 +118,7 @@
         if ahead < blocks:
             waiting = jnp.concatenate(scaled[first:last], axis=0), first, last
     return jnp.concatenate(
-        [jnp.where(lane <= sub + ROWS * k, scaled[k], 0.0) for k in range(blocks)], axis=0
+        [jnp.where(lane <= sub + ROWS * k, scaled[k] * norms, 0.0) for k in range(blocks)], axis=0
     )
 
 

time: 70.1 us -> 70.1 us (level)
  transfers between devices with their start and end apart: 16 -> 16, of which waited for: 6 -> 6; matrix products, arithmetic and copies ran while one was open for 0% -> 0% of each run, Pallas kernels for 27% -> 28%
where the time goes in v22:
time: 70.1 us; the launch traced here: 69.7 us
  starting transfers between devices  31.7 us (45%)
  Pallas kernels  20.8 us (30%)
  waiting for transfers between devices  12.5 us (18%)
  local copies, waits for them, and re-layouts  3.65 us (5%)
  between operations  1.06 us (2%)
    ppermute x16, starting transfers between devices, permuted(): return lax.ppermute(value, BOTH, pairs)  31.7 us
    pallas_call x15, Pallas kernels, call(): pl.pallas_call(kernel, out_shape=outs, in_specs=specs, out_specs=out_spec...  20.8 us
    ppermute x16, waiting for transfers between devices, permuted(): return lax.ppermute(value, BOTH, pairs)  12.5 us
    unnamed x14, local copies, waits for them, and re-layouts  3.63 us
  transfers between devices with their start and end apart: 16, of which 6 were waited for; matrix products, arithmetic and copies ran while one was open for 0% of the time, Pallas kernels for 28%

profile of v22, /device:TPU:4, one launch (start us, length us, event | category | flops | bytes accessed | tf_op | source)
XLA Modules:
  0.0 69.7 jit_solution(6268166211450380234)
XLA Ops:
  0.6 5.8 %collective-permute-start = (f32[512,256]{1,0:T(8,128)}, f32[512,256]{1,0:T(8,128)S(1)}, u32[]{:S(2)}, u32[]{:S(2)}) collective-permute-start(f32[512,256]{1,0:T(8,128)} %probes.5), channel_id=1, source_target_pairs={{1,24},{2,25},{3,26},{4,27},{5,28},{6,29},{7,30},{8,0},{9,1},{10,2... | collective-permute-start | bytes 1572872 | tf_op jit(solution)/shard_map/ppermute | solution.py:322
  6.5 1.6 %copy-done = f32[512,2,512]{2,1,0:T(2,128)S(1)} copy-done((f32[512,2,512]{2,1,0:T(2,128)S(1)}, f32[512,2,512]{2,1,0:T(2,128)}, u32[]{:S(2)}) %copy-start) | copy-done | bytes 2097176
  10.0 1.9 %collective-permute-start.1 = (f32[512,128]{1,0:T(8,128)S(1)}, f32[512,128]{1,0:T(8,128)S(1)}, u32[]{:S(2)}, u32[]{:S(2)}) collective-permute-start(f32[512,128]{1,0:T(8,128)S(1)} %shard_map.87), channel_id=1, source_target_pairs={{0,8},{1,9},{2,10},{3,11},{4,12},{5,13},{6,14},{7,15},{8,16},{9,17... | collective-permute-start | bytes 786440 | tf_op jit(solution)/shard_map/ppermute | solution.py:322
  13.6 1.6 %shard_map.84 = (f32[512,256]{1,0:T(8,128)S(1)}, f32[512,128]{1,0:T(8,128)S(1)}) custom-call(f32[4096,128]{1,0:T(8,128)S(1)} %bitcast.6, f32[512,256]{1,0:T(8,128)S(1)} %copy-done.3, f32[512,256]{1,0:T(8,128)S(1)} %copy-done.2), custom_call_target="tpu_custom_call" | custom-call | flops 805306368 | bytes 3932160 | tf_op jit(solution)/shard_map/pallas_call | solution.py:303
  15.3 3.8 %collective-permute-done.following = f32[512,256]{1,0:T(8,128)S(1)} collective-permute-done((f32[512,256]{1,0:T(8,128)}, f32[512,256]{1,0:T(8,128)S(1)}, u32[]{:S(2)}, u32[]{:S(2)}) %collective-permute-start) | collective-permute-done | bytes 524320 | tf_op jit(solution)/shard_map/ppermute | solution.py:322
  19.1 1.2 %shard_map.86 = (f32[512,128]{1,0:T(8,128)S(1)}, f32[512,128]{1,0:T(8,128)S(1)}, f32[512,128]{1,0:T(8,128)S(1)}) custom-call(f32[4096,128]{1,0:T(8,128)S(1)} %bitcast.7, f32[512,256]{1,0:T(8,128)S(1)} %get-tuple-element.44.rest, f32[512,256]{1,0:T(8,128)S(1)} %collective-permute-done.following, ...), custom_call_target="tpu_custom_call", output_to_operand_aliasing={{2}: (3, {})} | custom-call | flops 805306368 | bytes 4194304 | tf_op jit(solution)/shard_map/pallas_call | solution.py:303
  20.3 1.9 %collective-permute-start.3 = (f32[512,128]{1,0:T(8,128)S(1)}, f32[512,128]{1,0:T(8,128)S(1)}, u32[]{:S(2)}, u32[]{:S(2)}) collective-permute-start(f32[512,128]{1,0:T(8,128)S(1)} %get-tuple-element.53), channel_id=1, source_target_pairs={{0,8},{1,9},{2,10},{3,11},{4,12},{5,13},{6,14},{7,15},{8,16},{9,17... | collective-permute-start | bytes 786440 | tf_op jit(solution)/shard_map/ppermute | solution.py:322
  22.2 2.4 %collective-permute-done.1.handed = f32[512,128]{1,0:T(8,128)S(1)} collective-permute-done((f32[512,128]{1,0:T(8,128)S(1)}, f32[512,128]{1,0:T(8,128)S(1)}, u32[]{:S(2)}, u32[]{:S(2)}) %collective-permute-start.1) | collective-permute-done | bytes 262176 | tf_op jit(solution)/shard_map/ppermute | solution.py:322
  24.6 4.0 %shard_map.88 = (f32[512,128]{1,0:T(8,128)S(1)}, f32[128,128]{1,0:T(8,128)S(1)}, f32[128,128]{1,0:T(8,128)S(1)}, f32[128,256]{1,0:T(8,128)S(1)}) custom-call(f32[512,128]{1,0:T(8,128)S(1)} %get-tuple-element.51.rest, f32[512,128]{1,0:T(8,128)S(1)} %collective-permute-done.1.handed, f32[512,256]{1,0:T(8,128)S(1)} %copy-done.4), custom_call_target="tpu_custom_call" | custom-call | flops 805306368 | bytes 1572864 | tf_op jit(solution)/shard_map/pallas_call | solution.py:303
  28.7 2.6 %collective-permute-start.2 = (f32[128,128]{1,0:T(8,128)S(1)}, f32[128,128]{1,0:T(8,128)S(1)}, u32[]{:S(2)}, u32[]{:S(2)}) collective-permute-start(f32[128,128]{1,0:T(8,128)S(1)} %get-tuple-element.85), channel_id=1, source_target_pairs={{0,16},{1,17},{2,18},{3,19},{4,20},{5,21},{6,22},{7,23},{8,24},{9,... | collective-permute-start | bytes 196616 | tf_op jit(solution)/shard_map/ppermute | solution.py:322
  31.3 2.6 %collective-permute-start.4 = (f32[128,128]{1,0:T(8,128)S(1)}, f32[128,128]{1,0:T(8,128)S(1)}, u32[]{:S(2)}, u32[]{:S(2)}) collective-permute-start(f32[128,128]{1,0:T(8,128)S(1)} %get-tuple-element.85), channel_id=1, source_target_pairs={{1,16},{2,17},{3,18},{4,19},{5,20},{6,21},{7,22},{9,24},{10,25},{1... | collective-permute-start | bytes 196616 | tf_op jit(solution)/shard_map/ppermute | solution.py:322
  33.9 1.6 %collective-permute-start.6 = (f32[128,256]{1,0:T(8,128)S(1)}, f32[128,256]{1,0:T(8,128)S(1)}, u32[]{:S(2)}, u32[]{:S(2)}) collective-permute-start(f32[128,256]{1,0:T(8,128)S(1)} %get-tuple-element.52.mine_probes), channel_id=1, source_target_pairs={{0,8},{1,9},{2,10},{3,11},{4,12},{5,13},{6,14},{7,15},{8,0},{9,1},... | collective-permute-start | bytes 393224 | tf_op jit(solution)/shard_map/ppermute | solution.py:322
  35.5 2.6 %collective-permute-start.7 = (f32[128,128]{1,0:T(8,128)S(1)}, f32[128,128]{1,0:T(8,128)S(1)}, u32[]{:S(2)}, u32[]{:S(2)}) collective-permute-start(f32[128,128]{1,0:T(8,128)S(1)} %get-tuple-element.84.mine), channel_id=1, source_target_pairs={{1,0},{2,1},{3,2},{4,3},{5,4},{6,5},{7,6},{9,8},{10,9},{11,10},{12... | collective-permute-start | bytes 196616 | tf_op jit(solution)/shard_map/ppermute | solution.py:322
  38.2 1.5 %shard_map.89 = (f32[512,128]{1,0:T(8,128)}, f32[128,128]{1,0:T(8,128)S(1)}) custom-call(f32[512,128]{1,0:T(8,128)S(1)} %get-tuple-element.50.rest, f32[512,128]{1,0:T(8,128)S(1)} %collective-permute-done.3.handed, f32[512,128]{1,0:T(8,128)S(1)} %get-tuple-element.55.far, f32[128,128]{1,0:T(8,128)S(1)} %get-tuple-element.56.inverse), custom_call_target="tpu_custom_call" | custom-call | flops 805306368 | bytes 1179648 | tf_op jit(solution)/shard_map/pallas_call | solution.py:303
  42.2 1.4 %collective-permute-start.8 = (f32[128,128]{1,0:T(8,128)S(1)}, f32[128,128]{1,0:T(8,128)S(1)}, u32[]{:S(2)}, u32[]{:S(2)}) collective-permute-start(f32[128,128]{1,0:T(8,128)S(1)} %shard_map.92), channel_id=1, source_target_pairs={{0,16},{1,17},{2,18},{3,19},{4,20},{5,21},{6,22},{7,23},{8,24},{9,... | collective-permute-start | bytes 196616 | tf_op jit(solution)/shard_map/ppermute | solution.py:322
  43.7 1.6 %collective-permute-done.5.theirs = f32[128,128]{1,0:T(8,128)S(1)} collective-permute-done((f32[128,128]{1,0:T(8,128)S(1)}, f32[128,128]{1,0:T(8,128)S(1)}, u32[]{:S(2)}, u32[]{:S(2)}) %collective-permute-start.5) | collective-permute-done | bytes 65568 | tf_op jit(solution)/shard_map/ppermute | solution.py:322
  45.3 3.8 %shard_map.91 = (f32[128,128]{1,0:T(8,128)S(1)}, f32[128,256]{1,0:T(8,128)S(1)}, f32[128,128]{1,0:T(8,128)S(1)}) custom-call(f32[128,128]{1,0:T(8,128)S(1)} %shard_map.90.mine, f32[128,128]{1,0:T(8,128)S(1)} %collective-permute-done.5.theirs, f32[128,256]{1,0:T(8,128)S(1)} %get-tuple-element.52.mine_probes, f32[128,256]{1,0:T(8,128)S(1)} %collective-permute-done.6.theirs_probes), custom_call_target="tpu_custom_call" | custom-call | flops 6442450944 | bytes 655360 | tf_op jit(solution)/shard_map/pallas_call | solution.py:303
  49.1 2.5 %collective-permute-start.9 = (f32[128,256]{1,0:T(8,128)S(1)}, f32[128,256]{1,0:T(8,128)S(1)}, u32[]{:S(2)}, u32[]{:S(2)}) collective-permute-start(f32[128,256]{1,0:T(8,128)S(1)} %get-tuple-element.70.refs_2_), channel_id=1, source_target_pairs={{1,2},{2,1},{3,4},{4,3},{5,6},{6,5},{9,10},{10,9},{11,12},{12,11},... | collective-permute-start | bytes 393224 | tf_op jit(solution)/shard_map/ppermute | solution.py:322
  51.7 2.8 %collective-permute-start.13 = (f32[128,128]{1,0:T(8,128)S(1)}, f32[128,128]{1,0:T(8,128)S(1)}, u32[]{:S(2)}, u32[]{:S(2)}) collective-permute-start(f32[128,128]{1,0:T(8,128)S(1)} %get-tuple-element.77), channel_id=1, source_target_pairs={{0,16},{1,17},{2,18},{3,19},{4,20},{5,21},{6,22},{7,23},{8,24},{9,... | collective-permute-start | bytes 196616 | tf_op jit(solution)/shard_map/ppermute | solution.py:322
  56.6 3.0 %collective-permute-start.11 = (f32[128,128]{1,0:T(8,128)S(1)}, f32[128,128]{1,0:T(8,128)S(1)}, u32[]{:S(2)}, u32[]{:S(2)}) collective-permute-start(f32[128,128]{1,0:T(8,128)S(1)} %get-tuple-element.74.mine.refs_0_), channel_id=1, source_target_pairs={{0,16},{1,17},{2,18},{3,19},{4,20},{5,21},{6,22},{7,23},{8,24},{9,... | collective-permute-start | bytes 196616 | tf_op jit(solution)/shard_map/ppermute | solution.py:322
  60.3 1.6 %collective-permute-start.15 = (f32[128,128]{1,0:T(8,128)S(1)}, f32[128,128]{1,0:T(8,128)S(1)}, u32[]{:S(2)}, u32[]{:S(2)}) collective-permute-start(f32[128,128]{1,0:T(8,128)S(1)} %get-tuple-element.79.refs_5_), channel_id=1, source_target_pairs={{0,8},{1,9},{2,10},{3,11},{4,12},{5,13},{6,14},{7,15},{8,0},{9,1},... | collective-permute-start | bytes 196616 | tf_op jit(solution)/shard_map/ppermute | solution.py:322
  61.9 2.7 %collective-permute-done.11.theirs.refs_3_ = f32[128,128]{1,0:T(8,128)S(1)} collective-permute-done((f32[128,128]{1,0:T(8,128)S(1)}, f32[128,128]{1,0:T(8,128)S(1)}, u32[]{:S(2)}, u32[]{:S(2)}) %collective-permute-start.11) | collective-permute-done | bytes 65568 | tf_op jit(solution)/shard_map/ppermute | solution.py:322
  64.6 3.4 %shard_map.96.inverse = f32[128,128]{1,0:T(8,128)S(1)} custom-call(f32[128,128]{1,0:T(8,128)S(1)} %get-tuple-element.74.mine.refs_0_, f32[128,128]{1,0:T(8,128)S(1)} %collective-permute-done.11.theirs.refs_3_), custom_call_target="tpu_custom_call" | custom-call | bytes 196608 | tf_op jit(solution)/shard_map/pallas_call | solution.py:303
  68.0 1.6 %shard_map.98 = (f32[1,2,256,128]{3,2,1,0:T(8,128)}, f32[1,128,256]{2,1,0:T(8,128)}, f32[1,128,256]{2,1,0:T(8,128)}) custom-call(f32[128,128]{1,0:T(8,128)S(1)} %shard_map.96.inverse, f32[128,128]{1,0:T(8,128)S(1)} %get-tuple-element.74.mine.refs_0_, f32[128,128]{1,0:T(8,128)S(1)} %get-tuple-element.78.refs_1_, f32[128,256]{1,0:T(8,128)S(1)} %get-tuple-element.70.refs_2_, ...), custom_call_target="tpu_custom_call" | custom-call | bytes 1245184 | tf_op jit(solution)/shard_map/pallas_call | solution.py:303
  (39 shorter events, 9.1 us)
Async XLA Ops:
  0.6 11.3 %copy-start.6 = (s32[1,3]{1,0:T(1,128)S(1)}, s32[1,3]{1,0:T(1,128)}, u32[]{:S(2)}) copy-start(s32[1,3]{1,0:T(1,128)} %slots.1) | copy-start | bytes 40
  0.6 18.5 %collective-permute-start = (f32[512,256]{1,0:T(8,128)}, f32[512,256]{1,0:T(8,128)S(1)}, u32[]{:S(2)}, u32[]{:S(2)}) collective-permute-start(f32[512,256]{1,0:T(8,128)} %probes.5), channel_id=1, source_target_pairs={{1,24},{2,25},{3,26},{4,27},{5,28},{6,29},{7,30},{8,0},{9,1},{10,2... | collective-permute-start | bytes 1572872 | tf_op jit(solution)/shard_map/ppermute | solution.py:322
  6.5 1.6 %copy-start = (f32[512,2,512]{2,1,0:T(2,128)S(1)}, f32[512,2,512]{2,1,0:T(2,128)}, u32[]{:S(2)}) copy-start(f32[512,2,512]{2,1,0:T(2,128)} %param.7) | copy-start | bytes 6291460
  8.1 1.0 %copy-start.3 = (f32[512,256]{1,0:T(8,128)S(1)}, f32[512,256]{1,0:T(8,128)}, u32[]{:S(2)}) copy-start(f32[512,256]{1,0:T(8,128)} %probes.5) | copy-start | bytes 1572868
  9.1 4.5 %copy-start.1 = (f32[512,2,512]{2,1,0:T(2,128)S(1)}, f32[512,2,512]{2,1,0:T(2,128)}, u32[]{:S(2)}) copy-start(f32[512,2,512]{2,1,0:T(2,128)} %param.7) | copy-start | bytes 6291460
  9.1 4.5 %copy-start.2 = (f32[512,256]{1,0:T(8,128)S(1)}, f32[512,256]{1,0:T(8,128)}, u32[]{:S(2)}) copy-start(f32[512,256]{1,0:T(8,128)} %samples.1) | copy-start | bytes 1572868
  10.0 14.6 %collective-permute-start.1 = (f32[512,128]{1,0:T(8,128)S(1)}, f32[512,128]{1,0:T(8,128)S(1)}, u32[]{:S(2)}, u32[]{:S(2)}) collective-permute-start(f32[512,128]{1,0:T(8,128)S(1)} %shard_map.87), channel_id=1, source_target_pairs={{0,8},{1,9},{2,10},{3,11},{4,12},{5,13},{6,14},{7,15},{8,16},{9,17... | collective-permute-start | bytes 786440 | tf_op jit(solution)/shard_map/ppermute | solution.py:322
  11.9 1.0 %copy-start.5 = (f32[1,3,2,128,128]{4,3,2,1,0:T(8,128)S(1)}, f32[1,3,2,128,128]{4,3,2,1,0:T(8,128)}, u32[]{:S(2)}) copy-start(f32[1,3,2,128,128]{4,3,2,1,0:T(8,128)} %couplings.1) | copy-start | bytes 1179652
  15.3 9.4 %copy-start.4 = (f32[512,256]{1,0:T(8,128)S(1)}, f32[512,256]{1,0:T(8,128)}, u32[]{:S(2)}) copy-start(f32[512,256]{1,0:T(8,128)} %probes.5) | copy-start | bytes 1572868
  20.3 17.9 %collective-permute-start.3 = (f32[512,128]{1,0:T(8,128)S(1)}, f32[512,128]{1,0:T(8,128)S(1)}, u32[]{:S(2)}, u32[]{:S(2)}) collective-permute-start(f32[512,128]{1,0:T(8,128)S(1)} %get-tuple-element.53), channel_id=1, source_target_pairs={{0,8},{1,9},{2,10},{3,11},{4,12},{5,13},{6,14},{7,15},{8,16},{9,17... | collective-permute-start | bytes 786440 | tf_op jit(solution)/shard_map/ppermute | solution.py:322
  28.7 9.5 %collective-permute-start.2 = (f32[128,128]{1,0:T(8,128)S(1)}, f32[128,128]{1,0:T(8,128)S(1)}, u32[]{:S(2)}, u32[]{:S(2)}) collective-permute-start(f32[128,128]{1,0:T(8,128)S(1)} %get-tuple-element.85), channel_id=1, source_target_pairs={{0,16},{1,17},{2,18},{3,19},{4,20},{5,21},{6,22},{7,23},{8,24},{9,... | collective-permute-start | bytes 196616 | tf_op jit(solution)/shard_map/ppermute | solution.py:322
  31.3 9.4 %collective-permute-start.4 = (f32[128,128]{1,0:T(8,128)S(1)}, f32[128,128]{1,0:T(8,128)S(1)}, u32[]{:S(2)}, u32[]{:S(2)}) collective-permute-start(f32[128,128]{1,0:T(8,128)S(1)} %get-tuple-element.85), channel_id=1, source_target_pairs={{1,16},{2,17},{3,18},{4,19},{5,20},{6,21},{7,22},{9,24},{10,25},{1... | collective-permute-start | bytes 196616 | tf_op jit(solution)/shard_map/ppermute | solution.py:322
  33.9 9.8 %collective-permute-start.6 = (f32[128,256]{1,0:T(8,128)S(1)}, f32[128,256]{1,0:T(8,128)S(1)}, u32[]{:S(2)}, u32[]{:S(2)}) collective-permute-start(f32[128,256]{1,0:T(8,128)S(1)} %get-tuple-element.52.mine_probes), channel_id=1, source_target_pairs={{0,8},{1,9},{2,10},{3,11},{4,12},{5,13},{6,14},{7,15},{8,0},{9,1},... | collective-permute-start | bytes 393224 | tf_op jit(solution)/shard_map/ppermute | solution.py:322
  35.5 6.4 %collective-permute-start.7 = (f32[128,128]{1,0:T(8,128)S(1)}, f32[128,128]{1,0:T(8,128)S(1)}, u32[]{:S(2)}, u32[]{:S(2)}) collective-permute-start(f32[128,128]{1,0:T(8,128)S(1)} %get-tuple-element.84.mine), channel_id=1, source_target_pairs={{1,0},{2,1},{3,2},{4,3},{5,4},{6,5},{7,6},{9,8},{10,9},{11,10},{12... | collective-permute-start | bytes 196616 | tf_op jit(solution)/shard_map/ppermute | solution.py:322
  40.9 4.3 %collective-permute-start.5 = (f32[128,128]{1,0:T(8,128)S(1)}, f32[128,128]{1,0:T(8,128)S(1)}, u32[]{:S(2)}, u32[]{:S(2)}) collective-permute-start(f32[128,128]{1,0:T(8,128)S(1)} %shard_map.90.mine), channel_id=1, source_target_pairs={{0,8},{1,9},{2,10},{3,11},{4,12},{5,13},{6,14},{7,15},{8,0},{9,1},... | collective-permute-start | bytes 196616 | tf_op jit(solution)/shard_map/ppermute | solution.py:322
  42.2 6.8 %collective-permute-start.8 = (f32[128,128]{1,0:T(8,128)S(1)}, f32[128,128]{1,0:T(8,128)S(1)}, u32[]{:S(2)}, u32[]{:S(2)}) collective-permute-start(f32[128,128]{1,0:T(8,128)S(1)} %shard_map.92), channel_id=1, source_target_pairs={{0,16},{1,17},{2,18},{3,19},{4,20},{5,21},{6,22},{7,23},{8,24},{9,... | collective-permute-start | bytes 196616 | tf_op jit(solution)/shard_map/ppermute | solution.py:322
  49.1 6.3 %collective-permute-start.10 = (f32[128,256]{1,0:T(8,128)S(1)}, f32[128,256]{1,0:T(8,128)S(1)}, u32[]{:S(2)}, u32[]{:S(2)}) collective-permute-start(f32[128,256]{1,0:T(8,128)S(1)} %get-tuple-element.70.refs_2_), channel_id=1, source_target_pairs={{0,1},{1,0},{2,3},{3,2},{4,5},{5,4},{6,7},{7,6},{8,9},{9,8},{10,11... | collective-permute-start | bytes 393224 | tf_op jit(solution)/shard_map/ppermute | solution.py:322
  49.1 7.2 %collective-permute-start.9 = (f32[128,256]{1,0:T(8,128)S(1)}, f32[128,256]{1,0:T(8,128)S(1)}, u32[]{:S(2)}, u32[]{:S(2)}) collective-permute-start(f32[128,256]{1,0:T(8,128)S(1)} %get-tuple-element.70.refs_2_), channel_id=1, source_target_pairs={{1,2},{2,1},{3,4},{4,3},{5,6},{6,5},{9,10},{10,9},{11,12},{12,11},... | collective-permute-start | bytes 393224 | tf_op jit(solution)/shard_map/ppermute | solution.py:322
  51.7 7.9 %collective-permute-start.13 = (f32[128,128]{1,0:T(8,128)S(1)}, f32[128,128]{1,0:T(8,128)S(1)}, u32[]{:S(2)}, u32[]{:S(2)}) collective-permute-start(f32[128,128]{1,0:T(8,128)S(1)} %get-tuple-element.77), channel_id=1, source_target_pairs={{0,16},{1,17},{2,18},{3,19},{4,20},{5,21},{6,22},{7,23},{8,24},{9,... | collective-permute-start | bytes 196616 | tf_op jit(solution)/shard_map/ppermute | solution.py:322
  54.5 5.1 %collective-permute-start.12 = (f32[128,128]{1,0:T(8,128)S(1)}, f32[128,128]{1,0:T(8,128)S(1)}, u32[]{:S(2)}, u32[]{:S(2)}) collective-permute-start(f32[128,128]{1,0:T(8,128)S(1)} %sub.3.mine_last), channel_id=1, source_target_pairs={{0,8},{1,9},{2,10},{3,11},{4,12},{5,13},{6,14},{7,15},{8,0},{9,1},... | collective-permute-start | bytes 196616 | tf_op jit(solution)/shard_map/ppermute | solution.py:322
  56.6 7.9 %collective-permute-start.11 = (f32[128,128]{1,0:T(8,128)S(1)}, f32[128,128]{1,0:T(8,128)S(1)}, u32[]{:S(2)}, u32[]{:S(2)}) collective-permute-start(f32[128,128]{1,0:T(8,128)S(1)} %get-tuple-element.74.mine.refs_0_), channel_id=1, source_target_pairs={{0,16},{1,17},{2,18},{3,19},{4,20},{5,21},{6,22},{7,23},{8,24},{9,... | collective-permute-start | bytes 196616 | tf_op jit(solution)/shard_map/ppermute | solution.py:322
  60.2 7.8 %collective-permute-start.14 = (f32[128,128]{1,0:T(8,128)S(1)}, f32[128,128]{1,0:T(8,128)S(1)}, u32[]{:S(2)}, u32[]{:S(2)}) collective-permute-start(f32[128,128]{1,0:T(8,128)S(1)} %get-tuple-element.78.refs_1_), channel_id=1, source_target_pairs={{0,16},{1,17},{2,18},{3,19},{4,20},{5,21},{6,22},{7,23},{8,24},{9,... | collective-permute-start | bytes 196616 | tf_op jit(solution)/shard_map/ppermute | solution.py:322
  60.3 7.7 %collective-permute-start.15 = (f32[128,128]{1,0:T(8,128)S(1)}, f32[128,128]{1,0:T(8,128)S(1)}, u32[]{:S(2)}, u32[]{:S(2)}) collective-permute-start(f32[128,128]{1,0:T(8,128)S(1)} %get-tuple-element.79.refs_5_), channel_id=1, source_target_pairs={{0,8},{1,9},{2,10},{3,11},{4,12},{5,13},{6,14},{7,15},{8,0},{9,1},... | collective-permute-start | bytes 196616 | tf_op jit(solution)/shard_map/ppermute | solution.py:322
